TPU v7x, 32 devices: a whole 2x2x4 slice. The times are simulated.
32 devices in a mesh: dp: 2 (over y), expert: 8 (over z, x), shard: 2 (over core).
Axes of the slice: x: 2, y: 2, z: 4, core: 2. Of those that a mesh axis runs over, the one named last changes fastest.
Arguments:
- hidden_in: bfloat16 [12288, 1536], P(('dp', 'expert', 'shard')), may hold values from -6 to 6
- cotangent: bfloat16 [12288, 1536], P(('dp', 'expert', 'shard')), may hold values from -6 to 6
- deal_order: int32 [32, 384], P(('dp', 'expert', 'shard')), may hold values from 0 to 383, each once within a row
- lengths: int32 [32, 3], P(('dp', 'expert', 'shard')), may hold values from 1 to 288, 384 in all within a row
- routes: int32 [12288, 4], P(('dp', 'expert', 'shard')), may hold values from 0 to 7, all different within a row; in each aligned block of 384 rows (0 to 383, 384 to 767, ...) at most 288 rows name the same one
- attention_gain: bfloat16 [1536], P('shard'), may hold values from 0.5 to 1.5
- expert_gain: bfloat16 [1536], P('shard'), may hold values from 0.5 to 1.5
- qkv_weight: bfloat16 [1536, 2048], P('shard'), may hold values from -0.15625 to 0.15625
- out_weight: bfloat16 [1536, 1536], P('shard'), may hold values from -0.75 to 0.75
- router_weight: bfloat16 [1536, 8], P('shard'), may hold values from -0.078125 to 0.078125
- gate_up_weight: bfloat16 [8, 1536, 1536], P('expert'), may hold values from -0.15625 to 0.15625
- down_weight: bfloat16 [8, 768, 1536], P('expert'), may hold values from -0.4375 to 0.4375
Outputs:
- layer_out: bfloat16 [12288, 1536], P(('dp', 'expert', 'shard'))
- input_gradient: bfloat16 [12288, 1536], P(('dp', 'expert', 'shard'))
- attention_gain_gradient: float32 [1536], P('shard')
- expert_gain_gradient: float32 [1536], P('shard')
- qkv_gradient: float32 [1536, 2048], P('shard')
- out_gradient: float32 [1536, 1536], P('shard')
- router_gradient: float32 [1536, 8], P('shard')
- gate_up_gradient: float32 [8, 1536, 1536], P('expert', ('dp', 'shard'))
- down_gradient: float32 [8, 768, 1536], P('expert', ('dp', 'shard'))
Inputs may be any that keep to these rules, and one draw needn't show every extreme that they name: `deal_order`: each device's row is a permutation of 0 to 383. Each device's 3 lengths sum to 384, and the largest is 288. `routes`: each token names 4 different experts; among the rows of one device no expert is named more than 288 times, a bound that some block reaches.
All inputs are finite; a program needn't handle non-finite values.
Results may differ from a plain program's by a relative error of at most 0.017.
Values may be sent and summed in bfloat16 or wider, within the bound.
No kernel may reach another device: no remote copies, remote signals or barrier semaphores. Data moves between devices by JAX's collectives and lax.ppermute only.
A program may use at most 256 MiB of HBM per device.

v0:
```python
import jax
import jax.numpy as jnp
from jax import lax
from jax.sharding import PartitionSpec as P

QUERY_HEADS = 12
KEY_VALUE_HEADS = 2
HEAD_SIZE = 128
TOP = 4


EPS = 1e-06
THETA = 1000000.0


def positions_of(lengths_dev, count_of_rows):
    seq_ends = jnp.cumsum(lengths_dev)
    starts = seq_ends - lengths_dev
    places = jnp.arange(count_of_rows, dtype=jnp.int32)
    segment = jnp.sum((places[:, None] >= seq_ends[None, :]).astype(jnp.int32), axis=1)
    member = segment[:, None] == jnp.arange(lengths_dev.shape[0], dtype=jnp.int32)[None, :]
    start_of = jnp.sum(jnp.where(member, starts[None, :], 0), axis=1)
    return (segment, places - start_of)


def apply_rotation(field, token_position, direction):
    half_dim = field.shape[-1] // 2
    frequency = THETA ** (-jnp.arange(half_dim, dtype=jnp.float32) / half_dim)
    angles = token_position.astype(jnp.float32)[:, None] * frequency[None, :]
    cosine = jnp.cos(angles)[:, None, :]
    sine_term = direction * jnp.sin(angles)[:, None, :]
    lead_part = field[..., :half_dim]
    tail_part = field[..., half_dim:]
    return jnp.concatenate(
        [lead_part * cosine - tail_part * sine_term, tail_part * cosine + lead_part * sine_term],
        axis=-1,
    )


def masked_scores(query_block, key_matrix_rows, segment_block, segment, row_start):
    raw_scores = jnp.einsum(
        "ihgd,jhd->hgij", query_block, key_matrix_rows, preferred_element_type=jnp.float32
    ) * HEAD_SIZE ** (-0.5)
    query_at = row_start + jnp.arange(query_block.shape[0], dtype=jnp.int32)
    key_at = jnp.arange(key_matrix_rows.shape[0], dtype=jnp.int32)
    allowed = (segment_block[:, None] == segment[None, :]) & (key_at[None, :] <= query_at[:, None])
    return jnp.where(allowed, raw_scores, -1e30)


def norm_back(field, inv_scale, gain_vec, grad_normed):
    scaled = grad_normed * gain_vec
    grad_field = inv_scale * scaled - field * inv_scale**3 * jnp.mean(
        scaled * field, axis=1, keepdims=True
    )
    grad_gain = jnp.sum(field * inv_scale * grad_normed, axis=0)
    return (grad_field, grad_gain)


def activate(gate_up):
    hidden_width = gate_up.shape[1] // 2
    return jax.nn.gelu(gate_up[:, :hidden_width], approximate=True) * gate_up[:, hidden_width:]


def shards(
    hidden_in,
    cotangent,
    deal_order,
    lengths,
    routes,
    attention_gain,
    expert_gain,
    qkv_weight,
    out_weight,
    router_weight,
    gate_up_weight,
    down_weight,
):
    count_of_rows = hidden_in.shape[0]
    model_width = hidden_in.shape[1]
    head_groups = QUERY_HEADS // KEY_VALUE_HEADS
    arrived_in, arrived_ct = (
        lax.all_to_all(hidden_in, "dp", split_axis=0, concat_axis=0, tiled=True),
        lax.all_to_all(cotangent, "dp", split_axis=0, concat_axis=0, tiled=True),
    )
    deal_rows = deal_order[0]
    tokens = arrived_in[deal_rows]
    upstream = arrived_ct[deal_rows].astype(jnp.float32)
    gain_first, gain_second, full_qkv, full_out, full_router = (
        lax.all_gather(attention_gain, "shard", axis=0, tiled=True),
        lax.all_gather(expert_gain, "shard", axis=0, tiled=True),
        lax.all_gather(qkv_weight, "shard", axis=0, tiled=True),
        lax.all_gather(out_weight, "shard", axis=0, tiled=True),
        lax.all_gather(router_weight, "shard", axis=0, tiled=True),
    )
    gain_first = gain_first.astype(jnp.float32)
    gain_second = gain_second.astype(jnp.float32)
    residual = tokens.astype(jnp.float32)
    inv_first = lax.rsqrt(jnp.mean(residual * residual, axis=1, keepdims=True) + EPS)
    normed_attn = (residual * inv_first * gain_first).astype(jnp.bfloat16)
    projected_rows = jnp.dot(normed_attn, full_qkv, preferred_element_type=jnp.float32)
    segment, token_position = positions_of(lengths[0], count_of_rows)
    query_matrix_rows = (
        apply_rotation(
            projected_rows[:, : QUERY_HEADS * HEAD_SIZE].reshape(
                count_of_rows, QUERY_HEADS, HEAD_SIZE
            ),
            token_position,
            1.0,
        )
        .astype(jnp.bfloat16)
        .reshape(count_of_rows, KEY_VALUE_HEADS, head_groups, HEAD_SIZE)
    )
    key_matrix_rows = apply_rotation(
        projected_rows[
            :, QUERY_HEADS * HEAD_SIZE : (QUERY_HEADS + KEY_VALUE_HEADS) * HEAD_SIZE
        ].reshape(count_of_rows, KEY_VALUE_HEADS, HEAD_SIZE),
        token_position,
        1.0,
    ).astype(jnp.bfloat16)
    value_matrix_rows = (
        projected_rows[:, (QUERY_HEADS + KEY_VALUE_HEADS) * HEAD_SIZE :]
        .reshape(count_of_rows, KEY_VALUE_HEADS, HEAD_SIZE)
        .astype(jnp.bfloat16)
    )
    block_rows = min(count_of_rows, 512)
    block_starts = jnp.arange(count_of_rows // block_rows, dtype=jnp.int32) * block_rows

    def forward_block(row_start):
        scores = masked_scores(query_matrix_rows, key_matrix_rows, segment, segment, row_start)
        row_max = jnp.max(scores, axis=-1, keepdims=True)
        exp_scores = jnp.exp(scores - row_max)
        exp_total = jnp.sum(exp_scores, axis=-1, keepdims=True)
        soft_probs = (exp_scores / exp_total).astype(jnp.bfloat16)
        mix_block = jnp.einsum(
            "hgij,jhd->ihgd", soft_probs, value_matrix_rows, preferred_element_type=jnp.float32
        )
        return (mix_block, (row_max + jnp.log(exp_total))[..., 0])

    mix_blocks, logsum = lax.map(forward_block, block_starts)
    attn_mix = mix_blocks.reshape(count_of_rows, QUERY_HEADS * HEAD_SIZE).astype(jnp.bfloat16)
    middle = residual + jnp.dot(attn_mix, full_out, preferred_element_type=jnp.float32)
    inv_second = lax.rsqrt(jnp.mean(middle * middle, axis=1, keepdims=True) + EPS)
    normed_moe = (middle * inv_second * gain_second).astype(jnp.bfloat16)
    logits = jnp.dot(normed_moe, full_router, preferred_element_type=jnp.float32)
    gate_probs = jax.nn.softmax(jnp.take_along_axis(logits, routes, axis=1), axis=-1)
    expert_count = full_router.shape[1]
    peer_count = lax.axis_size("expert")
    capacity = min(count_of_rows, max(2, 3 * count_of_rows * TOP // (2 * expert_count)))
    flat_routes = routes.reshape(-1)
    expert_ids = jnp.arange(expert_count, dtype=jnp.int32)
    onehot = (flat_routes[:, None] == expert_ids[None, :]).astype(jnp.int32)
    slot_rank = jnp.sum(jnp.cumsum(onehot, axis=0) * onehot, axis=1) - 1
    target = flat_routes * capacity + slot_rank
    pair_count = count_of_rows * TOP
    slot_pair = (
        jnp.full((expert_count * capacity,), pair_count, jnp.int32)
        .at[target]
        .set(jnp.arange(pair_count, dtype=jnp.int32))
    )
    padded = jnp.concatenate([normed_moe, jnp.zeros((1, model_width), jnp.bfloat16)], axis=0)
    sending = padded[slot_pair // TOP].reshape(peer_count, capacity, model_width)
    received = lax.all_to_all(sending, "expert", split_axis=0, concat_axis=0, tiled=True)
    rows_in = received.reshape(peer_count * capacity, model_width)
    gate_up = jnp.dot(rows_in, gate_up_weight[0], preferred_element_type=jnp.float32)
    hidden_rows = activate(gate_up).astype(jnp.bfloat16)
    expert_out = jnp.dot(hidden_rows, down_weight[0], preferred_element_type=jnp.float32).astype(
        jnp.bfloat16
    )
    returned = lax.all_to_all(
        expert_out.reshape(peer_count, capacity, model_width),
        "expert",
        split_axis=0,
        concat_axis=0,
        tiled=True,
    )
    per_pair = returned.reshape(peer_count * capacity, model_width)[target].reshape(
        count_of_rows, TOP, model_width
    )
    expert_sum = jnp.zeros((count_of_rows, model_width), jnp.float32)
    for choice_slot in range(TOP):
        expert_sum = expert_sum + gate_probs[:, choice_slot : choice_slot + 1] * per_pair[
            :, choice_slot
        ].astype(jnp.float32)
    final_rows = middle + expert_sum
    grad_pairs = (gate_probs[:, :, None] * upstream[:, None, :]).astype(jnp.bfloat16)
    grad_gates = jnp.stack(
        [
            jnp.sum(per_pair[:, choice_slot].astype(jnp.float32) * upstream, axis=1)
            for choice_slot in range(TOP)
        ],
        axis=1,
    )
    padded_grad = jnp.concatenate(
        [grad_pairs.reshape(pair_count, model_width), jnp.zeros((1, model_width), jnp.bfloat16)],
        axis=0,
    )
    sending_back = padded_grad[slot_pair].reshape(peer_count, capacity, model_width)
    grad_rows = lax.all_to_all(
        sending_back, "expert", split_axis=0, concat_axis=0, tiled=True
    ).reshape(peer_count * capacity, model_width)
    grad_hidden = jnp.dot(grad_rows, down_weight[0].T, preferred_element_type=jnp.float32)
    grad_gate_up = jax.vjp(activate, gate_up)[1](grad_hidden)[0].astype(jnp.bfloat16)
    term_down = jnp.dot(hidden_rows.T, grad_rows, preferred_element_type=jnp.float32)
    term_gate_up = jnp.dot(rows_in.T, grad_gate_up, preferred_element_type=jnp.float32)
    grad_rows_in = jnp.dot(
        grad_gate_up, gate_up_weight[0].T, preferred_element_type=jnp.float32
    ).astype(jnp.bfloat16)
    back_rows = lax.all_to_all(
        grad_rows_in.reshape(peer_count, capacity, model_width),
        "expert",
        split_axis=0,
        concat_axis=0,
        tiled=True,
    )
    back_pairs = back_rows.reshape(peer_count * capacity, model_width)[target].reshape(
        count_of_rows, TOP, model_width
    )
    grad_normed = jnp.zeros((count_of_rows, model_width), jnp.float32)
    for choice_slot in range(TOP):
        grad_normed = grad_normed + back_pairs[:, choice_slot].astype(jnp.float32)
    mean_term = jnp.sum(gate_probs * grad_gates, axis=1, keepdims=True)
    grad_chosen = gate_probs * (grad_gates - mean_term)
    grad_logits = jnp.sum(
        jnp.where(routes[:, :, None] == expert_ids[None, None, :], grad_chosen[:, :, None], 0.0),
        axis=1,
    ).astype(jnp.bfloat16)
    term_router = jnp.dot(normed_moe.T, grad_logits, preferred_element_type=jnp.float32)
    grad_normed = grad_normed + jnp.dot(
        grad_logits, full_router.T, preferred_element_type=jnp.float32
    )
    grad_middle_norm, term_gain_second = norm_back(middle, inv_second, gain_second, grad_normed)
    grad_middle = upstream + grad_middle_norm
    grad_attn_out = grad_middle.astype(jnp.bfloat16)
    term_out = jnp.dot(attn_mix.T, grad_attn_out, preferred_element_type=jnp.float32)
    grad_mix = (
        jnp.dot(grad_attn_out, full_out.T, preferred_element_type=jnp.float32)
        .astype(jnp.bfloat16)
        .reshape(count_of_rows, KEY_VALUE_HEADS, head_groups, HEAD_SIZE)
    )

    def backward_block(accums, inputs):
        acc_key, value_accumulator = accums
        row_start, logsum_block = inputs
        scores = masked_scores(query_matrix_rows, key_matrix_rows, segment, segment, row_start)
        soft_probs = jnp.exp(scores - logsum_block[..., None])
        grad_probs = jnp.einsum(
            "ihgd,jhd->hgij", grad_mix, value_matrix_rows, preferred_element_type=jnp.float32
        )
        value_accumulator = value_accumulator + jnp.einsum(
            "hgij,ihgd->jhd",
            soft_probs.astype(jnp.bfloat16),
            grad_mix,
            preferred_element_type=jnp.float32,
        )
        grad_scores = (
            soft_probs * (grad_probs - jnp.sum(soft_probs * grad_probs, axis=-1, keepdims=True))
        ).astype(jnp.bfloat16)
        grad_query = HEAD_SIZE ** (-0.5) * jnp.einsum(
            "hgij,jhd->ihgd", grad_scores, key_matrix_rows, preferred_element_type=jnp.float32
        )
        acc_key = acc_key + HEAD_SIZE ** (-0.5) * jnp.einsum(
            "hgij,ihgd->jhd", grad_scores, query_matrix_rows, preferred_element_type=jnp.float32
        )
        return ((acc_key, value_accumulator), grad_query)

    zero_key_value = jnp.zeros((count_of_rows, KEY_VALUE_HEADS, HEAD_SIZE), jnp.float32)
    (acc_key, value_accumulator), grad_query = lax.scan(
        backward_block, (zero_key_value, zero_key_value), (block_starts, logsum)
    )
    grad_query = apply_rotation(
        grad_query.reshape(count_of_rows, QUERY_HEADS, HEAD_SIZE), token_position, -1.0
    )
    key_gradient = apply_rotation(acc_key, token_position, -1.0)
    grad_projected = jnp.concatenate(
        [
            grad_query.reshape(count_of_rows, QUERY_HEADS * HEAD_SIZE),
            key_gradient.reshape(count_of_rows, KEY_VALUE_HEADS * HEAD_SIZE),
            value_accumulator.reshape(count_of_rows, KEY_VALUE_HEADS * HEAD_SIZE),
        ],
        axis=1,
    ).astype(jnp.bfloat16)
    term_qkv = jnp.dot(normed_attn.T, grad_projected, preferred_element_type=jnp.float32)
    grad_normed_attn = jnp.dot(grad_projected, full_qkv.T, preferred_element_type=jnp.float32)
    grad_resid_norm, term_gain_first = norm_back(residual, inv_first, gain_first, grad_normed_attn)
    grad_tokens = (grad_middle + grad_resid_norm).astype(jnp.bfloat16)
    inverse = (
        jnp.zeros((count_of_rows,), jnp.int32)
        .at[deal_rows]
        .set(jnp.arange(count_of_rows, dtype=jnp.int32))
    )
    layer_out, input_gradient = (
        lax.all_to_all(
            final_rows.astype(jnp.bfloat16)[inverse], "dp", split_axis=0, concat_axis=0, tiled=True
        ),
        lax.all_to_all(grad_tokens[inverse], "dp", split_axis=0, concat_axis=0, tiled=True),
    )
    shard_terms = (
        lax.psum_scatter(
            term_gain_first.astype(jnp.bfloat16), "shard", scatter_dimension=0, tiled=True
        ).astype(jnp.float32),
        lax.psum_scatter(
            term_gain_second.astype(jnp.bfloat16), "shard", scatter_dimension=0, tiled=True
        ).astype(jnp.float32),
        lax.psum_scatter(
            term_qkv.astype(jnp.bfloat16), "shard", scatter_dimension=0, tiled=True
        ).astype(jnp.float32),
        lax.psum_scatter(
            term_out.astype(jnp.bfloat16), "shard", scatter_dimension=0, tiled=True
        ).astype(jnp.float32),
        lax.psum_scatter(
            term_router.astype(jnp.bfloat16), "shard", scatter_dimension=0, tiled=True
        ).astype(jnp.float32),
    )
    gain_first_grad, gain_second_grad, qkv_grad, out_grad, router_grad = lax.psum(
        (shard_terms[0], shard_terms[1], shard_terms[2], shard_terms[3], shard_terms[4]),
        ("dp", "expert"),
    )
    gate_up_grad, down_grad = (
        lax.psum_scatter(
            term_gate_up[None].astype(jnp.bfloat16),
            ("dp", "shard"),
            scatter_dimension=1,
            tiled=True,
        ).astype(jnp.float32),
        lax.psum_scatter(
            term_down[None].astype(jnp.bfloat16), ("dp", "shard"), scatter_dimension=1, tiled=True
        ).astype(jnp.float32),
    )
    return (
        layer_out,
        input_gradient,
        gain_first_grad,
        gain_second_grad,
        qkv_grad,
        out_grad,
        router_grad,
        gate_up_grad,
        down_grad,
    )


def solution(mesh):
    return jax.shard_map(
        shards,
        mesh=mesh,
        in_specs=(
            P(("dp", "expert", "shard"), None),
            P(("dp", "expert", "shard"), None),
            P(("dp", "expert", "shard"), None),
            P(("dp", "expert", "shard"), None),
            P(("dp", "expert", "shard"), None),
            P("shard"),
            P("shard"),
            P("shard", None),
            P("shard", None),
            P("shard", None),
            P("expert", None, None),
            P("expert", None, None),
        ),
        out_specs=(
            P(("dp", "expert", "shard"), None),
            P(("dp", "expert", "shard"), None),
            P("shard"),
            P("shard"),
            P("shard", None),
            P("shard", None),
            P("shard", None),
            P("expert", ("dp", "shard"), None),
            P("expert", ("dp", "shard"), None),
        ),
        check_vma=False,
    )
```

profile of v0, /device:TPU:0, one launch (start us, length us, event | category | flops | bytes accessed | tf_op | source)
XLA Modules:
  0.0 1499.1 jit_solution(5756195884709320204)
XLA Ops:
  7.9 4.2 all-to-all-start
  33.1 5.1 reduce-window.11
  43.7 1.8 broadcast_multiply_fusion
  52.8 7.1 scatter_custom_fusion
  62.8 2.9 gather_fusion
  67.9 5.1 fusion.57
  75.5 3.1 copy.203
  79.5 3.0 subtract_convert_fusion.1
  84.1 2.5 copy.205
  89.5 2.1 fusion.90
  92.6 1.8 copy-done.2
  94.6 2.5 fusion.43
  97.1 4.9 multiply_reduce_fusion.2
  105.1 16.6 %gather_fusion.1 = bf16[2304,1536]{1,0:T(8,128)(2,1)} fusion(bf16[385,1536]{1,0:T(8,128)(2,1)} %concatenate.37, s32[3072]{0:T(1024)S(1)} %copy-done.63), kind=kCustom, calls=%fused_computation.1 | custom fusion | bytes 14164992 | tf_op jit(solution)/shard_map/gather | solution.py:161
  121.6 162.0 %all_to_all.68 = bf16[8,288,1536]{2,1,0:T(8,128)(2,1)} all-to-all(bf16[8,288,1536]{2,1,0:T(8,128)(2,1)} %bitcast.172), channel_id=1, replica_groups=mesh['dp'=2,'expert'=8,'shard'=2] {'expert'}, dimensions={0} | all-to-all | bytes 14155776 | tf_op jit(solution)/shard_map/all_to_all | solution.py:162
  283.6 3.6 all-to-all-start.4
  287.3 15.0 fusion.13
  302.2 2.5 multiply_convert_fusion.1
  304.8 2.5 copy-done.19
  309.1 7.6 convolution_convert_fusion.1
  316.7 4.8 all-to-all-start.2
  323.5 3.1 all_gather.19
  327.9 3.4 gather_fusion.4
  331.3 6.1 mul.510
  337.3 11.8 mul.511
  350.8 9.4 gather_fusion.8
  361.2 114.5 %all-to-all-done.2 = bf16[8,288,1536]{2,1,0:T(8,128)(2,1)} async-done(((bf16[8,288,1536]{2,1,0:T(8,128)(2,1)}), bf16[8,288,1536]{2,1,0:T(8,128)(2,1)}, u32[]{:S(2)}, u32[]{:S(2)}) %all-to-all-start.2) | async-done | bytes 7077920 | tf_op jit(solution)/shard_map/all_to_all | solution.py:169
  475.7 14.3 gather_fusion.2
  490.0 8.8 reshape.420
  498.9 15.2 %fusion.88 = (bf16[384,1,1536]{2,1,0:T(2,128)(2,1)S(1)}, bf16[384,1,1536]{2,1,0:T(2,128)(2,1)S(1)}, bf16[384,1,1536]{2,1,0:T(2,128)(2,1)S(1)}, bf16[384,1,1536]{2,1,0:T(2,128)(2,1)S(1)}) fusion(bf16[384,4,1536]{2,1,0:T(4,128)(2,1)} %reshape.420), kind=kLoop, calls=%fused_computation.207 | loop fusion | bytes 9437184 | tf_op jit(solution)/shard_map/slice | solution.py:181
  521.0 4.2 multiply_convert_fusion
  525.3 2.5 concatenate.38
  527.8 18.1 %gather_fusion.5 = bf16[2304,1536]{1,0:T(8,128)(2,1)} fusion(bf16[1537,1536]{1,0:T(8,128)(2,1)} %concatenate.38, s32[3072]{0:T(1024)} %get-tuple-element.122), kind=kCustom, calls=%fused_computation.5 | custom fusion | bytes 14164992 | tf_op jit(solution)/shard_map/gather | solution.py:197
  545.9 158.8 %all_to_all.69 = bf16[8,288,1536]{2,1,0:T(8,128)(2,1)S(1)} all-to-all(bf16[8,288,1536]{2,1,0:T(8,128)(2,1)} %bitcast.173), channel_id=1, replica_groups=mesh['dp'=2,'expert'=8,'shard'=2] {'expert'}, dimensions={0} | all-to-all | bytes 14155776 | tf_op jit(solution)/shard_map/all_to_all | solution.py:198
  704.7 18.1 %fusion.22 = (f32[2304,768]{1,0:T(8,128)}, f32[2304,768]{1,0:T(8,128)}) fusion(f32[2304,1536]{1,0:T(8,128)} %copy-done.19, bf16[2304,1536]{1,0:T(8,128)(2,1)S(1)} %bitcast.186, bf16[1,768,1536]{2,1,0:T(8,128)(2,1)S(1)} %copy-done), kind=kOutput, calls=%fused_computation.66 | convolution fusion | flops 5474746368 | bytes 37748736 | tf_op jit(solution)/shard_map/dot_general | solution.py:201
  722.8 17.7 %convolution_convert_fusion = bf16[2304,1536]{1,0:T(8,128)(2,1)} fusion(bf16[1,1536,1536]{2,1,0:T(8,128)(2,1)} %param.22, f32[2304,768]{1,0:T(8,128)} %get-tuple-element.84, f32[2304,768]{1,0:T(8,128)} %get-tuple-element.83), kind=kOutput, calls=%fused_computation.12 | convolution fusion | flops 10882252800 | bytes 25952256 | tf_op jit(solution)/shard_map/dot_general | solution.py:205
  740.6 5.0 all-to-all-start.6
  746.6 10.4 fusion.19
  757.1 18.6 %fusion.9 = bf16[1,1536,1536]{2,1,0:T(8,128)(2,1)} fusion(bf16[2304,1536]{1,0:T(8,128)(2,1)} %bitcast.183, f32[2304,768]{1,0:T(8,128)} %get-tuple-element.84, f32[2304,768]{1,0:T(8,128)} %get-tuple-element.83), kind=kOutput, calls=%fused_computation.37 | convolution fusion | flops 10881073152 | bytes 25952256 | tf_op jit(solution)/shard_map/dot_general | solution.py:204
  776.4 123.2 %all-to-all-done.6 = bf16[8,288,1536]{2,1,0:T(8,128)(2,1)} async-done(((bf16[8,288,1536]{2,1,0:T(8,128)(2,1)}), bf16[8,288,1536]{2,1,0:T(8,128)(2,1)}, u32[]{:S(2)}, u32[]{:S(2)}) %all-to-all-start.6) | async-done | bytes 7077920 | tf_op jit(solution)/shard_map/all_to_all | solution.py:208
  899.6 14.7 gather_fusion.6
  914.3 8.8 reshape.425
  923.2 15.2 %fusion.87 = (bf16[384,1,1536]{2,1,0:T(2,128)(2,1)S(1)}, bf16[384,1,1536]{2,1,0:T(2,128)(2,1)S(1)}, bf16[384,1,1536]{2,1,0:T(2,128)(2,1)S(1)}, bf16[384,1,1536]{2,1,0:T(2,128)(2,1)S(1)}) fusion(bf16[384,4,1536]{2,1,0:T(4,128)(2,1)} %reshape.425), kind=kLoop, calls=%fused_computation.206 | loop fusion | bytes 9437184 | tf_op jit(solution)/shard_map/slice | solution.py:220
  942.2 2.0 convert_add_fusion.1
  945.7 4.2 convolution_convert_fusion.2
  952.2 5.1 convolution_convert_fusion.6
  958.2 8.3 fusion.6
  966.6 4.5 fusion.8
  971.2 3.5 fusion.48
  975.7 3.0 convolution_multiply_fusion
  980.0 4.6 fusion.49
  984.6 6.8 convolution_convert_fusion.3
  991.5 3.0 scatter_custom_fusion.1
  994.6 2.8 gather_fusion.3
  997.4 4.0 all-to-all-start.3
  1001.5 7.7 fusion.24
  1009.8 2.8 gather_fusion.7
  1012.6 2.9 all-to-all-done.3
  1015.5 3.6 all-to-all-start.7
  1020.4 2.2 convert_element_type.245
  1022.7 3.0 convert_element_type.242
  1025.6 2.5 all-reduce.7
  1028.3 4.0 all-to-all-done.7
  1032.3 457.1 %all-reduce.9 = (f32[768]{0:T(1024)}, f32[768]{0:T(1024)}, f32[768,2048]{1,0:T(8,128)}, f32[768,1536]{1,0:T(8,128)}, f32[768,8]{0,1:T(8,128)}) all-reduce(f32[768]{0:T(1024)S(1)} %dynamic-slice_convert_fusion.1, f32[768]{0:T(1024)S(1)} %dynamic-slice_convert_fusion, ...), channel_id=1, replica_groups=mesh['dp'=2,'expert'=8,'shard'=2] {'dp','expert'}, use_global_device_ids=true, to_apply=%region_25.26 | all-reduce | flops 2760192 | bytes 16564224 | tf_op jit(solution)/shard_map/psum | solution.py:314
  (300 shorter events, 82.5 us)
Async XLA Ops:
  7.2 301.9 %copy-start = (bf16[1,768,1536]{2,1,0:T(8,128)(2,1)S(1)}, bf16[1,768,1536]{2,1,0:T(8,128)(2,1)}, u32[]{:S(2)}) copy-start(bf16[1,768,1536]{2,1,0:T(8,128)(2,1)} %param.23) | copy-start | bytes 7077892
  7.2 60.7 %all-gather.5.cloned.1.call-start = ((), (), s32[]{:S(2)}) async-start(), calls=%async_computation.13 | async-start | bytes 9437184 | tf_op jit(solution)/shard_map/all_gather | solution.py:91
  7.9 5.0 copy-start.52
  7.9 54.9 %all-to-all-start = ((bf16[2,192,1536]{2,1,0:T(8,128)(2,1)}), bf16[2,192,1536]{2,1,0:T(8,128)(2,1)S(1)}, u32[]{:S(2)}, u32[]{:S(2)}) async-start(bf16[2,192,1536]{2,1,0:T(8,128)(2,1)} %bitcast.193), calls=%async_computation | async-start | bytes 2359296 | tf_op jit(solution)/shard_map/all_to_all | solution.py:82
  12.2 84.9 %all-gather.7.cloned.1.call-start = ((), (), s32[]{:S(2)}) async-start(), calls=%async_computation.14 | async-start | bytes 7077888 | tf_op jit(solution)/shard_map/all_gather | solution.py:92
  48.8 53.8 %copy-start.57 = (f32[1536]{0:T(1024)}, f32[1536]{0:T(1024)S(1)}, u32[]{:S(2)}) copy-start(f32[1536]{0:T(1024)S(1)} %reshape.535) | copy-start | bytes 18436
  67.9 5.1 copy-start.82
  75.5 4.0 copy-start.37
  75.5 4.0 copy-start.44
  84.1 5.4 copy-start.22
  283.6 33.1 %all-to-all-start.4 = ((bf16[2,192,1536]{2,1,0:T(8,128)(2,1)}), bf16[2,192,1536]{2,1,0:T(8,128)(2,1)S(1)}, u32[]{:S(2)}, u32[]{:S(2)}) async-start(bf16[2,192,1536]{2,1,0:T(8,128)(2,1)} %bitcast.194), calls=%async_computation.4 | async-start | bytes 2359296 | tf_op jit(solution)/shard_map/all_to_all | solution.py:83
  302.2 5.0 copy-start.19
  316.7 159.0 %all-to-all-start.2 = ((bf16[8,288,1536]{2,1,0:T(8,128)(2,1)}), bf16[8,288,1536]{2,1,0:T(8,128)(2,1)}, u32[]{:S(2)}, u32[]{:S(2)}) async-start(bf16[8,288,1536]{2,1,0:T(8,128)(2,1)} %bitcast.185), calls=%async_computation.2 | async-start | bytes 14155776 | tf_op jit(solution)/shard_map/all_to_all | solution.py:169
  337.3 11.8 copy-start.55
  350.8 124.9 %copy-start.59 = (s32[2048]{0:T(1024)S(1)}, s32[2048]{0:T(1024)}, u32[]{:S(2)}) copy-start(s32[2048]{0:T(1024)} %pad_clamp_fusion.2) | copy-start | bytes 24580
  360.6 129.5 %copy-start.61 = (f32[384,4]{0,1:T(4,128)}, f32[384,4]{0,1:T(4,128)S(1)}, u32[]{:S(2)}) copy-start(f32[384,4]{0,1:T(4,128)S(1)} %get-tuple-element.82) | copy-start | bytes 18436
  360.6 129.5 %copy-start.70 = (f32[384]{0:T(512)}, f32[384]{0:T(512)S(1)}, u32[]{:S(2)}) copy-start(f32[384]{0:T(512)S(1)} %get-tuple-element.81) | copy-start | bytes 4612
  498.9 15.3 %copy-start.14 = (bf16[384,1536]{1,0:T(8,128)(2,1)S(1)}, bf16[384,1536]{1,0:T(8,128)(2,1)}, u32[]{:S(2)}) copy-start(bf16[384,1536]{1,0:T(8,128)(2,1)} %gather_fusion.4) | copy-start | bytes 3538948
  514.1 3.7 copy-start.62
  514.1 3.7 copy-start.71
  514.2 3.7 copy-start.88
  704.7 18.1 %copy-start.27 = (bf16[8,288,1536]{2,1,0:T(8,128)(2,1)}, bf16[8,288,1536]{2,1,0:T(8,128)(2,1)S(1)}, u32[]{:S(2)}) copy-start(bf16[8,288,1536]{2,1,0:T(8,128)(2,1)S(1)} %all_to_all.69) | copy-start | bytes 21233668
  740.5 5.1 copy-start.73
  740.5 5.1 copy-start.75
  740.5 5.1 copy-start.77
  740.5 5.1 copy-start.79
  740.5 5.1 copy-start.87
  740.5 5.1 copy-start.16
  740.6 159.1 %all-to-all-start.6 = ((bf16[8,288,1536]{2,1,0:T(8,128)(2,1)}), bf16[8,288,1536]{2,1,0:T(8,128)(2,1)}, u32[]{:S(2)}, u32[]{:S(2)}) async-start(bf16[8,288,1536]{2,1,0:T(8,128)(2,1)} %bitcast.184), calls=%async_computation.6 | async-start | bytes 14155776 | tf_op jit(solution)/shard_map/all_to_all | solution.py:208
  745.5 274.9 %reduce-scatter.10.cloned.1.call-start = ((), (), s32[]{:S(2)}) async-start(), calls=%async_computation.17 | async-start | bytes 36864 | tf_op jit(solution)/shard_map/reduce_scatter | solution.py:310
  745.7 11.4 copy-start.66
  746.6 273.9 %reduce-scatter.14.cloned.1.call-start = ((), (), s32[]{:S(2)}) async-start(), calls=%async_computation.19 | async-start | bytes 2949120 | tf_op jit(solution)/shard_map/reduce_scatter | solution.py:325
  757.1 265.6 %reduce-scatter.12.cloned.1.call-start = ((), (), s32[]{:S(2)}) async-start(), calls=%async_computation.18 | async-start | bytes 5898240 | tf_op jit(solution)/shard_map/reduce_scatter | solution.py:319
  775.7 123.9 %copy-start.60 = (s32[2048]{0:T(1024)S(1)}, s32[2048]{0:T(1024)}, u32[]{:S(2)}) copy-start(s32[2048]{0:T(1024)} %pad_clamp_fusion.2) | copy-start | bytes 24580
  775.8 256.5 %reduce-scatter.8.cloned.1.call-start = ((), (), s32[]{:S(2)}) async-start(), calls=%async_computation.16 | async-start | bytes 7077888 | tf_op jit(solution)/shard_map/reduce_scatter | solution.py:307
  923.2 15.3 %copy-start.13 = (f32[384,1536]{1,0:T(8,128)S(1)}, f32[384,1536]{1,0:T(8,128)}, u32[]{:S(2)}) copy-start(f32[384,1536]{1,0:T(8,128)} %copy-done.12) | copy-start | bytes 7077892
  923.2 15.3 %copy-start.56 = (bf16[1536,8]{0,1:T(8,128)(2,1)S(1)}, bf16[1536,8]{0,1:T(8,128)(2,1)}, u32[]{:S(2)}) copy-start(bf16[1536,8]{0,1:T(8,128)(2,1)} %all_gather.19) | copy-start | bytes 73732
  923.2 15.3 %copy-start.58 = (f32[1536]{0:T(1024)S(1)}, f32[1536]{0:T(1024)}, u32[]{:S(2)}) copy-start(f32[1536]{0:T(1024)} %copy-done.57) | copy-start | bytes 18436
  923.2 15.3 %copy-start.67 = (bf16[384,8]{0,1:T(8,128)(2,1)S(1)}, bf16[384,8]{0,1:T(8,128)(2,1)}, u32[]{:S(2)}) copy-start(bf16[384,8]{0,1:T(8,128)(2,1)} %copy-done.66) | copy-start | bytes 18436
  923.2 15.3 %copy-start.69 = (f32[384]{0:T(512)S(1)}, f32[384]{0:T(512)}, u32[]{:S(2)}) copy-start(f32[384]{0:T(512)} %copy-done.68) | copy-start | bytes 4612
  938.5 3.7 copy-start.11
  938.5 3.7 copy-start.84
  949.9 82.4 %reduce-scatter.6.cloned.1.call-start = ((), (), s32[]{:S(2)}) async-start(), calls=%async_computation.15 | async-start | bytes 9437184 | tf_op jit(solution)/shard_map/reduce_scatter | solution.py:304
  958.2 8.4 copy-start.20
  958.2 8.4 slice-start
  958.2 8.3 slice-start.1
  958.2 8.3 copy-start.47
  966.6 4.5 copy-start.23
  975.7 8.9 copy-start.50
  980.0 4.6 copy-start.40
  980.0 4.6 copy-start.18
  980.0 4.6 copy-start.65
  980.0 4.6 copy-start.83
  984.6 6.9 copy-start.51
  997.4 4.0 copy-start.41
  997.4 18.1 %all-to-all-start.3 = ((bf16[2,192,1536]{2,1,0:T(8,128)(2,1)}), bf16[2,192,1536]{2,1,0:T(8,128)(2,1)S(1)}, u32[]{:S(2)}, u32[]{:S(2)}) async-start(bf16[2,192,1536]{2,1,0:T(8,128)(2,1)} %bitcast.190), calls=%async_computation.3 | async-start | bytes 2359296 | tf_op jit(solution)/shard_map/all_to_all | solution.py:292
  1001.5 7.7 copy-start.26
  1001.5 7.7 copy-start.81
  1012.6 6.5 copy-start.91
  1015.5 16.8 %all-to-all-start.7 = ((bf16[2,192,1536]{2,1,0:T(8,128)(2,1)}), bf16[2,192,1536]{2,1,0:T(8,128)(2,1)S(1)}, u32[]{:S(2)}, u32[]{:S(2)}) async-start(bf16[2,192,1536]{2,1,0:T(8,128)(2,1)} %bitcast.56), calls=%async_computation.7 | async-start | bytes 2359296 | tf_op jit(solution)/shard_map/all_to_all | solution.py:295
  1020.4 5.3 copy-start.89
  1020.4 5.3 copy-start.90
  1020.4 11.8 copy-start.80
  1032.2 457.1 %copy-start.28 = (bf16[2,192,1536]{2,1,0:T(8,128)(2,1)}, bf16[2,192,1536]{2,1,0:T(8,128)(2,1)S(1)}, u32[]{:S(2)}) copy-start(bf16[2,192,1536]{2,1,0:T(8,128)(2,1)S(1)} %all-to-all-done.7) | copy-start | bytes 3538948
  (43 other events, 95.3 us)
Sparse Core Ops, SparseCore 0:
  9.6 19.4 all-gather.4
  30.6 15.6 all-gather.6
  748.5 9.2 reduce-scatter.9
  760.3 34.2 reduce-scatter.13
  797.1 47.8 reduce-scatter.11
  950.0 12.1 reduce-scatter.7
  991.6 14.6 reduce-scatter.5
where the time goes:
time: 1510 us; the launch traced here: 1500 us
  blocking collectives  787 us (52%)
  waiting for transfers between devices  246 us (16%)
  local copies, waits for them, and re-layouts  219 us (15%)
  matrix products  149 us (10%)
  other arithmetic  55.4 us (4%)
  starting transfers between devices  25.5 us (2%)
  between operations  16.2 us (1%)
    psum x1, blocking collectives, shards(): lax.psum((shard_terms[0], shard_terms[1], shard_terms[2], shard_terms[3],...  457 us
    all_to_all x1, blocking collectives, shards(): lax.all_to_all(sending, 'expert', split_axis=0, concat_axis=0, tiled=True)  162 us
    all_to_all x1, blocking collectives, shards(): lax.all_to_all(sending_back, 'expert', split_axis=0, concat_axis=0, tiled...  159 us
    all_to_all x1, waiting for transfers between devices, shards(): lax.all_to_all(grad_rows_in.reshape(peer_count, capacity, model_width), '...  123 us
    all_to_all x1, waiting for transfers between devices, shards(): lax.all_to_all(expert_out.reshape(peer_count, capacity, model_width), 'ex...  115 us
  transfers between devices with their start and end apart: 13, of which 4 were waited for; matrix products, arithmetic and copies ran while one was open for 19% of the time, Pallas kernels for 0%

commit v1 on v0

--- a/solution.py
+++ b/solution.py
@@ -61,7 +61,7 @@
     return jax.nn.gelu(gate_up[:, :hidden_width], approximate=True) * gate_up[:, hidden_width:]
 
 
-def shards(
+def routed_shards(
     hidden_in,
     cotangent,
     deal_order,
@@ -339,7 +339,353 @@
     )
 
 
+RING_NEXT = (1, 3, 0, 2)
+
+
+def other_core(field):
+    return lax.ppermute(field, "shard", [(0, 1), (1, 0)])
+
+
+def other_dp(field):
+    return lax.ppermute(field, "dp", [(0, 1), (1, 0)])
+
+
+def across_x(field):
+    return lax.ppermute(field, "expert", [(i, i ^ 1) for i in range(8)])
+
+
+def across_dp_x(field):
+    pairs = [(d * 8 + e, (1 - d) * 8 + (e ^ 1)) for d in range(2) for e in range(8)]
+    return lax.ppermute(field, ("dp", "expert"), pairs)
+
+
+def across_z(field, distance):
+    return lax.ppermute(field, "expert", [(i, i ^ (2 * distance)) for i in range(8)])
+
+
+def ring_z(field):
+    pairs = [(2 * z + x, 2 * RING_NEXT[z] + x) for z in range(4) for x in range(2)]
+    return lax.ppermute(field, "expert", pairs)
+
+
+def to_owner(field):
+    pairs = [(e * 2 + c, (e ^ 1) * 2 + c) for e in range(8) for c in range(2) if e % 2 != c]
+    return lax.ppermute(field, ("expert", "shard"), pairs)
+
+
+def from_owner(field):
+    pairs = [(e * 2 + c, (e ^ 1) * 2 + c) for e in range(8) for c in range(2) if e % 2 == c]
+    return lax.ppermute(field, ("expert", "shard"), pairs)
+
+
+def in_order(first, own, received):
+    return jnp.where(
+        first, jnp.concatenate([own, received], axis=0), jnp.concatenate([received, own], axis=0)
+    )
+
+
+def block(field, index, count):
+    rows = field.shape[0] // count
+    return lax.dynamic_slice_in_dim(field, index * rows, rows, axis=0)
+
+
+def sum_blocks(*fields):
+    total = fields[0].astype(jnp.float32)
+    for field in fields[1:]:
+        total = total + field.astype(jnp.float32)
+    return total
+
+
+def reduce_weight(term, place):
+    dp, x, z, core = place
+    mine, theirs = block(term, core, 2), block(term, 1 - core, 2)
+    part = sum_blocks(mine, other_core(theirs)).astype(jnp.bfloat16)
+    own = 2 * dp + x
+    part = sum_blocks(
+        block(part, own, 4),
+        other_dp(block(part, own ^ 2, 4)),
+        across_x(block(part, own ^ 1, 4)),
+        across_dp_x(block(part, own ^ 3, 4)),
+    ).astype(jnp.bfloat16)
+    part = sum_blocks(
+        block(part, z, 4), *[across_z(block(part, z ^ k, 4), k) for k in (1, 2, 3)]
+    ).astype(jnp.bfloat16)
+    pieces = jnp.stack([part] + [across_z(part, k) for k in (1, 2, 3)])
+    part = jnp.concatenate([lax.dynamic_index_in_dim(pieces, z ^ b, 0, False) for b in range(4)])
+    pieces = jnp.stack([part, across_x(part), other_dp(part), across_dp_x(part)])
+    whole = jnp.concatenate(
+        [lax.dynamic_index_in_dim(pieces, own ^ b, 0, False) for b in range(4)]
+    )
+    return whole.astype(jnp.float32)
+
+
+def reduce_small(term):
+    part = term + other_core(term)
+    part = part + other_dp(part) + across_x(part) + across_dp_x(part)
+    return part + across_z(part, 1) + across_z(part, 2) + across_z(part, 3)
+
+
+def reduce_expert(term, place):
+    dp, x, _, core = place
+    half = term.shape[1] // 2
+    first, second = term[:, :half].astype(jnp.bfloat16), term[:, half:].astype(jnp.bfloat16)
+    first = sum_blocks(first, to_owner(first)).astype(jnp.bfloat16)
+    first = sum_blocks(block(first, dp, 2), other_dp(block(first, 1 - dp, 2)))
+    second = sum_blocks(block(second, dp, 2), other_dp(block(second, 1 - dp, 2)))
+    second = second.astype(jnp.bfloat16)
+    second = sum_blocks(second, to_owner(second))
+    both = jnp.concatenate([first, second], axis=1).astype(jnp.bfloat16)
+    mine, theirs = block(both, core, 2), block(both, 1 - core, 2)
+    return jnp.where(core == x, mine, other_core(theirs)).astype(jnp.float32)
+
+
+def expert_block(rows, upstream, weighting, up_matrix, down_matrix):
+    gate_up = jnp.dot(rows, up_matrix, preferred_element_type=jnp.float32)
+    hidden = activate(gate_up).astype(jnp.bfloat16)
+    out = jnp.dot(hidden, down_matrix, preferred_element_type=jnp.float32).astype(jnp.bfloat16)
+    out = out.astype(jnp.float32)
+    ct = upstream.astype(jnp.float32)
+    weighted = (weighting * out).astype(jnp.bfloat16)
+    grad_out = (weighting * ct).astype(jnp.bfloat16)
+    grad_gate = jnp.sum(ct * out, axis=1)
+    grad_hidden = jnp.dot(grad_out, down_matrix.T, preferred_element_type=jnp.float32)
+    grad_gate_up = jax.vjp(activate, gate_up)[1](grad_hidden)[0].astype(jnp.bfloat16)
+    grad_rows = jnp.dot(grad_gate_up, up_matrix.T, preferred_element_type=jnp.float32)
+    return hidden, weighted, grad_out, grad_gate, grad_gate_up, grad_rows.astype(jnp.bfloat16)
+
+
+def ring_shards(
+    hidden_in,
+    cotangent,
+    deal_order,
+    lengths,
+    routes,
+    attention_gain,
+    expert_gain,
+    qkv_weight,
+    out_weight,
+    router_weight,
+    gate_up_weight,
+    down_weight,
+):
+    count_of_rows = hidden_in.shape[0]
+    model_width = hidden_in.shape[1]
+    half_rows = count_of_rows // 2
+    head_groups = QUERY_HEADS // KEY_VALUE_HEADS
+    expert_count = router_weight.shape[1]
+    dp, core, at = lax.axis_index("dp"), lax.axis_index("shard"), lax.axis_index("expert")
+    x, z = at % 2, at // 2
+    place = (dp, x, z, core)
+    expert_ids = jnp.arange(expert_count, dtype=jnp.int32)
+
+    def from_dealt(field):
+        return jnp.concatenate([block(field, dp, 2), other_dp(block(field, 1 - dp, 2))], axis=0)
+
+    def to_dealt(field):
+        return in_order(dp == 0, field[:half_rows], other_dp(field[half_rows:]))
+
+    deal_rows = deal_order[0]
+    held_at = jnp.where(deal_rows // half_rows == dp, 0, half_rows) + deal_rows % half_rows
+    deal = (held_at[:, None] == jnp.arange(count_of_rows, dtype=jnp.int32)[None, :]).astype(
+        jnp.bfloat16
+    )
+
+    def permute(matrix, field):
+        return jnp.dot(matrix, field, preferred_element_type=jnp.float32).astype(jnp.bfloat16)
+
+    tokens = permute(deal, from_dealt(hidden_in))
+    upstream_low = permute(deal, from_dealt(cotangent))
+    small = jnp.concatenate([attention_gain[None], expert_gain[None], router_weight.T], axis=0)
+    small_other = other_core(small)
+    small = jnp.where(
+        core == 0,
+        jnp.concatenate([small, small_other], axis=1),
+        jnp.concatenate([small_other, small], axis=1),
+    )
+    gain_first, gain_second = small[0].astype(jnp.float32), small[1].astype(jnp.float32)
+    full_router = small[2:].T
+    full_qkv = in_order(core == 0, qkv_weight, other_core(qkv_weight))
+    full_out = in_order(core == 0, out_weight, other_core(out_weight))
+    up_matrix = jnp.where(core == x, gate_up_weight[0], from_owner(gate_up_weight[0]))
+    down_matrix = jnp.where(core == x, down_weight[0], from_owner(down_weight[0]))
+    upstream_ring = [upstream_low]
+    for _ in range(3):
+        upstream_ring.append(ring_z(upstream_ring[-1]))
+    upstream_units = [jnp.concatenate([unit, other_core(unit)]) for unit in upstream_ring]
+
+    upstream = upstream_low.astype(jnp.float32)
+    residual = tokens.astype(jnp.float32)
+    inv_first = lax.rsqrt(jnp.mean(residual * residual, axis=1, keepdims=True) + EPS)
+    normed_attn = (residual * inv_first * gain_first).astype(jnp.bfloat16)
+    projected_rows = jnp.dot(normed_attn, full_qkv, preferred_element_type=jnp.float32)
+    segment, token_position = positions_of(lengths[0], count_of_rows)
+    query_matrix_rows = (
+        apply_rotation(
+            projected_rows[:, : QUERY_HEADS * HEAD_SIZE].reshape(
+                count_of_rows, QUERY_HEADS, HEAD_SIZE
+            ),
+            token_position,
+            1.0,
+        )
+        .astype(jnp.bfloat16)
+        .reshape(count_of_rows, KEY_VALUE_HEADS, head_groups, HEAD_SIZE)
+    )
+    key_matrix_rows = apply_rotation(
+        projected_rows[
+            :, QUERY_HEADS * HEAD_SIZE : (QUERY_HEADS + KEY_VALUE_HEADS) * HEAD_SIZE
+        ].reshape(count_of_rows, KEY_VALUE_HEADS, HEAD_SIZE),
+        token_position,
+        1.0,
+    ).astype(jnp.bfloat16)
+    value_matrix_rows = (
+        projected_rows[:, (QUERY_HEADS + KEY_VALUE_HEADS) * HEAD_SIZE :]
+        .reshape(count_of_rows, KEY_VALUE_HEADS, HEAD_SIZE)
+        .astype(jnp.bfloat16)
+    )
+    scores = masked_scores(query_matrix_rows, key_matrix_rows, segment, segment, 0)
+    row_max = jnp.max(scores, axis=-1, keepdims=True)
+    exp_scores = jnp.exp(scores - row_max)
+    exp_total = jnp.sum(exp_scores, axis=-1, keepdims=True)
+    soft_probs = (exp_scores / exp_total).astype(jnp.bfloat16)
+    attn_mix = (
+        jnp.einsum(
+            "hgij,jhd->ihgd", soft_probs, value_matrix_rows, preferred_element_type=jnp.float32
+        )
+        .reshape(count_of_rows, QUERY_HEADS * HEAD_SIZE)
+        .astype(jnp.bfloat16)
+    )
+    logsum = (row_max + jnp.log(exp_total))[..., 0]
+    middle = residual + jnp.dot(attn_mix, full_out, preferred_element_type=jnp.float32)
+    inv_second = lax.rsqrt(jnp.mean(middle * middle, axis=1, keepdims=True) + EPS)
+    normed_moe = (middle * inv_second * gain_second).astype(jnp.bfloat16)
+    logits = jnp.dot(normed_moe, full_router, preferred_element_type=jnp.float32)
+    named = jnp.any(routes[:, :, None] == expert_ids[None, None, :], axis=1)
+    top_logit = jnp.max(jnp.where(named, logits, -jnp.inf), axis=1, keepdims=True)
+    exp_logits = jnp.where(named, jnp.exp(jnp.where(named, logits - top_logit, 0.0)), 0.0)
+    gates = exp_logits / jnp.sum(exp_logits, axis=1, keepdims=True)
+
+    own_expert = 2 * z + core
+    own_row = (expert_ids == own_expert)[:, None]
+    normed_ring, gates_ring = [normed_moe], [gates.T]
+    for _ in range(3):
+        normed_ring.append(ring_z(normed_ring[-1]))
+        gates_ring.append(ring_z(gates_ring[-1]))
+    steps = []
+    arrived_grad = arrived_gate = None
+    for step in (1, 2, 3, 0):
+        rows = jnp.concatenate([normed_ring[step], other_core(normed_ring[step])])
+        all_gates = jnp.concatenate([gates_ring[step], other_core(gates_ring[step])], axis=1)
+        weighting = jnp.sum(jnp.where(own_row, all_gates, 0.0), axis=0)[:, None]
+        hidden, weighted, grad_out, grad_gate, grad_gate_up, grad_rows = expert_block(
+            rows, upstream_units[step], weighting, up_matrix, down_matrix
+        )
+        steps.append((rows, hidden, grad_out, grad_gate_up, weighted))
+        gate_rows = jnp.where(own_row, grad_gate[None, :], 0.0)
+        unit_grad = sum_blocks(grad_rows[:count_of_rows], other_core(grad_rows[count_of_rows:]))
+        unit_gate = gate_rows[:, :count_of_rows] + other_core(gate_rows[:, count_of_rows:])
+        if arrived_grad is not None:
+            unit_grad = unit_grad + arrived_grad.astype(jnp.float32)
+            unit_gate = unit_gate + arrived_gate
+        if step:
+            arrived_grad = ring_z(unit_grad.astype(jnp.bfloat16))
+            arrived_gate = ring_z(unit_gate)
+    grad_normed, grad_gates = unit_grad, unit_gate.T
+    all_rows, all_hidden, all_grad_out, all_grad_gate_up, _ = [
+        jnp.concatenate(list(fields)) for fields in zip(*steps)
+    ]
+    term_down = jnp.dot(all_hidden.T, all_grad_out, preferred_element_type=jnp.float32)
+    term_gate_up = jnp.dot(all_rows.T, all_grad_gate_up, preferred_element_type=jnp.float32)
+    gate_up_grad = reduce_expert(term_gate_up, place)[None]
+    down_grad = reduce_expert(term_down, place)[None]
+
+    mean_term = jnp.sum(gates * grad_gates, axis=1, keepdims=True)
+    grad_logits = (gates * (grad_gates - mean_term)).astype(jnp.bfloat16)
+    term_router = jnp.dot(normed_moe.T, grad_logits, preferred_element_type=jnp.float32)
+    grad_normed = grad_normed + jnp.dot(
+        grad_logits, full_router.T, preferred_element_type=jnp.float32
+    )
+    grad_middle_norm, term_gain_second = norm_back(middle, inv_second, gain_second, grad_normed)
+    grad_middle = upstream + grad_middle_norm
+    grad_attn_out = grad_middle.astype(jnp.bfloat16)
+
+    arrived = None
+    for step in (0, 1, 2, 3):
+        weighted = steps[step][4]
+        unit = sum_blocks(weighted[:count_of_rows], other_core(weighted[count_of_rows:]))
+        if arrived is not None:
+            unit = unit + arrived.astype(jnp.float32)
+        if step < 3:
+            arrived = ring_z(unit.astype(jnp.bfloat16))
+    final_rows = (middle + unit).astype(jnp.bfloat16)
+    layer_out = to_dealt(permute(deal.T, final_rows))
+
+    term_out = jnp.dot(attn_mix.T, grad_attn_out, preferred_element_type=jnp.float32)
+    out_grad = reduce_weight(term_out.astype(jnp.bfloat16), place)
+    grad_mix = (
+        jnp.dot(grad_attn_out, full_out.T, preferred_element_type=jnp.float32)
+        .astype(jnp.bfloat16)
+        .reshape(count_of_rows, KEY_VALUE_HEADS, head_groups, HEAD_SIZE)
+    )
+    scores = masked_scores(query_matrix_rows, key_matrix_rows, segment, segment, 0)
+    soft_probs = jnp.exp(scores - logsum[..., None])
+    grad_probs = jnp.einsum(
+        "ihgd,jhd->hgij", grad_mix, value_matrix_rows, preferred_element_type=jnp.float32
+    )
+    grad_value = jnp.einsum(
+        "hgij,ihgd->jhd",
+        soft_probs.astype(jnp.bfloat16),
+        grad_mix,
+        preferred_element_type=jnp.float32,
+    )
+    grad_scores = (
+        soft_probs * (grad_probs - jnp.sum(soft_probs * grad_probs, axis=-1, keepdims=True))
+    ).astype(jnp.bfloat16)
+    grad_query = HEAD_SIZE ** (-0.5) * jnp.einsum(
+        "hgij,jhd->ihgd", grad_scores, key_matrix_rows, preferred_element_type=jnp.float32
+    )
+    grad_key = HEAD_SIZE ** (-0.5) * jnp.einsum(
+        "hgij,ihgd->jhd", grad_scores, query_matrix_rows, preferred_element_type=jnp.float32
+    )
+    grad_query = apply_rotation(
+        grad_query.reshape(count_of_rows, QUERY_HEADS, HEAD_SIZE), token_position, -1.0
+    )
+    grad_key = apply_rotation(grad_key, token_position, -1.0)
+    grad_projected = jnp.concatenate(
+        [
+            grad_query.reshape(count_of_rows, QUERY_HEADS * HEAD_SIZE),
+            grad_key.reshape(count_of_rows, KEY_VALUE_HEADS * HEAD_SIZE),
+            grad_value.reshape(count_of_rows, KEY_VALUE_HEADS * HEAD_SIZE),
+        ],
+        axis=1,
+    ).astype(jnp.bfloat16)
+    term_qkv = jnp.dot(normed_attn.T, grad_projected, preferred_element_type=jnp.float32)
+    qkv_grad = reduce_weight(term_qkv.astype(jnp.bfloat16), place)
+    grad_normed_attn = jnp.dot(grad_projected, full_qkv.T, preferred_element_type=jnp.float32)
+    grad_resid_norm, term_gain_first = norm_back(residual, inv_first, gain_first, grad_normed_attn)
+    grad_tokens = (grad_middle + grad_resid_norm).astype(jnp.bfloat16)
+    input_gradient = to_dealt(permute(deal.T, grad_tokens))
+    small_grad = reduce_small(
+        jnp.concatenate([term_gain_first[None], term_gain_second[None], term_router.T], axis=0)
+    )
+    small_grad = lax.dynamic_slice_in_dim(
+        small_grad, core * (model_width // 2), model_width // 2, axis=1
+    )
+    return (
+        layer_out,
+        input_gradient,
+        small_grad[0],
+        small_grad[1],
+        qkv_grad,
+        out_grad,
+        small_grad[2:].T,
+        gate_up_grad,
+        down_grad,
+    )
+
+
 def solution(mesh):
+    ringed = (mesh.shape["dp"], mesh.shape["expert"], mesh.shape["shard"]) == (2, 8, 2)
+    shards = ring_shards if ringed else routed_shards
     return jax.shard_map(
         shards,
         mesh=mesh,

time: 1510 us -> 748 us (0.50)
  blocking collectives: 787 us -> 0 us
  local copies, waits for them, and re-layouts: 219 us -> 62 us
  waiting for transfers between devices: 246 us -> 343 us
  starting transfers between devices: 25.5 us -> 100 us
  matrix products: 149 us -> 167 us
    psum x1 -> x0, blocking collectives: 457 us -> none  [shards(): lax.psum((shard_terms[0], shard_terms[1], shard_terms[2], shard_terms[3],...]
    ppermute x0 -> x94, waiting for transfers between devices: none -> 343 us  [the longest x13 153 us: other_dp(): return lax.ppermute(field, 'dp', [(0, 1), (1, 0)])]
    all_to_all x2 -> x0, blocking collectives: 321 us -> none  [the longest x1 162 us: shards(): lax.all_to_all(sending, 'expert', split_axis=0, concat_axis=0, tiled=True)]
    all_to_all x6 -> x0, waiting for transfers between devices: 245 us -> none  [the longest x1 123 us: shards(): lax.all_to_all(grad_rows_in.reshape(peer_count, capacity, model_width), '...]
    ppermute x0 -> x94, starting transfers between devices: none -> 100 us  [the longest x18 25.6 us: ring_z(): return lax.ppermute(field, 'expert', pairs)]
    gather x13 -> x0, local copies, waits for them, and re-layouts: 87.2 us -> none  [the longest x1 18.1 us: shards(): padded_grad[slot_pair].reshape(peer_count, capacity, model_width)]
    all_to_all x6 -> x0, starting transfers between devices: 25.2 us -> none  [the longest x1 4.96 us: shards(): lax.all_to_all(grad_rows_in.reshape(peer_count, capacity, model_width), '...]
    slice x8 -> x22, local copies, waits for them, and re-layouts: 37.5 us -> 13.1 us  [the longest x2 3.83 us: ring_shards(): projected_rows[:, :QUERY_HEADS * HEAD_SIZE]]
  transfers between devices with their start and end apart: 13 -> 94, of which waited for: 4 -> 36; matrix products, arithmetic and copies ran while one was open for 19% -> 37% of each run, Pallas kernels for 0% -> 0%
where the time goes in v1:
time: 748 us; the launch traced here: 743 us
  waiting for transfers between devices  343 us (46%)
  matrix products  167 us (22%)
  starting transfers between devices  100 us (13%)
  other arithmetic  67.5 us (9%)
  local copies, waits for them, and re-layouts  62 us (8%)
    ppermute x13, waiting for transfers between devices, other_dp(): return lax.ppermute(field, 'dp', [(0, 1), (1, 0)])  153 us
    ppermute x18, waiting for transfers between devices, ring_z(): return lax.ppermute(field, 'expert', pairs)  103 us
    ppermute x15, waiting for transfers between devices, across_z(): lax.ppermute(field, 'expert', [(i, i ^ 2 * distance) for i in range(8)])  40 us
    unnamed x239, local copies, waits for them, and re-layouts  29.3 us
    ppermute x18, starting transfers between devices, ring_z(): return lax.ppermute(field, 'expert', pairs)  25.6 us
    dot_general x4, matrix products, expert_block(): gate_up = jnp.dot(rows, up_matrix, preferred_element_type=jnp.float32)  24.2 us
    ppermute x15, starting transfers between devices, across_z(): lax.ppermute(field, 'expert', [(i, i ^ 2 * distance) for i in range(8)])  22.9 us
    dot_general x1, matrix products, ring_shards(): jnp.dot(all_rows.T, all_grad_gate_up, preferred_element_type=jnp.float32)  19.4 us
  transfers between devices with their start and end apart: 94, of which 36 were waited for; matrix products, arithmetic and copies ran while one was open for 37% of the time, Pallas kernels for 0%

profile of v1, /device:TPU:0, one launch (start us, length us, event | category | flops | bytes accessed | tf_op | source)
XLA Modules:
  0.0 743.1 jit_solution(10296234149540027997)
XLA Ops:
  7.8 24.0 %collective-permute-done.28 = bf16[192,1536]{1,0:T(8,128)(2,1)S(1)} collective-permute-done((bf16[192,1536]{1,0:T(8,128)(2,1)}, bf16[192,1536]{1,0:T(8,128)(2,1)S(1)}, u32[]{:S(2)}, u32[]{:S(2)}) %collective-permute-start.28) | collective-permute-done | bytes 589856 | tf_op jit(solution)/shard_map/ppermute | solution.py:350
  38.6 5.9 collective-permute-start.6
  44.5 2.7 collective-permute-start.7
  49.9 13.3 %collective-permute-done.31 = bf16[384,1536]{1,0:T(8,128)(2,1)} collective-permute-done((bf16[384,1536]{1,0:T(8,128)(2,1)S(1)}, bf16[384,1536]{1,0:T(8,128)(2,1)}, u32[]{:S(2)}, u32[]{:S(2)}) %collective-permute-start.31) | collective-permute-done | bytes 1179680 | tf_op jit(solution)/shard_map/ppermute | solution.py:368
  64.1 5.1 fusion.129
  90.1 4.8 multiply_reduce_fusion.2
  96.8 3.6 collective-permute-start.9
  104.2 15.2 %collective-permute-done.7 = bf16[768,1536]{1,0:T(8,128)(2,1)} collective-permute-done((bf16[768,1536]{1,0:T(8,128)(2,1)}, bf16[768,1536]{1,0:T(8,128)(2,1)}, u32[]{:S(2)}, u32[]{:S(2)}) %collective-permute-start.7) | collective-permute-done | bytes 2359328 | tf_op jit(solution)/shard_map/ppermute | solution.py:378
  132.9 3.6 fusion.34
  137.6 21.1 %collective-permute-done.33 = bf16[384,1536]{1,0:T(8,128)(2,1)} collective-permute-done((bf16[384,1536]{1,0:T(8,128)(2,1)}, bf16[384,1536]{1,0:T(8,128)(2,1)}, u32[]{:S(2)}, u32[]{:S(2)}) %collective-permute-start.33) | collective-permute-done | bytes 1179680 | tf_op jit(solution)/shard_map/ppermute | solution.py:368
  158.7 3.5 fusion.32
  162.2 20.8 %collective-permute-done.13 = bf16[384,1536]{1,0:T(8,128)(2,1)} collective-permute-done((bf16[384,1536]{1,0:T(8,128)(2,1)S(1)}, bf16[384,1536]{1,0:T(8,128)(2,1)}, u32[]{:S(2)}, u32[]{:S(2)}) %collective-permute-start.13) | collective-permute-done | bytes 1179680 | tf_op jit(solution)/shard_map/ppermute | solution.py:368
  186.4 6.0 fusion.86
  192.4 3.5 fusion.130
  195.9 2.9 fusion.29
  200.8 4.5 convolution_convert_fusion.5
  208.6 6.3 fusion.98
  214.9 3.5 fusion.133
  218.4 4.3 fusion.35
  225.8 4.1 convolution_convert_fusion.2
  239.1 6.9 fusion.94
  246.0 5.2 fusion.132
  251.3 3.9 fusion.33
  260.5 4.1 convolution_convert_fusion.3
  270.3 15.5 %collective-permute-done.24 = bf16[384,1536]{1,0:T(8,128)(2,1)} collective-permute-done((bf16[384,1536]{1,0:T(8,128)(2,1)S(1)}, bf16[384,1536]{1,0:T(8,128)(2,1)}, u32[]{:S(2)}, u32[]{:S(2)}) %collective-permute-start.24) | collective-permute-done | bytes 1179680 | tf_op jit(solution)/shard_map/ppermute | solution.py:368
  285.8 3.1 add_convert_fusion.16
  292.7 5.1 fusion.90
  297.8 4.5 fusion.131
  304.0 3.0 constant_dynamic-update-slice_fusion
  307.0 19.4 %fusion.16 = bf16[1536,1536]{0,1:T(8,128)(2,1)S(1)} fusion(bf16[3072,1536]{1,0:T(8,128)(2,1)} %constant_dynamic-update-slice_fusion, bf16[768,1536]{1,0:T(8,128)(2,1)S(1)} %add_convert_fusion.6, bf16[768,1536]{1,0:T(8,128)(2,1)} %add_convert_fusion.5, bf16[768,1536]{1,0:T(8,128)(2,1)S(1)} %copy-done.28, bf16[768,1536]{1,0:T(8,128)(2,1)S(1)} %copy-done.26), kind=kOutput, calls=%fused_computation.16 | convolution fusion | flops 14535622656 | bytes 23592960 | tf_op jit(solution)/shard_map/dot_general | solution.py:597
  329.3 13.0 %fusion.47 = bf16[768,1536]{1,0:T(8,128)(2,1)} fusion(bf16[768,1536]{1,0:T(8,128)(2,1)} %copy-done.33, bf16[768,1536]{1,0:T(8,128)(2,1)} %copy-done.35, bf16[768,1536]{1,0:T(8,128)(2,1)} %fusion.32, bf16[768,1536]{1,0:T(8,128)(2,1)} %fusion.34, bf16[768,768]{1,0:T(8,128)(2,1)} %copy-done.107, bf16[768,768]{1,0:T(8,128)(2,1)} %get-tuple-element.70, ...), kind=kOutput, calls=%fused_computation.95 | convolution fusion | flops 7305560064 | bytes 16515072 | tf_op jit(solution)/shard_map/dot_general | solution.py:596
  342.3 4.9 fusion.31
  348.9 6.5 convolution_convert_fusion.4
  364.7 23.7 %collective-permute-done.48 = f32[8,384]{1,0:T(8,128)S(1)} collective-permute-done((f32[8,384]{1,0:T(8,128)S(1)}, f32[8,384]{1,0:T(8,128)S(1)}, u32[]{:S(2)}, u32[]{:S(2)}) %collective-permute-start.48) | collective-permute-done | bytes 12320 | tf_op jit(solution)/shard_map/ppermute | solution.py:368
  389.0 4.0 collective-permute-done.49
  395.5 10.4 %collective-permute-done.91 = bf16[384,768]{1,0:T(8,128)(2,1)S(1)} collective-permute-done((bf16[384,768]{1,0:T(8,128)(2,1)S(1)}, bf16[384,768]{1,0:T(8,128)(2,1)S(1)}, u32[]{:S(2)}, u32[]{:S(2)}) %collective-permute-start.91) | collective-permute-done | bytes 589856 | tf_op jit(solution)/shard_map/ppermute | solution.py:350
  414.5 21.4 %collective-permute-done.86 = bf16[768,768]{0,1:T(8,128)(2,1)S(1)} collective-permute-done((bf16[768,768]{0,1:T(8,128)(2,1)S(1)}, bf16[768,768]{0,1:T(8,128)(2,1)S(1)}, u32[]{:S(2)}, u32[]{:S(2)}) %collective-permute-start.86) | collective-permute-done | bytes 1179680 | tf_op jit(solution)/shard_map/ppermute | solution.py:350
  438.8 8.8 %collective-permute-done.90 = bf16[384,768]{1,0:T(8,128)(2,1)S(1)} collective-permute-done((bf16[384,768]{1,0:T(8,128)(2,1)S(1)}, bf16[384,768]{1,0:T(8,128)(2,1)S(1)}, u32[]{:S(2)}, u32[]{:S(2)}) %collective-permute-start.90) | collective-permute-done | bytes 589856 | tf_op jit(solution)/shard_map/ppermute | solution.py:350
  457.5 5.4 convolution_convert_fusion.10
  464.9 8.3 %fusion.19 = (f32[2,6,384]{2,1,0:T(8,128)}, f32[2,384,384,6]{2,1,3,0:T(8,128)}) fusion(f32[2,6,384,384]{2,3,1,0:T(8,128)} %copy-done, f32[2,6,384]{2,1,0:T(8,128)} %log_add_fusion, bf16[384,2,6,128]{0,3,2,1:T(8,128)(2,1)S(1)} %bitcast.184, bf16[384,2,128,1]{2,1,0,3:T(2,128)(2,1)} %bitcast.200), kind=kOutput, calls=%fused_computation.21 | convolution fusion | flops 458288640 | bytes 15568896 | tf_op jit(solution)/shard_map/ihgd,jhd->hgij/dot_general | solution.py:631
  473.2 4.4 fusion.21
  477.6 2.8 fusion.107
  491.6 5.4 convolution_convert_fusion.1
  497.0 6.1 fusion.55
  505.1 2.8 convolution_convert_fusion
  527.0 3.1 collective-permute-done.57
  530.6 4.0 collective-permute-done.56
  540.3 18.8 %collective-permute-done.50 = bf16[192,1536]{1,0:T(8,128)(2,1)S(1)} collective-permute-done((bf16[192,1536]{1,0:T(8,128)(2,1)S(1)}, bf16[192,1536]{1,0:T(8,128)(2,1)S(1)}, u32[]{:S(2)}, u32[]{:S(2)}) %collective-permute-start.50) | collective-permute-done | bytes 589856 | tf_op jit(solution)/shard_map/ppermute | solution.py:350
  563.6 20.7 %collective-permute-done.85 = bf16[768,768]{0,1:T(8,128)(2,1)S(1)} collective-permute-done((bf16[768,768]{0,1:T(8,128)(2,1)S(1)}, bf16[768,768]{0,1:T(8,128)(2,1)S(1)}, u32[]{:S(2)}, u32[]{:S(2)}) %collective-permute-start.85) | collective-permute-done | bytes 1179680 | tf_op jit(solution)/shard_map/ppermute | solution.py:350
  584.6 9.5 %collective-permute-done.72 = bf16[192,1536]{1,0:T(8,128)(2,1)S(1)} collective-permute-done((bf16[192,1536]{1,0:T(8,128)(2,1)S(1)}, bf16[192,1536]{1,0:T(8,128)(2,1)S(1)}, u32[]{:S(2)}, u32[]{:S(2)}) %collective-permute-start.72) | collective-permute-done | bytes 589856 | tf_op jit(solution)/shard_map/ppermute | solution.py:350
  596.3 3.2 collective-permute-start.76
  599.8 3.3 collective-permute-done.77
  603.1 5.8 collective-permute-done.76
  622.4 3.3 copy.104
  626.7 12.1 %collective-permute-done.61 = bf16[192,2048]{1,0:T(8,128)(2,1)S(1)} collective-permute-done((bf16[192,2048]{1,0:T(8,128)(2,1)}, bf16[192,2048]{1,0:T(8,128)(2,1)S(1)}, u32[]{:S(2)}, u32[]{:S(2)}) %collective-permute-start.61) | collective-permute-done | bytes 786464 | tf_op jit(solution)/shard_map/ppermute | solution.py:359
  638.8 12.3 %collective-permute-done.60 = bf16[192,2048]{1,0:T(8,128)(2,1)} collective-permute-done((bf16[192,2048]{1,0:T(8,128)(2,1)}, bf16[192,2048]{1,0:T(8,128)(2,1)}, u32[]{:S(2)}, u32[]{:S(2)}) %collective-permute-start.60) | collective-permute-done | bytes 786464 | tf_op jit(solution)/shard_map/ppermute | solution.py:354
  659.2 5.3 collective-permute-done.64
  664.5 9.5 %collective-permute-done.63 = bf16[48,2048]{1,0:T(8,128)(2,1)S(1)} collective-permute-done((bf16[48,2048]{1,0:T(8,128)(2,1)S(1)}, bf16[48,2048]{1,0:T(8,128)(2,1)S(1)}, u32[]{:S(2)}, u32[]{:S(2)}) %collective-permute-start.63) | collective-permute-done | bytes 196640 | tf_op jit(solution)/shard_map/ppermute | solution.py:363
  681.1 2.7 collective-permute-done.67
  684.9 6.4 collective-permute-done.66
  696.9 23.3 %collective-permute-done.82 = bf16[192,1536]{1,0:T(8,128)(2,1)S(1)} collective-permute-done((bf16[192,1536]{1,0:T(8,128)(2,1)S(1)}, bf16[192,1536]{1,0:T(8,128)(2,1)S(1)}, u32[]{:S(2)}, u32[]{:S(2)}) %collective-permute-start.82) | collective-permute-done | bytes 589856 | tf_op jit(solution)/shard_map/ppermute | solution.py:350
  720.7 2.8 maximum_convert_fusion.1
  725.4 13.7 %collective-permute-done.69 = bf16[192,2048]{1,0:T(8,128)(2,1)S(1)} collective-permute-done((bf16[192,2048]{1,0:T(8,128)(2,1)S(1)}, bf16[192,2048]{1,0:T(8,128)(2,1)S(1)}, u32[]{:S(2)}, u32[]{:S(2)}) %collective-permute-start.69) | collective-permute-done | bytes 786464 | tf_op jit(solution)/shard_map/ppermute | solution.py:350
  739.8 3.1 maximum_convert_fusion
  (546 shorter events, 220.1 us)
Async XLA Ops:
  0.7 62.6 %collective-permute-start.2 = (bf16[768,2048]{1,0:T(8,128)(2,1)}, bf16[768,2048]{1,0:T(8,128)(2,1)}, u32[]{:S(2)}, u32[]{:S(2)}) collective-permute-start(bf16[768,2048]{1,0:T(8,128)(2,1)} %param.19), channel_id=1, source_target_pairs={{0,1},{1,0},{2,3},{3,2},{4,5},{5,4},{6,7},{7,6},{8,9},{9,8},{10,11... | collective-permute-start | bytes 9437192 | tf_op jit(solution)/shard_map/ppermute | solution.py:346
  2.6 42.0 %collective-permute-start = (bf16[192,1536]{1,0:T(8,128)(2,1)S(1)}, bf16[192,1536]{1,0:T(8,128)(2,1)}, u32[]{:S(2)}, u32[]{:S(2)}) collective-permute-start(bf16[192,1536]{1,0:T(8,128)(2,1)S(1)} %get-tuple-element.110), channel_id=1, source_target_pairs={{0,16},{16,0},{1,17},{17,1},{2,18},{18,2},{3,19},{19,3},{4,20},{20... | collective-permute-start | bytes 1769480 | tf_op jit(solution)/shard_map/ppermute | solution.py:350
  5.9 32.7 %collective-permute-start.1 = (bf16[10,768]{1,0:T(8,128)(2,1)}, bf16[10,768]{1,0:T(8,128)(2,1)S(1)}, u32[]{:S(2)}, u32[]{:S(2)}) collective-permute-start(bf16[10,768]{1,0:T(8,128)(2,1)} %pad_maximum_fusion.19), channel_id=1, source_target_pairs={{0,1},{1,0},{2,3},{3,2},{4,5},{5,4},{6,7},{7,6},{8,9},{9,8},{10,11... | collective-permute-start | bytes 46088 | tf_op jit(solution)/shard_map/ppermute | solution.py:346
  6.0 83.5 %collective-permute-start.3 = (bf16[768,1536]{1,0:T(8,128)(2,1)}, bf16[768,1536]{1,0:T(8,128)(2,1)}, u32[]{:S(2)}, u32[]{:S(2)}) collective-permute-start(bf16[768,1536]{1,0:T(8,128)(2,1)} %param.20), channel_id=1, source_target_pairs={{0,1},{1,0},{2,3},{3,2},{4,5},{5,4},{6,7},{7,6},{8,9},{9,8},{10,11... | collective-permute-start | bytes 7077896 | tf_op jit(solution)/shard_map/ppermute | solution.py:346
  7.3 24.5 %collective-permute-start.28 = (bf16[192,1536]{1,0:T(8,128)(2,1)}, bf16[192,1536]{1,0:T(8,128)(2,1)S(1)}, u32[]{:S(2)}, u32[]{:S(2)}) collective-permute-start(bf16[192,1536]{1,0:T(8,128)(2,1)} %get-tuple-element.104), channel_id=1, source_target_pairs={{0,16},{16,0},{1,17},{17,1},{2,18},{18,2},{3,19},{19,3},{4,20},{20... | collective-permute-start | bytes 1769480 | tf_op jit(solution)/shard_map/ppermute | solution.py:350
  34.5 28.8 %collective-permute-start.31 = (bf16[384,1536]{1,0:T(8,128)(2,1)S(1)}, bf16[384,1536]{1,0:T(8,128)(2,1)}, u32[]{:S(2)}, u32[]{:S(2)}) collective-permute-start(bf16[384,1536]{1,0:T(8,128)(2,1)S(1)} %convolution_convert_fusion.12), channel_id=1, source_target_pairs={{0,4},{2,6},{4,12},{6,14},{8,0},{10,2},{12,8},{14,10},{1,5},{3,7},... | collective-permute-start | bytes 3538952 | tf_op jit(solution)/shard_map/ppermute | solution.py:368
  38.6 147.2 %collective-permute-start.6 = (bf16[1536,1536]{1,0:T(8,128)(2,1)}, bf16[1536,1536]{1,0:T(8,128)(2,1)}, u32[]{:S(2)}, u32[]{:S(2)}) collective-permute-start(bf16[1536,1536]{1,0:T(8,128)(2,1)} %bitcast.194), channel_id=1, source_target_pairs={{0,2},{3,1},{4,6},{7,5},{8,10},{11,9},{12,14},{15,13},{16,18},{19,... | collective-permute-start | bytes 14155784 | tf_op jit(solution)/shard_map/ppermute | solution.py:378
  44.5 74.9 %collective-permute-start.7 = (bf16[768,1536]{1,0:T(8,128)(2,1)}, bf16[768,1536]{1,0:T(8,128)(2,1)}, u32[]{:S(2)}, u32[]{:S(2)}) collective-permute-start(bf16[768,1536]{1,0:T(8,128)(2,1)} %bitcast.197), channel_id=1, source_target_pairs={{0,2},{3,1},{4,6},{7,5},{8,10},{11,9},{12,14},{15,13},{16,18},{19,... | collective-permute-start | bytes 7077896 | tf_op jit(solution)/shard_map/ppermute | solution.py:378
  63.3 68.1 %collective-permute-start.38 = (bf16[384,1536]{1,0:T(8,128)(2,1)}, bf16[384,1536]{1,0:T(8,128)(2,1)}, u32[]{:S(2)}, u32[]{:S(2)}) collective-permute-start(bf16[384,1536]{1,0:T(8,128)(2,1)} %collective-permute-done.31), channel_id=1, source_target_pairs={{0,1},{1,0},{2,3},{3,2},{4,5},{5,4},{6,7},{7,6},{8,9},{9,8},{10,11... | collective-permute-start | bytes 3538952 | tf_op jit(solution)/shard_map/ppermute | solution.py:346
  63.3 56.2 %collective-permute-start.32 = (bf16[384,1536]{1,0:T(8,128)(2,1)}, bf16[384,1536]{1,0:T(8,128)(2,1)}, u32[]{:S(2)}, u32[]{:S(2)}) collective-permute-start(bf16[384,1536]{1,0:T(8,128)(2,1)} %collective-permute-done.31), channel_id=1, source_target_pairs={{0,4},{2,6},{4,12},{6,14},{8,0},{10,2},{12,8},{14,10},{1,5},{3,7},... | collective-permute-start | bytes 3538952 | tf_op jit(solution)/shard_map/ppermute | solution.py:368
  101.8 18.1 %collective-permute-start.10 = (f32[8,384]{1,0:T(8,128)}, f32[8,384]{1,0:T(8,128)}, u32[]{:S(2)}, u32[]{:S(2)}) collective-permute-start(f32[8,384]{1,0:T(8,128)} %collective-permute-done.9), channel_id=1, source_target_pairs={{0,4},{2,6},{4,12},{6,14},{8,0},{10,2},{12,8},{14,10},{1,5},{3,7},... | collective-permute-start | bytes 36872 | tf_op jit(solution)/shard_map/ppermute | solution.py:368
  127.9 30.7 %collective-permute-start.36 = (bf16[384,1536]{1,0:T(8,128)(2,1)}, bf16[384,1536]{1,0:T(8,128)(2,1)S(1)}, u32[]{:S(2)}, u32[]{:S(2)}) collective-permute-start(bf16[384,1536]{1,0:T(8,128)(2,1)} %collective-permute-done.32), channel_id=1, source_target_pairs={{0,1},{1,0},{2,3},{3,2},{4,5},{5,4},{6,7},{7,6},{8,9},{9,8},{10,11... | collective-permute-start | bytes 3538952 | tf_op jit(solution)/shard_map/ppermute | solution.py:346
  128.6 30.0 %collective-permute-start.33 = (bf16[384,1536]{1,0:T(8,128)(2,1)}, bf16[384,1536]{1,0:T(8,128)(2,1)}, u32[]{:S(2)}, u32[]{:S(2)}) collective-permute-start(bf16[384,1536]{1,0:T(8,128)(2,1)} %collective-permute-done.32), channel_id=1, source_target_pairs={{0,4},{2,6},{4,12},{6,14},{8,0},{10,2},{12,8},{14,10},{1,5},{3,7},... | collective-permute-start | bytes 3538952 | tf_op jit(solution)/shard_map/ppermute | solution.py:368
  131.3 51.7 %collective-permute-start.13 = (bf16[384,1536]{1,0:T(8,128)(2,1)S(1)}, bf16[384,1536]{1,0:T(8,128)(2,1)}, u32[]{:S(2)}, u32[]{:S(2)}) collective-permute-start(bf16[384,1536]{1,0:T(8,128)(2,1)S(1)} %multiply_convert_fusion.4), channel_id=1, source_target_pairs={{0,4},{2,6},{4,12},{6,14},{8,0},{10,2},{12,8},{14,10},{1,5},{3,7},... | collective-permute-start | bytes 3538952 | tf_op jit(solution)/shard_map/ppermute | solution.py:368
  136.6 49.8 %collective-permute-start.5 = (bf16[384,1536]{1,0:T(8,128)(2,1)S(1)}, bf16[384,1536]{1,0:T(8,128)(2,1)}, u32[]{:S(2)}, u32[]{:S(2)}) collective-permute-start(bf16[384,1536]{1,0:T(8,128)(2,1)S(1)} %multiply_convert_fusion.4), channel_id=1, source_target_pairs={{0,1},{1,0},{2,3},{3,2},{4,5},{5,4},{6,7},{7,6},{8,9},{9,8},{10,11... | collective-permute-start | bytes 3538952 | tf_op jit(solution)/shard_map/ppermute | solution.py:346
  158.6 47.8 %collective-permute-start.34 = (bf16[384,1536]{1,0:T(8,128)(2,1)}, bf16[384,1536]{1,0:T(8,128)(2,1)}, u32[]{:S(2)}, u32[]{:S(2)}) collective-permute-start(bf16[384,1536]{1,0:T(8,128)(2,1)} %collective-permute-done.33), channel_id=1, source_target_pairs={{0,1},{1,0},{2,3},{3,2},{4,5},{5,4},{6,7},{7,6},{8,9},{9,8},{10,11... | collective-permute-start | bytes 3538952 | tf_op jit(solution)/shard_map/ppermute | solution.py:346
  183.0 25.5 %collective-permute-start.22 = (bf16[384,1536]{1,0:T(8,128)(2,1)}, bf16[384,1536]{1,0:T(8,128)(2,1)}, u32[]{:S(2)}, u32[]{:S(2)}) collective-permute-start(bf16[384,1536]{1,0:T(8,128)(2,1)} %collective-permute-done.13), channel_id=1, source_target_pairs={{0,1},{1,0},{2,3},{3,2},{4,5},{5,4},{6,7},{7,6},{8,9},{9,8},{10,11... | collective-permute-start | bytes 3538952 | tf_op jit(solution)/shard_map/ppermute | solution.py:346
  183.1 42.6 %collective-permute-start.14 = (bf16[384,1536]{1,0:T(8,128)(2,1)}, bf16[384,1536]{1,0:T(8,128)(2,1)}, u32[]{:S(2)}, u32[]{:S(2)}) collective-permute-start(bf16[384,1536]{1,0:T(8,128)(2,1)} %collective-permute-done.13), channel_id=1, source_target_pairs={{0,4},{2,6},{4,12},{6,14},{8,0},{10,2},{12,8},{14,10},{1,5},{3,7},... | collective-permute-start | bytes 3538952 | tf_op jit(solution)/shard_map/ppermute | solution.py:368
  229.9 26.4 %collective-permute-start.39 = (bf16[384,1536]{1,0:T(8,128)(2,1)S(1)}, bf16[384,1536]{1,0:T(8,128)(2,1)S(1)}, u32[]{:S(2)}, u32[]{:S(2)}) collective-permute-start(bf16[384,1536]{1,0:T(8,128)(2,1)S(1)} %slice.276), channel_id=1, source_target_pairs={{0,1},{1,0},{2,3},{3,2},{4,5},{5,4},{6,7},{7,6},{8,9},{9,8},{10,11... | collective-permute-start | bytes 3538952 | tf_op jit(solution)/shard_map/ppermute | solution.py:346
  230.5 30.0 %collective-permute-start.15 = (bf16[384,1536]{1,0:T(8,128)(2,1)}, bf16[384,1536]{1,0:T(8,128)(2,1)}, u32[]{:S(2)}, u32[]{:S(2)}) collective-permute-start(bf16[384,1536]{1,0:T(8,128)(2,1)} %collective-permute-done.14), channel_id=1, source_target_pairs={{0,4},{2,6},{4,12},{6,14},{8,0},{10,2},{12,8},{14,10},{1,5},{3,7},... | collective-permute-start | bytes 3538952 | tf_op jit(solution)/shard_map/ppermute | solution.py:368
  237.8 48.0 %collective-permute-start.24 = (bf16[384,1536]{1,0:T(8,128)(2,1)S(1)}, bf16[384,1536]{1,0:T(8,128)(2,1)}, u32[]{:S(2)}, u32[]{:S(2)}) collective-permute-start(bf16[384,1536]{1,0:T(8,128)(2,1)S(1)} %add_convert_fusion.17), channel_id=1, source_target_pairs={{0,4},{2,6},{4,12},{6,14},{8,0},{10,2},{12,8},{14,10},{1,5},{3,7},... | collective-permute-start | bytes 3538952 | tf_op jit(solution)/shard_map/ppermute | solution.py:368
  256.3 29.5 %collective-permute-start.20 = (bf16[384,1536]{1,0:T(8,128)(2,1)}, bf16[384,1536]{1,0:T(8,128)(2,1)}, u32[]{:S(2)}, u32[]{:S(2)}) collective-permute-start(bf16[384,1536]{1,0:T(8,128)(2,1)} %slice.262), channel_id=1, source_target_pairs={{0,1},{1,0},{2,3},{3,2},{4,5},{5,4},{6,7},{7,6},{8,9},{9,8},{10,11... | collective-permute-start | bytes 3538952 | tf_op jit(solution)/shard_map/ppermute | solution.py:346
  256.6 98.8 %collective-permute-start.40 = (bf16[384,1536]{1,0:T(8,128)(2,1)S(1)}, bf16[384,1536]{1,0:T(8,128)(2,1)}, u32[]{:S(2)}, u32[]{:S(2)}) collective-permute-start(bf16[384,1536]{1,0:T(8,128)(2,1)S(1)} %add_convert_fusion.13), channel_id=1, source_target_pairs={{0,4},{2,6},{4,12},{6,14},{8,0},{10,2},{12,8},{14,10},{1,5},{3,7},... | collective-permute-start | bytes 3538952 | tf_op jit(solution)/shard_map/ppermute | solution.py:368
  260.5 29.7 %collective-permute-start.16 = (bf16[384,1536]{1,0:T(8,128)(2,1)}, bf16[384,1536]{1,0:T(8,128)(2,1)S(1)}, u32[]{:S(2)}, u32[]{:S(2)}) collective-permute-start(bf16[384,1536]{1,0:T(8,128)(2,1)} %collective-permute-done.15), channel_id=1, source_target_pairs={{0,1},{1,0},{2,3},{3,2},{4,5},{5,4},{6,7},{7,6},{8,9},{9,8},{10,11... | collective-permute-start | bytes 3538952 | tf_op jit(solution)/shard_map/ppermute | solution.py:346
  265.8 89.8 %collective-permute-start.37 = (bf16[384,1536]{1,0:T(8,128)(2,1)}, bf16[384,1536]{1,0:T(8,128)(2,1)}, u32[]{:S(2)}, u32[]{:S(2)}) collective-permute-start(bf16[384,1536]{1,0:T(8,128)(2,1)} %slice.274), channel_id=1, source_target_pairs={{0,1},{1,0},{2,3},{3,2},{4,5},{5,4},{6,7},{7,6},{8,9},{9,8},{10,11... | collective-permute-start | bytes 3538952 | tf_op jit(solution)/shard_map/ppermute | solution.py:346
  288.9 121.5 %collective-permute-start.25 = (bf16[384,1536]{1,0:T(8,128)(2,1)}, bf16[384,1536]{1,0:T(8,128)(2,1)}, u32[]{:S(2)}, u32[]{:S(2)}) collective-permute-start(bf16[384,1536]{1,0:T(8,128)(2,1)} %add_convert_fusion.16), channel_id=1, source_target_pairs={{0,4},{2,6},{4,12},{6,14},{8,0},{10,2},{12,8},{14,10},{1,5},{3,7},... | collective-permute-start | bytes 3538952 | tf_op jit(solution)/shard_map/ppermute | solution.py:368
  355.5 33.4 %collective-permute-start.43 = (f32[8,384]{1,0:T(8,128)S(1)}, f32[8,384]{1,0:T(8,128)S(1)}, u32[]{:S(2)}, u32[]{:S(2)}) collective-permute-start(f32[8,384]{1,0:T(8,128)S(1)} %slice.278), channel_id=1, source_target_pairs={{0,1},{1,0},{2,3},{3,2},{4,5},{5,4},{6,7},{7,6},{8,9},{9,8},{10,11... | collective-permute-start | bytes 36872 | tf_op jit(solution)/shard_map/ppermute | solution.py:346
  359.6 47.4 %collective-permute-start.41 = (bf16[384,1536]{1,0:T(8,128)(2,1)S(1)}, bf16[384,1536]{1,0:T(8,128)(2,1)S(1)}, u32[]{:S(2)}, u32[]{:S(2)}) collective-permute-start(bf16[384,1536]{1,0:T(8,128)(2,1)S(1)} %add_convert_fusion.12), channel_id=1, source_target_pairs={{0,4},{2,6},{4,12},{6,14},{8,0},{10,2},{12,8},{14,10},{1,5},{3,7},... | collective-permute-start | bytes 3538952 | tf_op jit(solution)/shard_map/ppermute | solution.py:368
  362.9 25.5 %collective-permute-start.48 = (f32[8,384]{1,0:T(8,128)S(1)}, f32[8,384]{1,0:T(8,128)S(1)}, u32[]{:S(2)}, u32[]{:S(2)}) collective-permute-start(f32[8,384]{1,0:T(8,128)S(1)} %fusion.162), channel_id=1, source_target_pairs={{0,4},{2,6},{4,12},{6,14},{8,0},{10,2},{12,8},{14,10},{1,5},{3,7},... | collective-permute-start | bytes 36872 | tf_op jit(solution)/shard_map/ppermute | solution.py:368
  363.3 42.8 %collective-permute-start.89 = (bf16[768,768]{1,0:T(8,128)(2,1)S(1)}, bf16[768,768]{1,0:T(8,128)(2,1)S(1)}, u32[]{:S(2)}, u32[]{:S(2)}) collective-permute-start(bf16[768,768]{1,0:T(8,128)(2,1)S(1)} %get-tuple-element.85), channel_id=1, source_target_pairs={{1,3},{2,0},{5,7},{6,4},{9,11},{10,8},{13,15},{14,12},{17,19},{18,... | collective-permute-start | bytes 3538952 | tf_op jit(solution)/shard_map/ppermute | solution.py:373
  388.9 19.7 %collective-permute-start.35 = (bf16[384,1536]{1,0:T(8,128)(2,1)S(1)}, bf16[384,1536]{1,0:T(8,128)(2,1)S(1)}, u32[]{:S(2)}, u32[]{:S(2)}) collective-permute-start(bf16[384,1536]{1,0:T(8,128)(2,1)S(1)} %slice.272), channel_id=1, source_target_pairs={{0,1},{1,0},{2,3},{3,2},{4,5},{5,4},{6,7},{7,6},{8,9},{9,8},{10,11... | collective-permute-start | bytes 3538952 | tf_op jit(solution)/shard_map/ppermute | solution.py:346
  406.1 43.7 %collective-permute-start.30 = (bf16[384,1536]{1,0:T(8,128)(2,1)S(1)}, bf16[384,1536]{1,0:T(8,128)(2,1)S(1)}, u32[]{:S(2)}, u32[]{:S(2)}) collective-permute-start(bf16[384,1536]{1,0:T(8,128)(2,1)S(1)} %copy-done.50), channel_id=1, source_target_pairs={{0,1},{1,0},{2,3},{3,2},{4,5},{5,4},{6,7},{7,6},{8,9},{9,8},{10,11... | collective-permute-start | bytes 3538952 | tf_op jit(solution)/shard_map/ppermute | solution.py:346
  407.0 28.9 %collective-permute-start.86 = (bf16[768,768]{0,1:T(8,128)(2,1)S(1)}, bf16[768,768]{0,1:T(8,128)(2,1)S(1)}, u32[]{:S(2)}, u32[]{:S(2)}) collective-permute-start(bf16[768,768]{0,1:T(8,128)(2,1)S(1)} %constant_dynamic-slice_fusion.2), channel_id=1, source_target_pairs={{0,16},{16,0},{1,17},{17,1},{2,18},{18,2},{3,19},{19,3},{4,20},{20... | collective-permute-start | bytes 3538952 | tf_op jit(solution)/shard_map/ppermute | solution.py:350
  408.6 28.6 %collective-permute-start.92 = (bf16[384,768]{1,0:T(8,128)(2,1)S(1)}, bf16[384,768]{1,0:T(8,128)(2,1)S(1)}, u32[]{:S(2)}, u32[]{:S(2)}) collective-permute-start(bf16[384,768]{1,0:T(8,128)(2,1)S(1)} %add_convert_fusion.21), channel_id=1, source_target_pairs={{1,3},{2,0},{5,7},{6,4},{9,11},{10,8},{13,15},{14,12},{17,19},{18,... | collective-permute-start | bytes 1769480 | tf_op jit(solution)/shard_map/ppermute | solution.py:373
  410.4 40.8 %collective-permute-start.42 = (bf16[384,1536]{1,0:T(8,128)(2,1)S(1)}, bf16[384,1536]{1,0:T(8,128)(2,1)S(1)}, u32[]{:S(2)}, u32[]{:S(2)}) collective-permute-start(bf16[384,1536]{1,0:T(8,128)(2,1)S(1)} %add_convert_fusion.11), channel_id=1, source_target_pairs={{0,4},{2,6},{4,12},{6,14},{8,0},{10,2},{12,8},{14,10},{1,5},{3,7},... | collective-permute-start | bytes 3538952 | tf_op jit(solution)/shard_map/ppermute | solution.py:368
  411.3 36.3 %collective-permute-start.90 = (bf16[384,768]{1,0:T(8,128)(2,1)S(1)}, bf16[384,768]{1,0:T(8,128)(2,1)S(1)}, u32[]{:S(2)}, u32[]{:S(2)}) collective-permute-start(bf16[384,768]{1,0:T(8,128)(2,1)S(1)} %constant_dynamic-slice_fusion.1), channel_id=1, source_target_pairs={{0,16},{16,0},{1,17},{17,1},{2,18},{18,2},{3,19},{19,3},{4,20},{20... | collective-permute-start | bytes 1769480 | tf_op jit(solution)/shard_map/ppermute | solution.py:350
  435.9 48.7 %collective-permute-start.8 = (bf16[384,1536]{1,0:T(8,128)(2,1)}, bf16[384,1536]{1,0:T(8,128)(2,1)}, u32[]{:S(2)}, u32[]{:S(2)}) collective-permute-start(bf16[384,1536]{1,0:T(8,128)(2,1)} %slice.254), channel_id=1, source_target_pairs={{0,1},{1,0},{2,3},{3,2},{4,5},{5,4},{6,7},{7,6},{8,9},{9,8},{10,11... | collective-permute-start | bytes 3538952 | tf_op jit(solution)/shard_map/ppermute | solution.py:346
  437.3 74.4 %collective-permute-start.84 = (bf16[1536,768]{0,1:T(8,128)(2,1)}, bf16[1536,768]{0,1:T(8,128)(2,1)}, u32[]{:S(2)}, u32[]{:S(2)}) collective-permute-start(bf16[1536,768]{0,1:T(8,128)(2,1)} %get-tuple-element.68), channel_id=1, source_target_pairs={{1,3},{2,0},{5,7},{6,4},{9,11},{10,8},{13,15},{14,12},{17,19},{18,... | collective-permute-start | bytes 7077896 | tf_op jit(solution)/shard_map/ppermute | solution.py:373
  447.6 37.0 %collective-permute-start.26 = (bf16[384,1536]{1,0:T(8,128)(2,1)}, bf16[384,1536]{1,0:T(8,128)(2,1)}, u32[]{:S(2)}, u32[]{:S(2)}) collective-permute-start(bf16[384,1536]{1,0:T(8,128)(2,1)} %add_convert_fusion.15), channel_id=1, source_target_pairs={{0,4},{2,6},{4,12},{6,14},{8,0},{10,2},{12,8},{14,10},{1,5},{3,7},... | collective-permute-start | bytes 3538952 | tf_op jit(solution)/shard_map/ppermute | solution.py:368
  449.7 58.4 %collective-permute-start.87 = (bf16[768,768]{0,1:T(8,128)(2,1)}, bf16[768,768]{0,1:T(8,128)(2,1)}, u32[]{:S(2)}, u32[]{:S(2)}) collective-permute-start(bf16[768,768]{0,1:T(8,128)(2,1)} %add_convert_fusion.9), channel_id=1, source_target_pairs={{1,3},{2,0},{5,7},{6,4},{9,11},{10,8},{13,15},{14,12},{17,19},{18,... | collective-permute-start | bytes 3538952 | tf_op jit(solution)/shard_map/ppermute | solution.py:373
  451.2 64.9 %collective-permute-start.93 = (bf16[192,1536]{1,0:T(8,128)(2,1)}, bf16[192,1536]{1,0:T(8,128)(2,1)}, u32[]{:S(2)}, u32[]{:S(2)}) collective-permute-start(bf16[192,1536]{1,0:T(8,128)(2,1)} %fusion.134), channel_id=1, source_target_pairs={{0,1},{1,0},{2,3},{3,2},{4,5},{5,4},{6,7},{7,6},{8,9},{9,8},{10,11... | collective-permute-start | bytes 1769480 | tf_op jit(solution)/shard_map/ppermute | solution.py:346
  488.2 50.8 %collective-permute-start.27 = (bf16[192,1536]{1,0:T(8,128)(2,1)}, bf16[192,1536]{1,0:T(8,128)(2,1)}, u32[]{:S(2)}, u32[]{:S(2)}) collective-permute-start(bf16[192,1536]{1,0:T(8,128)(2,1)} %get-tuple-element.106), channel_id=1, source_target_pairs={{0,16},{16,0},{1,17},{17,1},{2,18},{18,2},{3,19},{19,3},{4,20},{20... | collective-permute-start | bytes 1769480 | tf_op jit(solution)/shard_map/ppermute | solution.py:350
  508.1 28.1 %collective-permute-start.71 = (bf16[768,1536]{1,0:T(8,128)(2,1)S(1)}, bf16[768,1536]{1,0:T(8,128)(2,1)S(1)}, u32[]{:S(2)}, u32[]{:S(2)}) collective-permute-start(bf16[768,1536]{1,0:T(8,128)(2,1)S(1)} %constant_dynamic-slice_fusion.10), channel_id=1, source_target_pairs={{0,1},{1,0},{2,3},{3,2},{4,5},{5,4},{6,7},{7,6},{8,9},{9,8},{10,11... | collective-permute-start | bytes 7077896 | tf_op jit(solution)/shard_map/ppermute | solution.py:346
  530.1 28.9 %collective-permute-start.50 = (bf16[192,1536]{1,0:T(8,128)(2,1)S(1)}, bf16[192,1536]{1,0:T(8,128)(2,1)S(1)}, u32[]{:S(2)}, u32[]{:S(2)}) collective-permute-start(bf16[192,1536]{1,0:T(8,128)(2,1)S(1)} %get-tuple-element.102), channel_id=1, source_target_pairs={{0,16},{16,0},{1,17},{17,1},{2,18},{18,2},{3,19},{19,3},{4,20},{20... | collective-permute-start | bytes 1769480 | tf_op jit(solution)/shard_map/ppermute | solution.py:350
  534.7 78.7 %collective-permute-start.58 = (bf16[768,2048]{1,0:T(8,128)(2,1)S(1)}, bf16[768,2048]{1,0:T(8,128)(2,1)S(1)}, u32[]{:S(2)}, u32[]{:S(2)}) collective-permute-start(bf16[768,2048]{1,0:T(8,128)(2,1)S(1)} %constant_dynamic-slice_fusion.17), channel_id=1, source_target_pairs={{0,1},{1,0},{2,3},{3,2},{4,5},{5,4},{6,7},{7,6},{8,9},{9,8},{10,11... | collective-permute-start | bytes 9437192 | tf_op jit(solution)/shard_map/ppermute | solution.py:346
  534.7 49.6 %collective-permute-start.85 = (bf16[768,768]{0,1:T(8,128)(2,1)S(1)}, bf16[768,768]{0,1:T(8,128)(2,1)S(1)}, u32[]{:S(2)}, u32[]{:S(2)}) collective-permute-start(bf16[768,768]{0,1:T(8,128)(2,1)S(1)} %constant_dynamic-slice_fusion.3), channel_id=1, source_target_pairs={{0,16},{16,0},{1,17},{17,1},{2,18},{18,2},{3,19},{19,3},{4,20},{20... | collective-permute-start | bytes 3538952 | tf_op jit(solution)/shard_map/ppermute | solution.py:350
  537.1 47.5 %collective-permute-start.74 = (bf16[192,1536]{1,0:T(8,128)(2,1)S(1)}, bf16[192,1536]{1,0:T(8,128)(2,1)S(1)}, u32[]{:S(2)}, u32[]{:S(2)}) collective-permute-start(bf16[192,1536]{1,0:T(8,128)(2,1)S(1)} %get-tuple-element.91), channel_id=1, source_target_pairs={{0,18},{2,16},{4,22},{6,20},{8,26},{10,24},{12,30},{14,28},{16,2},... | collective-permute-start | bytes 1769480 | tf_op jit(solution)/shard_map/ppermute | solution.py:359
  539.0 45.6 %collective-permute-start.73 = (bf16[192,1536]{1,0:T(8,128)(2,1)S(1)}, bf16[192,1536]{1,0:T(8,128)(2,1)S(1)}, u32[]{:S(2)}, u32[]{:S(2)}) collective-permute-start(bf16[192,1536]{1,0:T(8,128)(2,1)S(1)} %get-tuple-element.92), channel_id=1, source_target_pairs={{0,2},{2,0},{4,6},{6,4},{8,10},{10,8},{12,14},{14,12},{1,3},{3,1},... | collective-permute-start | bytes 1769480 | tf_op jit(solution)/shard_map/ppermute | solution.py:354
  559.0 35.1 %collective-permute-start.72 = (bf16[192,1536]{1,0:T(8,128)(2,1)S(1)}, bf16[192,1536]{1,0:T(8,128)(2,1)S(1)}, u32[]{:S(2)}, u32[]{:S(2)}) collective-permute-start(bf16[192,1536]{1,0:T(8,128)(2,1)S(1)} %get-tuple-element.90), channel_id=1, source_target_pairs={{0,16},{16,0},{1,17},{17,1},{2,18},{18,2},{3,19},{19,3},{4,20},{20... | collective-permute-start | bytes 1769480 | tf_op jit(solution)/shard_map/ppermute | solution.py:350
  599.7 17.7 %collective-permute-start.88 = (bf16[384,1536]{0,1:T(8,128)(2,1)S(1)}, bf16[384,1536]{0,1:T(8,128)(2,1)S(1)}, u32[]{:S(2)}, u32[]{:S(2)}) collective-permute-start(bf16[384,1536]{0,1:T(8,128)(2,1)S(1)} %fusion.109), channel_id=1, source_target_pairs={{0,1},{1,0},{2,3},{3,2},{4,5},{5,4},{6,7},{7,6},{8,9},{9,8},{10,11... | collective-permute-start | bytes 3538952 | tf_op jit(solution)/shard_map/ppermute | solution.py:346
  610.8 14.9 %collective-permute-start.78 = (bf16[48,1536]{1,0:T(8,128)(2,1)S(1)}, bf16[48,1536]{1,0:T(8,128)(2,1)}, u32[]{:S(2)}, u32[]{:S(2)}) collective-permute-start(bf16[48,1536]{1,0:T(8,128)(2,1)S(1)} %add_convert_fusion.29), channel_id=1, source_target_pairs={{0,4},{2,6},{4,0},{6,2},{8,12},{10,14},{12,8},{14,10},{1,5},{3,7},... | collective-permute-start | bytes 442376 | tf_op jit(solution)/shard_map/ppermute | solution.py:363
  617.2 21.6 %collective-permute-start.61 = (bf16[192,2048]{1,0:T(8,128)(2,1)}, bf16[192,2048]{1,0:T(8,128)(2,1)S(1)}, u32[]{:S(2)}, u32[]{:S(2)}) collective-permute-start(bf16[192,2048]{1,0:T(8,128)(2,1)} %get-tuple-element.78), channel_id=1, source_target_pairs={{0,18},{2,16},{4,22},{6,20},{8,26},{10,24},{12,30},{14,28},{16,2},... | collective-permute-start | bytes 2359304 | tf_op jit(solution)/shard_map/ppermute | solution.py:359
  617.4 33.7 %collective-permute-start.60 = (bf16[192,2048]{1,0:T(8,128)(2,1)}, bf16[192,2048]{1,0:T(8,128)(2,1)}, u32[]{:S(2)}, u32[]{:S(2)}) collective-permute-start(bf16[192,2048]{1,0:T(8,128)(2,1)} %get-tuple-element.79), channel_id=1, source_target_pairs={{0,2},{2,0},{4,6},{6,4},{8,10},{10,8},{12,14},{14,12},{1,3},{3,1},... | collective-permute-start | bytes 2359304 | tf_op jit(solution)/shard_map/ppermute | solution.py:354
  618.9 33.6 %collective-permute-start.59 = (bf16[192,2048]{1,0:T(8,128)(2,1)}, bf16[192,2048]{1,0:T(8,128)(2,1)}, u32[]{:S(2)}, u32[]{:S(2)}) collective-permute-start(bf16[192,2048]{1,0:T(8,128)(2,1)} %get-tuple-element.77), channel_id=1, source_target_pairs={{0,16},{16,0},{1,17},{17,1},{2,18},{18,2},{3,19},{19,3},{4,20},{20... | collective-permute-start | bytes 2359304 | tf_op jit(solution)/shard_map/ppermute | solution.py:350
  656.7 17.2 %collective-permute-start.63 = (bf16[48,2048]{1,0:T(8,128)(2,1)S(1)}, bf16[48,2048]{1,0:T(8,128)(2,1)S(1)}, u32[]{:S(2)}, u32[]{:S(2)}) collective-permute-start(bf16[48,2048]{1,0:T(8,128)(2,1)S(1)} %get-tuple-element.119), channel_id=1, source_target_pairs={{0,8},{2,10},{4,12},{6,14},{8,0},{10,2},{12,4},{14,6},{1,9},{3,11}... | collective-permute-start | bytes 589832 | tf_op jit(solution)/shard_map/ppermute | solution.py:363
  656.7 17.2 %collective-permute-start.62 = (bf16[48,2048]{1,0:T(8,128)(2,1)S(1)}, bf16[48,2048]{1,0:T(8,128)(2,1)S(1)}, u32[]{:S(2)}, u32[]{:S(2)}) collective-permute-start(bf16[48,2048]{1,0:T(8,128)(2,1)S(1)} %get-tuple-element.117), channel_id=1, source_target_pairs={{0,4},{2,6},{4,0},{6,2},{8,12},{10,14},{12,8},{14,10},{1,5},{3,7},... | collective-permute-start | bytes 589832 | tf_op jit(solution)/shard_map/ppermute | solution.py:363
  676.1 15.2 %collective-permute-start.66 = (bf16[48,2048]{1,0:T(8,128)(2,1)S(1)}, bf16[48,2048]{1,0:T(8,128)(2,1)S(1)}, u32[]{:S(2)}, u32[]{:S(2)}) collective-permute-start(bf16[48,2048]{1,0:T(8,128)(2,1)S(1)} %add_convert_fusion.26), channel_id=1, source_target_pairs={{0,8},{2,10},{4,12},{6,14},{8,0},{10,2},{12,4},{14,6},{1,9},{3,11}... | collective-permute-start | bytes 589832 | tf_op jit(solution)/shard_map/ppermute | solution.py:363
  676.1 15.2 %collective-permute-start.65 = (bf16[48,2048]{1,0:T(8,128)(2,1)S(1)}, bf16[48,2048]{1,0:T(8,128)(2,1)S(1)}, u32[]{:S(2)}, u32[]{:S(2)}) collective-permute-start(bf16[48,2048]{1,0:T(8,128)(2,1)S(1)} %add_convert_fusion.26), channel_id=1, source_target_pairs={{0,4},{2,6},{4,0},{6,2},{8,12},{10,14},{12,8},{14,10},{1,5},{3,7},... | collective-permute-start | bytes 589832 | tf_op jit(solution)/shard_map/ppermute | solution.py:363
  678.6 17.2 %collective-permute-start.83 = (bf16[192,1536]{1,0:T(8,128)(2,1)S(1)}, bf16[192,1536]{1,0:T(8,128)(2,1)S(1)}, u32[]{:S(2)}, u32[]{:S(2)}) collective-permute-start(bf16[192,1536]{1,0:T(8,128)(2,1)S(1)} %get-tuple-element.123), channel_id=1, source_target_pairs={{0,18},{2,16},{4,22},{6,20},{8,26},{10,24},{12,30},{14,28},{16,2},... | collective-permute-start | bytes 1769480 | tf_op jit(solution)/shard_map/ppermute | solution.py:359
  679.2 41.0 %collective-permute-start.82 = (bf16[192,1536]{1,0:T(8,128)(2,1)S(1)}, bf16[192,1536]{1,0:T(8,128)(2,1)S(1)}, u32[]{:S(2)}, u32[]{:S(2)}) collective-permute-start(bf16[192,1536]{1,0:T(8,128)(2,1)S(1)} %get-tuple-element.123), channel_id=1, source_target_pairs={{0,16},{16,0},{1,17},{17,1},{2,18},{18,2},{3,19},{19,3},{4,20},{20... | collective-permute-start | bytes 1769480 | tf_op jit(solution)/shard_map/ppermute | solution.py:350
  683.9 36.3 %collective-permute-start.81 = (bf16[192,1536]{1,0:T(8,128)(2,1)S(1)}, bf16[192,1536]{1,0:T(8,128)(2,1)S(1)}, u32[]{:S(2)}, u32[]{:S(2)}) collective-permute-start(bf16[192,1536]{1,0:T(8,128)(2,1)S(1)} %get-tuple-element.123), channel_id=1, source_target_pairs={{0,2},{2,0},{4,6},{6,4},{8,10},{10,8},{12,14},{14,12},{1,3},{3,1},... | collective-permute-start | bytes 1769480 | tf_op jit(solution)/shard_map/ppermute | solution.py:354
  691.7 33.7 %collective-permute-start.70 = (bf16[192,2048]{1,0:T(8,128)(2,1)S(1)}, bf16[192,2048]{1,0:T(8,128)(2,1)S(1)}, u32[]{:S(2)}, u32[]{:S(2)}) collective-permute-start(bf16[192,2048]{1,0:T(8,128)(2,1)S(1)} %get-tuple-element.112), channel_id=1, source_target_pairs={{0,18},{2,16},{4,22},{6,20},{8,26},{10,24},{12,30},{14,28},{16,2},... | collective-permute-start | bytes 2359304 | tf_op jit(solution)/shard_map/ppermute | solution.py:359
  692.1 46.9 %collective-permute-start.69 = (bf16[192,2048]{1,0:T(8,128)(2,1)S(1)}, bf16[192,2048]{1,0:T(8,128)(2,1)S(1)}, u32[]{:S(2)}, u32[]{:S(2)}) collective-permute-start(bf16[192,2048]{1,0:T(8,128)(2,1)S(1)} %get-tuple-element.112), channel_id=1, source_target_pairs={{0,16},{16,0},{1,17},{17,1},{2,18},{18,2},{3,19},{19,3},{4,20},{20... | collective-permute-start | bytes 2359304 | tf_op jit(solution)/shard_map/ppermute | solution.py:350
  695.8 43.2 %collective-permute-start.68 = (bf16[192,2048]{1,0:T(8,128)(2,1)S(1)}, bf16[192,2048]{1,0:T(8,128)(2,1)S(1)}, u32[]{:S(2)}, u32[]{:S(2)}) collective-permute-start(bf16[192,2048]{1,0:T(8,128)(2,1)S(1)} %get-tuple-element.112), channel_id=1, source_target_pairs={{0,2},{2,0},{4,6},{6,4},{8,10},{10,8},{12,14},{14,12},{1,3},{3,1},... | collective-permute-start | bytes 2359304 | tf_op jit(solution)/shard_map/ppermute | solution.py:354
  (147 other events, 1756.4 us)

commit v2 on v0

--- a/solution.py
+++ b/solution.py
@@ -1,6 +1,10 @@
+import functools
+
 import jax
 import jax.numpy as jnp
 from jax import lax
+from jax.experimental import pallas as pl
+from jax.experimental.pallas import tpu as pltpu
 from jax.sharding import PartitionSpec as P
 
 QUERY_HEADS = 12
@@ -61,7 +65,7 @@
     return jax.nn.gelu(gate_up[:, :hidden_width], approximate=True) * gate_up[:, hidden_width:]
 
 
-def shards(
+def routed_shards(
     hidden_in,
     cotangent,
     deal_order,
@@ -339,7 +343,857 @@
     )
 
 
+RING_NEXT = (1, 3, 0, 2)
+LAST_WITH_LAST = (((1,), (1,)), ((), ()))
+
+
+def after(value, *earlier):
+    return lax.optimization_barrier((value, *earlier))[0]
+
+
+def part(*fields):
+    return lax.optimization_barrier(fields)
+
+
+def other_core(field):
+    return lax.ppermute(field, "shard", [(0, 1), (1, 0)])
+
+
+def other_dp(field):
+    return lax.ppermute(field, "dp", [(0, 1), (1, 0)])
+
+
+def across_x(field):
+    return lax.ppermute(field, "expert", [(i, i ^ 1) for i in range(8)])
+
+
+def across_dp_x(field):
+    pairs = [(d * 8 + e, (1 - d) * 8 + (e ^ 1)) for d in range(2) for e in range(8)]
+    return lax.ppermute(field, ("dp", "expert"), pairs)
+
+
+def across_z(field, distance):
+    return lax.ppermute(field, "expert", [(i, i ^ (2 * distance)) for i in range(8)])
+
+
+def ring_z(field):
+    pairs = [(2 * z + x, 2 * RING_NEXT[z] + x) for z in range(4) for x in range(2)]
+    return lax.ppermute(field, "expert", pairs)
+
+
+def to_owner(field):
+    pairs = [(e * 2 + c, (e ^ 1) * 2 + c) for e in range(8) for c in range(2) if e % 2 != c]
+    return lax.ppermute(field, ("expert", "shard"), pairs)
+
+
+def from_owner(field):
+    pairs = [(e * 2 + c, (e ^ 1) * 2 + c) for e in range(8) for c in range(2) if e % 2 == c]
+    return lax.ppermute(field, ("expert", "shard"), pairs)
+
+
+def in_order(first, own, received, axis=0):
+    return jnp.where(
+        first,
+        jnp.concatenate([own, received], axis=axis),
+        jnp.concatenate([received, own], axis=axis),
+    )
+
+
+def block(field, index, count):
+    rows = field.shape[0] // count
+    return lax.dynamic_slice_in_dim(field, index * rows, rows, axis=0)
+
+
+def sum_blocks(*fields):
+    total = fields[0].astype(jnp.float32)
+    for field in fields[1:]:
+        total = total + field.astype(jnp.float32)
+    return total
+
+
+def low(field):
+    return field.astype(jnp.bfloat16)
+
+
+def reduce_chip(term, core):
+    return low(sum_blocks(block(term, core, 2), other_core(block(term, 1 - core, 2))))
+
+
+def slab_first(part, place):
+    dp, x, _, _ = place
+    first, second = jnp.split(part, 2)
+    return across_x(block(first, 1 - x, 2)), other_dp(block(second, 1 - dp, 2))
+
+
+def slab_second(part, sent, place):
+    dp, x, _, _ = place
+    first, second = jnp.split(part, 2)
+    first = low(sum_blocks(block(first, x, 2), sent[0]))
+    second = low(sum_blocks(block(second, dp, 2), sent[1]))
+    first = low(sum_blocks(block(first, dp, 2), other_dp(block(first, 1 - dp, 2))))
+    second = low(sum_blocks(block(second, x, 2), across_x(block(second, 1 - x, 2))))
+    return jnp.concatenate([first, second])
+
+
+def reduce_line(part, z):
+    return low(
+        sum_blocks(
+            block(part, z, 4), *[across_z(block(part, z ^ k, 4), k) for k in (1, 2, 3)]
+        )
+    )
+
+
+def put_in_order(pieces, own):
+    stacked = jnp.stack(pieces)
+    return jnp.concatenate(
+        [lax.dynamic_index_in_dim(stacked, own ^ b, 0, False) for b in range(len(pieces))]
+    )
+
+
+def spread_line(part, z):
+    return put_in_order([part] + [across_z(part, k) for k in (1, 2, 3)], z)
+
+
+def spread_first(part, place):
+    dp, x, _, _ = place
+    first, second = jnp.split(part, 2)
+    return in_order(dp == 0, first, other_dp(first)), in_order(x == 0, second, across_x(second))
+
+
+def spread_second(parts, place):
+    dp, x, _, _ = place
+    first, second = parts
+    first = in_order(x == 0, first, across_x(first))
+    second = in_order(dp == 0, second, other_dp(second))
+    return jnp.concatenate([first, second])
+
+
+def matmul(left, right, dims=(((1,), (0,)), ((), ()))):
+    return lax.dot_general(left, right, dims, preferred_element_type=jnp.float32)
+
+
+FIRST_WITH_FIRST = (((0,), (0,)), ((), ()))
+
+
+def expert_kernel(
+    is_own,
+    own_rows,
+    other_rows,
+    own_ct,
+    other_ct,
+    weight_ref,
+    up_own,
+    up_other,
+    down_own,
+    down_other,
+    *refs,
+    columns,
+):
+    (
+        own_sum,
+        other_sum,
+        own_back,
+        other_back,
+        gate_ref,
+        hidden_ref,
+        grad_out_ref,
+        grad_up_ref,
+        rows_ref,
+        ct_ref,
+        up_ref,
+        down_ref,
+        up_sem,
+        down_sem,
+    ) = refs[-14:]
+    width = down_ref.shape[0]
+    first = pl.program_id(0) == 0
+
+    @pl.when(first & (is_own[0] == 1))
+    def _():
+        pltpu.make_async_copy(up_own, up_ref, up_sem).start()
+        pltpu.make_async_copy(down_own, down_ref, down_sem).start()
+
+    @pl.when(first & (is_own[0] == 0))
+    def _():
+        pltpu.make_async_copy(up_other, up_ref, up_sem).start()
+        pltpu.make_async_copy(down_other, down_ref, down_sem).start()
+
+    @pl.when(first)
+    def _():
+        rows_ref[...] = own_rows[...]
+        ct_ref[...] = own_ct[...]
+        pltpu.make_async_copy(up_own, up_ref, up_sem).wait()
+        pltpu.make_async_copy(down_own, down_ref, down_sem).wait()
+
+    @pl.when(pl.program_id(0) == 1)
+    def _():
+        rows_ref[...] = other_rows[...]
+        ct_ref[...] = other_ct[...]
+
+    rows, weighting = rows_ref[...], weight_ref[...]
+    ct = ct_ref[...].astype(jnp.float32)
+    grad_out = low(weighting * ct)
+    grad_out_ref[...] = grad_out
+    for start in range(0, width, columns):
+        gate, up = pl.ds(start, columns), pl.ds(width + start, columns)
+        a, b = matmul(rows, up_ref[:, gate]), matmul(rows, up_ref[:, up])
+        tanh = jnp.tanh(0.7978845608028654 * (a + 0.044715 * a * a * a))
+        half = 0.5 * (1.0 + tanh)
+        gelu = a * half
+        hidden_ref[:, gate] = low(gelu * b)
+        grad_hidden = matmul(grad_out, down_ref[gate, :], LAST_WITH_LAST)
+        slope = half + 0.5 * a * (1.0 - tanh * tanh) * (
+            0.7978845608028654 * (1.0 + 3.0 * 0.044715 * a * a)
+        )
+        grad_up_ref[:, gate] = low(grad_hidden * b * slope)
+        grad_up_ref[:, up] = low(grad_hidden * gelu)
+    out = low(matmul(hidden_ref[...], down_ref[...])).astype(jnp.float32)
+    gate_ref[...] = jnp.sum(ct * out, axis=1, keepdims=True)
+    weighted = low(weighting * out)
+    back = low(matmul(grad_up_ref[...], up_ref[...], LAST_WITH_LAST))
+
+    @pl.when(pl.program_id(0) == 0)
+    def _():
+        own_sum[...], own_back[...] = weighted, back
+
+    @pl.when(pl.program_id(0) == 1)
+    def _():
+        other_sum[...], other_back[...] = weighted, back
+
+
+SHORT = pl.CostEstimate(flops=1000, bytes_accessed=1000, transcendentals=0)
+
+
+def expert_step(step, is_own, rows, upstream, weighting, matrices, kept):
+    tile, model_width = rows[0].shape
+    width = matrices[2].shape[0]
+    anywhere = pl.BlockSpec(memory_space=pl.ANY)
+
+    def placed(columns):
+        return pl.BlockSpec((tile, columns), lambda i: (2 * step + i, 0))
+
+    def shape(count, columns, dtype=jnp.bfloat16):
+        return jax.ShapeDtypeStruct((count * tile, columns), dtype)
+
+    same = pl.BlockSpec((tile, model_width), lambda i: (0, 0))
+    out_shape = [
+        *[shape(1, model_width)] * 4,
+        shape(2, 1, jnp.float32),
+        shape(8, width),
+        shape(8, model_width),
+        shape(8, 2 * width),
+        shape(8, model_width),
+    ]
+    operands = [is_own, *rows, *upstream, weighting, *matrices]
+    in_specs = [pl.BlockSpec(memory_space=pltpu.SMEM)] + [same] * 4 + [placed(1)] + [anywhere] * 4
+    aliases = {}
+    if kept is not None:
+        aliases = {len(operands) + i: 5 + i for i in range(4)}
+        operands += list(kept)
+        in_specs += [anywhere] * 4
+    results = pl.pallas_call(
+        functools.partial(expert_kernel, columns=256),
+        grid=(2,),
+        in_specs=in_specs,
+        out_specs=[
+            *[same] * 4,
+            pl.BlockSpec((tile, 1), lambda i: (i, 0)),
+            placed(width),
+            placed(model_width),
+            placed(2 * width),
+            placed(model_width),
+        ],
+        out_shape=out_shape,
+        scratch_shapes=[
+            pltpu.VMEM((tile, model_width), jnp.bfloat16),
+            pltpu.VMEM((model_width, 2 * width), jnp.bfloat16),
+            pltpu.VMEM((width, model_width), jnp.bfloat16),
+            pltpu.SemaphoreType.DMA,
+            pltpu.SemaphoreType.DMA,
+        ],
+        input_output_aliases=aliases,
+        compiler_params=pltpu.CompilerParams(vmem_limit_bytes=50 * 2**20),
+        cost_estimate=SHORT,
+    )(*operands)
+    return results[:2], results[2:4], results[4], results[5:]
+
+
+def middle_back_kernel(
+    back_own,
+    back_other,
+    back_ring,
+    logits_ref,
+    router_ref,
+    middle_ref,
+    scale_ref,
+    gain_ref,
+    ct_ref,
+    weight_ref,
+    grad_ref,
+    low_ref,
+    mix_ref,
+    gain_grad,
+):
+    rows = middle_ref.shape[0]
+    total = jnp.zeros(gain_grad.shape, jnp.float32)
+    for start in range(0, rows, HEAD_SIZE):
+        at = pl.ds(start, HEAD_SIZE)
+        grad = sum_blocks(back_own[at, :], back_other[at, :], back_ring[at, :])
+        grad = grad + matmul(logits_ref[:, at], router_ref[...], FIRST_WITH_FIRST)
+        middle, scale = middle_ref[at, :], scale_ref[at, :]
+        scaled = grad * gain_ref[...]
+        mean = jnp.mean(scaled * middle, axis=1, keepdims=True)
+        out = ct_ref[at, :].astype(jnp.float32) + scale * scaled - middle * (scale**3 * mean)
+        total = total + jnp.sum(middle * scale * grad, axis=0, keepdims=True)
+        grad_ref[at, :] = out
+        low_ref[at, :] = low(out)
+    gain_grad[...] = total
+    for start in range(0, weight_ref.shape[0], 256):
+        at = pl.ds(start, 256)
+        mix_ref[:, at] = low(matmul(low_ref[...], weight_ref[at, :], LAST_WITH_LAST))
+
+
+def middle_back(back, logits, router, middle, scale, gain, upstream, out_weight):
+    rows, model_width = middle.shape
+    shapes = [
+        ((rows, model_width), jnp.float32),
+        ((rows, model_width), jnp.bfloat16),
+        ((rows, out_weight.shape[0]), jnp.bfloat16),
+        ((1, model_width), jnp.float32),
+    ]
+    return pl.pallas_call(
+        middle_back_kernel,
+        out_shape=[jax.ShapeDtypeStruct(*shape) for shape in shapes],
+        compiler_params=pltpu.CompilerParams(vmem_limit_bytes=40 * 2**20),
+        cost_estimate=SHORT,
+    )(*back, logits, router, middle, scale, gain[None], upstream, out_weight)
+
+
+def product_kernel(left_ref, right_ref, out_ref):
+    out_ref[...] = low(matmul(left_ref[...], right_ref[...], FIRST_WITH_FIRST))
+
+
+def product(left, right):
+    depth, rows = left.shape
+    columns = right.shape[1]
+    tile = 384
+    return pl.pallas_call(
+        product_kernel,
+        grid=(rows // tile,),
+        in_specs=[
+            pl.BlockSpec((depth, tile), lambda i: (0, i)),
+            pl.BlockSpec((depth, columns), lambda i: (0, 0)),
+        ],
+        out_specs=pl.BlockSpec((tile, columns), lambda i: (i, 0)),
+        out_shape=jax.ShapeDtypeStruct((rows, columns), jnp.bfloat16),
+        compiler_params=pltpu.CompilerParams(vmem_limit_bytes=24 * 2**20),
+        cost_estimate=SHORT,
+    )(left, right)
+
+
+def turn(field, cosine, sine):
+    half = field.shape[1] // 2
+    turned = jnp.concatenate([field[:, half:], field[:, :half]], axis=1)
+    return field * cosine + turned * sine
+
+
+def attend_kernel(query_in, key_in, value_in, cos_ref, sin_ref, seg_row, seg_column, *refs):
+    query_ref, key_ref, value_ref, mix_ref = refs
+    cosine, sine = cos_ref[...], sin_ref[...]
+    query = low(turn(query_in[...], cosine, sine))
+    key = low(turn(key_in[...], cosine, sine))
+    value = low(value_in[...])
+    query_ref[...], key_ref[...], value_ref[...] = query, key, value
+    probs = probabilities(query, key, seg_row[...], seg_column[...])
+    mix_ref[...] = low(matmul(low(probs), value, FIRST_WITH_FIRST))
+
+
+def probabilities(query, key, seg_row, seg_column):
+    scores = matmul(key, query, LAST_WITH_LAST) * HEAD_SIZE ** (-0.5)
+    key_at = lax.broadcasted_iota(jnp.int32, scores.shape, 0)
+    query_at = lax.broadcasted_iota(jnp.int32, scores.shape, 1)
+    scores = jnp.where((seg_row == seg_column) & (key_at <= query_at), scores, -1e30)
+    raised = jnp.exp(scores - jnp.max(scores, axis=0, keepdims=True))
+    return raised / jnp.sum(raised, axis=0, keepdims=True)
+
+
+def attend(projected, cosine, sine, segment):
+    rows, width = projected.shape
+    groups, heads = KEY_VALUE_HEADS, QUERY_HEADS
+
+    def head(index):
+        return pl.BlockSpec((rows, HEAD_SIZE), lambda i: (0, index(i)))
+
+    def whole(*shape):
+        return pl.BlockSpec(shape, lambda i: (0, 0))
+
+    def shape(count):
+        return jax.ShapeDtypeStruct((rows, count * HEAD_SIZE), jnp.bfloat16)
+
+    group = lambda i: i // (heads // groups)
+    return pl.pallas_call(
+        attend_kernel,
+        grid=(heads,),
+        in_specs=[
+            head(lambda i: i),
+            head(lambda i: heads + group(i)),
+            head(lambda i: heads + groups + group(i)),
+            whole(rows, HEAD_SIZE),
+            whole(rows, HEAD_SIZE),
+            whole(1, rows),
+            whole(rows, 1),
+        ],
+        out_specs=[head(lambda i: i), head(group), head(group), head(lambda i: i)],
+        out_shape=[shape(heads), shape(groups), shape(groups), shape(heads)],
+        compiler_params=pltpu.CompilerParams(vmem_limit_bytes=16 * 2**20),
+        cost_estimate=SHORT,
+    )(projected, projected, projected, cosine, sine, segment[None, :], segment[:, None])
+
+
+def attend_back_kernel(
+    query_ref, key_ref, value_ref, grad_ref, cos_ref, sin_ref, seg_row, seg_column, out_ref, *sums
+):
+    key_sum, value_sum = sums
+    step = pl.program_id(0)
+    heads = pl.num_programs(0)
+    groups = KEY_VALUE_HEADS
+    group, place = step // (heads // groups), step % (heads // groups)
+    query, key, value, grad_mix = query_ref[...], key_ref[...], value_ref[...], grad_ref[...]
+    probs = probabilities(query, key, seg_row[...], seg_column[...])
+    grad_probs = matmul(value, grad_mix, LAST_WITH_LAST)
+    grad_scores = low(
+        probs * (grad_probs - jnp.sum(probs * grad_probs, axis=0, keepdims=True))
+    )
+    grad_query = matmul(grad_scores, key, FIRST_WITH_FIRST) * HEAD_SIZE ** (-0.5)
+    grad_query = turn(grad_query, cos_ref[...], -sin_ref[...])
+    grad_key = matmul(grad_scores, query) * HEAD_SIZE ** (-0.5)
+    grad_value = matmul(low(probs), grad_mix)
+
+    def put(head, field):
+        at = pl.multiple_of(head * HEAD_SIZE, HEAD_SIZE)
+        out_ref[:, pl.ds(at, HEAD_SIZE)] = low(field)
+
+    put(step, grad_query)
+
+    @pl.when(place == 0)
+    def _():
+        key_sum[...] = grad_key
+        value_sum[...] = grad_value
+
+    @pl.when(place > 0)
+    def _():
+        key_sum[...] += grad_key
+        value_sum[...] += grad_value
+
+    @pl.when(place == heads // groups - 1)
+    def _():
+        put(heads + group, turn(key_sum[...], cos_ref[...], -sin_ref[...]))
+        put(heads + groups + group, value_sum[...])
+
+
+def attend_back(query, key, value, grad_mix, cosine, sine, segment):
+    rows = query.shape[0]
+    heads, groups = QUERY_HEADS, KEY_VALUE_HEADS
+
+    def whole(*shape):
+        return pl.BlockSpec(shape, lambda i: (0, 0))
+
+    head = pl.BlockSpec((rows, HEAD_SIZE), lambda i: (0, i))
+    shared = pl.BlockSpec((rows, HEAD_SIZE), lambda i: (0, i // (heads // groups)))
+    width = (heads + 2 * groups) * HEAD_SIZE
+    return pl.pallas_call(
+        attend_back_kernel,
+        grid=(heads,),
+        in_specs=[
+            head,
+            shared,
+            shared,
+            head,
+            whole(rows, HEAD_SIZE),
+            whole(rows, HEAD_SIZE),
+            whole(1, rows),
+            whole(rows, 1),
+        ],
+        out_specs=whole(rows, width),
+        out_shape=jax.ShapeDtypeStruct((rows, width), jnp.bfloat16),
+        scratch_shapes=[pltpu.VMEM((rows, HEAD_SIZE), jnp.float32)] * 2,
+        compiler_params=pltpu.CompilerParams(vmem_limit_bytes=16 * 2**20),
+        cost_estimate=SHORT,
+    )(query, key, value, grad_mix, cosine, sine, segment[None, :], segment[:, None])
+
+
+def ring_shards(
+    hidden_in,
+    cotangent,
+    deal_order,
+    lengths,
+    routes,
+    attention_gain,
+    expert_gain,
+    qkv_weight,
+    out_weight,
+    router_weight,
+    gate_up_weight,
+    down_weight,
+):
+    count_of_rows = hidden_in.shape[0]
+    model_width = hidden_in.shape[1]
+    half_rows = count_of_rows // 2
+    expert_count = router_weight.shape[1]
+    dp, core, at = lax.axis_index("dp"), lax.axis_index("shard"), lax.axis_index("expert")
+    x, z = at % 2, at // 2
+    place = (dp, x, z, core)
+    expert_ids = jnp.arange(expert_count, dtype=jnp.int32)
+    row_ids = jnp.arange(count_of_rows, dtype=jnp.int32)
+
+    outer = (z == 0) | (z == 3)
+
+    def by_step(k1, k2, k3):
+        return [jnp.where(outer, k2, k1), k3, jnp.where(outer, k1, k2)]
+
+    def held_at(deal_rows):
+        return jnp.where(deal_rows // half_rows == dp, 0, half_rows) + deal_rows % half_rows
+
+    def arrange(own_half, other_half, order):
+        chosen = low(held_at(order)[:, None] == row_ids[None, :])
+        return low(matmul(chosen, jnp.concatenate([own_half, other_half], axis=0)))
+
+    def from_dealt(field, order):
+        return arrange(block(field, dp, 2), other_dp(block(field, 1 - dp, 2)), order)
+
+    def to_dealt(field):
+        chosen = low(held_at(deal_order[0])[None, :] == row_ids[:, None])
+        field = low(matmul(chosen, field))
+        return in_order(dp == 0, field[:half_rows], other_dp(field[half_rows:]))
+
+    hidden_out = block(hidden_in, 1 - dp, 2)
+    hidden_arrived = other_dp(hidden_out)
+    qkv_other, out_other, ct_1, up_other = (
+        send(after(field, hidden_out))
+        for send, field in (
+            (other_core, qkv_weight),
+            (other_core, out_weight),
+            (ring_z, cotangent),
+            (from_owner, gate_up_weight[0]),
+        )
+    )
+    small = jnp.concatenate([attention_gain[None], expert_gain[None], router_weight.T], axis=0)
+    small = in_order(core == 0, small, other_core(small), axis=1)
+    full_qkv = in_order(core == 0, qkv_weight, qkv_other)
+    full_out = in_order(core == 0, out_weight, out_other)
+    gain_first, gain_second = small[0].astype(jnp.float32), small[1].astype(jnp.float32)
+    full_router = small[2:].T
+    segment, token_position = positions_of(lengths[0], count_of_rows)
+    frequency = THETA ** (-jnp.arange(HEAD_SIZE // 2, dtype=jnp.float32) / (HEAD_SIZE // 2))
+    angles = token_position.astype(jnp.float32)[:, None] * frequency[None, :]
+    cosine = jnp.concatenate([jnp.cos(angles)] * 2, axis=1)
+    sine = jnp.concatenate([-jnp.sin(angles), jnp.sin(angles)], axis=1)
+    cosine, sine, full_qkv, hidden_arrived, gain_first, gain_second, full_router = part(
+        cosine, sine, full_qkv, hidden_arrived, gain_first, gain_second, full_router
+    )
+    tokens = arrange(block(hidden_in, dp, 2), hidden_arrived, deal_order[0])
+    residual = tokens.astype(jnp.float32)
+    inv_first = lax.rsqrt(jnp.mean(residual * residual, axis=1, keepdims=True) + EPS)
+    normed_attn = low(residual * inv_first * gain_first)
+    projected = matmul(normed_attn, full_qkv)
+    ct_1, projected, cotangent, full_out, down_own, routes = part(
+        ct_1, projected, cotangent, full_out, down_weight[0], routes
+    )
+
+    ct_2 = ring_z(ct_1)
+    down_other = from_owner(down_own)
+    ct_0_other = other_dp(block(cotangent, 1 - dp, 2))
+    query, key, value, attn_mix = attend(projected, cosine, sine, segment)
+    middle = residual + matmul(attn_mix, full_out)
+    inv_second = lax.rsqrt(jnp.mean(middle * middle, axis=1, keepdims=True) + EPS)
+    normed_0 = low(middle * inv_second * gain_second)
+    ct_2, ct_0_other, normed_0, up_other, deal_order = part(
+        ct_2, ct_0_other, normed_0, up_other, deal_order
+    )
+
+    normed_1 = ring_z(normed_0)
+    logits = matmul(normed_0, full_router)
+    named = jnp.any(routes[:, :, None] == expert_ids[None, None, :], axis=1)
+    top_logit = jnp.max(jnp.where(named, logits, -jnp.inf), axis=1, keepdims=True)
+    exp_logits = jnp.where(named, jnp.exp(jnp.where(named, logits - top_logit, 0.0)), 0.0)
+    gates = (exp_logits / jnp.sum(exp_logits, axis=1, keepdims=True)).T
+    order_here = jnp.pad(deal_order.astype(jnp.float32), ((0, 7), (0, 0)))
+    gates_here = jnp.concatenate([gates, order_here], axis=0)
+    gates_here = [gates_here] + by_step(*[across_z(gates_here, k) for k in (1, 2, 3)])
+    orders = [field[expert_count].astype(jnp.int32) for field in gates_here]
+    gates_here = jnp.stack([field[:expert_count] for field in gates_here], axis=1)
+    own_row = (expert_ids == 2 * z + core)[:, None]
+    weighting = jnp.stack([gates_here, other_core(gates_here)], axis=2)
+    weighting = jnp.sum(jnp.where(own_row[:, :, None, None], weighting, 0.0), axis=0)
+    weighting = weighting.reshape(8 * count_of_rows, 1)
+    ct_0 = arrange(block(cotangent, dp, 2), ct_0_other, deal_order[0])
+    ct_0_other, normed_0_other = other_core(ct_0), other_core(normed_0)
+    ct_1, ct_1_other = block(ct_1, dp, 2), other_dp(block(ct_1, 1 - dp, 2))
+    (
+        normed_1,
+        weighting,
+        ct_0_other,
+        normed_0_other,
+        ct_1,
+        ct_1_other,
+        ct_2,
+        down_other,
+    ) = part(
+        normed_1,
+        weighting,
+        ct_0_other,
+        normed_0_other,
+        ct_1,
+        ct_1_other,
+        ct_2,
+        down_other,
+    )
+    is_own = (core == x).astype(jnp.int32)[None]
+    matrices = (gate_up_weight[0], up_other, down_weight[0], down_other)
+
+    def expert(step, rows, ct, kept):
+        return expert_step(step, is_own, rows, ct, weighting, matrices, kept)
+
+    ct_3 = ring_z(ct_2)
+    ct_2, ct_2_other = block(ct_2, dp, 2), other_dp(block(ct_2, 1 - dp, 2))
+    ct_1 = arrange(ct_1, ct_1_other, orders[1])
+    ct_1_other, normed_1_other = other_core(ct_1), other_core(normed_1)
+    sums_0, back_0, gate_0, kept = expert(0, (normed_0, normed_0_other), (ct_0, ct_0_other), None)
+    ct_3, ct_2, ct_2_other, ct_1, ct_1_other, normed_1, normed_1_other, kept = part(
+        ct_3, ct_2, ct_2_other, ct_1, ct_1_other, normed_1, normed_1_other, kept
+    )
+
+    normed_2 = ring_z(normed_1)
+    ct_3, ct_3_other = block(ct_3, dp, 2), other_dp(block(ct_3, 1 - dp, 2))
+    ct_2 = arrange(ct_2, ct_2_other, orders[2])
+    ct_2_other = other_core(ct_2)
+    sums_1, back_1, gate_1, kept = expert(1, (normed_1, normed_1_other), (ct_1, ct_1_other), kept)
+    normed_2, ct_3, ct_3_other, ct_2, ct_2_other, back_1, kept = part(
+        normed_2, ct_3, ct_3_other, ct_2, ct_2_other, back_1, kept
+    )
+
+    normed_3 = ring_z(normed_2)
+    back_1 = low(sum_blocks(back_1[0], other_core(back_1[1])))
+    normed_2_other = other_core(normed_2)
+    ct_3 = arrange(ct_3, ct_3_other, orders[3])
+    ct_3_other = other_core(ct_3)
+    sums_2, back_2, gate_2, kept = expert(2, (normed_2, normed_2_other), (ct_2, ct_2_other), kept)
+    normed_3, back_1, ct_3, ct_3_other, back_2, kept = part(
+        normed_3, back_1, ct_3, ct_3_other, back_2, kept
+    )
+
+    back_1 = ring_z(back_1)
+    normed_3_other = other_core(normed_3)
+    back_2_other = other_core(back_2[1])
+    sums_1 = low(sum_blocks(sums_1[0], other_core(sums_1[1])))
+    sums_3, back_3, gate_3, kept = expert(3, (normed_3, normed_3_other), (ct_3, ct_3_other), kept)
+    back_1, back_2_other, back_3, sums_1, kept = part(back_1, back_2_other, back_3, sums_1, kept)
+
+    back_2 = ring_z(low(sum_blocks(back_2[0], back_2_other, back_1)))
+    back_3_other = other_core(back_3[1])
+    all_hidden, all_grad_out, all_grad_up, all_rows = kept
+    half_width = model_width // 2
+    up_first = low(matmul(all_rows.T, all_grad_up[:, :half_width]))
+    up_second = low(matmul(all_rows.T, all_grad_up[:, half_width:]))
+    grad_gates = jnp.concatenate([gate_0, gate_1, gate_2, gate_3]).reshape(4, 2 * count_of_rows)
+    other_gates = other_core(grad_gates[:, count_of_rows:])
+    back_2, back_3_other, up_first, up_second, grad_gates, other_gates, sums_2 = part(
+        back_2, back_3_other, up_first, up_second, grad_gates, other_gates, sums_2
+    )
+
+    back_3 = ring_z(low(sum_blocks(back_3[0], back_3_other, back_2)))
+    up_first_other = to_owner(up_first)
+    up_second_other = other_dp(block(up_second, 1 - dp, 2))
+    back_0_other = other_core(back_0[1])
+    pairs = in_order(core == 0, grad_gates[:, None, :count_of_rows], other_gates[:, None], axis=1)
+    pairs = jnp.where((expert_ids // 2 == z)[None, :, None], jnp.tile(pairs, (1, 4, 1)), 0.0)
+    home = jnp.where(outer, pairs[3], pairs[1]), jnp.where(outer, pairs[1], pairs[3]), pairs[2]
+    home = [pairs[0]] + [across_z(home[k - 1], k) for k in (1, 2, 3)]
+    down_first = low(matmul(all_hidden.T, all_grad_out[:, :half_width]))
+    down_second = low(matmul(all_hidden.T, all_grad_out[:, half_width:]))
+    (
+        back_3,
+        up_first,
+        up_first_other,
+        up_second,
+        up_second_other,
+        down_first,
+        down_second,
+        home,
+        sums_1,
+        back_0_other,
+    ) = part(
+        back_3,
+        up_first,
+        up_first_other,
+        up_second,
+        up_second_other,
+        down_first,
+        down_second,
+        home,
+        sums_1,
+        back_0_other,
+    )
+
+    sums_1 = ring_z(sums_1)
+    down_first_other = to_owner(down_first)
+    down_second_other = other_dp(block(down_second, 1 - dp, 2))
+    up_first = low(sum_blocks(up_first, up_first_other))
+    up_second = low(sum_blocks(block(up_second, dp, 2), up_second_other))
+    up_first_other = other_dp(block(up_first, 1 - dp, 2))
+    up_second_other = to_owner(up_second)
+    sums_2_other = other_core(sums_2[1])
+    grad_gates = sum_blocks(*home)
+    mean_term = jnp.sum(gates * grad_gates, axis=0, keepdims=True)
+    grad_logits = low(gates * (grad_gates - mean_term))
+    grad_middle, grad_attn_out, grad_mix, term_gain_second = middle_back(
+        (back_0[0], back_0_other, back_3),
+        grad_logits,
+        full_router.T,
+        middle,
+        inv_second,
+        gain_second,
+        ct_0,
+        full_out,
+    )
+    grad_projected = attend_back(query, key, value, grad_mix, cosine, sine, segment)
+    term_out = product(attn_mix, grad_attn_out)
+    term_qkv = product(normed_attn, grad_projected)
+    (
+        sums_1,
+        down_first,
+        down_first_other,
+        down_second,
+        down_second_other,
+        up_first,
+        up_first_other,
+        up_second,
+        up_second_other,
+        sums_2_other,
+        term_out,
+        term_qkv,
+        grad_projected,
+    ) = part(
+        sums_1,
+        down_first,
+        down_first_other,
+        down_second,
+        down_second_other,
+        up_first,
+        up_first_other,
+        up_second,
+        up_second_other,
+        sums_2_other,
+        term_out,
+        term_qkv,
+        grad_projected,
+    )
+
+    sums_2 = ring_z(low(sum_blocks(sums_2[0], sums_2_other, sums_1)))
+    sums_3_other = other_core(sums_3[1])
+    chip_out, chip_qkv = reduce_chip(term_out, core), reduce_chip(term_qkv, core)
+    down_first = low(sum_blocks(down_first, down_first_other))
+    down_second = low(sum_blocks(block(down_second, dp, 2), down_second_other))
+    down_first_other = other_dp(block(down_first, 1 - dp, 2))
+    down_second_other = to_owner(down_second)
+    up_grad = [
+        sum_blocks(block(up_first, dp, 2), up_first_other),
+        sum_blocks(up_second, up_second_other),
+    ]
+    up_grad = low(jnp.concatenate(up_grad, axis=1))
+    up_grad_other = other_core(block(up_grad, 1 - core, 2))
+    grad_normed_attn = matmul(grad_projected, full_qkv, LAST_WITH_LAST)
+    grad_resid_norm, term_gain_first = norm_back(residual, inv_first, gain_first, grad_normed_attn)
+    grad_tokens = low(grad_middle + grad_resid_norm)
+    term_router = matmul(grad_logits, normed_0)
+    small_grad = jnp.concatenate([term_gain_first[None], term_gain_second, term_router])
+    (
+        sums_2,
+        sums_3_other,
+        chip_out,
+        chip_qkv,
+        down_first,
+        down_first_other,
+        down_second,
+        down_second_other,
+        up_grad,
+        up_grad_other,
+        grad_tokens,
+        small_grad,
+    ) = part(
+        sums_2,
+        sums_3_other,
+        chip_out,
+        chip_qkv,
+        down_first,
+        down_first_other,
+        down_second,
+        down_second_other,
+        up_grad,
+        up_grad_other,
+        grad_tokens,
+        small_grad,
+    )
+
+    sums_3 = ring_z(low(sum_blocks(sums_3[0], sums_3_other, sums_2)))
+    sums_0_other = other_core(sums_0[1])
+    out_sent, qkv_sent = slab_first(chip_out, place), slab_first(chip_qkv, place)
+    down_grad = [
+        sum_blocks(block(down_first, dp, 2), down_first_other),
+        sum_blocks(down_second, down_second_other),
+    ]
+    down_grad = low(jnp.concatenate(down_grad, axis=1))
+    down_grad_other = other_core(block(down_grad, 1 - core, 2))
+    down_grad = jnp.where(core == x, block(down_grad, core, 2), down_grad_other)
+    up_grad = jnp.where(core == x, block(up_grad, core, 2), up_grad_other)
+    down_grad, gate_up_grad = (field[None].astype(jnp.float32) for field in (down_grad, up_grad))
+    small_grad = small_grad + other_core(small_grad)
+    sums_3, sums_0_other, out_sent, qkv_sent, small_grad, grad_tokens = part(
+        sums_3, sums_0_other, out_sent, qkv_sent, small_grad, grad_tokens
+    )
+
+    slab_out, slab_qkv = (
+        slab_second(chip, sent, place) for chip, sent in ((chip_out, out_sent), (chip_qkv, qkv_sent))
+    )
+    input_gradient = to_dealt(grad_tokens)
+    layer_out = low(middle + sum_blocks(sums_0[0], sums_0_other, sums_3))
+    small_sent = other_dp(small_grad), across_x(small_grad), across_dp_x(small_grad)
+    slab_out, slab_qkv, small_grad, small_sent, layer_out = part(
+        slab_out, slab_qkv, small_grad, small_sent, layer_out
+    )
+
+    line_out, line_qkv = reduce_line(slab_out, z), reduce_line(slab_qkv, z)
+    layer_out = to_dealt(layer_out)
+    small_grad = sum_blocks(small_grad, *small_sent)
+    line_out, line_qkv, small_grad = part(line_out, line_qkv, small_grad)
+
+    line_out, line_qkv = spread_line(line_out, z), spread_line(line_qkv, z)
+    small_grad = sum_blocks(small_grad, *[across_z(small_grad, k) for k in (1, 2, 3)])
+    line_out, line_qkv, small_grad = part(line_out, line_qkv, small_grad)
+
+    out_parts, qkv_parts = spread_first(line_out, place), spread_first(line_qkv, place)
+    out_parts, qkv_parts = part(out_parts, qkv_parts)
+    out_grad = spread_second(out_parts, place).astype(jnp.float32)
+    qkv_grad = spread_second(qkv_parts, place).astype(jnp.float32)
+    small_grad = lax.dynamic_slice_in_dim(
+        small_grad, core * (model_width // 2), model_width // 2, axis=1
+    )
+    return (
+        layer_out,
+        input_gradient,
+        small_grad[0],
+        small_grad[1],
+        qkv_grad,
+        out_grad,
+        small_grad[2:].T,
+        gate_up_grad,
+        down_grad,
+    )
+
+
 def solution(mesh):
+    ringed = (mesh.shape["dp"], mesh.shape["expert"], mesh.shape["shard"]) == (2, 8, 2)
+    shards = ring_shards if ringed else routed_shards
     return jax.shard_map(
         shards,
         mesh=mesh,

time: 1510 us -> 622 us (0.41)
  blocking collectives: 787 us -> 0 us
  local copies, waits for them, and re-layouts: 219 us -> 50.9 us
  Pallas kernels: 0 us -> 117 us
  matrix products: 149 us -> 61.9 us
  starting transfers between devices: 25.5 us -> 102 us
  waiting for transfers between devices: 246 us -> 204 us
  other arithmetic: 55.4 us -> 72.7 us
    psum x1 -> x0, blocking collectives: 457 us -> none  [shards(): lax.psum((shard_terms[0], shard_terms[1], shard_terms[2], shard_terms[3],...]
    all_to_all x2 -> x0, blocking collectives: 321 us -> none  [the longest x1 162 us: shards(): lax.all_to_all(sending, 'expert', split_axis=0, concat_axis=0, tiled=True)]
    all_to_all x6 -> x0, waiting for transfers between devices: 245 us -> none  [the longest x1 123 us: shards(): lax.all_to_all(grad_rows_in.reshape(peer_count, capacity, model_width), '...]
    ppermute x0 -> x95, waiting for transfers between devices: none -> 204 us  [the longest x21 59.7 us: across_z(): lax.ppermute(field, 'expert', [(i, i ^ 2 * distance) for i in range(8)])]
    pallas_call x0 -> x9, Pallas kernels: none -> 117 us  [the longest x4 82 us: expert_step(): pl.pallas_call(functools.partial(expert_kernel, columns=256), grid=(2,),...]
    ppermute x0 -> x95, starting transfers between devices: none -> 102 us  [the longest x21 29.6 us: across_z(): lax.ppermute(field, 'expert', [(i, i ^ 2 * distance) for i in range(8)])]
    dot_general x21 -> x16, matrix products: 149 us -> 61.9 us  [matmul(): lax.dot_general(left, right, dims, preferred_element_type=jnp.float32)]
    gather x13 -> x0, local copies, waits for them, and re-layouts: 87.2 us -> none  [the longest x1 18.1 us: shards(): padded_grad[slot_pair].reshape(peer_count, capacity, model_width)]
  transfers between devices with their start and end apart: 13 -> 95, of which waited for: 4 -> 36; matrix products, arithmetic and copies ran while one was open for 19% -> 26% of each run, Pallas kernels for 0% -> 19%
where the time goes in v2:
time: 622 us; the launch traced here: 612 us
  waiting for transfers between devices  204 us (33%)
  Pallas kernels  117 us (19%)
  starting transfers between devices  102 us (16%)
  other arithmetic  72.7 us (12%)
  matrix products  61.9 us (10%)
  local copies, waits for them, and re-layouts  50.9 us (8%)
    pallas_call x4, Pallas kernels, expert_step(): pl.pallas_call(functools.partial(expert_kernel, columns=256), grid=(2,),...  82 us
    dot_general x16, matrix products, matmul(): lax.dot_general(left, right, dims, preferred_element_type=jnp.float32)  61.9 us
    ppermute x21, waiting for transfers between devices, across_z(): lax.ppermute(field, 'expert', [(i, i ^ 2 * distance) for i in range(8)])  59.7 us
    ppermute x20, waiting for transfers between devices, other_dp(): return lax.ppermute(field, 'dp', [(0, 1), (1, 0)])  53.3 us
    ppermute x9, waiting for transfers between devices, across_x(): return lax.ppermute(field, 'expert', [(i, i ^ 1) for i in range(8)])  48.5 us
    ppermute x12, waiting for transfers between devices, ring_z(): return lax.ppermute(field, 'expert', pairs)  39.2 us
    ppermute x21, starting transfers between devices, across_z(): lax.ppermute(field, 'expert', [(i, i ^ 2 * distance) for i in range(8)])  29.6 us
    convert_element_type x27, other arithmetic, low(): return field.astype(jnp.bfloat16)  28.6 us
  transfers between devices with their start and end apart: 95, of which 36 were waited for; matrix products, arithmetic and copies ran while one was open for 26% of the time, Pallas kernels for 19%

profile of v2, /device:TPU:0, one launch (start us, length us, event | category | flops | bytes accessed | tf_op | source)
XLA Modules:
  0.0 611.8 jit_solution(14011115554643365043)
XLA Ops:
  5.8 2.5 collective-permute-start.2
  12.1 3.7 collective-permute-start.7
  17.9 4.0 maximum_select_fusion.1.weight_ref
  21.9 6.6 %maximum_select_fusion = bf16[1536,2048]{1,0:T(8,128)(2,1)S(1)} fusion(bf16[768,2048]{1,0:T(8,128)(2,1)} %collective-permute-done.1, bf16[768,2048]{1,0:T(8,128)(2,1)S(1)} %copy-done.45, pred[]{:T(512)S(6)} %eq.234), kind=kLoop, calls=%fused_computation | loop fusion | flops 28311552 | bytes 12582913 | tf_op jit(solution)/shard_map/jit(_where)/select_n | solution.py:395
  28.6 2.4 fusion.18
  32.6 2.6 fusion.93.query_in.key_in.value_in
  35.2 2.4 collective-permute-done
  39.1 4.8 collective-permute-start.16
  43.9 9.1 %shard_map.187 = (bf16[384,1536]{1,0:T(8,128)(2,1)S(1)}, bf16[384,256]{1,0:T(8,128)(2,1)S(1)}, bf16[384,256]{1,0:T(8,128)(2,1)S(1)}, bf16[384,1536]{1,0:T(8,128)(2,1)S(1)}) custom-call(f32[384,2048]{1,0:T(8,128)S(1)} %fusion.93.query_in.key_in.value_in, f32[384,2048]{1,0:T(8,128)S(1)} %fusion.93.query_in.key_in.value_in, ...), custom_call_target="tpu_custom_call" | custom-call | flops 1000 | bytes 1000 | tf_op jit(solution)/shard_map/pallas_call | solution.py:734
  58.8 8.0 %collective-permute-done.5 = bf16[384,1536]{1,0:T(8,128)(2,1)} collective-permute-done((bf16[384,1536]{1,0:T(8,128)(2,1)}, bf16[384,1536]{1,0:T(8,128)(2,1)}, u32[]{:S(2)}, u32[]{:S(2)}) %collective-permute-start.5) | collective-permute-done | bytes 1179680 | tf_op jit(solution)/shard_map/ppermute | solution.py:381
  68.1 2.6 select_reduce_fusion.1
  70.8 2.7 collective-permute-start.11
  86.0 11.6 %collective-permute-done.15 = bf16[192,1536]{1,0:T(8,128)(2,1)} collective-permute-done((bf16[192,1536]{1,0:T(8,128)(2,1)}, bf16[192,1536]{1,0:T(8,128)(2,1)}, u32[]{:S(2)}, u32[]{:S(2)}) %collective-permute-start.15) | collective-permute-done | bytes 589856 | tf_op jit(solution)/shard_map/ppermute | solution.py:363
  97.6 9.1 %collective-permute-done.8.own_rows = bf16[384,1536]{1,0:T(8,128)(2,1)} collective-permute-done((bf16[384,1536]{1,0:T(8,128)(2,1)}, bf16[384,1536]{1,0:T(8,128)(2,1)}, u32[]{:S(2)}, u32[]{:S(2)}) %collective-permute-start.8) | collective-permute-done | bytes 1179680 | tf_op jit(solution)/shard_map/ppermute | solution.py:381
  106.8 3.1 convolution_convert_fusion.4.own_ct
  116.3 2.4 copy.60.weight_ref
  118.6 20.4 %shard_map.188 = (bf16[384,1536]{1,0:T(8,128)(2,1)S(1)}, bf16[384,1536]{1,0:T(8,128)(2,1)S(1)}, bf16[384,1536]{1,0:T(8,128)(2,1)S(1)}, bf16[384,1536]{1,0:T(8,12...) custom-call(s32[1]{0:T(128)} %bitcast.16.is_own, ...), custom_call_target="tpu_custom_call" | custom-call | flops 1000 | bytes 1000 | tf_op jit(solution)/shard_map/pallas_call | solution.py:594
  142.6 3.6 collective-permute-start.21
  148.1 20.7 %shard_map.189 = (bf16[384,1536]{1,0:T(8,128)(2,1)S(1)}, bf16[384,1536]{1,0:T(8,128)(2,1)}, bf16[384,1536]{1,0:T(8,128)(2,1)S(1)}, bf16[384,1536]{1,0:T(8,128)(2...) custom-call(s32[1]{0:T(128)} %bitcast.16.is_own, ...), custom_call_target="tpu_custom_call", output_to_operand_aliasing={{5}: (10, {}), {6}: (11, {}), {7}: (12, {}), {8}: (13, {})} | custom-call | flops 1000 | bytes 1000 | tf_op jit(solution)/shard_map/pallas_call | solution.py:594
  168.9 3.4 collective-permute-done.21.own_rows
  174.6 2.6 collective-permute-start.24
  178.4 20.6 %shard_map.190 = (bf16[384,1536]{1,0:T(8,128)(2,1)S(1)}, bf16[384,1536]{1,0:T(8,128)(2,1)}, bf16[384,1536]{1,0:T(8,128)(2,1)S(1)}, bf16[384,1536]{1,0:T(8,128)(2...) custom-call(s32[1]{0:T(128)} %bitcast.16.is_own, ...), custom_call_target="tpu_custom_call", output_to_operand_aliasing={{5}: (10, {}), {6}: (11, {}), {7}: (12, {}), {8}: (13, {})} | custom-call | flops 1000 | bytes 1000 | tf_op jit(solution)/shard_map/pallas_call | solution.py:594
  199.1 3.4 add_convert_fusion.13
  210.4 2.9 add_convert_fusion.12
  215.0 20.3 %shard_map.191 = (bf16[384,1536]{1,0:T(8,128)(2,1)S(1)}, bf16[384,1536]{1,0:T(8,128)(2,1)S(1)}, bf16[384,1536]{1,0:T(8,128)(2,1)S(1)}, bf16[384,1536]{1,0:T(8,12...) custom-call(s32[1]{0:T(128)} %bitcast.16.is_own, ...), custom_call_target="tpu_custom_call", output_to_operand_aliasing={{5}: (10, {}), {6}: (11, {}), {7}: (12, {}), {8}: (13, {})} | custom-call | flops 1000 | bytes 1000 | tf_op jit(solution)/shard_map/pallas_call | solution.py:594
  244.5 2.6 add_convert_fusion.11
  247.1 2.7 collective-permute-start.32
  249.8 13.4 %fusion.11 = bf16[1536,768]{1,0:T(8,128)(2,1)} fusion(bf16[3072,1536]{1,0:T(8,128)(2,1)} %get-tuple-element.285, bf16[3072,1536]{1,0:T(8,128)(2,1)} %get-tuple-element.286), kind=kOutput, calls=%fused_computation.19 | convolution fusion | flops 7248936960 | bytes 16515072 | tf_op jit(solution)/shard_map/dot_general | solution.py:472
  263.2 8.9 %fusion.8 = bf16[1536,768]{1,0:T(8,128)(2,1)} fusion(bf16[3072,1536]{1,0:T(8,128)(2,1)S(1)} %bitcast.102, bf16[3072,1536]{1,0:T(8,128)(2,1)S(1)} %bitcast.100), kind=kOutput, calls=%fused_computation.18 | convolution fusion | flops 7248936960 | bytes 16515072 | tf_op jit(solution)/shard_map/dot_general | solution.py:472
  272.2 4.6 collective-permute-done.32
  288.3 9.5 %fusion.27 = bf16[768,768]{1,0:T(8,128)(2,1)} fusion(bf16[3072,768]{1,0:T(8,128)(2,1)} %get-tuple-element.299, bf16[3072,1536]{1,0:T(8,128)(2,1)} %get-tuple-element.300), kind=kOutput, calls=%fused_computation.60 | convolution fusion | flops 3624468480 | bytes 10616832 | tf_op jit(solution)/shard_map/dot_general | solution.py:472
  301.3 4.9 fusion.24
  306.2 11.8 %collective-permute-done.38 = f32[8,384]{1,0:T(8,128)S(1)} collective-permute-done((f32[8,384]{1,0:T(8,128)S(1)}, f32[8,384]{1,0:T(8,128)S(1)}, u32[]{:S(2)}, u32[]{:S(2)}) %collective-permute-start.38) | collective-permute-done | bytes 12320 | tf_op jit(solution)/shard_map/ppermute | solution.py:376
  333.4 6.7 %shard_map.192 = (f32[384,1536]{1,0:T(8,128)S(1)}, bf16[384,1536]{1,0:T(8,128)(2,1)S(1)}, bf16[384,1536]{1,0:T(8,128)(2,1)S(1)}, f32[1,1536]{1,0:T(1,128)S(1)}) custom-call(bf16[384,1536]{1,0:T(8,128)(2,1)S(1)} %copy-done.14, bf16[384,1536]{1,0:T(8,128)(2,1)} %collective-permute-done.41.back_other, bf16[384,1536]{1,0:T(8,128)(2,1)S(1)} %copy-done.20, ...), custom_call_target="tpu_custom_call" | custom-call | flops 1000 | bytes 1000 | tf_op jit(solution)/shard_map/pallas_call | solution.py:664
  340.2 12.1 %shard_map.194.right_ref = bf16[384,2048]{1,0:T(8,128)(2,1)S(1)} custom-call(bf16[384,1536]{1,0:T(8,128)(2,1)S(1)} %copy-done.12, bf16[384,256]{1,0:T(8,128)(2,1)S(1)} %copy-done.31, bf16[384,256]{1,0:T(8,128)(2,1)S(1)} %copy-done.33, bf16[384,1536]{1,0:T(8,128)(2,1)S(1)} %get-tuple-element.324.grad_ref, f32[384,128]{1,0:T(8,128)S(1)} %copy-done.1, ...), custom_call_target="tpu_custom_call" | custom-call | flops 1000 | bytes 1000 | tf_op jit(solution)/shard_map/pallas_call | solution.py:804
  352.4 3.4 shard_map.193
  355.8 4.2 shard_map.195
  361.5 4.4 collective-permute-done.44
  367.4 4.4 fusion.17
  385.7 3.1 add_convert_fusion.8
  397.4 12.1 %collective-permute-done.52 = bf16[384,768]{1,0:T(8,128)(2,1)S(1)} collective-permute-done((bf16[384,768]{1,0:T(8,128)(2,1)}, bf16[384,768]{1,0:T(8,128)(2,1)S(1)}, u32[]{:S(2)}, u32[]{:S(2)}) %collective-permute-start.52) | collective-permute-done | bytes 589856 | tf_op jit(solution)/shard_map/ppermute | solution.py:363
  409.5 11.1 %collective-permute-done.48 = bf16[384,1536]{1,0:T(8,128)(2,1)S(1)} collective-permute-done((bf16[384,1536]{1,0:T(8,128)(2,1)}, bf16[384,1536]{1,0:T(8,128)(2,1)S(1)}, u32[]{:S(2)}, u32[]{:S(2)}) %collective-permute-start.48) | collective-permute-done | bytes 1179680 | tf_op jit(solution)/shard_map/ppermute | solution.py:381
  434.0 3.3 collective-permute-done.57
  437.3 7.5 %collective-permute-done.58 = bf16[192,1536]{1,0:T(8,128)(2,1)S(1)} collective-permute-done((bf16[192,1536]{1,0:T(8,128)(2,1)S(1)}, bf16[192,1536]{1,0:T(8,128)(2,1)S(1)}, u32[]{:S(2)}, u32[]{:S(2)}) %collective-permute-start.58) | collective-permute-done | bytes 589856 | tf_op jit(solution)/shard_map/ppermute | solution.py:363
  444.8 9.2 %collective-permute-done.59 = bf16[192,2048]{1,0:T(8,128)(2,1)S(1)} collective-permute-done((bf16[192,2048]{1,0:T(8,128)(2,1)S(1)}, bf16[192,2048]{1,0:T(8,128)(2,1)S(1)}, u32[]{:S(2)}, u32[]{:S(2)}) %collective-permute-start.59) | collective-permute-done | bytes 786464 | tf_op jit(solution)/shard_map/ppermute | solution.py:367
  454.0 7.1 %collective-permute-done.60 = bf16[192,2048]{1,0:T(8,128)(2,1)S(1)} collective-permute-done((bf16[192,2048]{1,0:T(8,128)(2,1)S(1)}, bf16[192,2048]{1,0:T(8,128)(2,1)S(1)}, u32[]{:S(2)}, u32[]{:S(2)}) %collective-permute-start.60) | collective-permute-done | bytes 786464 | tf_op jit(solution)/shard_map/ppermute | solution.py:363
  470.2 4.8 collective-permute-done.62
  476.5 8.2 %collective-permute-done.65 = bf16[96,2048]{1,0:T(8,128)(2,1)S(1)} collective-permute-done((bf16[96,2048]{1,0:T(8,128)(2,1)S(1)}, bf16[96,2048]{1,0:T(8,128)(2,1)S(1)}, u32[]{:S(2)}, u32[]{:S(2)}) %collective-permute-start.65) | collective-permute-done | bytes 393248 | tf_op jit(solution)/shard_map/ppermute | solution.py:367
  492.8 4.4 collective-permute-done.71
  499.0 11.6 %collective-permute-done.72 = bf16[48,1536]{1,0:T(8,128)(2,1)S(1)} collective-permute-done((bf16[48,1536]{1,0:T(8,128)(2,1)S(1)}, bf16[48,1536]{1,0:T(8,128)(2,1)S(1)}, u32[]{:S(2)}, u32[]{:S(2)}) %collective-permute-start.72) | collective-permute-done | bytes 147488 | tf_op jit(solution)/shard_map/ppermute | solution.py:376
  510.7 6.8 %collective-permute-done.75 = bf16[48,2048]{1,0:T(8,128)(2,1)S(1)} collective-permute-done((bf16[48,2048]{1,0:T(8,128)(2,1)S(1)}, bf16[48,2048]{1,0:T(8,128)(2,1)S(1)}, u32[]{:S(2)}, u32[]{:S(2)}) %collective-permute-start.75) | collective-permute-done | bytes 196640 | tf_op jit(solution)/shard_map/ppermute | solution.py:376
  519.5 2.6 collective-permute-start.83
  526.6 2.8 collective-permute-done.84
  529.4 2.5 collective-permute-start.77
  535.1 9.6 %collective-permute-done.78 = bf16[48,1536]{1,0:T(8,128)(2,1)S(1)} collective-permute-done((bf16[48,1536]{1,0:T(8,128)(2,1)S(1)}, bf16[48,1536]{1,0:T(8,128)(2,1)S(1)}, u32[]{:S(2)}, u32[]{:S(2)}) %collective-permute-start.78) | collective-permute-done | bytes 147488 | tf_op jit(solution)/shard_map/ppermute | solution.py:376
  544.7 2.5 collective-permute-start.80
  547.4 9.2 %collective-permute-done.81 = bf16[48,2048]{1,0:T(8,128)(2,1)S(1)} collective-permute-done((bf16[48,2048]{1,0:T(8,128)(2,1)S(1)}, bf16[48,2048]{1,0:T(8,128)(2,1)S(1)}, u32[]{:S(2)}, u32[]{:S(2)}) %collective-permute-start.81) | collective-permute-done | bytes 196640 | tf_op jit(solution)/shard_map/ppermute | solution.py:376
  559.9 7.0 %collective-permute-done.87 = bf16[96,1536]{1,0:T(8,128)(2,1)S(1)} collective-permute-done((bf16[96,1536]{1,0:T(8,128)(2,1)S(1)}, bf16[96,1536]{1,0:T(8,128)(2,1)S(1)}, u32[]{:S(2)}, u32[]{:S(2)}) %collective-permute-start.87) | collective-permute-done | bytes 294944 | tf_op jit(solution)/shard_map/ppermute | solution.py:367
  567.9 5.7 collective-permute-done.89
  583.1 8.1 %collective-permute-done.92 = bf16[192,1536]{1,0:T(8,128)(2,1)S(1)} collective-permute-done((bf16[192,1536]{1,0:T(8,128)(2,1)S(1)}, bf16[192,1536]{1,0:T(8,128)(2,1)S(1)}, u32[]{:S(2)}, u32[]{:S(2)}) %collective-permute-start.92) | collective-permute-done | bytes 589856 | tf_op jit(solution)/shard_map/ppermute | solution.py:367
  591.6 2.7 collective-permute-done.93
  594.7 2.8 maximum_convert_fusion.1
  597.5 7.0 %collective-permute-done.90 = bf16[192,2048]{1,0:T(8,128)(2,1)S(1)} collective-permute-done((bf16[192,2048]{1,0:T(8,128)(2,1)S(1)}, bf16[192,2048]{1,0:T(8,128)(2,1)S(1)}, u32[]{:S(2)}, u32[]{:S(2)}) %collective-permute-start.90) | collective-permute-done | bytes 786464 | tf_op jit(solution)/shard_map/ppermute | solution.py:367
  608.1 3.5 maximum_convert_fusion
  (507 shorter events, 184.7 us)
Async XLA Ops:
  5.8 22.8 %collective-permute-start.2 = (bf16[192,1536]{1,0:T(8,128)(2,1)}, bf16[192,1536]{1,0:T(8,128)(2,1)}, u32[]{:S(2)}, u32[]{:S(2)}) collective-permute-start(bf16[192,1536]{1,0:T(8,128)(2,1)} %get-tuple-element.417), channel_id=1, source_target_pairs={{0,16},{16,0},{1,17},{17,1},{2,18},{18,2},{3,19},{19,3},{4,20},{20... | collective-permute-start | bytes 1769480 | tf_op jit(solution)/shard_map/ppermute | solution.py:363
  8.3 29.3 %collective-permute-start = (bf16[384,1536]{1,0:T(8,128)(2,1)}, bf16[384,1536]{1,0:T(8,128)(2,1)}, u32[]{:S(2)}, u32[]{:S(2)}) collective-permute-start(bf16[384,1536]{1,0:T(8,128)(2,1)} %param.13), channel_id=1, source_target_pairs={{0,4},{2,6},{4,12},{6,14},{8,0},{10,2},{12,8},{14,10},{1,5},{3,7},... | collective-permute-start | bytes 3538952 | tf_op jit(solution)/shard_map/ppermute | solution.py:381
  12.1 55.3 %collective-permute-start.7 = (bf16[1536,1536]{1,0:T(8,128)(2,1)}, bf16[1536,1536]{1,0:T(8,128)(2,1)S(1)}, u32[]{:S(2)}, u32[]{:S(2)}) collective-permute-start(bf16[1536,1536]{1,0:T(8,128)(2,1)} %bitcast.103), channel_id=1, source_target_pairs={{0,2},{3,1},{4,6},{7,5},{8,10},{11,9},{12,14},{15,13},{16,18},{19,... | collective-permute-start | bytes 14155784 | tf_op jit(solution)/shard_map/ppermute | solution.py:391
  37.7 21.1 %collective-permute-start.6 = (bf16[192,1536]{1,0:T(8,128)(2,1)S(1)}, bf16[192,1536]{1,0:T(8,128)(2,1)S(1)}, u32[]{:S(2)}, u32[]{:S(2)}) collective-permute-start(bf16[192,1536]{1,0:T(8,128)(2,1)S(1)} %get-tuple-element.415), channel_id=1, source_target_pairs={{0,16},{16,0},{1,17},{17,1},{2,18},{18,2},{3,19},{19,3},{4,20},{20... | collective-permute-start | bytes 1769480 | tf_op jit(solution)/shard_map/ppermute | solution.py:363
  38.2 28.5 %collective-permute-start.5 = (bf16[384,1536]{1,0:T(8,128)(2,1)}, bf16[384,1536]{1,0:T(8,128)(2,1)}, u32[]{:S(2)}, u32[]{:S(2)}) collective-permute-start(bf16[384,1536]{1,0:T(8,128)(2,1)} %collective-permute-done), channel_id=1, source_target_pairs={{0,4},{2,6},{4,12},{6,14},{8,0},{10,2},{12,8},{14,10},{1,5},{3,7},... | collective-permute-start | bytes 3538952 | tf_op jit(solution)/shard_map/ppermute | solution.py:381
  39.1 58.5 %collective-permute-start.16 = (bf16[768,1536]{1,0:T(8,128)(2,1)}, bf16[768,1536]{1,0:T(8,128)(2,1)}, u32[]{:S(2)}, u32[]{:S(2)}) collective-permute-start(bf16[768,1536]{1,0:T(8,128)(2,1)} %bitcast.6.down_own), channel_id=1, source_target_pairs={{0,2},{3,1},{4,6},{7,5},{8,10},{11,9},{12,14},{15,13},{16,18},{19,... | collective-permute-start | bytes 7077896 | tf_op jit(solution)/shard_map/ppermute | solution.py:391
  75.3 22.3 %collective-permute-start.14 = (bf16[384,1536]{1,0:T(8,128)(2,1)}, bf16[384,1536]{1,0:T(8,128)(2,1)}, u32[]{:S(2)}, u32[]{:S(2)}) collective-permute-start(bf16[384,1536]{1,0:T(8,128)(2,1)} %multiply_convert_fusion.own_rows), channel_id=1, source_target_pairs={{0,1},{1,0},{2,3},{3,2},{4,5},{5,4},{6,7},{7,6},{8,9},{9,8},{10,11... | collective-permute-start | bytes 3538952 | tf_op jit(solution)/shard_map/ppermute | solution.py:359
  77.3 29.4 %collective-permute-start.8 = (bf16[384,1536]{1,0:T(8,128)(2,1)}, bf16[384,1536]{1,0:T(8,128)(2,1)}, u32[]{:S(2)}, u32[]{:S(2)}) collective-permute-start(bf16[384,1536]{1,0:T(8,128)(2,1)} %multiply_convert_fusion.own_rows), channel_id=1, source_target_pairs={{0,4},{2,6},{4,12},{6,14},{8,0},{10,2},{12,8},{14,10},{1,5},{3,7},... | collective-permute-start | bytes 3538952 | tf_op jit(solution)/shard_map/ppermute | solution.py:381
  78.9 18.8 %collective-permute-start.13 = (bf16[384,1536]{1,0:T(8,128)(2,1)}, bf16[384,1536]{1,0:T(8,128)(2,1)}, u32[]{:S(2)}, u32[]{:S(2)}) collective-permute-start(bf16[384,1536]{1,0:T(8,128)(2,1)} %convolution_convert_fusion.5.own_ct.ct_ref), channel_id=1, source_target_pairs={{0,1},{1,0},{2,3},{3,2},{4,5},{5,4},{6,7},{7,6},{8,9},{9,8},{10,11... | collective-permute-start | bytes 3538952 | tf_op jit(solution)/shard_map/ppermute | solution.py:359
  81.8 15.8 %collective-permute-start.15 = (bf16[192,1536]{1,0:T(8,128)(2,1)}, bf16[192,1536]{1,0:T(8,128)(2,1)}, u32[]{:S(2)}, u32[]{:S(2)}) collective-permute-start(bf16[192,1536]{1,0:T(8,128)(2,1)} %get-tuple-element.412), channel_id=1, source_target_pairs={{0,16},{16,0},{1,17},{17,1},{2,18},{18,2},{3,19},{19,3},{4,20},{20... | collective-permute-start | bytes 1769480 | tf_op jit(solution)/shard_map/ppermute | solution.py:363
  109.8 30.3 %collective-permute-start.19 = (bf16[384,1536]{1,0:T(8,128)(2,1)}, bf16[384,1536]{1,0:T(8,128)(2,1)}, u32[]{:S(2)}, u32[]{:S(2)}) collective-permute-start(bf16[384,1536]{1,0:T(8,128)(2,1)} %convolution_convert_fusion.4.own_ct), channel_id=1, source_target_pairs={{0,1},{1,0},{2,3},{3,2},{4,5},{5,4},{6,7},{7,6},{8,9},{9,8},{10,11... | collective-permute-start | bytes 3538952 | tf_op jit(solution)/shard_map/ppermute | solution.py:359
  109.8 30.3 %collective-permute-start.17 = (bf16[384,1536]{1,0:T(8,128)(2,1)}, bf16[384,1536]{1,0:T(8,128)(2,1)}, u32[]{:S(2)}, u32[]{:S(2)}) collective-permute-start(bf16[384,1536]{1,0:T(8,128)(2,1)} %collective-permute-done.5), channel_id=1, source_target_pairs={{0,4},{2,6},{4,12},{6,14},{8,0},{10,2},{12,8},{14,10},{1,5},{3,7},... | collective-permute-start | bytes 3538952 | tf_op jit(solution)/shard_map/ppermute | solution.py:381
  111.1 29.0 %collective-permute-start.20 = (bf16[384,1536]{1,0:T(8,128)(2,1)}, bf16[384,1536]{1,0:T(8,128)(2,1)}, u32[]{:S(2)}, u32[]{:S(2)}) collective-permute-start(bf16[384,1536]{1,0:T(8,128)(2,1)} %collective-permute-done.8.own_rows), channel_id=1, source_target_pairs={{0,1},{1,0},{2,3},{3,2},{4,5},{5,4},{6,7},{7,6},{8,9},{9,8},{10,11... | collective-permute-start | bytes 3538952 | tf_op jit(solution)/shard_map/ppermute | solution.py:359
  113.7 26.4 %collective-permute-start.18 = (bf16[192,1536]{1,0:T(8,128)(2,1)}, bf16[192,1536]{1,0:T(8,128)(2,1)}, u32[]{:S(2)}, u32[]{:S(2)}) collective-permute-start(bf16[192,1536]{1,0:T(8,128)(2,1)} %get-tuple-element.410), channel_id=1, source_target_pairs={{0,16},{16,0},{1,17},{17,1},{2,18},{18,2},{3,19},{19,3},{4,20},{20... | collective-permute-start | bytes 1769480 | tf_op jit(solution)/shard_map/ppermute | solution.py:363
  142.5 26.4 %collective-permute-start.23 = (bf16[384,1536]{1,0:T(8,128)(2,1)S(1)}, bf16[384,1536]{1,0:T(8,128)(2,1)S(1)}, u32[]{:S(2)}, u32[]{:S(2)}) collective-permute-start(bf16[384,1536]{1,0:T(8,128)(2,1)S(1)} %convolution_convert_fusion.3.own_ct), channel_id=1, source_target_pairs={{0,1},{1,0},{2,3},{3,2},{4,5},{5,4},{6,7},{7,6},{8,9},{9,8},{10,11... | collective-permute-start | bytes 3538952 | tf_op jit(solution)/shard_map/ppermute | solution.py:359
  142.6 29.7 %collective-permute-start.21 = (bf16[384,1536]{1,0:T(8,128)(2,1)}, bf16[384,1536]{1,0:T(8,128)(2,1)S(1)}, u32[]{:S(2)}, u32[]{:S(2)}) collective-permute-start(bf16[384,1536]{1,0:T(8,128)(2,1)} %collective-permute-done.8.own_rows), channel_id=1, source_target_pairs={{0,4},{2,6},{4,12},{6,14},{8,0},{10,2},{12,8},{14,10},{1,5},{3,7},... | collective-permute-start | bytes 3538952 | tf_op jit(solution)/shard_map/ppermute | solution.py:381
  147.5 21.4 %collective-permute-start.22 = (bf16[192,1536]{1,0:T(8,128)(2,1)S(1)}, bf16[192,1536]{1,0:T(8,128)(2,1)S(1)}, u32[]{:S(2)}, u32[]{:S(2)}) collective-permute-start(bf16[192,1536]{1,0:T(8,128)(2,1)S(1)} %get-tuple-element.408), channel_id=1, source_target_pairs={{0,16},{16,0},{1,17},{17,1},{2,18},{18,2},{3,19},{19,3},{4,20},{20... | collective-permute-start | bytes 1769480 | tf_op jit(solution)/shard_map/ppermute | solution.py:363
  172.3 26.7 %collective-permute-start.25 = (bf16[384,1536]{1,0:T(8,128)(2,1)}, bf16[384,1536]{1,0:T(8,128)(2,1)}, u32[]{:S(2)}, u32[]{:S(2)}) collective-permute-start(bf16[384,1536]{1,0:T(8,128)(2,1)} %get-tuple-element.249), channel_id=1, source_target_pairs={{0,1},{1,0},{2,3},{3,2},{4,5},{5,4},{6,7},{7,6},{8,9},{9,8},{10,11... | collective-permute-start | bytes 3538952 | tf_op jit(solution)/shard_map/ppermute | solution.py:359
  174.5 28.0 %collective-permute-start.26 = (bf16[384,1536]{1,0:T(8,128)(2,1)S(1)}, bf16[384,1536]{1,0:T(8,128)(2,1)S(1)}, u32[]{:S(2)}, u32[]{:S(2)}) collective-permute-start(bf16[384,1536]{1,0:T(8,128)(2,1)S(1)} %convolution_convert_fusion.2.own_ct), channel_id=1, source_target_pairs={{0,1},{1,0},{2,3},{3,2},{4,5},{5,4},{6,7},{7,6},{8,9},{9,8},{10,11... | collective-permute-start | bytes 3538952 | tf_op jit(solution)/shard_map/ppermute | solution.py:359
  174.6 29.6 %collective-permute-start.24 = (bf16[384,1536]{1,0:T(8,128)(2,1)S(1)}, bf16[384,1536]{1,0:T(8,128)(2,1)}, u32[]{:S(2)}, u32[]{:S(2)}) collective-permute-start(bf16[384,1536]{1,0:T(8,128)(2,1)S(1)} %collective-permute-done.21.own_rows), channel_id=1, source_target_pairs={{0,4},{2,6},{4,12},{6,14},{8,0},{10,2},{12,8},{14,10},{1,5},{3,7},... | collective-permute-start | bytes 3538952 | tf_op jit(solution)/shard_map/ppermute | solution.py:381
  177.2 33.2 %collective-permute-start.31 = (bf16[384,1536]{1,0:T(8,128)(2,1)}, bf16[384,1536]{1,0:T(8,128)(2,1)}, u32[]{:S(2)}, u32[]{:S(2)}) collective-permute-start(bf16[384,1536]{1,0:T(8,128)(2,1)} %get-tuple-element.277), channel_id=1, source_target_pairs={{0,1},{1,0},{2,3},{3,2},{4,5},{5,4},{6,7},{7,6},{8,9},{9,8},{10,11... | collective-permute-start | bytes 3538952 | tf_op jit(solution)/shard_map/ppermute | solution.py:359
  204.1 35.0 %collective-permute-start.28 = (bf16[384,1536]{1,0:T(8,128)(2,1)}, bf16[384,1536]{1,0:T(8,128)(2,1)}, u32[]{:S(2)}, u32[]{:S(2)}) collective-permute-start(bf16[384,1536]{1,0:T(8,128)(2,1)} %add_convert_fusion.13), channel_id=1, source_target_pairs={{0,4},{2,6},{4,12},{6,14},{8,0},{10,2},{12,8},{14,10},{1,5},{3,7},... | collective-permute-start | bytes 3538952 | tf_op jit(solution)/shard_map/ppermute | solution.py:381
  205.8 33.3 %collective-permute-start.29 = (bf16[384,1536]{1,0:T(8,128)(2,1)}, bf16[384,1536]{1,0:T(8,128)(2,1)}, u32[]{:S(2)}, u32[]{:S(2)}) collective-permute-start(bf16[384,1536]{1,0:T(8,128)(2,1)} %get-tuple-element.266), channel_id=1, source_target_pairs={{0,1},{1,0},{2,3},{3,2},{4,5},{5,4},{6,7},{7,6},{8,9},{9,8},{10,11... | collective-permute-start | bytes 3538952 | tf_op jit(solution)/shard_map/ppermute | solution.py:359
  208.3 89.4 %collective-permute-start.41 = (bf16[384,1536]{1,0:T(8,128)(2,1)}, bf16[384,1536]{1,0:T(8,128)(2,1)}, u32[]{:S(2)}, u32[]{:S(2)}) collective-permute-start(bf16[384,1536]{1,0:T(8,128)(2,1)} %get-tuple-element.304), channel_id=1, source_target_pairs={{0,1},{1,0},{2,3},{3,2},{4,5},{5,4},{6,7},{7,6},{8,9},{9,8},{10,11... | collective-permute-start | bytes 3538952 | tf_op jit(solution)/shard_map/ppermute | solution.py:359
  244.3 27.9 %collective-permute-start.34 = (f32[4,384]{1,0:T(4,128)S(1)}, f32[4,384]{1,0:T(4,128)S(1)}, u32[]{:S(2)}, u32[]{:S(2)}) collective-permute-start(f32[4,384]{1,0:T(4,128)S(1)} %slice.115), channel_id=1, source_target_pairs={{0,1},{1,0},{2,3},{3,2},{4,5},{5,4},{6,7},{7,6},{8,9},{9,8},{10,11... | collective-permute-start | bytes 18440 | tf_op jit(solution)/shard_map/ppermute | solution.py:359
  247.1 29.7 %collective-permute-start.32 = (bf16[384,1536]{1,0:T(8,128)(2,1)S(1)}, bf16[384,1536]{1,0:T(8,128)(2,1)}, u32[]{:S(2)}, u32[]{:S(2)}) collective-permute-start(bf16[384,1536]{1,0:T(8,128)(2,1)S(1)} %add_convert_fusion.11), channel_id=1, source_target_pairs={{0,4},{2,6},{4,12},{6,14},{8,0},{10,2},{12,8},{14,10},{1,5},{3,7},... | collective-permute-start | bytes 3538952 | tf_op jit(solution)/shard_map/ppermute | solution.py:381
  249.8 27.0 %collective-permute-start.33 = (bf16[384,1536]{1,0:T(8,128)(2,1)S(1)}, bf16[384,1536]{1,0:T(8,128)(2,1)}, u32[]{:S(2)}, u32[]{:S(2)}) collective-permute-start(bf16[384,1536]{1,0:T(8,128)(2,1)S(1)} %copy-done.82), channel_id=1, source_target_pairs={{0,1},{1,0},{2,3},{3,2},{4,5},{5,4},{6,7},{7,6},{8,9},{9,8},{10,11... | collective-permute-start | bytes 3538952 | tf_op jit(solution)/shard_map/ppermute | solution.py:359
  280.5 18.8 %collective-permute-start.40 = (f32[8,384]{1,0:T(8,128)S(1)}, f32[8,384]{1,0:T(8,128)S(1)}, u32[]{:S(2)}, u32[]{:S(2)}) collective-permute-start(f32[8,384]{1,0:T(8,128)S(1)} %get-tuple-element.436), channel_id=1, source_target_pairs={{0,12},{2,14},{4,8},{6,10},{8,4},{10,6},{12,0},{14,2},{1,13},{3,15... | collective-permute-start | bytes 36872 | tf_op jit(solution)/shard_map/ppermute | solution.py:376
  283.7 34.6 %collective-permute-start.37 = (bf16[768,768]{1,0:T(8,128)(2,1)S(1)}, bf16[768,768]{1,0:T(8,128)(2,1)S(1)}, u32[]{:S(2)}, u32[]{:S(2)}) collective-permute-start(bf16[768,768]{1,0:T(8,128)(2,1)S(1)} %constant_dynamic-slice_fusion.20), channel_id=1, source_target_pairs={{0,16},{16,0},{1,17},{17,1},{2,18},{18,2},{3,19},{19,3},{4,20},{20... | collective-permute-start | bytes 3538952 | tf_op jit(solution)/shard_map/ppermute | solution.py:363
  284.5 33.8 %collective-permute-start.36 = (bf16[1536,768]{1,0:T(8,128)(2,1)}, bf16[1536,768]{1,0:T(8,128)(2,1)S(1)}, u32[]{:S(2)}, u32[]{:S(2)}) collective-permute-start(bf16[1536,768]{1,0:T(8,128)(2,1)} %fusion.8), channel_id=1, source_target_pairs={{1,3},{2,0},{5,7},{6,4},{9,11},{10,8},{13,15},{14,12},{17,19},{18,... | collective-permute-start | bytes 7077896 | tf_op jit(solution)/shard_map/ppermute | solution.py:386
  288.1 30.2 %collective-permute-start.35 = (bf16[384,1536]{1,0:T(8,128)(2,1)S(1)}, bf16[384,1536]{1,0:T(8,128)(2,1)S(1)}, u32[]{:S(2)}, u32[]{:S(2)}) collective-permute-start(bf16[384,1536]{1,0:T(8,128)(2,1)S(1)} %add_convert_fusion.10), channel_id=1, source_target_pairs={{0,4},{2,6},{4,12},{6,14},{8,0},{10,2},{12,8},{14,10},{1,5},{3,7},... | collective-permute-start | bytes 3538952 | tf_op jit(solution)/shard_map/ppermute | solution.py:381
  297.8 20.2 %collective-permute-start.38 = (f32[8,384]{1,0:T(8,128)S(1)}, f32[8,384]{1,0:T(8,128)S(1)}, u32[]{:S(2)}, u32[]{:S(2)}) collective-permute-start(f32[8,384]{1,0:T(8,128)S(1)} %get-tuple-element.437), channel_id=1, source_target_pairs={{0,4},{2,6},{4,0},{6,2},{8,12},{10,14},{12,8},{14,10},{1,5},{3,7},... | collective-permute-start | bytes 36872 | tf_op jit(solution)/shard_map/ppermute | solution.py:376
  299.9 18.4 %collective-permute-start.39 = (f32[8,384]{1,0:T(8,128)S(1)}, f32[8,384]{1,0:T(8,128)S(1)}, u32[]{:S(2)}, u32[]{:S(2)}) collective-permute-start(f32[8,384]{1,0:T(8,128)S(1)} %get-tuple-element.438), channel_id=1, source_target_pairs={{0,8},{2,10},{4,12},{6,14},{8,0},{10,2},{12,4},{14,6},{1,9},{3,11}... | collective-permute-start | bytes 36872 | tf_op jit(solution)/shard_map/ppermute | solution.py:376
  319.7 47.6 %collective-permute-start.46 = (bf16[768,768]{1,0:T(8,128)(2,1)}, bf16[768,768]{1,0:T(8,128)(2,1)}, u32[]{:S(2)}, u32[]{:S(2)}) collective-permute-start(bf16[768,768]{1,0:T(8,128)(2,1)} %add_convert_fusion.9), channel_id=1, source_target_pairs={{1,3},{2,0},{5,7},{6,4},{9,11},{10,8},{13,15},{14,12},{17,19},{18,... | collective-permute-start | bytes 3538952 | tf_op jit(solution)/shard_map/ppermute | solution.py:386
  321.1 46.2 %collective-permute-start.42 = (bf16[384,1536]{1,0:T(8,128)(2,1)}, bf16[384,1536]{1,0:T(8,128)(2,1)}, u32[]{:S(2)}, u32[]{:S(2)}) collective-permute-start(bf16[384,1536]{1,0:T(8,128)(2,1)} %add_convert_fusion.12), channel_id=1, source_target_pairs={{0,4},{2,6},{4,12},{6,14},{8,0},{10,2},{12,8},{14,10},{1,5},{3,7},... | collective-permute-start | bytes 3538952 | tf_op jit(solution)/shard_map/ppermute | solution.py:381
  321.2 46.1 %collective-permute-start.43 = (bf16[768,768]{1,0:T(8,128)(2,1)}, bf16[768,768]{1,0:T(8,128)(2,1)}, u32[]{:S(2)}, u32[]{:S(2)}) collective-permute-start(bf16[768,768]{1,0:T(8,128)(2,1)} %fusion.24), channel_id=1, source_target_pairs={{1,3},{2,0},{5,7},{6,4},{9,11},{10,8},{13,15},{14,12},{17,19},{18,... | collective-permute-start | bytes 3538952 | tf_op jit(solution)/shard_map/ppermute | solution.py:386
  325.8 41.5 %collective-permute-start.45 = (bf16[768,768]{1,0:T(8,128)(2,1)}, bf16[768,768]{1,0:T(8,128)(2,1)}, u32[]{:S(2)}, u32[]{:S(2)}) collective-permute-start(bf16[768,768]{1,0:T(8,128)(2,1)} %constant_dynamic-slice_fusion.18), channel_id=1, source_target_pairs={{0,16},{16,0},{1,17},{17,1},{2,18},{18,2},{3,19},{19,3},{4,20},{20... | collective-permute-start | bytes 3538952 | tf_op jit(solution)/shard_map/ppermute | solution.py:363
  330.0 35.9 %collective-permute-start.44 = (bf16[384,768]{1,0:T(8,128)(2,1)S(1)}, bf16[384,768]{1,0:T(8,128)(2,1)S(1)}, u32[]{:S(2)}, u32[]{:S(2)}) collective-permute-start(bf16[384,768]{1,0:T(8,128)(2,1)S(1)} %constant_dynamic-slice_fusion.19), channel_id=1, source_target_pairs={{0,16},{16,0},{1,17},{17,1},{2,18},{18,2},{3,19},{19,3},{4,20},{20... | collective-permute-start | bytes 1769480 | tf_op jit(solution)/shard_map/ppermute | solution.py:363
  365.9 31.4 %collective-permute-start.49 = (bf16[384,1536]{1,0:T(8,128)(2,1)S(1)}, bf16[384,1536]{1,0:T(8,128)(2,1)}, u32[]{:S(2)}, u32[]{:S(2)}) collective-permute-start(bf16[384,1536]{1,0:T(8,128)(2,1)S(1)} %copy-done.37), channel_id=1, source_target_pairs={{0,1},{1,0},{2,3},{3,2},{4,5},{5,4},{6,7},{7,6},{8,9},{9,8},{10,11... | collective-permute-start | bytes 3538952 | tf_op jit(solution)/shard_map/ppermute | solution.py:359
  372.8 24.6 %collective-permute-start.53 = (bf16[384,768]{1,0:T(8,128)(2,1)}, bf16[384,768]{1,0:T(8,128)(2,1)}, u32[]{:S(2)}, u32[]{:S(2)}) collective-permute-start(bf16[384,768]{1,0:T(8,128)(2,1)} %add_convert_fusion.20), channel_id=1, source_target_pairs={{1,3},{2,0},{5,7},{6,4},{9,11},{10,8},{13,15},{14,12},{17,19},{18,... | collective-permute-start | bytes 1769480 | tf_op jit(solution)/shard_map/ppermute | solution.py:386
  379.1 30.5 %collective-permute-start.54 = (bf16[384,1536]{1,0:T(8,128)(2,1)}, bf16[384,1536]{1,0:T(8,128)(2,1)}, u32[]{:S(2)}, u32[]{:S(2)}) collective-permute-start(bf16[384,1536]{1,0:T(8,128)(2,1)} %fusion.30), channel_id=1, source_target_pairs={{0,1},{1,0},{2,3},{3,2},{4,5},{5,4},{6,7},{7,6},{8,9},{9,8},{10,11... | collective-permute-start | bytes 3538952 | tf_op jit(solution)/shard_map/ppermute | solution.py:359
  391.1 29.5 %collective-permute-start.48 = (bf16[384,1536]{1,0:T(8,128)(2,1)}, bf16[384,1536]{1,0:T(8,128)(2,1)S(1)}, u32[]{:S(2)}, u32[]{:S(2)}) collective-permute-start(bf16[384,1536]{1,0:T(8,128)(2,1)} %add_convert_fusion.8), channel_id=1, source_target_pairs={{0,4},{2,6},{4,12},{6,14},{8,0},{10,2},{12,8},{14,10},{1,5},{3,7},... | collective-permute-start | bytes 3538952 | tf_op jit(solution)/shard_map/ppermute | solution.py:381
  393.8 15.7 %collective-permute-start.52 = (bf16[384,768]{1,0:T(8,128)(2,1)}, bf16[384,768]{1,0:T(8,128)(2,1)S(1)}, u32[]{:S(2)}, u32[]{:S(2)}) collective-permute-start(bf16[384,768]{1,0:T(8,128)(2,1)} %constant_dynamic-slice_fusion.15), channel_id=1, source_target_pairs={{0,16},{16,0},{1,17},{17,1},{2,18},{18,2},{3,19},{19,3},{4,20},{20... | collective-permute-start | bytes 1769480 | tf_op jit(solution)/shard_map/ppermute | solution.py:363
  397.3 31.1 %collective-permute-start.56 = (bf16[384,1536]{1,0:T(8,128)(2,1)S(1)}, bf16[384,1536]{1,0:T(8,128)(2,1)S(1)}, u32[]{:S(2)}, u32[]{:S(2)}) collective-permute-start(bf16[384,1536]{1,0:T(8,128)(2,1)S(1)} %copy-done.35), channel_id=1, source_target_pairs={{0,1},{1,0},{2,3},{3,2},{4,5},{5,4},{6,7},{7,6},{8,9},{9,8},{10,11... | collective-permute-start | bytes 3538952 | tf_op jit(solution)/shard_map/ppermute | solution.py:359
  420.9 16.5 %collective-permute-start.57 = (bf16[192,1536]{1,0:T(8,128)(2,1)S(1)}, bf16[192,1536]{1,0:T(8,128)(2,1)S(1)}, u32[]{:S(2)}, u32[]{:S(2)}) collective-permute-start(bf16[192,1536]{1,0:T(8,128)(2,1)S(1)} %constant_dynamic-slice_fusion.14), channel_id=1, source_target_pairs={{0,2},{2,0},{4,6},{6,4},{8,10},{10,8},{12,14},{14,12},{1,3},{3,1},... | collective-permute-start | bytes 1769480 | tf_op jit(solution)/shard_map/ppermute | solution.py:367
  426.9 34.2 %collective-permute-start.55 = (bf16[384,1536]{1,0:T(8,128)(2,1)S(1)}, bf16[384,1536]{1,0:T(8,128)(2,1)S(1)}, u32[]{:S(2)}, u32[]{:S(2)}) collective-permute-start(bf16[384,1536]{1,0:T(8,128)(2,1)S(1)} %add_convert_fusion.4), channel_id=1, source_target_pairs={{0,4},{2,6},{4,12},{6,14},{8,0},{10,2},{12,8},{14,10},{1,5},{3,7},... | collective-permute-start | bytes 3538952 | tf_op jit(solution)/shard_map/ppermute | solution.py:381
  428.4 16.4 %collective-permute-start.58 = (bf16[192,1536]{1,0:T(8,128)(2,1)S(1)}, bf16[192,1536]{1,0:T(8,128)(2,1)S(1)}, u32[]{:S(2)}, u32[]{:S(2)}) collective-permute-start(bf16[192,1536]{1,0:T(8,128)(2,1)S(1)} %constant_dynamic-slice_fusion.13), channel_id=1, source_target_pairs={{0,16},{16,0},{1,17},{17,1},{2,18},{18,2},{3,19},{19,3},{4,20},{20... | collective-permute-start | bytes 1769480 | tf_op jit(solution)/shard_map/ppermute | solution.py:363
  430.7 23.3 %collective-permute-start.59 = (bf16[192,2048]{1,0:T(8,128)(2,1)S(1)}, bf16[192,2048]{1,0:T(8,128)(2,1)S(1)}, u32[]{:S(2)}, u32[]{:S(2)}) collective-permute-start(bf16[192,2048]{1,0:T(8,128)(2,1)S(1)} %constant_dynamic-slice_fusion.12), channel_id=1, source_target_pairs={{0,2},{2,0},{4,6},{6,4},{8,10},{10,8},{12,14},{14,12},{1,3},{3,1},... | collective-permute-start | bytes 2359304 | tf_op jit(solution)/shard_map/ppermute | solution.py:367
  431.0 30.1 %collective-permute-start.60 = (bf16[192,2048]{1,0:T(8,128)(2,1)S(1)}, bf16[192,2048]{1,0:T(8,128)(2,1)S(1)}, u32[]{:S(2)}, u32[]{:S(2)}) collective-permute-start(bf16[192,2048]{1,0:T(8,128)(2,1)S(1)} %constant_dynamic-slice_fusion.11), channel_id=1, source_target_pairs={{0,16},{16,0},{1,17},{17,1},{2,18},{18,2},{3,19},{19,3},{4,20},{20... | collective-permute-start | bytes 2359304 | tf_op jit(solution)/shard_map/ppermute | solution.py:363
  461.1 25.2 %collective-permute-start.68 = (f32[10,1536]{1,0:T(8,128)S(1)}, f32[10,1536]{1,0:T(8,128)S(1)}, u32[]{:S(2)}, u32[]{:S(2)}) collective-permute-start(f32[10,1536]{1,0:T(8,128)S(1)} %add.464), channel_id=1, source_target_pairs={{0,18},{2,16},{4,22},{6,20},{8,26},{10,24},{12,30},{14,28},{16,2},... | collective-permute-start | bytes 184328 | tf_op jit(solution)/shard_map/ppermute | solution.py:372
  462.3 24.0 %collective-permute-start.67 = (f32[10,1536]{1,0:T(8,128)S(1)}, f32[10,1536]{1,0:T(8,128)S(1)}, u32[]{:S(2)}, u32[]{:S(2)}) collective-permute-start(f32[10,1536]{1,0:T(8,128)S(1)} %add.464), channel_id=1, source_target_pairs={{0,2},{2,0},{4,6},{6,4},{8,10},{10,8},{12,14},{14,12},{1,3},{3,1},... | collective-permute-start | bytes 184328 | tf_op jit(solution)/shard_map/ppermute | solution.py:367
  464.3 22.0 %collective-permute-start.66 = (f32[10,1536]{1,0:T(8,128)S(1)}, f32[10,1536]{1,0:T(8,128)S(1)}, u32[]{:S(2)}, u32[]{:S(2)}) collective-permute-start(f32[10,1536]{1,0:T(8,128)S(1)} %add.464), channel_id=1, source_target_pairs={{0,16},{16,0},{1,17},{17,1},{2,18},{18,2},{3,19},{19,3},{4,20},{20... | collective-permute-start | bytes 184328 | tf_op jit(solution)/shard_map/ppermute | solution.py:363
  484.7 91.3 %collective-permute-start.70 = (bf16[192,1536]{1,0:T(8,128)(2,1)S(1)}, bf16[192,1536]{1,0:T(8,128)(2,1)S(1)}, u32[]{:S(2)}, u32[]{:S(2)}) collective-permute-start(bf16[192,1536]{1,0:T(8,128)(2,1)S(1)} %get-tuple-element.405), channel_id=1, source_target_pairs={{0,16},{16,0},{1,17},{17,1},{2,18},{18,2},{3,19},{19,3},{4,20},{20... | collective-permute-start | bytes 1769480 | tf_op jit(solution)/shard_map/ppermute | solution.py:363
  489.4 21.2 %collective-permute-start.72 = (bf16[48,1536]{1,0:T(8,128)(2,1)S(1)}, bf16[48,1536]{1,0:T(8,128)(2,1)S(1)}, u32[]{:S(2)}, u32[]{:S(2)}) collective-permute-start(bf16[48,1536]{1,0:T(8,128)(2,1)S(1)} %get-tuple-element.435), channel_id=1, source_target_pairs={{0,8},{2,10},{4,12},{6,14},{8,0},{10,2},{12,4},{14,6},{1,9},{3,11}... | collective-permute-start | bytes 442376 | tf_op jit(solution)/shard_map/ppermute | solution.py:376
  489.9 20.8 %collective-permute-start.74 = (bf16[48,2048]{1,0:T(8,128)(2,1)S(1)}, bf16[48,2048]{1,0:T(8,128)(2,1)S(1)}, u32[]{:S(2)}, u32[]{:S(2)}) collective-permute-start(bf16[48,2048]{1,0:T(8,128)(2,1)S(1)} %get-tuple-element.424), channel_id=1, source_target_pairs={{0,4},{2,6},{4,0},{6,2},{8,12},{10,14},{12,8},{14,10},{1,5},{3,7},... | collective-permute-start | bytes 589832 | tf_op jit(solution)/shard_map/ppermute | solution.py:376
  499.0 18.5 %collective-permute-start.75 = (bf16[48,2048]{1,0:T(8,128)(2,1)S(1)}, bf16[48,2048]{1,0:T(8,128)(2,1)S(1)}, u32[]{:S(2)}, u32[]{:S(2)}) collective-permute-start(bf16[48,2048]{1,0:T(8,128)(2,1)S(1)} %get-tuple-element.426), channel_id=1, source_target_pairs={{0,8},{2,10},{4,12},{6,14},{8,0},{10,2},{12,4},{14,6},{1,9},{3,11}... | collective-permute-start | bytes 589832 | tf_op jit(solution)/shard_map/ppermute | solution.py:376
  522.2 57.4 %collective-permute-start.69 = (bf16[192,1536]{1,0:T(8,128)(2,1)S(1)}, bf16[192,1536]{1,0:T(8,128)(2,1)S(1)}, u32[]{:S(2)}, u32[]{:S(2)}) collective-permute-start(bf16[192,1536]{1,0:T(8,128)(2,1)S(1)} %get-tuple-element.407), channel_id=1, source_target_pairs={{0,16},{16,0},{1,17},{17,1},{2,18},{18,2},{3,19},{19,3},{4,20},{20... | collective-permute-start | bytes 1769480 | tf_op jit(solution)/shard_map/ppermute | solution.py:363
  529.4 15.3 %collective-permute-start.78 = (bf16[48,1536]{1,0:T(8,128)(2,1)S(1)}, bf16[48,1536]{1,0:T(8,128)(2,1)S(1)}, u32[]{:S(2)}, u32[]{:S(2)}) collective-permute-start(bf16[48,1536]{1,0:T(8,128)(2,1)S(1)} %add_convert_fusion.26), channel_id=1, source_target_pairs={{0,8},{2,10},{4,12},{6,14},{8,0},{10,2},{12,4},{14,6},{1,9},{3,11}... | collective-permute-start | bytes 442376 | tf_op jit(solution)/shard_map/ppermute | solution.py:376
  529.4 15.3 %collective-permute-start.77 = (bf16[48,1536]{1,0:T(8,128)(2,1)S(1)}, bf16[48,1536]{1,0:T(8,128)(2,1)S(1)}, u32[]{:S(2)}, u32[]{:S(2)}) collective-permute-start(bf16[48,1536]{1,0:T(8,128)(2,1)S(1)} %add_convert_fusion.26), channel_id=1, source_target_pairs={{0,4},{2,6},{4,0},{6,2},{8,12},{10,14},{12,8},{14,10},{1,5},{3,7},... | collective-permute-start | bytes 442376 | tf_op jit(solution)/shard_map/ppermute | solution.py:376
  558.8 14.8 %collective-permute-start.89 = (bf16[96,2048]{1,0:T(8,128)(2,1)S(1)}, bf16[96,2048]{1,0:T(8,128)(2,1)S(1)}, u32[]{:S(2)}, u32[]{:S(2)}) collective-permute-start(bf16[96,2048]{1,0:T(8,128)(2,1)S(1)} %get-tuple-element.418), channel_id=1, source_target_pairs={{0,2},{2,0},{4,6},{6,4},{8,10},{10,8},{12,14},{14,12},{1,3},{3,1},... | collective-permute-start | bytes 1179656 | tf_op jit(solution)/shard_map/ppermute | solution.py:367
  574.8 16.3 %collective-permute-start.92 = (bf16[192,1536]{1,0:T(8,128)(2,1)S(1)}, bf16[192,1536]{1,0:T(8,128)(2,1)S(1)}, u32[]{:S(2)}, u32[]{:S(2)}) collective-permute-start(bf16[192,1536]{1,0:T(8,128)(2,1)S(1)} %maximum_select_fusion.10), channel_id=1, source_target_pairs={{0,2},{2,0},{4,6},{6,4},{8,10},{10,8},{12,14},{14,12},{1,3},{3,1},... | collective-permute-start | bytes 1769480 | tf_op jit(solution)/shard_map/ppermute | solution.py:367
  578.1 16.3 %collective-permute-start.93 = (bf16[192,1536]{1,0:T(8,128)(2,1)S(1)}, bf16[192,1536]{1,0:T(8,128)(2,1)S(1)}, u32[]{:S(2)}, u32[]{:S(2)}) collective-permute-start(bf16[192,1536]{1,0:T(8,128)(2,1)S(1)} %maximum_select_fusion.11), channel_id=1, source_target_pairs={{0,16},{16,0},{1,17},{17,1},{2,18},{18,2},{3,19},{19,3},{4,20},{20... | collective-permute-start | bytes 1769480 | tf_op jit(solution)/shard_map/ppermute | solution.py:363
  581.0 23.5 %collective-permute-start.90 = (bf16[192,2048]{1,0:T(8,128)(2,1)S(1)}, bf16[192,2048]{1,0:T(8,128)(2,1)S(1)}, u32[]{:S(2)}, u32[]{:S(2)}) collective-permute-start(bf16[192,2048]{1,0:T(8,128)(2,1)S(1)} %maximum_select_fusion.8), channel_id=1, source_target_pairs={{0,2},{2,0},{4,6},{6,4},{8,10},{10,8},{12,14},{14,12},{1,3},{3,1},... | collective-permute-start | bytes 2359304 | tf_op jit(solution)/shard_map/ppermute | solution.py:367
  581.9 25.6 %collective-permute-start.91 = (bf16[192,2048]{1,0:T(8,128)(2,1)S(1)}, bf16[192,2048]{1,0:T(8,128)(2,1)S(1)}, u32[]{:S(2)}, u32[]{:S(2)}) collective-permute-start(bf16[192,2048]{1,0:T(8,128)(2,1)S(1)} %maximum_select_fusion.9), channel_id=1, source_target_pairs={{0,16},{16,0},{1,17},{17,1},{2,18},{18,2},{3,19},{19,3},{4,20},{20... | collective-permute-start | bytes 2359304 | tf_op jit(solution)/shard_map/ppermute | solution.py:363
  (128 other events, 1252.5 us)

commit v3 on v2

--- a/solution.py
+++ b/solution.py
@@ -363,6 +363,13 @@
     return lax.ppermute(field, "dp", [(0, 1), (1, 0)])
 
 
+def owners_dp(field):
+    pairs = [
+        ((d * 8 + e) * 2 + e % 2, ((1 - d) * 8 + e) * 2 + e % 2) for d in range(2) for e in range(8)
+    ]
+    return lax.ppermute(field, ("dp", "expert", "shard"), pairs)
+
+
 def across_x(field):
     return lax.ppermute(field, "expert", [(i, i ^ 1) for i in range(8)])
 
@@ -415,32 +422,31 @@
     return field.astype(jnp.bfloat16)
 
 
-def reduce_chip(term, core):
-    return low(sum_blocks(block(term, core, 2), other_core(block(term, 1 - core, 2))))
-
-
-def slab_first(part, place):
+def chip_send(theirs, mine):
+    return mine, other_core(theirs)
+
+
+def slab_send(fields, place):
     dp, x, _, _ = place
-    first, second = jnp.split(part, 2)
-    return across_x(block(first, 1 - x, 2)), other_dp(block(second, 1 - dp, 2))
-
-
-def slab_second(part, sent, place):
+    first, second = jnp.split(low(sum_blocks(*fields)), 2)
+    return (
+        (block(first, x, 2), across_x(block(first, 1 - x, 2))),
+        (block(second, dp, 2), other_dp(block(second, 1 - dp, 2))),
+    )
+
+
+def slab_send_on(fields, place):
     dp, x, _, _ = place
-    first, second = jnp.split(part, 2)
-    first = low(sum_blocks(block(first, x, 2), sent[0]))
-    second = low(sum_blocks(block(second, dp, 2), sent[1]))
-    first = low(sum_blocks(block(first, dp, 2), other_dp(block(first, 1 - dp, 2))))
-    second = low(sum_blocks(block(second, x, 2), across_x(block(second, 1 - x, 2))))
-    return jnp.concatenate([first, second])
-
-
-def reduce_line(part, z):
-    return low(
-        sum_blocks(
-            block(part, z, 4), *[across_z(block(part, z ^ k, 4), k) for k in (1, 2, 3)]
-        )
-    )
+    first, second = (low(sum_blocks(*pair)) for pair in fields)
+    return (
+        (block(first, dp, 2), other_dp(block(first, 1 - dp, 2))),
+        (block(second, x, 2), across_x(block(second, 1 - x, 2))),
+    )
+
+
+def line_send(fields, z):
+    part = low(jnp.concatenate([sum_blocks(*pair) for pair in fields]))
+    return [block(part, z, 4)] + [across_z(block(part, z ^ k, 4), k) for k in (1, 2, 3)]
 
 
 def put_in_order(pieces, own):
@@ -450,22 +456,27 @@
     )
 
 
-def spread_line(part, z):
-    return put_in_order([part] + [across_z(part, k) for k in (1, 2, 3)], z)
-
-
-def spread_first(part, place):
+def line_spread(fields):
+    part = low(sum_blocks(*fields))
+    return [part] + [across_z(part, k) for k in (1, 2, 3)]
+
+
+def slab_spread(fields, z):
+    first, second = jnp.split(put_in_order(fields, z), 2)
+    return (first, other_dp(first)), (second, across_x(second))
+
+
+def slab_spread_on(fields, place):
     dp, x, _, _ = place
-    first, second = jnp.split(part, 2)
-    return in_order(dp == 0, first, other_dp(first)), in_order(x == 0, second, across_x(second))
-
-
-def spread_second(parts, place):
+    first, second = fields
+    first, second = in_order(dp == 0, *first), in_order(x == 0, *second)
+    return (first, across_x(first)), (second, other_dp(second))
+
+
+def whole_of(fields, place):
     dp, x, _, _ = place
-    first, second = parts
-    first = in_order(x == 0, first, across_x(first))
-    second = in_order(dp == 0, second, other_dp(second))
-    return jnp.concatenate([first, second])
+    first, second = fields
+    return jnp.concatenate([in_order(x == 0, *first), in_order(dp == 0, *second)])
 
 
 def matmul(left, right, dims=(((1,), (0,)), ((), ()))):
@@ -475,13 +486,28 @@
 FIRST_WITH_FIRST = (((0,), (0,)), ((), ()))
 
 
+EXTRA = 16
+
+
+def packed(field, columns):
+    high = low(field)
+    rest = low(field - high.astype(jnp.float32))
+    pad = jnp.zeros((field.shape[0], columns - 2 * field.shape[1]), jnp.bfloat16)
+    block = jnp.concatenate([high, rest, pad], axis=1)
+    return jnp.concatenate([block, jnp.zeros((EXTRA - field.shape[0], columns), jnp.bfloat16)])
+
+
+def unpacked(extra, rows):
+    field = extra.astype(jnp.float32)[: EXTRA // 2]
+    return field[:, :rows] + field[:, rows : 2 * rows]
+
+
 def expert_kernel(
-    is_own,
+    choice,
     own_rows,
     other_rows,
     own_ct,
     other_ct,
-    weight_ref,
     up_own,
     up_other,
     down_own,
@@ -494,11 +520,11 @@
         other_sum,
         own_back,
         other_back,
-        gate_ref,
         hidden_ref,
         grad_out_ref,
         grad_up_ref,
         rows_ref,
+        unit_ref,
         ct_ref,
         up_ref,
         down_ref,
@@ -508,29 +534,35 @@
     width = down_ref.shape[0]
     first = pl.program_id(0) == 0
 
-    @pl.when(first & (is_own[0] == 1))
+    @pl.when(first & (choice[0] == 1))
     def _():
         pltpu.make_async_copy(up_own, up_ref, up_sem).start()
         pltpu.make_async_copy(down_own, down_ref, down_sem).start()
 
-    @pl.when(first & (is_own[0] == 0))
+    @pl.when(first & (choice[0] == 0))
     def _():
         pltpu.make_async_copy(up_other, up_ref, up_sem).start()
         pltpu.make_async_copy(down_other, down_ref, down_sem).start()
 
     @pl.when(first)
     def _():
-        rows_ref[...] = own_rows[...]
+        unit_ref[...] = own_rows[...]
         ct_ref[...] = own_ct[...]
         pltpu.make_async_copy(up_own, up_ref, up_sem).wait()
         pltpu.make_async_copy(down_own, down_ref, down_sem).wait()
 
     @pl.when(pl.program_id(0) == 1)
     def _():
-        rows_ref[...] = other_rows[...]
+        unit_ref[...] = other_rows[...]
         ct_ref[...] = other_ct[...]
 
-    rows, weighting = rows_ref[...], weight_ref[...]
+    count = ct_ref.shape[0]
+    rows = unit_ref[:count, :]
+    rows_ref[...] = rows
+    gates = unpacked(unit_ref[count:, :], count)
+    mine = lax.broadcasted_iota(jnp.int32, gates.shape, 0) == choice[1]
+    weighting = jnp.sum(jnp.where(mine, gates, 0.0), axis=0, keepdims=True)
+    weighting = jnp.broadcast_to(weighting, (HEAD_SIZE, rows.shape[0])).T[:, :1]
     ct = ct_ref[...].astype(jnp.float32)
     grad_out = low(weighting * ct)
     grad_out_ref[...] = grad_out
@@ -548,24 +580,26 @@
         grad_up_ref[:, gate] = low(grad_hidden * b * slope)
         grad_up_ref[:, up] = low(grad_hidden * gelu)
     out = low(matmul(hidden_ref[...], down_ref[...])).astype(jnp.float32)
-    gate_ref[...] = jnp.sum(ct * out, axis=1, keepdims=True)
+    grad = jnp.sum(ct * out, axis=1, keepdims=True)
+    grad = jnp.broadcast_to(grad, (rows.shape[0], HEAD_SIZE)).T[: mine.shape[0], :]
+    grad = packed(jnp.where(mine, grad, 0.0), rows.shape[1])
     weighted = low(weighting * out)
     back = low(matmul(grad_up_ref[...], up_ref[...], LAST_WITH_LAST))
 
     @pl.when(pl.program_id(0) == 0)
     def _():
-        own_sum[...], own_back[...] = weighted, back
+        own_sum[...], own_back[:count, :], own_back[count:, :] = weighted, back, grad
 
     @pl.when(pl.program_id(0) == 1)
     def _():
-        other_sum[...], other_back[...] = weighted, back
+        other_sum[...], other_back[:count, :], other_back[count:, :] = weighted, back, grad
 
 
 SHORT = pl.CostEstimate(flops=1000, bytes_accessed=1000, transcendentals=0)
 
 
-def expert_step(step, is_own, rows, upstream, weighting, matrices, kept):
-    tile, model_width = rows[0].shape
+def expert_step(step, choice, rows, upstream, matrices, kept):
+    tile, model_width = upstream[0].shape
     width = matrices[2].shape[0]
     anywhere = pl.BlockSpec(memory_space=pl.ANY)
 
@@ -576,19 +610,20 @@
         return jax.ShapeDtypeStruct((count * tile, columns), dtype)
 
     same = pl.BlockSpec((tile, model_width), lambda i: (0, 0))
+    unit = pl.BlockSpec((tile + EXTRA, model_width), lambda i: (0, 0))
     out_shape = [
-        *[shape(1, model_width)] * 4,
-        shape(2, 1, jnp.float32),
+        *[shape(1, model_width)] * 2,
+        *[jax.ShapeDtypeStruct((tile + EXTRA, model_width), jnp.bfloat16)] * 2,
         shape(8, width),
         shape(8, model_width),
         shape(8, 2 * width),
         shape(8, model_width),
     ]
-    operands = [is_own, *rows, *upstream, weighting, *matrices]
-    in_specs = [pl.BlockSpec(memory_space=pltpu.SMEM)] + [same] * 4 + [placed(1)] + [anywhere] * 4
+    operands = [choice, *rows, *upstream, *matrices]
+    in_specs = [pl.BlockSpec(memory_space=pltpu.SMEM), unit, unit, same, same] + [anywhere] * 4
     aliases = {}
     if kept is not None:
-        aliases = {len(operands) + i: 5 + i for i in range(4)}
+        aliases = {len(operands) + i: 4 + i for i in range(4)}
         operands += list(kept)
         in_specs += [anywhere] * 4
     results = pl.pallas_call(
@@ -596,8 +631,8 @@
         grid=(2,),
         in_specs=in_specs,
         out_specs=[
-            *[same] * 4,
-            pl.BlockSpec((tile, 1), lambda i: (i, 0)),
+            *[same] * 2,
+            *[unit] * 2,
             placed(width),
             placed(model_width),
             placed(2 * width),
@@ -605,6 +640,7 @@
         ],
         out_shape=out_shape,
         scratch_shapes=[
+            pltpu.VMEM((tile + EXTRA, model_width), jnp.bfloat16),
             pltpu.VMEM((tile, model_width), jnp.bfloat16),
             pltpu.VMEM((model_width, 2 * width), jnp.bfloat16),
             pltpu.VMEM((width, model_width), jnp.bfloat16),
@@ -615,14 +651,14 @@
         compiler_params=pltpu.CompilerParams(vmem_limit_bytes=50 * 2**20),
         cost_estimate=SHORT,
     )(*operands)
-    return results[:2], results[2:4], results[4], results[5:]
+    return results[:2], results[2:4], results[4:]
 
 
 def middle_back_kernel(
     back_own,
     back_other,
     back_ring,
-    logits_ref,
+    gates_ref,
     router_ref,
     middle_ref,
     scale_ref,
@@ -633,13 +669,24 @@
     low_ref,
     mix_ref,
     gain_grad,
+    logits_grad,
+    weight_here,
+    weight_sem,
 ):
     rows = middle_ref.shape[0]
+    pltpu.make_async_copy(weight_ref, weight_here, weight_sem).start()
+    gates = gates_ref[...]
+    grad_gates = unpacked(
+        sum_blocks(back_own[rows:, :], back_other[rows:, :], back_ring[rows:, :]), rows
+    )
+    mean_term = jnp.sum(gates * grad_gates, axis=0, keepdims=True)
+    logits = low(gates * (grad_gates - mean_term))
+    logits_grad[...] = logits
     total = jnp.zeros(gain_grad.shape, jnp.float32)
     for start in range(0, rows, HEAD_SIZE):
         at = pl.ds(start, HEAD_SIZE)
         grad = sum_blocks(back_own[at, :], back_other[at, :], back_ring[at, :])
-        grad = grad + matmul(logits_ref[:, at], router_ref[...], FIRST_WITH_FIRST)
+        grad = grad + matmul(logits[:, start : start + HEAD_SIZE], router_ref[...], FIRST_WITH_FIRST)
         middle, scale = middle_ref[at, :], scale_ref[at, :]
         scaled = grad * gain_ref[...]
         mean = jnp.mean(scaled * middle, axis=1, keepdims=True)
@@ -648,47 +695,212 @@
         grad_ref[at, :] = out
         low_ref[at, :] = low(out)
     gain_grad[...] = total
-    for start in range(0, weight_ref.shape[0], 256):
+    pltpu.make_async_copy(weight_ref, weight_here, weight_sem).wait()
+    for start in range(0, weight_here.shape[0], 256):
         at = pl.ds(start, 256)
-        mix_ref[:, at] = low(matmul(low_ref[...], weight_ref[at, :], LAST_WITH_LAST))
-
-
-def middle_back(back, logits, router, middle, scale, gain, upstream, out_weight):
+        mix_ref[:, at] = low(matmul(low_ref[...], weight_here[at, :], LAST_WITH_LAST))
+
+
+def middle_back(back, gates, router, middle, scale, gain, upstream, out_weight):
     rows, model_width = middle.shape
     shapes = [
         ((rows, model_width), jnp.float32),
         ((rows, model_width), jnp.bfloat16),
         ((rows, out_weight.shape[0]), jnp.bfloat16),
         ((1, model_width), jnp.float32),
+        (gates.shape, jnp.bfloat16),
     ]
     return pl.pallas_call(
         middle_back_kernel,
+        in_specs=[pl.BlockSpec(memory_space=pltpu.VMEM)] * 9 + [pl.BlockSpec(memory_space=pl.ANY)],
         out_shape=[jax.ShapeDtypeStruct(*shape) for shape in shapes],
+        scratch_shapes=[pltpu.VMEM(out_weight.shape, jnp.bfloat16), pltpu.SemaphoreType.DMA],
+        compiler_params=pltpu.CompilerParams(vmem_limit_bytes=60 * 2**20),
+        cost_estimate=SHORT,
+    )(*back, gates, router, middle, scale, gain, upstream, out_weight)
+
+
+def middle_kernel(
+    mix_ref, weight_ref, tokens_ref, gain_ref, router_ref, routes_ref, *outs
+):
+    middle_ref, scale_ref, unit_ref, gates_ref = outs
+    rows, columns = tokens_ref.shape
+    for start in range(0, columns, 256):
+        at = pl.ds(start, 256)
+        middle_ref[:, at] = tokens_ref[:, at].astype(jnp.float32) + matmul(
+            mix_ref[...], weight_ref[:, at]
+        )
+    for start in range(0, rows, HEAD_SIZE):
+        at = pl.ds(start, HEAD_SIZE)
+        middle = middle_ref[at, :]
+        scale = lax.rsqrt(jnp.mean(middle * middle, axis=1, keepdims=True) + EPS)
+        scale_ref[at, :] = scale
+        unit_ref[at, :] = low(middle * scale * gain_ref[...])
+    logits = matmul(router_ref[...], unit_ref[:rows, :], LAST_WITH_LAST)
+    expert = lax.broadcasted_iota(jnp.int32, logits.shape, 0)
+    named = expert == routes_ref[0:1, :]
+    for choice in range(1, routes_ref.shape[0]):
+        named = named | (expert == routes_ref[choice : choice + 1, :])
+    logits = jnp.where(named, logits, -1e30)
+    raised = jnp.exp(logits - jnp.max(logits, axis=0, keepdims=True))
+    raised = jnp.where(named, raised, 0.0)
+    gates = raised / jnp.sum(raised, axis=0, keepdims=True)
+    gates_ref[...] = gates
+    unit_ref[rows:, :] = packed(gates, columns)
+
+
+def middle_of(mix, out_weight, tokens, gain, router, routes):
+    rows, columns = tokens.shape
+    shapes = [
+        ((rows, columns), jnp.float32),
+        ((rows, 1), jnp.float32),
+        ((rows + EXTRA, columns), jnp.bfloat16),
+        ((router.shape[0], rows), jnp.float32),
+    ]
+    return pl.pallas_call(
+        middle_kernel,
+        out_shape=[jax.ShapeDtypeStruct(*shape) for shape in shapes],
+        compiler_params=pltpu.CompilerParams(vmem_limit_bytes=32 * 2**20),
+        cost_estimate=SHORT,
+    )(mix, out_weight, tokens, gain, router, routes)
+
+
+def tokens_back_kernel(
+    grad_ref, weight_ref, tokens_ref, scale_ref, gain_ref, middle_grad, out_ref, normed
+):
+    rows, columns = tokens_ref.shape
+    for start in range(0, columns, 256):
+        at = pl.ds(start, 256)
+        normed[:, at] = matmul(grad_ref[...], weight_ref[at, :], LAST_WITH_LAST)
+    for start in range(0, rows, HEAD_SIZE):
+        at = pl.ds(start, HEAD_SIZE)
+        tokens, scale, grad = tokens_ref[at, :].astype(jnp.float32), scale_ref[at, :], normed[at, :]
+        scaled = grad * gain_ref[...]
+        mean = jnp.mean(scaled * tokens, axis=1, keepdims=True)
+        out_ref[at, :] = low(
+            middle_grad[at, :] + scale * scaled - tokens * (scale**3 * mean)
+        )
+
+
+def tokens_back(grad_projected, qkv_weight, tokens, scale, gain, grad_middle):
+    return pl.pallas_call(
+        tokens_back_kernel,
+        out_shape=jax.ShapeDtypeStruct(tokens.shape, jnp.bfloat16),
+        scratch_shapes=[pltpu.VMEM(tokens.shape, jnp.float32)],
         compiler_params=pltpu.CompilerParams(vmem_limit_bytes=40 * 2**20),
         cost_estimate=SHORT,
-    )(*back, logits, router, middle, scale, gain[None], upstream, out_weight)
-
-
-def product_kernel(left_ref, right_ref, out_ref):
-    out_ref[...] = low(matmul(left_ref[...], right_ref[...], FIRST_WITH_FIRST))
-
-
-def product(left, right):
-    depth, rows = left.shape
-    columns = right.shape[1]
-    tile = 384
+    )(grad_projected, qkv_weight, tokens, scale, gain, grad_middle)
+
+
+def halves_kernel(fill, core_ref, *refs):
+    theirs_ref, mine_ref = refs[-2:]
+
+    @pl.when(pl.program_id(0) == 0)
+    def _():
+        fill(*refs[:-2], theirs_ref)
+
+    @pl.when(pl.program_id(0) == 1)
+    def _():
+        fill(*refs[:-2], mine_ref)
+
+
+def in_halves(fill, core, tiled, whole, total):
+    columns = tiled[0].shape[1]
+    tile = columns // 4
+
+    def chosen(half, i, core_ref):
+        return jnp.where(half == 1, core_ref[0], 1 - core_ref[0]) * 2 + i
+
+    def cut(field):
+        return pl.BlockSpec(
+            (field.shape[0], tile), lambda half, i, core_ref: (0, chosen(half, i, core_ref))
+        )
+
+    def kept(field):
+        return pl.BlockSpec(field.shape, lambda half, i, core_ref: (0, 0))
+
     return pl.pallas_call(
-        product_kernel,
-        grid=(rows // tile,),
-        in_specs=[
-            pl.BlockSpec((depth, tile), lambda i: (0, i)),
-            pl.BlockSpec((depth, columns), lambda i: (0, 0)),
-        ],
-        out_specs=pl.BlockSpec((tile, columns), lambda i: (i, 0)),
-        out_shape=jax.ShapeDtypeStruct((rows, columns), jnp.bfloat16),
+        functools.partial(halves_kernel, fill),
+        grid_spec=pltpu.PrefetchScalarGridSpec(
+            num_scalar_prefetch=1,
+            grid=(2, 2),
+            in_specs=[cut(field) for field in tiled] + [kept(field) for field in whole],
+            out_specs=[
+                pl.BlockSpec((tile, total), lambda half, i, core_ref: (jnp.where(half == 0, i, 1), 0)),
+                pl.BlockSpec((tile, total), lambda half, i, core_ref: (jnp.where(half == 1, i, 0), 0)),
+            ],
+        ),
+        out_shape=[jax.ShapeDtypeStruct((columns // 2, total), jnp.bfloat16)] * 2,
         compiler_params=pltpu.CompilerParams(vmem_limit_bytes=24 * 2**20),
         cost_estimate=SHORT,
-    )(left, right)
+    )(core[None].astype(jnp.int32), *tiled, *whole)
+
+
+def fill_product(left_ref, right_ref, out_ref):
+    out_ref[...] = low(matmul(left_ref[...], right_ref[...], FIRST_WITH_FIRST))
+
+
+def product(left, right, core):
+    return in_halves(fill_product, core, [left], [right], right.shape[1])
+
+
+def fill_out_grads(mix_ref, rows_ref, gain_ref, grad_out, logits_ref, out_ref):
+    rows, width = grad_out.shape
+    out_ref[:, :width] = low(matmul(mix_ref[...], grad_out[...], FIRST_WITH_FIRST))
+    logits = logits_ref[...]
+    experts = logits.shape[0]
+    logits = jnp.concatenate([logits] + [jnp.zeros_like(logits)] * (HEAD_SIZE // experts - 1))
+    small = matmul(rows_ref[:rows, :], logits, (((0,), (1,)), ((), ())))
+    lane = lax.broadcasted_iota(jnp.int32, small.shape, 1)
+    gain = jnp.broadcast_to(gain_ref[...], (HEAD_SIZE, small.shape[0])).T
+    out_ref[:, width:] = low(jnp.where(lane == experts, gain, small))
+
+
+def out_grads(mix, grad_out, unit, logits, gain, core):
+    total = grad_out.shape[1] + HEAD_SIZE
+    return in_halves(fill_out_grads, core, [mix, unit, gain], [grad_out, logits], total)
+
+
+def finish_kernel(place_ref, own_0, got_0, own_1, got_1, weight_ref, gain_ref, out_ref, grad_ref):
+    step = pl.program_id(0)
+
+    def put(field):
+        field = field[...].astype(jnp.float32)
+        out_ref[...] = field
+        total = jnp.sum(field * weight_ref[...].astype(jnp.float32), axis=1, keepdims=True)
+        grad_ref[...] = total / gain_ref[...]
+
+    for half, (own, got) in enumerate(((own_0, got_0), (own_1, got_1))):
+        here = 2 * half + place_ref[half]
+        pl.when(step == here)(functools.partial(put, own))
+        pl.when(step == 4 * half + 1 - here)(functools.partial(put, got))
+
+
+def finish(fields, place, weight, gain):
+    dp, x, _, _ = place
+    (own_0, got_0), (own_1, got_1) = fields
+    rows, columns = own_0.shape
+    whole = pl.BlockSpec((rows, columns), lambda i: (0, 0))
+    return pl.pallas_call(
+        finish_kernel,
+        grid=(4,),
+        in_specs=[
+            pl.BlockSpec(memory_space=pltpu.SMEM),
+            *[whole] * 4,
+            pl.BlockSpec((rows, columns), lambda i: (i, 0)),
+            pl.BlockSpec((rows, 1), lambda i: (i, 0)),
+        ],
+        out_specs=[
+            pl.BlockSpec((rows, columns), lambda i: (i, 0)),
+            pl.BlockSpec((rows, 1), lambda i: (i, 0)),
+        ],
+        out_shape=[
+            jax.ShapeDtypeStruct((4 * rows, columns), jnp.float32),
+            jax.ShapeDtypeStruct((4 * rows, 1), jnp.float32),
+        ],
+        compiler_params=pltpu.CompilerParams(vmem_limit_bytes=24 * 2**20),
+        cost_estimate=SHORT,
+    )(jnp.stack([x, dp]).astype(jnp.int32), own_0, got_0, own_1, got_1, weight, gain)
 
 
 def turn(field, cosine, sine):
@@ -697,15 +909,21 @@
     return field * cosine + turned * sine
 
 
+HEADS_AT_ONCE = 2
+
+
 def attend_kernel(query_in, key_in, value_in, cos_ref, sin_ref, seg_row, seg_column, *refs):
     query_ref, key_ref, value_ref, mix_ref = refs
     cosine, sine = cos_ref[...], sin_ref[...]
-    query = low(turn(query_in[...], cosine, sine))
     key = low(turn(key_in[...], cosine, sine))
     value = low(value_in[...])
-    query_ref[...], key_ref[...], value_ref[...] = query, key, value
-    probs = probabilities(query, key, seg_row[...], seg_column[...])
-    mix_ref[...] = low(matmul(low(probs), value, FIRST_WITH_FIRST))
+    key_ref[...], value_ref[...] = key, value
+    for half in range(HEADS_AT_ONCE):
+        columns = slice(half * HEAD_SIZE, (half + 1) * HEAD_SIZE)
+        query = low(turn(query_in[:, columns], cosine, sine))
+        query_ref[:, columns] = query
+        probs = probabilities(query, key, seg_row[...], seg_column[...])
+        mix_ref[:, columns] = low(matmul(low(probs), value, FIRST_WITH_FIRST))
 
 
 def probabilities(query, key, seg_row, seg_column):
@@ -721,7 +939,9 @@
     rows, width = projected.shape
     groups, heads = KEY_VALUE_HEADS, QUERY_HEADS
 
-    def head(index):
+    steps = heads // HEADS_AT_ONCE
+
+    def one(index):
         return pl.BlockSpec((rows, HEAD_SIZE), lambda i: (0, index(i)))
 
     def whole(*shape):
@@ -730,22 +950,25 @@
     def shape(count):
         return jax.ShapeDtypeStruct((rows, count * HEAD_SIZE), jnp.bfloat16)
 
-    group = lambda i: i // (heads // groups)
+    def group(i):
+        return i // (steps // groups)
+
+    head = pl.BlockSpec((rows, HEADS_AT_ONCE * HEAD_SIZE), lambda i: (0, i))
     return pl.pallas_call(
         attend_kernel,
-        grid=(heads,),
+        grid=(steps,),
         in_specs=[
-            head(lambda i: i),
-            head(lambda i: heads + group(i)),
-            head(lambda i: heads + groups + group(i)),
+            head,
+            one(lambda i: heads + group(i)),
+            one(lambda i: heads + groups + group(i)),
             whole(rows, HEAD_SIZE),
             whole(rows, HEAD_SIZE),
             whole(1, rows),
             whole(rows, 1),
         ],
-        out_specs=[head(lambda i: i), head(group), head(group), head(lambda i: i)],
+        out_specs=[head, one(group), one(group), head],
         out_shape=[shape(heads), shape(groups), shape(groups), shape(heads)],
-        compiler_params=pltpu.CompilerParams(vmem_limit_bytes=16 * 2**20),
+        compiler_params=pltpu.CompilerParams(vmem_limit_bytes=24 * 2**20),
         cost_estimate=SHORT,
     )(projected, projected, projected, cosine, sine, segment[None, :], segment[:, None])
 
@@ -755,25 +978,29 @@
 ):
     key_sum, value_sum = sums
     step = pl.program_id(0)
-    heads = pl.num_programs(0)
-    groups = KEY_VALUE_HEADS
-    group, place = step // (heads // groups), step % (heads // groups)
-    query, key, value, grad_mix = query_ref[...], key_ref[...], value_ref[...], grad_ref[...]
-    probs = probabilities(query, key, seg_row[...], seg_column[...])
-    grad_probs = matmul(value, grad_mix, LAST_WITH_LAST)
-    grad_scores = low(
-        probs * (grad_probs - jnp.sum(probs * grad_probs, axis=0, keepdims=True))
-    )
-    grad_query = matmul(grad_scores, key, FIRST_WITH_FIRST) * HEAD_SIZE ** (-0.5)
-    grad_query = turn(grad_query, cos_ref[...], -sin_ref[...])
-    grad_key = matmul(grad_scores, query) * HEAD_SIZE ** (-0.5)
-    grad_value = matmul(low(probs), grad_mix)
+    heads, groups = QUERY_HEADS, KEY_VALUE_HEADS
+    steps = pl.num_programs(0) // groups
+    group, place = step // steps, step % steps
+    key, value = key_ref[...], value_ref[...]
+    cosine, sine = cos_ref[...], -sin_ref[...]
 
     def put(head, field):
         at = pl.multiple_of(head * HEAD_SIZE, HEAD_SIZE)
         out_ref[:, pl.ds(at, HEAD_SIZE)] = low(field)
 
-    put(step, grad_query)
+    grad_key = grad_value = 0.0
+    for half in range(HEADS_AT_ONCE):
+        columns = slice(half * HEAD_SIZE, (half + 1) * HEAD_SIZE)
+        query, grad_mix = query_ref[:, columns], grad_ref[:, columns]
+        probs = probabilities(query, key, seg_row[...], seg_column[...])
+        grad_probs = matmul(value, grad_mix, LAST_WITH_LAST)
+        grad_scores = low(
+            probs * (grad_probs - jnp.sum(probs * grad_probs, axis=0, keepdims=True))
+        )
+        grad_query = matmul(grad_scores, key, FIRST_WITH_FIRST) * HEAD_SIZE ** (-0.5)
+        put(step * HEADS_AT_ONCE + half, turn(grad_query, cosine, sine))
+        grad_key = grad_key + matmul(grad_scores, query) * HEAD_SIZE ** (-0.5)
+        grad_value = grad_value + matmul(low(probs), grad_mix)
 
     @pl.when(place == 0)
     def _():
@@ -785,25 +1012,26 @@
         key_sum[...] += grad_key
         value_sum[...] += grad_value
 
-    @pl.when(place == heads // groups - 1)
+    @pl.when(place == steps - 1)
     def _():
-        put(heads + group, turn(key_sum[...], cos_ref[...], -sin_ref[...]))
+        put(heads + group, turn(key_sum[...], cosine, sine))
         put(heads + groups + group, value_sum[...])
 
 
 def attend_back(query, key, value, grad_mix, cosine, sine, segment):
     rows = query.shape[0]
     heads, groups = QUERY_HEADS, KEY_VALUE_HEADS
+    steps = heads // HEADS_AT_ONCE
 
     def whole(*shape):
         return pl.BlockSpec(shape, lambda i: (0, 0))
 
-    head = pl.BlockSpec((rows, HEAD_SIZE), lambda i: (0, i))
-    shared = pl.BlockSpec((rows, HEAD_SIZE), lambda i: (0, i // (heads // groups)))
+    head = pl.BlockSpec((rows, HEADS_AT_ONCE * HEAD_SIZE), lambda i: (0, i))
+    shared = pl.BlockSpec((rows, HEAD_SIZE), lambda i: (0, i // (steps // groups)))
     width = (heads + 2 * groups) * HEAD_SIZE
     return pl.pallas_call(
         attend_back_kernel,
-        grid=(heads,),
+        grid=(steps,),
         in_specs=[
             head,
             shared,
@@ -817,7 +1045,7 @@
         out_specs=whole(rows, width),
         out_shape=jax.ShapeDtypeStruct((rows, width), jnp.bfloat16),
         scratch_shapes=[pltpu.VMEM((rows, HEAD_SIZE), jnp.float32)] * 2,
-        compiler_params=pltpu.CompilerParams(vmem_limit_bytes=16 * 2**20),
+        compiler_params=pltpu.CompilerParams(vmem_limit_bytes=24 * 2**20),
         cost_estimate=SHORT,
     )(query, key, value, grad_mix, cosine, sine, segment[None, :], segment[:, None])
 
@@ -843,349 +1071,225 @@
     dp, core, at = lax.axis_index("dp"), lax.axis_index("shard"), lax.axis_index("expert")
     x, z = at % 2, at // 2
     place = (dp, x, z, core)
-    expert_ids = jnp.arange(expert_count, dtype=jnp.int32)
     row_ids = jnp.arange(count_of_rows, dtype=jnp.int32)
 
-    outer = (z == 0) | (z == 3)
-
-    def by_step(k1, k2, k3):
-        return [jnp.where(outer, k2, k1), k3, jnp.where(outer, k1, k2)]
-
-    def held_at(deal_rows):
-        return jnp.where(deal_rows // half_rows == dp, 0, half_rows) + deal_rows % half_rows
+    def half_of(field, index):
+        return lax.dynamic_slice_in_dim(field, index * half_rows, half_rows, axis=0)
+
+    def sent_dealt(field):
+        return half_of(field, dp), other_dp(half_of(field, 1 - dp)), field[count_of_rows:]
 
     def arrange(own_half, other_half, order):
-        chosen = low(held_at(order)[:, None] == row_ids[None, :])
+        held_at = jnp.where(order[1, :count_of_rows] == dp, 0, half_rows)
+        held_at = held_at + order[0, :count_of_rows].astype(jnp.int32)
+        chosen = low(held_at[:, None] == row_ids[None, :])
         return low(matmul(chosen, jnp.concatenate([own_half, other_half], axis=0)))
 
-    def from_dealt(field, order):
-        return arrange(block(field, dp, 2), other_dp(block(field, 1 - dp, 2)), order)
+    def swapped(field):
+        return field, other_core(field)
 
     def to_dealt(field):
-        chosen = low(held_at(deal_order[0])[None, :] == row_ids[:, None])
+        held_at = jnp.where(deal_order[0] // half_rows == dp, 0, half_rows)
+        held_at = held_at + deal_order[0] % half_rows
+        chosen = low(held_at[None, :] == row_ids[:, None])
         field = low(matmul(chosen, field))
         return in_order(dp == 0, field[:half_rows], other_dp(field[half_rows:]))
 
-    hidden_out = block(hidden_in, 1 - dp, 2)
+    order = jnp.concatenate([deal_order % half_rows, deal_order // half_rows])
+    order = jnp.pad(low(order), ((0, EXTRA - 2), (0, model_width - count_of_rows)))
+    ct_0 = jnp.concatenate([cotangent, order])
+    ct_1 = ring_z(ct_0)
+    hidden_out = half_of(after(hidden_in, ct_0), 1 - dp)
     hidden_arrived = other_dp(hidden_out)
-    qkv_other, out_other, ct_1, up_other = (
+    qkv_other, out_other, up_other = (
         send(after(field, hidden_out))
         for send, field in (
             (other_core, qkv_weight),
             (other_core, out_weight),
-            (ring_z, cotangent),
             (from_owner, gate_up_weight[0]),
         )
     )
-    small = jnp.concatenate([attention_gain[None], expert_gain[None], router_weight.T], axis=0)
+    small = jnp.concatenate(
+        [router_weight.T, attention_gain[None], expert_gain[None], jnp.zeros_like(router_weight.T[:6])]
+    )
     small = in_order(core == 0, small, other_core(small), axis=1)
+    router = small[:expert_count]
+    gain_first = small[expert_count : expert_count + 1].astype(jnp.float32)
+    gain_second = small[expert_count + 1 : expert_count + 2].astype(jnp.float32)
     full_qkv = in_order(core == 0, qkv_weight, qkv_other)
-    full_out = in_order(core == 0, out_weight, out_other)
-    gain_first, gain_second = small[0].astype(jnp.float32), small[1].astype(jnp.float32)
-    full_router = small[2:].T
     segment, token_position = positions_of(lengths[0], count_of_rows)
     frequency = THETA ** (-jnp.arange(HEAD_SIZE // 2, dtype=jnp.float32) / (HEAD_SIZE // 2))
     angles = token_position.astype(jnp.float32)[:, None] * frequency[None, :]
     cosine = jnp.concatenate([jnp.cos(angles)] * 2, axis=1)
     sine = jnp.concatenate([-jnp.sin(angles), jnp.sin(angles)], axis=1)
-    cosine, sine, full_qkv, hidden_arrived, gain_first, gain_second, full_router = part(
-        cosine, sine, full_qkv, hidden_arrived, gain_first, gain_second, full_router
-    )
-    tokens = arrange(block(hidden_in, dp, 2), hidden_arrived, deal_order[0])
+    cosine, sine, full_qkv, hidden_arrived, gain_first, gain_second, router, routes = part(
+        cosine, sine, full_qkv, hidden_arrived, gain_first, gain_second, router, routes.T
+    )
+    tokens = arrange(half_of(hidden_in, dp), hidden_arrived, order)
     residual = tokens.astype(jnp.float32)
     inv_first = lax.rsqrt(jnp.mean(residual * residual, axis=1, keepdims=True) + EPS)
     normed_attn = low(residual * inv_first * gain_first)
     projected = matmul(normed_attn, full_qkv)
-    ct_1, projected, cotangent, full_out, down_own, routes = part(
-        ct_1, projected, cotangent, full_out, down_weight[0], routes
+    ct_1, projected, ct_0, out_other, down_own = part(
+        ct_1, projected, ct_0, out_other, down_weight[0]
     )
 
     ct_2 = ring_z(ct_1)
+    ct_0 = sent_dealt(ct_0)
     down_other = from_owner(down_own)
-    ct_0_other = other_dp(block(cotangent, 1 - dp, 2))
+    full_out = in_order(core == 0, out_weight, out_other)
     query, key, value, attn_mix = attend(projected, cosine, sine, segment)
-    middle = residual + matmul(attn_mix, full_out)
-    inv_second = lax.rsqrt(jnp.mean(middle * middle, axis=1, keepdims=True) + EPS)
-    normed_0 = low(middle * inv_second * gain_second)
-    ct_2, ct_0_other, normed_0, up_other, deal_order = part(
-        ct_2, ct_0_other, normed_0, up_other, deal_order
-    )
-
-    normed_1 = ring_z(normed_0)
-    logits = matmul(normed_0, full_router)
-    named = jnp.any(routes[:, :, None] == expert_ids[None, None, :], axis=1)
-    top_logit = jnp.max(jnp.where(named, logits, -jnp.inf), axis=1, keepdims=True)
-    exp_logits = jnp.where(named, jnp.exp(jnp.where(named, logits - top_logit, 0.0)), 0.0)
-    gates = (exp_logits / jnp.sum(exp_logits, axis=1, keepdims=True)).T
-    order_here = jnp.pad(deal_order.astype(jnp.float32), ((0, 7), (0, 0)))
-    gates_here = jnp.concatenate([gates, order_here], axis=0)
-    gates_here = [gates_here] + by_step(*[across_z(gates_here, k) for k in (1, 2, 3)])
-    orders = [field[expert_count].astype(jnp.int32) for field in gates_here]
-    gates_here = jnp.stack([field[:expert_count] for field in gates_here], axis=1)
-    own_row = (expert_ids == 2 * z + core)[:, None]
-    weighting = jnp.stack([gates_here, other_core(gates_here)], axis=2)
-    weighting = jnp.sum(jnp.where(own_row[:, :, None, None], weighting, 0.0), axis=0)
-    weighting = weighting.reshape(8 * count_of_rows, 1)
-    ct_0 = arrange(block(cotangent, dp, 2), ct_0_other, deal_order[0])
-    ct_0_other, normed_0_other = other_core(ct_0), other_core(normed_0)
-    ct_1, ct_1_other = block(ct_1, dp, 2), other_dp(block(ct_1, 1 - dp, 2))
-    (
-        normed_1,
-        weighting,
-        ct_0_other,
-        normed_0_other,
-        ct_1,
-        ct_1_other,
-        ct_2,
-        down_other,
-    ) = part(
-        normed_1,
-        weighting,
-        ct_0_other,
-        normed_0_other,
-        ct_1,
-        ct_1_other,
-        ct_2,
-        down_other,
-    )
-    is_own = (core == x).astype(jnp.int32)[None]
+    middle, inv_second, unit_0, gates = middle_of(
+        attn_mix, full_out, tokens, gain_second, router, routes
+    )
+    ct_2, ct_0, ct_1, unit_0, up_other = part(ct_2, ct_0, ct_1, unit_0, up_other)
+
+    normed_1 = ring_z(unit_0)
+    normed_0 = swapped(unit_0)
+    ct_1 = sent_dealt(ct_1)
+    ct_0 = swapped(arrange(*ct_0))
+    normed_1, normed_0, ct_0, ct_1, ct_2, down_other = part(
+        normed_1, normed_0, ct_0, ct_1, ct_2, down_other
+    )
+    choice = jnp.stack([(core == x).astype(jnp.int32), (2 * z + core).astype(jnp.int32)])
     matrices = (gate_up_weight[0], up_other, down_weight[0], down_other)
 
-    def expert(step, rows, ct, kept):
-        return expert_step(step, is_own, rows, ct, weighting, matrices, kept)
-
     ct_3 = ring_z(ct_2)
-    ct_2, ct_2_other = block(ct_2, dp, 2), other_dp(block(ct_2, 1 - dp, 2))
-    ct_1 = arrange(ct_1, ct_1_other, orders[1])
-    ct_1_other, normed_1_other = other_core(ct_1), other_core(normed_1)
-    sums_0, back_0, gate_0, kept = expert(0, (normed_0, normed_0_other), (ct_0, ct_0_other), None)
-    ct_3, ct_2, ct_2_other, ct_1, ct_1_other, normed_1, normed_1_other, kept = part(
-        ct_3, ct_2, ct_2_other, ct_1, ct_1_other, normed_1, normed_1_other, kept
-    )
-
-    normed_2 = ring_z(normed_1)
-    ct_3, ct_3_other = block(ct_3, dp, 2), other_dp(block(ct_3, 1 - dp, 2))
-    ct_2 = arrange(ct_2, ct_2_other, orders[2])
-    ct_2_other = other_core(ct_2)
-    sums_1, back_1, gate_1, kept = expert(1, (normed_1, normed_1_other), (ct_1, ct_1_other), kept)
-    normed_2, ct_3, ct_3_other, ct_2, ct_2_other, back_1, kept = part(
-        normed_2, ct_3, ct_3_other, ct_2, ct_2_other, back_1, kept
-    )
+    ct_2 = sent_dealt(ct_2)
+    ct_1, normed_1 = swapped(arrange(*ct_1)), swapped(normed_1)
+    sums_0, back_0, kept = expert_step(0, choice, normed_0, ct_0, matrices, None)
+    ct_3, ct_1, normed_1, ct_2, kept = part(ct_3, ct_1, normed_1, ct_2, kept)
+
+    normed_2 = ring_z(normed_1[0])
+    ct_3 = sent_dealt(ct_3)
+    ct_2 = swapped(arrange(*ct_2))
+    sums_1, back_1, kept = expert_step(1, choice, normed_1, ct_1, matrices, kept)
+    normed_2, ct_3, ct_2, back_1, kept = part(normed_2, ct_3, ct_2, back_1, kept)
 
     normed_3 = ring_z(normed_2)
-    back_1 = low(sum_blocks(back_1[0], other_core(back_1[1])))
-    normed_2_other = other_core(normed_2)
-    ct_3 = arrange(ct_3, ct_3_other, orders[3])
-    ct_3_other = other_core(ct_3)
-    sums_2, back_2, gate_2, kept = expert(2, (normed_2, normed_2_other), (ct_2, ct_2_other), kept)
-    normed_3, back_1, ct_3, ct_3_other, back_2, kept = part(
-        normed_3, back_1, ct_3, ct_3_other, back_2, kept
-    )
+    normed_2, back_1_other = swapped(normed_2), other_core(back_1[1])
+    ct_3 = swapped(arrange(*ct_3))
+    sums_2, back_2, kept = expert_step(2, choice, normed_2, ct_2, matrices, kept)
+    back_1 = low(sum_blocks(back_1[0], back_1_other))
+    normed_3, back_1, ct_3, back_2, kept = part(normed_3, back_1, ct_3, back_2, kept)
 
     back_1 = ring_z(back_1)
-    normed_3_other = other_core(normed_3)
-    back_2_other = other_core(back_2[1])
-    sums_1 = low(sum_blocks(sums_1[0], other_core(sums_1[1])))
-    sums_3, back_3, gate_3, kept = expert(3, (normed_3, normed_3_other), (ct_3, ct_3_other), kept)
-    back_1, back_2_other, back_3, sums_1, kept = part(back_1, back_2_other, back_3, sums_1, kept)
+    normed_3, back_2_other = swapped(normed_3), other_core(back_2[1])
+    sums_3, back_3, kept = expert_step(3, choice, normed_3, ct_3, matrices, kept)
+    back_1, back_2_other, back_3, kept = part(back_1, back_2_other, back_3, kept)
 
     back_2 = ring_z(low(sum_blocks(back_2[0], back_2_other, back_1)))
-    back_3_other = other_core(back_3[1])
+    back_3_other, back_0_other = other_core(back_3[1]), other_core(back_0[1])
+    sums_1_other = other_core(sums_1[1])
     all_hidden, all_grad_out, all_grad_up, all_rows = kept
     half_width = model_width // 2
     up_first = low(matmul(all_rows.T, all_grad_up[:, :half_width]))
     up_second = low(matmul(all_rows.T, all_grad_up[:, half_width:]))
-    grad_gates = jnp.concatenate([gate_0, gate_1, gate_2, gate_3]).reshape(4, 2 * count_of_rows)
-    other_gates = other_core(grad_gates[:, count_of_rows:])
-    back_2, back_3_other, up_first, up_second, grad_gates, other_gates, sums_2 = part(
-        back_2, back_3_other, up_first, up_second, grad_gates, other_gates, sums_2
+    back_2, back_3_other, back_0_other, sums_1_other, up_first, up_second, all_grad_out = part(
+        back_2, back_3_other, back_0_other, sums_1_other, up_first, up_second, all_grad_out
     )
 
     back_3 = ring_z(low(sum_blocks(back_3[0], back_3_other, back_2)))
-    up_first_other = to_owner(up_first)
-    up_second_other = other_dp(block(up_second, 1 - dp, 2))
-    back_0_other = other_core(back_0[1])
-    pairs = in_order(core == 0, grad_gates[:, None, :count_of_rows], other_gates[:, None], axis=1)
-    pairs = jnp.where((expert_ids // 2 == z)[None, :, None], jnp.tile(pairs, (1, 4, 1)), 0.0)
-    home = jnp.where(outer, pairs[3], pairs[1]), jnp.where(outer, pairs[1], pairs[3]), pairs[2]
-    home = [pairs[0]] + [across_z(home[k - 1], k) for k in (1, 2, 3)]
     down_first = low(matmul(all_hidden.T, all_grad_out[:, :half_width]))
     down_second = low(matmul(all_hidden.T, all_grad_out[:, half_width:]))
-    (
-        back_3,
-        up_first,
-        up_first_other,
-        up_second,
-        up_second_other,
-        down_first,
-        down_second,
-        home,
-        sums_1,
-        back_0_other,
-    ) = part(
-        back_3,
-        up_first,
-        up_first_other,
-        up_second,
-        up_second_other,
-        down_first,
-        down_second,
-        home,
-        sums_1,
-        back_0_other,
+    sums_1 = low(sum_blocks(sums_1[0], sums_1_other))
+    sums_2_other = other_core(sums_2[1])
+    back_3, up_first, up_second, down_first, down_second, sums_1, sums_2_other = part(
+        back_3, up_first, up_second, down_first, down_second, sums_1, sums_2_other
     )
 
     sums_1 = ring_z(sums_1)
-    down_first_other = to_owner(down_first)
-    down_second_other = other_dp(block(down_second, 1 - dp, 2))
-    up_first = low(sum_blocks(up_first, up_first_other))
-    up_second = low(sum_blocks(block(up_second, dp, 2), up_second_other))
-    up_first_other = other_dp(block(up_first, 1 - dp, 2))
-    up_second_other = to_owner(up_second)
-    sums_2_other = other_core(sums_2[1])
-    grad_gates = sum_blocks(*home)
-    mean_term = jnp.sum(gates * grad_gates, axis=0, keepdims=True)
-    grad_logits = low(gates * (grad_gates - mean_term))
-    grad_middle, grad_attn_out, grad_mix, term_gain_second = middle_back(
+    up_first = up_first, to_owner(up_first)
+    up_second = block(up_second, dp, 2), other_dp(block(up_second, 1 - dp, 2))
+    sums_3_other = other_core(sums_3[1])
+    grad_middle, grad_attn_out, grad_mix, term_gain_second, grad_logits = middle_back(
         (back_0[0], back_0_other, back_3),
-        grad_logits,
-        full_router.T,
+        gates,
+        router,
         middle,
         inv_second,
         gain_second,
-        ct_0,
+        ct_0[0],
         full_out,
     )
+    out = out_grads(attn_mix, grad_attn_out, unit_0, grad_logits, term_gain_second, core)
     grad_projected = attend_back(query, key, value, grad_mix, cosine, sine, segment)
-    term_out = product(attn_mix, grad_attn_out)
-    term_qkv = product(normed_attn, grad_projected)
-    (
-        sums_1,
-        down_first,
-        down_first_other,
-        down_second,
-        down_second_other,
-        up_first,
-        up_first_other,
-        up_second,
-        up_second_other,
-        sums_2_other,
-        term_out,
-        term_qkv,
-        grad_projected,
-    ) = part(
-        sums_1,
-        down_first,
-        down_first_other,
-        down_second,
-        down_second_other,
-        up_first,
-        up_first_other,
-        up_second,
-        up_second_other,
-        sums_2_other,
-        term_out,
-        term_qkv,
-        grad_projected,
+    qkv = product(normed_attn, grad_projected, core)
+    sums_1, sums_3_other, out, qkv, grad_projected, up_first, up_second = part(
+        sums_1, sums_3_other, out, qkv, grad_projected, up_first, up_second
     )
 
     sums_2 = ring_z(low(sum_blocks(sums_2[0], sums_2_other, sums_1)))
-    sums_3_other = other_core(sums_3[1])
-    chip_out, chip_qkv = reduce_chip(term_out, core), reduce_chip(term_qkv, core)
-    down_first = low(sum_blocks(down_first, down_first_other))
-    down_second = low(sum_blocks(block(down_second, dp, 2), down_second_other))
-    down_first_other = other_dp(block(down_first, 1 - dp, 2))
-    down_second_other = to_owner(down_second)
-    up_grad = [
-        sum_blocks(block(up_first, dp, 2), up_first_other),
-        sum_blocks(up_second, up_second_other),
-    ]
-    up_grad = low(jnp.concatenate(up_grad, axis=1))
-    up_grad_other = other_core(block(up_grad, 1 - core, 2))
-    grad_normed_attn = matmul(grad_projected, full_qkv, LAST_WITH_LAST)
-    grad_resid_norm, term_gain_first = norm_back(residual, inv_first, gain_first, grad_normed_attn)
-    grad_tokens = low(grad_middle + grad_resid_norm)
-    term_router = matmul(grad_logits, normed_0)
-    small_grad = jnp.concatenate([term_gain_first[None], term_gain_second, term_router])
-    (
-        sums_2,
-        sums_3_other,
-        chip_out,
-        chip_qkv,
-        down_first,
-        down_first_other,
-        down_second,
-        down_second_other,
-        up_grad,
-        up_grad_other,
-        grad_tokens,
-        small_grad,
-    ) = part(
-        sums_2,
-        sums_3_other,
-        chip_out,
-        chip_qkv,
-        down_first,
-        down_first_other,
-        down_second,
-        down_second_other,
-        up_grad,
-        up_grad_other,
-        grad_tokens,
-        small_grad,
+    out, qkv = chip_send(*out), chip_send(*qkv)
+    down_first = down_first, to_owner(down_first)
+    down_second = block(down_second, dp, 2), other_dp(block(down_second, 1 - dp, 2))
+    up_first, up_second = low(sum_blocks(*up_first)), low(sum_blocks(*up_second))
+    sums_2, out, qkv, down_first, down_second, up_first, up_second, grad_projected = part(
+        sums_2, out, qkv, down_first, down_second, up_first, up_second, grad_projected
     )
 
     sums_3 = ring_z(low(sum_blocks(sums_3[0], sums_3_other, sums_2)))
+    out = slab_send(out, place)
+    up_first = block(up_first, dp, 2), owners_dp(block(up_first, 1 - dp, 2))
+    up_second = up_second, to_owner(up_second)
+    qkv = low(sum_blocks(*qkv))
+    down_first, down_second = low(sum_blocks(*down_first)), low(sum_blocks(*down_second))
+    grad_tokens = tokens_back(
+        grad_projected, full_qkv, tokens, inv_first, gain_first, grad_middle
+    )
+    sums_3, out, qkv, up_first, up_second, down_first, down_second, grad_tokens = part(
+        sums_3, out, qkv, up_first, up_second, down_first, down_second, grad_tokens
+    )
+
+    out = slab_send_on(out, place)
+    down_first = block(down_first, dp, 2), owners_dp(block(down_first, 1 - dp, 2))
+    down_second = down_second, to_owner(down_second)
     sums_0_other = other_core(sums_0[1])
-    out_sent, qkv_sent = slab_first(chip_out, place), slab_first(chip_qkv, place)
-    down_grad = [
-        sum_blocks(block(down_first, dp, 2), down_first_other),
-        sum_blocks(down_second, down_second_other),
-    ]
-    down_grad = low(jnp.concatenate(down_grad, axis=1))
-    down_grad_other = other_core(block(down_grad, 1 - core, 2))
-    down_grad = jnp.where(core == x, block(down_grad, core, 2), down_grad_other)
-    up_grad = jnp.where(core == x, block(up_grad, core, 2), up_grad_other)
-    down_grad, gate_up_grad = (field[None].astype(jnp.float32) for field in (down_grad, up_grad))
-    small_grad = small_grad + other_core(small_grad)
-    sums_3, sums_0_other, out_sent, qkv_sent, small_grad, grad_tokens = part(
-        sums_3, sums_0_other, out_sent, qkv_sent, small_grad, grad_tokens
-    )
-
-    slab_out, slab_qkv = (
-        slab_second(chip, sent, place) for chip, sent in ((chip_out, out_sent), (chip_qkv, qkv_sent))
-    )
+    up_grad = low(jnp.concatenate([sum_blocks(*up_first), sum_blocks(*up_second)], axis=1))
+    out, qkv, down_first, down_second, sums_0_other, up_grad, grad_tokens = part(
+        out, qkv, down_first, down_second, sums_0_other, up_grad, grad_tokens
+    )
+
+    out, qkv = line_send(out, z), slab_send((qkv,), place)
+    layer_out = low(middle + sum_blocks(sums_0[0], sums_0_other, sums_3))
+    down_grad = low(jnp.concatenate([sum_blocks(*down_first), sum_blocks(*down_second)], axis=1))
+    out, qkv, layer_out, down_grad, grad_tokens, up_grad = part(
+        out, qkv, layer_out, down_grad, grad_tokens, up_grad
+    )
+
+    out, qkv = line_spread(out), slab_send_on(qkv, place)
+    layer_out = to_dealt(layer_out)
+    out, qkv, layer_out, grad_tokens, up_grad = part(out, qkv, layer_out, grad_tokens, up_grad)
+
+    out, qkv = slab_spread(out, z), line_send(qkv, z)
     input_gradient = to_dealt(grad_tokens)
-    layer_out = low(middle + sum_blocks(sums_0[0], sums_0_other, sums_3))
-    small_sent = other_dp(small_grad), across_x(small_grad), across_dp_x(small_grad)
-    slab_out, slab_qkv, small_grad, small_sent, layer_out = part(
-        slab_out, slab_qkv, small_grad, small_sent, layer_out
-    )
-
-    line_out, line_qkv = reduce_line(slab_out, z), reduce_line(slab_qkv, z)
-    layer_out = to_dealt(layer_out)
-    small_grad = sum_blocks(small_grad, *small_sent)
-    line_out, line_qkv, small_grad = part(line_out, line_qkv, small_grad)
-
-    line_out, line_qkv = spread_line(line_out, z), spread_line(line_qkv, z)
-    small_grad = sum_blocks(small_grad, *[across_z(small_grad, k) for k in (1, 2, 3)])
-    line_out, line_qkv, small_grad = part(line_out, line_qkv, small_grad)
-
-    out_parts, qkv_parts = spread_first(line_out, place), spread_first(line_qkv, place)
-    out_parts, qkv_parts = part(out_parts, qkv_parts)
-    out_grad = spread_second(out_parts, place).astype(jnp.float32)
-    qkv_grad = spread_second(qkv_parts, place).astype(jnp.float32)
-    small_grad = lax.dynamic_slice_in_dim(
-        small_grad, core * (model_width // 2), model_width // 2, axis=1
-    )
+    out, qkv, input_gradient, up_grad, down_grad = part(
+        out, qkv, input_gradient, up_grad, down_grad
+    )
+
+    out, qkv = slab_spread_on(out, place), line_spread(qkv)
+    up_grad = up_grad, other_core(block(up_grad, 1 - core, 2))
+    out, qkv, up_grad, down_grad = part(out, qkv, up_grad, down_grad)
+
+    qkv = slab_spread(qkv, z)
+    down_grad = down_grad, other_core(block(down_grad, 1 - core, 2))
+    out = whole_of(out, place).astype(jnp.float32)
+    qkv, out, up_grad, down_grad = part(qkv, out, up_grad, down_grad)
+    qkv = slab_spread_on(qkv, place)
+    gate_up_grad, down_grad = (
+        jnp.where(core == x, block(field, core, 2), received)[None].astype(jnp.float32)
+        for field, received in (up_grad, down_grad)
+    )
+    gain = attention_gain.astype(jnp.float32)[:, None]
+    qkv_grad, gain_first_grad = finish(qkv, place, qkv_weight, gain)
     return (
         layer_out,
         input_gradient,
-        small_grad[0],
-        small_grad[1],
+        gain_first_grad[:, 0],
+        out[:, model_width + expert_count],
         qkv_grad,
-        out_grad,
-        small_grad[2:].T,
+        out[:, :model_width],
+        out[:, model_width : model_width + expert_count],
         gate_up_grad,
         down_grad,
     )

time: 622 us -> 552 us (0.89)
  the two profiles are of different devices: /device:TPU:0 before, /device:TPU:8 now
where the time goes in v3:
time: 552 us; the launch traced here: 543 us
  waiting for transfers between devices  166 us (30%)
  Pallas kernels  130 us (24%)
  starting transfers between devices  96.1 us (17%)
  other arithmetic  64 us (12%)
  matrix products  44.9 us (8%)
  local copies, waits for them, and re-layouts  39.7 us (7%)
    pallas_call x4, Pallas kernels, expert_step(): pl.pallas_call(functools.partial(expert_kernel, columns=256), grid=(2,),...  82.5 us
    ppermute x17, waiting for transfers between devices, other_dp(): return lax.ppermute(field, 'dp', [(0, 1), (1, 0)])  59.3 us
    ppermute x12, waiting for transfers between devices, ring_z(): return lax.ppermute(field, 'expert', pairs)  53 us
    dot_general x12, matrix products, matmul(): lax.dot_general(left, right, dims, preferred_element_type=jnp.float32)  44.9 us
    ppermute x12, waiting for transfers between devices, across_z(): lax.ppermute(field, 'expert', [(i, i ^ 2 * distance) for i in range(8)])  41 us
    convert_element_type x20, other arithmetic, low(): return field.astype(jnp.bfloat16)  28.7 us
    ppermute x12, starting transfers between devices, ring_z(): return lax.ppermute(field, 'expert', pairs)  28 us
    select_n x11, other arithmetic, in_order(): jnp.where(first, jnp.concatenate([own, received], axis=axis), jnp.concate...  19.8 us
  transfers between devices with their start and end apart: 80, of which 32 were waited for; matrix products, arithmetic and copies ran while one was open for 23% of the time, Pallas kernels for 23%

profile of v3, /device:TPU:8, one launch (start us, length us, event | category | flops | bytes accessed | tf_op | source)
XLA Modules:
  0.0 543.3 jit_solution(7235423984271004607)
XLA Ops:
  6.2 2.6 collective-permute-start
  9.0 5.5 %collective-permute-start.7 = (bf16[1536,1536]{1,0:T(8,128)(2,1)}, bf16[1536,1536]{1,0:T(8,128)(2,1)}, u32[]{:S(2)}, u32[]{:S(2)}) collective-permute-start(bf16[1536,1536]{1,0:T(8,128)(2,1)} %bitcast.60), channel_id=1, source_target_pairs={{0,2},{3,1},{4,6},{7,5},{8,10},{11,9},{12,14},{15,13},{16,18},{19,... | collective-permute-start | bytes 14155784 | tf_op jit(solution)/shard_map/ppermute | solution.py:398
  17.7 8.2 %maximum_select_fusion.weight_ref = bf16[1536,2048]{1,0:T(8,128)(2,1)} fusion(bf16[768,2048]{1,0:T(8,128)(2,1)} %collective-permute-done.1, bf16[768,2048]{1,0:T(8,128)(2,1)} %weight_ref.1, pred[]{:T(512)S(6)} %eq.194), kind=kLoop, calls=%fused_computation | loop fusion | flops 28311552 | bytes 12582913 | tf_op jit(solution)/shard_map/jit(_where)/select_n | solution.py:402
  28.9 2.6 fusion.82.query_in.key_in.value_in
  31.5 4.3 collective-permute-done
  35.8 3.4 collective-permute-start.5
  41.8 3.5 collective-permute-start.12
  45.3 7.5 %shard_map.187 = (bf16[384,1536]{1,0:T(8,128)(2,1)S(1)}, bf16[384,256]{1,0:T(8,128)(2,1)S(1)}, bf16[384,256]{1,0:T(8,128)(2,1)S(1)}, bf16[384,1536]{1,0:T(8,128)(2,1)S(1)}) custom-call(f32[384,2048]{1,0:T(8,128)S(1)} %fusion.82.query_in.key_in.value_in, f32[384,2048]{1,0:T(8,128)S(1)} %fusion.82.query_in.key_in.value_in, ...), custom_call_target="tpu_custom_call" | custom-call | flops 1000 | bytes 1000 | tf_op jit(solution)/shard_map/pallas_call | solution.py:957
  52.9 4.8 maximum_select_fusion.1.weight_ref
  57.8 2.7 shard_map.188
  62.7 2.5 collective-permute-done.5
  65.2 3.4 collective-permute-start.8
  72.8 14.3 %collective-permute-done.11 = bf16[192,1536]{1,0:T(8,128)(2,1)S(1)} collective-permute-done((bf16[192,1536]{1,0:T(8,128)(2,1)S(1)}, bf16[192,1536]{1,0:T(8,128)(2,1)S(1)}, u32[]{:S(2)}, u32[]{:S(2)}) %collective-permute-start.11) | collective-permute-done | bytes 589856 | tf_op jit(solution)/shard_map/ppermute | solution.py:363
  87.1 2.6 collective-permute-done.12.down_other
  89.6 4.1 collective-permute-done.8.own_rows
  93.7 3.5 collective-permute-start.13
  103.8 20.5 %shard_map.189 = (bf16[384,1536]{1,0:T(8,128)(2,1)S(1)}, bf16[384,1536]{1,0:T(8,128)(2,1)S(1)}, bf16[400,1536]{1,0:T(8,128)(2,1)}, bf16[400,1536]{1,0:T(8,128)(2...) custom-call(s32[2]{0:T(128)S(1)} %pad_add_fusion.choice, ...), custom_call_target="tpu_custom_call" | custom-call | flops 1000 | bytes 1000 | tf_op jit(solution)/shard_map/pallas_call | solution.py:629
  129.5 20.8 %shard_map.190 = (bf16[384,1536]{1,0:T(8,128)(2,1)S(1)}, bf16[384,1536]{1,0:T(8,128)(2,1)S(1)}, bf16[400,1536]{1,0:T(8,128)(2,1)}, bf16[400,1536]{1,0:T(8,128)(2...) custom-call(s32[2]{0:T(128)S(1)} %pad_add_fusion.choice, ...), custom_call_target="tpu_custom_call", output_to_operand_aliasing={{4}: (9, {}), {5}: (10, {}), {6}: (11, {}), {7}: (12, {})} | custom-call | flops 1000 | bytes 1000 | tf_op jit(solution)/shard_map/pallas_call | solution.py:629
  151.2 3.3 collective-permute-done.17.own_rows
  160.1 20.4 %shard_map.191 = (bf16[384,1536]{1,0:T(8,128)(2,1)S(1)}, bf16[384,1536]{1,0:T(8,128)(2,1)S(1)}, bf16[400,1536]{1,0:T(8,128)(2,1)}, bf16[400,1536]{1,0:T(8,128)(2...) custom-call(s32[2]{0:T(128)S(1)} %pad_add_fusion.choice, ...), custom_call_target="tpu_custom_call", output_to_operand_aliasing={{4}: (9, {}), {5}: (10, {}), {6}: (11, {}), {7}: (12, {})} | custom-call | flops 1000 | bytes 1000 | tf_op jit(solution)/shard_map/pallas_call | solution.py:629
  188.3 20.8 %shard_map.192 = (bf16[384,1536]{1,0:T(8,128)(2,1)S(1)}, bf16[384,1536]{1,0:T(8,128)(2,1)}, bf16[400,1536]{1,0:T(8,128)(2,1)}, bf16[400,1536]{1,0:T(8,128)(2,1)}...) custom-call(s32[2]{0:T(128)S(1)} %pad_add_fusion.choice, ...), custom_call_target="tpu_custom_call", output_to_operand_aliasing={{4}: (9, {}), {5}: (10, {}), {6}: (11, {}), {7}: (12, {})} | custom-call | flops 1000 | bytes 1000 | tf_op jit(solution)/shard_map/pallas_call | solution.py:629
  209.1 4.8 collective-permute-done.25
  213.9 2.6 add_convert_fusion.4
  216.5 3.6 collective-permute-start.27
  220.1 12.8 %fusion.11 = bf16[1536,768]{1,0:T(8,128)(2,1)} fusion(bf16[3072,1536]{1,0:T(8,128)(2,1)} %get-tuple-element.351, bf16[3072,1536]{1,0:T(8,128)(2,1)} %get-tuple-element.352), kind=kOutput, calls=%fused_computation.14 | convolution fusion | flops 7248936960 | bytes 16515072 | tf_op jit(solution)/shard_map/dot_general | solution.py:483
  232.9 12.8 %fusion.8 = bf16[1536,768]{1,0:T(8,128)(2,1)} fusion(bf16[3072,1536]{1,0:T(8,128)(2,1)} %get-tuple-element.351, bf16[3072,1536]{1,0:T(8,128)(2,1)} %get-tuple-element.352), kind=kOutput, calls=%fused_computation.13 | convolution fusion | flops 7248936960 | bytes 16515072 | tf_op jit(solution)/shard_map/dot_general | solution.py:483
  246.7 3.6 collective-permute-start.31
  250.4 5.0 fusion.20
  256.7 5.0 fusion.17
  261.7 14.1 %collective-permute-done.31.back_ring = bf16[400,1536]{1,0:T(8,128)(2,1)S(1)} collective-permute-done((bf16[400,1536]{1,0:T(8,128)(2,1)S(1)}, bf16[400,1536]{1,0:T(8,128)(2,1)S(1)}, u32[]{:S(2)}, u32[]{:S(2)}) %collective-permute-start.31) | collective-permute-done | bytes 1228832 | tf_op jit(solution)/shard_map/ppermute | solution.py:388
  279.4 3.2 constant_dynamic-slice_fusion.24
  284.1 2.4 collective-permute-start.33
  286.5 8.6 %shard_map.193 = (f32[384,1536]{1,0:T(8,128)}, bf16[384,1536]{1,0:T(8,128)(2,1)}, bf16[384,1536]{1,0:T(8,128)(2,1)}, f32[1,1536]{1,0:T(1,128)}, bf16[8,384]{1,0:T(8,128)(2,1)}) custom-call(bf16[400,1536]{1,0:T(8,128)(2,1)} %get-tuple-element.365.back_own, bf16[400,1536]{1,0:T(8,128)(2,1)} %collective-permute-done.29.back_other, ...), custom_call_target="tpu_custom_call" | custom-call | flops 1000 | bytes 1000 | tf_op jit(solution)/shard_map/pallas_call | solution.py:713
  297.8 10.0 %shard_map.195.refs_1_.grad_ref = bf16[384,2048]{1,0:T(8,128)(2,1)S(1)} custom-call(bf16[384,1536]{1,0:T(8,128)(2,1)S(1)} %copy-done.28, bf16[384,256]{1,0:T(8,128)(2,1)S(1)} %copy-done.38, bf16[384,256]{1,0:T(8,128)(2,1)S(1)} %copy-done.40, bf16[384,1536]{1,0:T(8,128)(2,1)S(1)} %copy-done.33, f32[384,128]{1,0:T(8,128)S(1)} %get-tuple-element.261.cos_ref, ...), custom_call_target="tpu_custom_call" | custom-call | flops 1000 | bytes 1000 | tf_op jit(solution)/shard_map/pallas_call | solution.py:1032
  307.8 5.5 %shard_map.196 = (bf16[768,2048]{1,0:T(8,128)(2,1)}, bf16[768,2048]{1,0:T(8,128)(2,1)S(1)}) custom-call(s32[1]{0:T(128)} %bitcast.10.core_ref, bf16[384,1536]{1,0:T(8,128)(2,1)S(1)} %copy-done.14, bf16[384,2048]{1,0:T(8,128)(2,1)S(1)} %shard_map.195.refs_1_.grad_ref), custom_call_target="tpu_custom_call" | custom-call | flops 1000 | bytes 1000 | tf_op jit(solution)/shard_map/pallas_call | solution.py:822
  315.0 5.1 shard_map.194
  322.1 3.1 add_convert_fusion.12
  328.9 3.1 add_convert_fusion.2
  332.0 7.6 %collective-permute-done.41 = bf16[384,768]{1,0:T(8,128)(2,1)S(1)} collective-permute-done((bf16[384,768]{1,0:T(8,128)(2,1)S(1)}, bf16[384,768]{1,0:T(8,128)(2,1)S(1)}, u32[]{:S(2)}, u32[]{:S(2)}) %collective-permute-start.41) | collective-permute-done | bytes 589856 | tf_op jit(solution)/shard_map/ppermute | solution.py:363
  339.6 11.2 %collective-permute-done.37 = bf16[384,1536]{1,0:T(8,128)(2,1)} collective-permute-done((bf16[384,1536]{1,0:T(8,128)(2,1)}, bf16[384,1536]{1,0:T(8,128)(2,1)}, u32[]{:S(2)}, u32[]{:S(2)}) %collective-permute-start.37) | collective-permute-done | bytes 1179680 | tf_op jit(solution)/shard_map/ppermute | solution.py:388
  350.9 2.4 add_convert_fusion.1
  355.2 5.5 %collective-permute-start.43 = (bf16[192,1664]{1,0:T(8,128)(2,1)}, bf16[192,1664]{1,0:T(8,128)(2,1)}, u32[]{:S(2)}, u32[]{:S(2)}) collective-permute-start(bf16[192,1664]{1,0:T(8,128)(2,1)} %get-tuple-element.549), channel_id=1, source_target_pairs={{0,2},{2,0},{4,6},{6,4},{8,10},{10,8},{12,14},{14,12},{1,3},{3,1},... | collective-permute-start | bytes 1916936 | tf_op jit(solution)/shard_map/ppermute | solution.py:374
  361.8 3.4 collective-permute-start.45
  370.2 3.3 shard_map.197
  376.2 3.3 add_convert_fusion
  379.7 3.9 collective-permute-done.45
  383.6 7.0 %collective-permute-done.42 = bf16[384,1536]{1,0:T(8,128)(2,1)S(1)} collective-permute-done((bf16[384,1536]{1,0:T(8,128)(2,1)S(1)}, bf16[384,1536]{1,0:T(8,128)(2,1)S(1)}, u32[]{:S(2)}, u32[]{:S(2)}) %collective-permute-start.42) | collective-permute-done | bytes 1179680 | tf_op jit(solution)/shard_map/ppermute | solution.py:388
  391.9 3.0 collective-permute-start.48
  394.9 3.5 collective-permute-start.49
  402.9 10.0 %collective-permute-done.47 = bf16[96,1664]{1,0:T(8,128)(2,1)S(1)} collective-permute-done((bf16[96,1664]{1,0:T(8,128)(2,1)S(1)}, bf16[96,1664]{1,0:T(8,128)(2,1)S(1)}, u32[]{:S(2)}, u32[]{:S(2)}) %collective-permute-start.47) | collective-permute-done | bytes 319520 | tf_op jit(solution)/shard_map/ppermute | solution.py:363
  420.0 2.5 collective-permute-done.52
  422.5 6.0 %collective-permute-done.53 = bf16[48,1664]{1,0:T(8,128)(2,1)S(1)} collective-permute-done((bf16[48,1664]{1,0:T(8,128)(2,1)S(1)}, bf16[48,1664]{1,0:T(8,128)(2,1)S(1)}, u32[]{:S(2)}, u32[]{:S(2)}) %collective-permute-start.53) | collective-permute-done | bytes 159776 | tf_op jit(solution)/shard_map/ppermute | solution.py:383
  428.4 3.8 collective-permute-done.54
  439.2 10.7 %collective-permute-done.62 = bf16[192,1536]{1,0:T(8,128)(2,1)S(1)} collective-permute-done((bf16[192,1536]{1,0:T(8,128)(2,1)S(1)}, bf16[192,1536]{1,0:T(8,128)(2,1)S(1)}, u32[]{:S(2)}, u32[]{:S(2)}) %collective-permute-start.62) | collective-permute-done | bytes 589856 | tf_op jit(solution)/shard_map/ppermute | solution.py:363
  451.3 5.6 %collective-permute-done.59 = bf16[48,1664]{1,0:T(8,128)(2,1)S(1)} collective-permute-done((bf16[48,1664]{1,0:T(8,128)(2,1)S(1)}, bf16[48,1664]{1,0:T(8,128)(2,1)S(1)}, u32[]{:S(2)}, u32[]{:S(2)}) %collective-permute-start.59) | collective-permute-done | bytes 159776 | tf_op jit(solution)/shard_map/ppermute | solution.py:383
  463.7 9.6 %collective-permute-done.68 = bf16[192,1536]{1,0:T(8,128)(2,1)S(1)} collective-permute-done((bf16[192,1536]{1,0:T(8,128)(2,1)S(1)}, bf16[192,1536]{1,0:T(8,128)(2,1)S(1)}, u32[]{:S(2)}, u32[]{:S(2)}) %collective-permute-start.68) | collective-permute-done | bytes 589856 | tf_op jit(solution)/shard_map/ppermute | solution.py:363
  474.8 6.4 %collective-permute-done.67 = bf16[48,2048]{1,0:T(8,128)(2,1)S(1)} collective-permute-done((bf16[48,2048]{1,0:T(8,128)(2,1)S(1)}, bf16[48,2048]{1,0:T(8,128)(2,1)S(1)}, u32[]{:S(2)}, u32[]{:S(2)}) %collective-permute-start.67) | collective-permute-done | bytes 196640 | tf_op jit(solution)/shard_map/ppermute | solution.py:383
  485.7 6.5 %collective-permute-done.71 = bf16[48,2048]{1,0:T(8,128)(2,1)S(1)} collective-permute-done((bf16[48,2048]{1,0:T(8,128)(2,1)S(1)}, bf16[48,2048]{1,0:T(8,128)(2,1)S(1)}, u32[]{:S(2)}, u32[]{:S(2)}) %collective-permute-start.71) | collective-permute-done | bytes 196640 | tf_op jit(solution)/shard_map/ppermute | solution.py:383
  495.2 10.0 %collective-permute-done.73 = bf16[48,2048]{1,0:T(8,128)(2,1)} collective-permute-done((bf16[48,2048]{1,0:T(8,128)(2,1)S(1)}, bf16[48,2048]{1,0:T(8,128)(2,1)}, u32[]{:S(2)}, u32[]{:S(2)}) %collective-permute-start.73) | collective-permute-done | bytes 196640 | tf_op jit(solution)/shard_map/ppermute | solution.py:383
  513.0 3.3 collective-permute-done.76
  521.1 2.8 slice.116
  526.6 3.2 bitcast_convert_fusion
  529.8 5.3 collective-permute-done.79.got_1
  537.6 4.7 shard_map.198
  (423 shorter events, 129.8 us)
Async XLA Ops:
  4.6 13.1 %collective-permute-start.1 = (bf16[768,2048]{1,0:T(8,128)(2,1)}, bf16[768,2048]{1,0:T(8,128)(2,1)}, u32[]{:S(2)}, u32[]{:S(2)}) collective-permute-start(bf16[768,2048]{1,0:T(8,128)(2,1)} %weight_ref.1), channel_id=1, source_target_pairs={{0,1},{1,0},{2,3},{3,2},{4,5},{5,4},{6,7},{7,6},{8,9},{9,8},{10,11... | collective-permute-start | bytes 9437192 | tf_op jit(solution)/shard_map/ppermute | solution.py:359
  4.7 21.3 %collective-permute-start.2 = (bf16[192,1536]{1,0:T(8,128)(2,1)S(1)}, bf16[192,1536]{1,0:T(8,128)(2,1)S(1)}, u32[]{:S(2)}, u32[]{:S(2)}) collective-permute-start(bf16[192,1536]{1,0:T(8,128)(2,1)S(1)} %constant_dynamic-slice_fusion.34), channel_id=1, source_target_pairs={{0,16},{16,0},{1,17},{17,1},{2,18},{18,2},{3,19},{19,3},{4,20},{20... | collective-permute-start | bytes 1769480 | tf_op jit(solution)/shard_map/ppermute | solution.py:363
  6.2 29.5 %collective-permute-start = (bf16[400,1536]{1,0:T(8,128)(2,1)}, bf16[400,1536]{1,0:T(8,128)(2,1)}, u32[]{:S(2)}, u32[]{:S(2)}) collective-permute-start(bf16[400,1536]{1,0:T(8,128)(2,1)} %pad_maximum_fusion.1), channel_id=1, source_target_pairs={{0,4},{2,6},{4,12},{6,14},{8,0},{10,2},{12,8},{14,10},{1,5},{3,7},... | collective-permute-start | bytes 3686408 | tf_op jit(solution)/shard_map/ppermute | solution.py:388
  9.0 56.3 %collective-permute-start.7 = (bf16[1536,1536]{1,0:T(8,128)(2,1)}, bf16[1536,1536]{1,0:T(8,128)(2,1)}, u32[]{:S(2)}, u32[]{:S(2)}) collective-permute-start(bf16[1536,1536]{1,0:T(8,128)(2,1)} %bitcast.60), channel_id=1, source_target_pairs={{0,2},{3,1},{4,6},{7,5},{8,10},{11,9},{12,14},{15,13},{16,18},{19,... | collective-permute-start | bytes 14155784 | tf_op jit(solution)/shard_map/ppermute | solution.py:398
  17.0 18.7 %collective-permute-start.4 = (bf16[768,1536]{1,0:T(8,128)(2,1)}, bf16[768,1536]{1,0:T(8,128)(2,1)}, u32[]{:S(2)}, u32[]{:S(2)}) collective-permute-start(bf16[768,1536]{1,0:T(8,128)(2,1)} %param.20), channel_id=1, source_target_pairs={{0,1},{1,0},{2,3},{3,2},{4,5},{5,4},{6,7},{7,6},{8,9},{9,8},{10,11... | collective-permute-start | bytes 7077896 | tf_op jit(solution)/shard_map/ppermute | solution.py:359
  35.8 29.5 %collective-permute-start.5 = (bf16[400,1536]{1,0:T(8,128)(2,1)}, bf16[400,1536]{1,0:T(8,128)(2,1)}, u32[]{:S(2)}, u32[]{:S(2)}) collective-permute-start(bf16[400,1536]{1,0:T(8,128)(2,1)} %collective-permute-done), channel_id=1, source_target_pairs={{0,4},{2,6},{4,12},{6,14},{8,0},{10,2},{12,8},{14,10},{1,5},{3,7},... | collective-permute-start | bytes 3686408 | tf_op jit(solution)/shard_map/ppermute | solution.py:388
  41.2 21.5 %collective-permute-start.6 = (bf16[192,1536]{1,0:T(8,128)(2,1)S(1)}, bf16[192,1536]{1,0:T(8,128)(2,1)S(1)}, u32[]{:S(2)}, u32[]{:S(2)}) collective-permute-start(bf16[192,1536]{1,0:T(8,128)(2,1)S(1)} %get-tuple-element.557), channel_id=1, source_target_pairs={{0,16},{16,0},{1,17},{17,1},{2,18},{18,2},{3,19},{19,3},{4,20},{20... | collective-permute-start | bytes 1769480 | tf_op jit(solution)/shard_map/ppermute | solution.py:363
  41.8 47.8 %collective-permute-start.12 = (bf16[768,1536]{1,0:T(8,128)(2,1)}, bf16[768,1536]{1,0:T(8,128)(2,1)S(1)}, u32[]{:S(2)}, u32[]{:S(2)}) collective-permute-start(bf16[768,1536]{1,0:T(8,128)(2,1)} %bitcast.67), channel_id=1, source_target_pairs={{0,2},{3,1},{4,6},{7,5},{8,10},{11,9},{12,14},{15,13},{16,18},{19,... | collective-permute-start | bytes 7077896 | tf_op jit(solution)/shard_map/ppermute | solution.py:398
  65.2 28.5 %collective-permute-start.8 = (bf16[400,1536]{1,0:T(8,128)(2,1)S(1)}, bf16[400,1536]{1,0:T(8,128)(2,1)}, u32[]{:S(2)}, u32[]{:S(2)}) collective-permute-start(bf16[400,1536]{1,0:T(8,128)(2,1)S(1)} %get-tuple-element.282.own_rows.refs_1_), channel_id=1, source_target_pairs={{0,4},{2,6},{4,12},{6,14},{8,0},{10,2},{12,8},{14,10},{1,5},{3,7},... | collective-permute-start | bytes 3686408 | tf_op jit(solution)/shard_map/ppermute | solution.py:388
  68.6 25.1 %collective-permute-start.9 = (bf16[400,1536]{1,0:T(8,128)(2,1)S(1)}, bf16[400,1536]{1,0:T(8,128)(2,1)S(1)}, u32[]{:S(2)}, u32[]{:S(2)}) collective-permute-start(bf16[400,1536]{1,0:T(8,128)(2,1)S(1)} %get-tuple-element.282.own_rows.refs_1_), channel_id=1, source_target_pairs={{0,1},{1,0},{2,3},{3,2},{4,5},{5,4},{6,7},{7,6},{8,9},{9,8},{10,11... | collective-permute-start | bytes 3686408 | tf_op jit(solution)/shard_map/ppermute | solution.py:359
  69.5 20.1 %collective-permute-start.10 = (bf16[384,1536]{1,0:T(8,128)(2,1)S(1)}, bf16[384,1536]{1,0:T(8,128)(2,1)S(1)}, u32[]{:S(2)}, u32[]{:S(2)}) collective-permute-start(bf16[384,1536]{1,0:T(8,128)(2,1)S(1)} %convolution_convert_fusion.5.own_ct.ct_ref), channel_id=1, source_target_pairs={{0,1},{1,0},{2,3},{3,2},{4,5},{5,4},{6,7},{7,6},{8,9},{9,8},{10,11... | collective-permute-start | bytes 3538952 | tf_op jit(solution)/shard_map/ppermute | solution.py:359
  71.4 15.7 %collective-permute-start.11 = (bf16[192,1536]{1,0:T(8,128)(2,1)S(1)}, bf16[192,1536]{1,0:T(8,128)(2,1)S(1)}, u32[]{:S(2)}, u32[]{:S(2)}) collective-permute-start(bf16[192,1536]{1,0:T(8,128)(2,1)S(1)} %get-tuple-element.555), channel_id=1, source_target_pairs={{0,16},{16,0},{1,17},{17,1},{2,18},{18,2},{3,19},{19,3},{4,20},{20... | collective-permute-start | bytes 1769480 | tf_op jit(solution)/shard_map/ppermute | solution.py:363
  93.7 31.5 %collective-permute-start.13 = (bf16[400,1536]{1,0:T(8,128)(2,1)}, bf16[400,1536]{1,0:T(8,128)(2,1)}, u32[]{:S(2)}, u32[]{:S(2)}) collective-permute-start(bf16[400,1536]{1,0:T(8,128)(2,1)} %collective-permute-done.5), channel_id=1, source_target_pairs={{0,4},{2,6},{4,12},{6,14},{8,0},{10,2},{12,8},{14,10},{1,5},{3,7},... | collective-permute-start | bytes 3686408 | tf_op jit(solution)/shard_map/ppermute | solution.py:388
  97.2 28.1 %collective-permute-start.15 = (bf16[400,1536]{1,0:T(8,128)(2,1)}, bf16[400,1536]{1,0:T(8,128)(2,1)}, u32[]{:S(2)}, u32[]{:S(2)}) collective-permute-start(bf16[400,1536]{1,0:T(8,128)(2,1)} %collective-permute-done.8.own_rows), channel_id=1, source_target_pairs={{0,1},{1,0},{2,3},{3,2},{4,5},{5,4},{6,7},{7,6},{8,9},{9,8},{10,11... | collective-permute-start | bytes 3686408 | tf_op jit(solution)/shard_map/ppermute | solution.py:359
  99.1 26.2 %collective-permute-start.14 = (bf16[384,1536]{1,0:T(8,128)(2,1)}, bf16[384,1536]{1,0:T(8,128)(2,1)}, u32[]{:S(2)}, u32[]{:S(2)}) collective-permute-start(bf16[384,1536]{1,0:T(8,128)(2,1)} %convolution_convert_fusion.4.own_ct), channel_id=1, source_target_pairs={{0,1},{1,0},{2,3},{3,2},{4,5},{5,4},{6,7},{7,6},{8,9},{9,8},{10,11... | collective-permute-start | bytes 3538952 | tf_op jit(solution)/shard_map/ppermute | solution.py:359
  101.9 23.3 %collective-permute-start.16 = (bf16[192,1536]{1,0:T(8,128)(2,1)}, bf16[192,1536]{1,0:T(8,128)(2,1)S(1)}, u32[]{:S(2)}, u32[]{:S(2)}) collective-permute-start(bf16[192,1536]{1,0:T(8,128)(2,1)} %get-tuple-element.553), channel_id=1, source_target_pairs={{0,16},{16,0},{1,17},{17,1},{2,18},{18,2},{3,19},{19,3},{4,20},{20... | collective-permute-start | bytes 1769480 | tf_op jit(solution)/shard_map/ppermute | solution.py:363
  125.3 29.1 %collective-permute-start.17 = (bf16[400,1536]{1,0:T(8,128)(2,1)}, bf16[400,1536]{1,0:T(8,128)(2,1)S(1)}, u32[]{:S(2)}, u32[]{:S(2)}) collective-permute-start(bf16[400,1536]{1,0:T(8,128)(2,1)} %collective-permute-done.8.own_rows), channel_id=1, source_target_pairs={{0,4},{2,6},{4,12},{6,14},{8,0},{10,2},{12,8},{14,10},{1,5},{3,7},... | collective-permute-start | bytes 3686408 | tf_op jit(solution)/shard_map/ppermute | solution.py:388
  126.5 24.7 %collective-permute-start.19 = (bf16[384,1536]{1,0:T(8,128)(2,1)S(1)}, bf16[384,1536]{1,0:T(8,128)(2,1)S(1)}, u32[]{:S(2)}, u32[]{:S(2)}) collective-permute-start(bf16[384,1536]{1,0:T(8,128)(2,1)S(1)} %convolution_convert_fusion.3.own_ct), channel_id=1, source_target_pairs={{0,1},{1,0},{2,3},{3,2},{4,5},{5,4},{6,7},{7,6},{8,9},{9,8},{10,11... | collective-permute-start | bytes 3538952 | tf_op jit(solution)/shard_map/ppermute | solution.py:359
  127.9 23.2 %collective-permute-start.18 = (bf16[192,1536]{1,0:T(8,128)(2,1)S(1)}, bf16[192,1536]{1,0:T(8,128)(2,1)S(1)}, u32[]{:S(2)}, u32[]{:S(2)}) collective-permute-start(bf16[192,1536]{1,0:T(8,128)(2,1)S(1)} %get-tuple-element.551), channel_id=1, source_target_pairs={{0,16},{16,0},{1,17},{17,1},{2,18},{18,2},{3,19},{19,3},{4,20},{20... | collective-permute-start | bytes 1769480 | tf_op jit(solution)/shard_map/ppermute | solution.py:363
  154.4 26.1 %collective-permute-start.21 = (bf16[400,1536]{1,0:T(8,128)(2,1)}, bf16[400,1536]{1,0:T(8,128)(2,1)}, u32[]{:S(2)}, u32[]{:S(2)}) collective-permute-start(bf16[400,1536]{1,0:T(8,128)(2,1)} %get-tuple-element.312), channel_id=1, source_target_pairs={{0,1},{1,0},{2,3},{3,2},{4,5},{5,4},{6,7},{7,6},{8,9},{9,8},{10,11... | collective-permute-start | bytes 3686408 | tf_op jit(solution)/shard_map/ppermute | solution.py:359
  155.0 29.2 %collective-permute-start.20 = (bf16[400,1536]{1,0:T(8,128)(2,1)S(1)}, bf16[400,1536]{1,0:T(8,128)(2,1)S(1)}, u32[]{:S(2)}, u32[]{:S(2)}) collective-permute-start(bf16[400,1536]{1,0:T(8,128)(2,1)S(1)} %collective-permute-done.17.own_rows), channel_id=1, source_target_pairs={{0,4},{2,6},{4,12},{6,14},{8,0},{10,2},{12,8},{14,10},{1,5},{3,7},... | collective-permute-start | bytes 3686408 | tf_op jit(solution)/shard_map/ppermute | solution.py:388
  157.2 25.7 %collective-permute-start.22 = (bf16[384,1536]{1,0:T(8,128)(2,1)S(1)}, bf16[384,1536]{1,0:T(8,128)(2,1)S(1)}, u32[]{:S(2)}, u32[]{:S(2)}) collective-permute-start(bf16[384,1536]{1,0:T(8,128)(2,1)S(1)} %convolution_convert_fusion.2.own_ct), channel_id=1, source_target_pairs={{0,1},{1,0},{2,3},{3,2},{4,5},{5,4},{6,7},{7,6},{8,9},{9,8},{10,11... | collective-permute-start | bytes 3538952 | tf_op jit(solution)/shard_map/ppermute | solution.py:359
  184.1 29.8 %collective-permute-start.25 = (bf16[400,1536]{1,0:T(8,128)(2,1)S(1)}, bf16[400,1536]{1,0:T(8,128)(2,1)}, u32[]{:S(2)}, u32[]{:S(2)}) collective-permute-start(bf16[400,1536]{1,0:T(8,128)(2,1)S(1)} %add_convert_fusion.5), channel_id=1, source_target_pairs={{0,4},{2,6},{4,12},{6,14},{8,0},{10,2},{12,8},{14,10},{1,5},{3,7},... | collective-permute-start | bytes 3686408 | tf_op jit(solution)/shard_map/ppermute | solution.py:388
  186.5 27.5 %collective-permute-start.26 = (bf16[400,1536]{1,0:T(8,128)(2,1)}, bf16[400,1536]{1,0:T(8,128)(2,1)}, u32[]{:S(2)}, u32[]{:S(2)}) collective-permute-start(bf16[400,1536]{1,0:T(8,128)(2,1)} %get-tuple-element.337), channel_id=1, source_target_pairs={{0,1},{1,0},{2,3},{3,2},{4,5},{5,4},{6,7},{7,6},{8,9},{9,8},{10,11... | collective-permute-start | bytes 3686408 | tf_op jit(solution)/shard_map/ppermute | solution.py:359
  186.7 59.0 %collective-permute-start.29 = (bf16[400,1536]{1,0:T(8,128)(2,1)}, bf16[400,1536]{1,0:T(8,128)(2,1)}, u32[]{:S(2)}, u32[]{:S(2)}) collective-permute-start(bf16[400,1536]{1,0:T(8,128)(2,1)} %get-tuple-element.349), channel_id=1, source_target_pairs={{0,1},{1,0},{2,3},{3,2},{4,5},{5,4},{6,7},{7,6},{8,9},{9,8},{10,11... | collective-permute-start | bytes 3686408 | tf_op jit(solution)/shard_map/ppermute | solution.py:359
  187.0 58.7 %collective-permute-start.30 = (bf16[384,1536]{1,0:T(8,128)(2,1)S(1)}, bf16[384,1536]{1,0:T(8,128)(2,1)S(1)}, u32[]{:S(2)}, u32[]{:S(2)}) collective-permute-start(bf16[384,1536]{1,0:T(8,128)(2,1)S(1)} %get-tuple-element.350), channel_id=1, source_target_pairs={{0,1},{1,0},{2,3},{3,2},{4,5},{5,4},{6,7},{7,6},{8,9},{9,8},{10,11... | collective-permute-start | bytes 3538952 | tf_op jit(solution)/shard_map/ppermute | solution.py:359
  187.2 74.5 %collective-permute-start.32 = (bf16[384,1536]{1,0:T(8,128)(2,1)S(1)}, bf16[384,1536]{1,0:T(8,128)(2,1)}, u32[]{:S(2)}, u32[]{:S(2)}) collective-permute-start(bf16[384,1536]{1,0:T(8,128)(2,1)S(1)} %get-tuple-element.362), channel_id=1, source_target_pairs={{0,1},{1,0},{2,3},{3,2},{4,5},{5,4},{6,7},{7,6},{8,9},{9,8},{10,11... | collective-permute-start | bytes 3538952 | tf_op jit(solution)/shard_map/ppermute | solution.py:359
  216.5 29.7 %collective-permute-start.27 = (bf16[400,1536]{1,0:T(8,128)(2,1)S(1)}, bf16[400,1536]{1,0:T(8,128)(2,1)S(1)}, u32[]{:S(2)}, u32[]{:S(2)}) collective-permute-start(bf16[400,1536]{1,0:T(8,128)(2,1)S(1)} %add_convert_fusion.4), channel_id=1, source_target_pairs={{0,4},{2,6},{4,12},{6,14},{8,0},{10,2},{12,8},{14,10},{1,5},{3,7},... | collective-permute-start | bytes 3686408 | tf_op jit(solution)/shard_map/ppermute | solution.py:388
  220.1 26.2 %collective-permute-start.28 = (bf16[400,1536]{1,0:T(8,128)(2,1)S(1)}, bf16[400,1536]{1,0:T(8,128)(2,1)S(1)}, u32[]{:S(2)}, u32[]{:S(2)}) collective-permute-start(bf16[400,1536]{1,0:T(8,128)(2,1)S(1)} %copy-done.82), channel_id=1, source_target_pairs={{0,1},{1,0},{2,3},{3,2},{4,5},{5,4},{6,7},{7,6},{8,9},{9,8},{10,11... | collective-permute-start | bytes 3686408 | tf_op jit(solution)/shard_map/ppermute | solution.py:359
  246.7 29.1 %collective-permute-start.31 = (bf16[400,1536]{1,0:T(8,128)(2,1)S(1)}, bf16[400,1536]{1,0:T(8,128)(2,1)S(1)}, u32[]{:S(2)}, u32[]{:S(2)}) collective-permute-start(bf16[400,1536]{1,0:T(8,128)(2,1)S(1)} %add_convert_fusion.3), channel_id=1, source_target_pairs={{0,4},{2,6},{4,12},{6,14},{8,0},{10,2},{12,8},{14,10},{1,5},{3,7},... | collective-permute-start | bytes 3686408 | tf_op jit(solution)/shard_map/ppermute | solution.py:388
  275.8 44.4 %collective-permute-start.35 = (bf16[1536,768]{1,0:T(8,128)(2,1)}, bf16[1536,768]{1,0:T(8,128)(2,1)}, u32[]{:S(2)}, u32[]{:S(2)}) collective-permute-start(bf16[1536,768]{1,0:T(8,128)(2,1)} %fusion.8), channel_id=1, source_target_pairs={{1,3},{2,0},{5,7},{6,4},{9,11},{10,8},{13,15},{14,12},{17,19},{18,... | collective-permute-start | bytes 7077896 | tf_op jit(solution)/shard_map/ppermute | solution.py:393
  277.1 43.1 %collective-permute-start.34 = (bf16[384,1536]{1,0:T(8,128)(2,1)}, bf16[384,1536]{1,0:T(8,128)(2,1)}, u32[]{:S(2)}, u32[]{:S(2)}) collective-permute-start(bf16[384,1536]{1,0:T(8,128)(2,1)} %get-tuple-element.364), channel_id=1, source_target_pairs={{0,1},{1,0},{2,3},{3,2},{4,5},{5,4},{6,7},{7,6},{8,9},{9,8},{10,11... | collective-permute-start | bytes 3538952 | tf_op jit(solution)/shard_map/ppermute | solution.py:359
  282.6 37.6 %collective-permute-start.36 = (bf16[768,768]{1,0:T(8,128)(2,1)}, bf16[768,768]{1,0:T(8,128)(2,1)}, u32[]{:S(2)}, u32[]{:S(2)}) collective-permute-start(bf16[768,768]{1,0:T(8,128)(2,1)} %get-tuple-element.541), channel_id=1, source_target_pairs={{0,16},{16,0},{1,17},{17,1},{2,18},{18,2},{3,19},{19,3},{4,20},{20... | collective-permute-start | bytes 3538952 | tf_op jit(solution)/shard_map/ppermute | solution.py:363
  284.1 36.1 %collective-permute-start.33 = (bf16[384,1536]{1,0:T(8,128)(2,1)}, bf16[384,1536]{1,0:T(8,128)(2,1)}, u32[]{:S(2)}, u32[]{:S(2)}) collective-permute-start(bf16[384,1536]{1,0:T(8,128)(2,1)} %add_convert_fusion.13), channel_id=1, source_target_pairs={{0,4},{2,6},{4,12},{6,14},{8,0},{10,2},{12,8},{14,10},{1,5},{3,7},... | collective-permute-start | bytes 3538952 | tf_op jit(solution)/shard_map/ppermute | solution.py:388
  320.2 30.6 %collective-permute-start.39 = (bf16[768,2048]{1,0:T(8,128)(2,1)}, bf16[768,2048]{1,0:T(8,128)(2,1)}, u32[]{:S(2)}, u32[]{:S(2)}) collective-permute-start(bf16[768,2048]{1,0:T(8,128)(2,1)} %get-tuple-element.391), channel_id=1, source_target_pairs={{0,1},{1,0},{2,3},{3,2},{4,5},{5,4},{6,7},{7,6},{8,9},{9,8},{10,11... | collective-permute-start | bytes 9437192 | tf_op jit(solution)/shard_map/ppermute | solution.py:359
  320.3 30.5 %collective-permute-start.38 = (bf16[768,1664]{1,0:T(8,128)(2,1)}, bf16[768,1664]{1,0:T(8,128)(2,1)}, u32[]{:S(2)}, u32[]{:S(2)}) collective-permute-start(bf16[768,1664]{1,0:T(8,128)(2,1)} %get-tuple-element.389), channel_id=1, source_target_pairs={{0,1},{1,0},{2,3},{3,2},{4,5},{5,4},{6,7},{7,6},{8,9},{9,8},{10,11... | collective-permute-start | bytes 7667720 | tf_op jit(solution)/shard_map/ppermute | solution.py:359
  320.8 18.8 %collective-permute-start.40 = (bf16[768,768]{1,0:T(8,128)(2,1)}, bf16[768,768]{1,0:T(8,128)(2,1)}, u32[]{:S(2)}, u32[]{:S(2)}) collective-permute-start(bf16[768,768]{1,0:T(8,128)(2,1)} %fusion.17), channel_id=1, source_target_pairs={{1,3},{2,0},{5,7},{6,4},{9,11},{10,8},{13,15},{14,12},{17,19},{18,... | collective-permute-start | bytes 3538952 | tf_op jit(solution)/shard_map/ppermute | solution.py:393
  325.2 25.7 %collective-permute-start.37 = (bf16[384,1536]{1,0:T(8,128)(2,1)}, bf16[384,1536]{1,0:T(8,128)(2,1)}, u32[]{:S(2)}, u32[]{:S(2)}) collective-permute-start(bf16[384,1536]{1,0:T(8,128)(2,1)} %add_convert_fusion.12), channel_id=1, source_target_pairs={{0,4},{2,6},{4,12},{6,14},{8,0},{10,2},{12,8},{14,10},{1,5},{3,7},... | collective-permute-start | bytes 3538952 | tf_op jit(solution)/shard_map/ppermute | solution.py:388
  353.6 26.0 %collective-permute-start.44 = (bf16[192,1664]{1,0:T(8,128)(2,1)S(1)}, bf16[192,1664]{1,0:T(8,128)(2,1)}, u32[]{:S(2)}, u32[]{:S(2)}) collective-permute-start(bf16[192,1664]{1,0:T(8,128)(2,1)S(1)} %get-tuple-element.547), channel_id=1, source_target_pairs={{0,16},{16,0},{1,17},{17,1},{2,18},{18,2},{3,19},{19,3},{4,20},{20... | collective-permute-start | bytes 1916936 | tf_op jit(solution)/shard_map/ppermute | solution.py:363
  355.2 24.5 %collective-permute-start.43 = (bf16[192,1664]{1,0:T(8,128)(2,1)}, bf16[192,1664]{1,0:T(8,128)(2,1)}, u32[]{:S(2)}, u32[]{:S(2)}) collective-permute-start(bf16[192,1664]{1,0:T(8,128)(2,1)} %get-tuple-element.549), channel_id=1, source_target_pairs={{0,2},{2,0},{4,6},{6,4},{8,10},{10,8},{12,14},{14,12},{1,3},{3,1},... | collective-permute-start | bytes 1916936 | tf_op jit(solution)/shard_map/ppermute | solution.py:374
  361.8 21.8 %collective-permute-start.45 = (bf16[768,768]{1,0:T(8,128)(2,1)}, bf16[768,768]{1,0:T(8,128)(2,1)S(1)}, u32[]{:S(2)}, u32[]{:S(2)}) collective-permute-start(bf16[768,768]{1,0:T(8,128)(2,1)} %get-tuple-element.539), channel_id=1, source_target_pairs={{0,16},{3,19},{4,20},{7,23},{8,24},{11,27},{12,28},{15,31},{16,0},... | collective-permute-start | bytes 3538952 | tf_op jit(solution)/shard_map/ppermute | solution.py:370
  367.5 23.1 %collective-permute-start.42 = (bf16[384,1536]{1,0:T(8,128)(2,1)S(1)}, bf16[384,1536]{1,0:T(8,128)(2,1)S(1)}, u32[]{:S(2)}, u32[]{:S(2)}) collective-permute-start(bf16[384,1536]{1,0:T(8,128)(2,1)S(1)} %add_convert_fusion.10), channel_id=1, source_target_pairs={{0,4},{2,6},{4,12},{6,14},{8,0},{10,2},{12,8},{14,10},{1,5},{3,7},... | collective-permute-start | bytes 3538952 | tf_op jit(solution)/shard_map/ppermute | solution.py:388
  368.9 21.7 %collective-permute-start.46 = (bf16[768,768]{1,0:T(8,128)(2,1)S(1)}, bf16[768,768]{1,0:T(8,128)(2,1)S(1)}, u32[]{:S(2)}, u32[]{:S(2)}) collective-permute-start(bf16[768,768]{1,0:T(8,128)(2,1)S(1)} %add_convert_fusion.11), channel_id=1, source_target_pairs={{1,3},{2,0},{5,7},{6,4},{9,11},{10,8},{13,15},{14,12},{17,19},{18,... | collective-permute-start | bytes 3538952 | tf_op jit(solution)/shard_map/ppermute | solution.py:393
  379.6 22.8 %collective-permute-start.51 = (bf16[384,1536]{1,0:T(8,128)(2,1)S(1)}, bf16[384,1536]{1,0:T(8,128)(2,1)S(1)}, u32[]{:S(2)}, u32[]{:S(2)}) collective-permute-start(bf16[384,1536]{1,0:T(8,128)(2,1)S(1)} %copy-done.50), channel_id=1, source_target_pairs={{0,1},{1,0},{2,3},{3,2},{4,5},{5,4},{6,7},{7,6},{8,9},{9,8},{10,11... | collective-permute-start | bytes 3538952 | tf_op jit(solution)/shard_map/ppermute | solution.py:359
  394.9 17.9 %collective-permute-start.49 = (bf16[384,768]{1,0:T(8,128)(2,1)S(1)}, bf16[384,768]{1,0:T(8,128)(2,1)S(1)}, u32[]{:S(2)}, u32[]{:S(2)}) collective-permute-start(bf16[384,768]{1,0:T(8,128)(2,1)S(1)} %get-tuple-element.563), channel_id=1, source_target_pairs={{0,16},{3,19},{4,20},{7,23},{8,24},{11,27},{12,28},{15,31},{16,0},... | collective-permute-start | bytes 1769480 | tf_op jit(solution)/shard_map/ppermute | solution.py:370
  399.8 13.1 %collective-permute-start.47 = (bf16[96,1664]{1,0:T(8,128)(2,1)S(1)}, bf16[96,1664]{1,0:T(8,128)(2,1)S(1)}, u32[]{:S(2)}, u32[]{:S(2)}) collective-permute-start(bf16[96,1664]{1,0:T(8,128)(2,1)S(1)} %get-tuple-element.589), channel_id=1, source_target_pairs={{0,16},{16,0},{1,17},{17,1},{2,18},{18,2},{3,19},{19,3},{4,20},{20... | collective-permute-start | bytes 958472 | tf_op jit(solution)/shard_map/ppermute | solution.py:363
  413.4 18.9 %collective-permute-start.55 = (bf16[192,2048]{1,0:T(8,128)(2,1)S(1)}, bf16[192,2048]{1,0:T(8,128)(2,1)S(1)}, u32[]{:S(2)}, u32[]{:S(2)}) collective-permute-start(bf16[192,2048]{1,0:T(8,128)(2,1)S(1)} %get-tuple-element.545), channel_id=1, source_target_pairs={{0,2},{2,0},{4,6},{6,4},{8,10},{10,8},{12,14},{14,12},{1,3},{3,1},... | collective-permute-start | bytes 2359304 | tf_op jit(solution)/shard_map/ppermute | solution.py:374
  413.6 19.1 %collective-permute-start.56 = (bf16[192,2048]{1,0:T(8,128)(2,1)S(1)}, bf16[192,2048]{1,0:T(8,128)(2,1)S(1)}, u32[]{:S(2)}, u32[]{:S(2)}) collective-permute-start(bf16[192,2048]{1,0:T(8,128)(2,1)S(1)} %get-tuple-element.543), channel_id=1, source_target_pairs={{0,16},{16,0},{1,17},{17,1},{2,18},{18,2},{3,19},{19,3},{4,20},{20... | collective-permute-start | bytes 2359304 | tf_op jit(solution)/shard_map/ppermute | solution.py:363
  417.1 15.1 %collective-permute-start.54 = (bf16[48,1664]{1,0:T(8,128)(2,1)S(1)}, bf16[48,1664]{1,0:T(8,128)(2,1)S(1)}, u32[]{:S(2)}, u32[]{:S(2)}) collective-permute-start(bf16[48,1664]{1,0:T(8,128)(2,1)S(1)} %get-tuple-element.583), channel_id=1, source_target_pairs={{0,12},{2,14},{4,8},{6,10},{8,4},{10,6},{12,0},{14,2},{1,13},{3,15... | collective-permute-start | bytes 479240 | tf_op jit(solution)/shard_map/ppermute | solution.py:383
  433.6 16.3 %collective-permute-start.62 = (bf16[192,1536]{1,0:T(8,128)(2,1)S(1)}, bf16[192,1536]{1,0:T(8,128)(2,1)S(1)}, u32[]{:S(2)}, u32[]{:S(2)}) collective-permute-start(bf16[192,1536]{1,0:T(8,128)(2,1)S(1)} %get-tuple-element.562), channel_id=1, source_target_pairs={{0,16},{16,0},{1,17},{17,1},{2,18},{18,2},{3,19},{19,3},{4,20},{20... | collective-permute-start | bytes 1769480 | tf_op jit(solution)/shard_map/ppermute | solution.py:363
  435.0 21.9 %collective-permute-start.61 = (bf16[96,2048]{1,0:T(8,128)(2,1)S(1)}, bf16[96,2048]{1,0:T(8,128)(2,1)S(1)}, u32[]{:S(2)}, u32[]{:S(2)}) collective-permute-start(bf16[96,2048]{1,0:T(8,128)(2,1)S(1)} %get-tuple-element.575), channel_id=1, source_target_pairs={{0,2},{2,0},{4,6},{6,4},{8,10},{10,8},{12,14},{14,12},{1,3},{3,1},... | collective-permute-start | bytes 1179656 | tf_op jit(solution)/shard_map/ppermute | solution.py:374
  435.7 21.1 %collective-permute-start.60 = (bf16[96,2048]{1,0:T(8,128)(2,1)S(1)}, bf16[96,2048]{1,0:T(8,128)(2,1)S(1)}, u32[]{:S(2)}, u32[]{:S(2)}) collective-permute-start(bf16[96,2048]{1,0:T(8,128)(2,1)S(1)} %get-tuple-element.577), channel_id=1, source_target_pairs={{0,16},{16,0},{1,17},{17,1},{2,18},{18,2},{3,19},{19,3},{4,20},{20... | collective-permute-start | bytes 1179656 | tf_op jit(solution)/shard_map/ppermute | solution.py:363
  436.9 14.4 %collective-permute-start.57 = (bf16[48,1664]{1,0:T(8,128)(2,1)S(1)}, bf16[48,1664]{1,0:T(8,128)(2,1)S(1)}, u32[]{:S(2)}, u32[]{:S(2)}) collective-permute-start(bf16[48,1664]{1,0:T(8,128)(2,1)S(1)} %add_convert_fusion.26), channel_id=1, source_target_pairs={{0,4},{2,6},{4,0},{6,2},{8,12},{10,14},{12,8},{14,10},{1,5},{3,7},... | collective-permute-start | bytes 479240 | tf_op jit(solution)/shard_map/ppermute | solution.py:383
  437.6 13.7 %collective-permute-start.58 = (bf16[48,1664]{1,0:T(8,128)(2,1)S(1)}, bf16[48,1664]{1,0:T(8,128)(2,1)S(1)}, u32[]{:S(2)}, u32[]{:S(2)}) collective-permute-start(bf16[48,1664]{1,0:T(8,128)(2,1)S(1)} %add_convert_fusion.26), channel_id=1, source_target_pairs={{0,8},{2,10},{4,12},{6,14},{8,0},{10,2},{12,4},{14,6},{1,9},{3,11}... | collective-permute-start | bytes 479240 | tf_op jit(solution)/shard_map/ppermute | solution.py:383
  457.8 15.6 %collective-permute-start.68 = (bf16[192,1536]{1,0:T(8,128)(2,1)S(1)}, bf16[192,1536]{1,0:T(8,128)(2,1)S(1)}, u32[]{:S(2)}, u32[]{:S(2)}) collective-permute-start(bf16[192,1536]{1,0:T(8,128)(2,1)S(1)} %get-tuple-element.560), channel_id=1, source_target_pairs={{0,16},{16,0},{1,17},{17,1},{2,18},{18,2},{3,19},{19,3},{4,20},{20... | collective-permute-start | bytes 1769480 | tf_op jit(solution)/shard_map/ppermute | solution.py:363
  459.1 22.1 %collective-permute-start.64 = (bf16[96,1664]{1,0:T(8,128)(2,1)S(1)}, bf16[96,1664]{1,0:T(8,128)(2,1)S(1)}, u32[]{:S(2)}, u32[]{:S(2)}) collective-permute-start(bf16[96,1664]{1,0:T(8,128)(2,1)S(1)} %pad_maximum_fusion.8), channel_id=1, source_target_pairs={{0,2},{2,0},{4,6},{6,4},{8,10},{10,8},{12,14},{14,12},{1,3},{3,1},... | collective-permute-start | bytes 958472 | tf_op jit(solution)/shard_map/ppermute | solution.py:374
  459.5 21.7 %collective-permute-start.63 = (bf16[96,1664]{1,0:T(8,128)(2,1)S(1)}, bf16[96,1664]{1,0:T(8,128)(2,1)S(1)}, u32[]{:S(2)}, u32[]{:S(2)}) collective-permute-start(bf16[96,1664]{1,0:T(8,128)(2,1)S(1)} %pad_maximum_fusion.7), channel_id=1, source_target_pairs={{0,16},{16,0},{1,17},{17,1},{2,18},{18,2},{3,19},{19,3},{4,20},{20... | collective-permute-start | bytes 958472 | tf_op jit(solution)/shard_map/ppermute | solution.py:363
  461.4 13.4 %collective-permute-start.65 = (bf16[48,2048]{1,0:T(8,128)(2,1)S(1)}, bf16[48,2048]{1,0:T(8,128)(2,1)S(1)}, u32[]{:S(2)}, u32[]{:S(2)}) collective-permute-start(bf16[48,2048]{1,0:T(8,128)(2,1)S(1)} %get-tuple-element.573), channel_id=1, source_target_pairs={{0,4},{2,6},{4,0},{6,2},{8,12},{10,14},{12,8},{14,10},{1,5},{3,7},... | collective-permute-start | bytes 589832 | tf_op jit(solution)/shard_map/ppermute | solution.py:383
  482.3 22.9 %collective-permute-start.74 = (bf16[384,1536]{1,0:T(8,128)(2,1)}, bf16[384,1536]{1,0:T(8,128)(2,1)}, u32[]{:S(2)}, u32[]{:S(2)}) collective-permute-start(bf16[384,1536]{1,0:T(8,128)(2,1)} %constant_dynamic-slice_fusion.1), channel_id=1, source_target_pairs={{0,1},{1,0},{2,3},{3,2},{4,5},{5,4},{6,7},{7,6},{8,9},{9,8},{10,11... | collective-permute-start | bytes 3538952 | tf_op jit(solution)/shard_map/ppermute | solution.py:359
  482.4 22.8 %collective-permute-start.70 = (bf16[192,1664]{1,0:T(8,128)(2,1)S(1)}, bf16[192,1664]{1,0:T(8,128)(2,1)}, u32[]{:S(2)}, u32[]{:S(2)}) collective-permute-start(bf16[192,1664]{1,0:T(8,128)(2,1)S(1)} %maximum_select_fusion.9), channel_id=1, source_target_pairs={{0,16},{16,0},{1,17},{17,1},{2,18},{18,2},{3,19},{19,3},{4,20},{20... | collective-permute-start | bytes 1916936 | tf_op jit(solution)/shard_map/ppermute | solution.py:363
  483.6 21.6 %collective-permute-start.69 = (bf16[192,1664]{1,0:T(8,128)(2,1)S(1)}, bf16[192,1664]{1,0:T(8,128)(2,1)}, u32[]{:S(2)}, u32[]{:S(2)}) collective-permute-start(bf16[192,1664]{1,0:T(8,128)(2,1)S(1)} %maximum_select_fusion.8), channel_id=1, source_target_pairs={{0,2},{2,0},{4,6},{6,4},{8,10},{10,8},{12,14},{14,12},{1,3},{3,1},... | collective-permute-start | bytes 1916936 | tf_op jit(solution)/shard_map/ppermute | solution.py:374
  492.3 12.9 %collective-permute-start.73 = (bf16[48,2048]{1,0:T(8,128)(2,1)S(1)}, bf16[48,2048]{1,0:T(8,128)(2,1)}, u32[]{:S(2)}, u32[]{:S(2)}) collective-permute-start(bf16[48,2048]{1,0:T(8,128)(2,1)S(1)} %add_convert_fusion.25), channel_id=1, source_target_pairs={{0,12},{2,14},{4,8},{6,10},{8,4},{10,6},{12,0},{14,2},{1,13},{3,15... | collective-permute-start | bytes 589832 | tf_op jit(solution)/shard_map/ppermute | solution.py:383
  517.8 17.2 %collective-permute-start.79 = (bf16[192,2048]{1,0:T(8,128)(2,1)S(1)}, bf16[192,2048]{1,0:T(8,128)(2,1)S(1)}, u32[]{:S(2)}, u32[]{:S(2)}) collective-permute-start(bf16[192,2048]{1,0:T(8,128)(2,1)S(1)} %maximum_select_fusion.7.own_1), channel_id=1, source_target_pairs={{0,16},{16,0},{1,17},{17,1},{2,18},{18,2},{3,19},{19,3},{4,20},{20... | collective-permute-start | bytes 2359304 | tf_op jit(solution)/shard_map/ppermute | solution.py:363
  519.3 17.2 %collective-permute-start.78 = (bf16[192,2048]{1,0:T(8,128)(2,1)S(1)}, bf16[192,2048]{1,0:T(8,128)(2,1)}, u32[]{:S(2)}, u32[]{:S(2)}) collective-permute-start(bf16[192,2048]{1,0:T(8,128)(2,1)S(1)} %maximum_select_fusion.6.own_0), channel_id=1, source_target_pairs={{0,2},{2,0},{4,6},{6,4},{8,10},{10,8},{12,14},{14,12},{1,3},{3,1},... | collective-permute-start | bytes 2359304 | tf_op jit(solution)/shard_map/ppermute | solution.py:374
  (107 other events, 1070.9 us)

commit v4 on v3

--- a/solution.py
+++ b/solution.py
@@ -422,31 +422,32 @@
     return field.astype(jnp.bfloat16)
 
 
-def chip_send(theirs, mine):
-    return mine, other_core(theirs)
-
-
-def slab_send(fields, place):
+def slab_cut(first, second, at, other):
+    return (
+        (block(first, at, 2), block(first, 1 - at, 2)),
+        (block(second, other, 2), block(second, 1 - other, 2)),
+    )
+
+
+def slab_sum(cuts, place):
     dp, x, _, _ = place
-    first, second = jnp.split(low(sum_blocks(*fields)), 2)
-    return (
-        (block(first, x, 2), across_x(block(first, 1 - x, 2))),
-        (block(second, dp, 2), other_dp(block(second, 1 - dp, 2))),
-    )
-
-
-def slab_send_on(fields, place):
-    dp, x, _, _ = place
-    first, second = (low(sum_blocks(*pair)) for pair in fields)
-    return (
-        (block(first, dp, 2), other_dp(block(first, 1 - dp, 2))),
-        (block(second, x, 2), across_x(block(second, 1 - x, 2))),
-    )
-
-
-def line_send(fields, z):
-    part = low(jnp.concatenate([sum_blocks(*pair) for pair in fields]))
-    return [block(part, z, 4)] + [across_z(block(part, z ^ k, 4), k) for k in (1, 2, 3)]
+    (first, first_out), (second, second_out) = cuts
+    first = low(sum_blocks(first, across_x(first_out)))
+    second = low(sum_blocks(second, other_dp(second_out)))
+    return slab_cut(first, second, dp, x)
+
+
+def slab_sum_on(cuts, place):
+    z = place[2]
+    (first, first_out), (second, second_out) = cuts
+    first = sum_blocks(first, other_dp(first_out))
+    second = sum_blocks(second, across_x(second_out))
+    part = low(jnp.concatenate([first, second]))
+    return [block(part, z ^ k, 4) for k in range(4)]
+
+
+def line_sum(cuts):
+    return low(sum_blocks(cuts[0], *[across_z(cuts[k], k) for k in (1, 2, 3)]))
 
 
 def put_in_order(pieces, own):
@@ -456,27 +457,20 @@
     )
 
 
-def line_spread(fields):
-    part = low(sum_blocks(*fields))
-    return [part] + [across_z(part, k) for k in (1, 2, 3)]
-
-
-def slab_spread(fields, z):
-    first, second = jnp.split(put_in_order(fields, z), 2)
-    return (first, other_dp(first)), (second, across_x(second))
-
-
-def slab_spread_on(fields, place):
+def line_spread(part, place):
+    part = put_in_order([part] + [across_z(part, k) for k in (1, 2, 3)], place[2])
+    return jnp.split(part, 2)
+
+
+def slab_spread(halves, place):
     dp, x, _, _ = place
-    first, second = fields
-    first, second = in_order(dp == 0, *first), in_order(x == 0, *second)
+    first, second = halves
+    return in_order(dp == 0, first, other_dp(first)), in_order(x == 0, second, across_x(second))
+
+
+def slab_spread_on(halves):
+    first, second = halves
     return (first, across_x(first)), (second, other_dp(second))
-
-
-def whole_of(fields, place):
-    dp, x, _, _ = place
-    first, second = fields
-    return jnp.concatenate([in_order(x == 0, *first), in_order(dp == 0, *second)])
 
 
 def matmul(left, right, dims=(((1,), (0,)), ((), ()))):
@@ -658,6 +652,9 @@
     back_own,
     back_other,
     back_ring,
+    extra_own,
+    extra_other,
+    extra_ring,
     gates_ref,
     router_ref,
     middle_ref,
@@ -666,58 +663,103 @@
     ct_ref,
     weight_ref,
     grad_ref,
-    low_ref,
+    unit_ref,
     mix_ref,
     gain_grad,
-    logits_grad,
+    logits_ref,
     weight_here,
     weight_sem,
 ):
-    rows = middle_ref.shape[0]
-    pltpu.make_async_copy(weight_ref, weight_here, weight_sem).start()
-    gates = gates_ref[...]
-    grad_gates = unpacked(
-        sum_blocks(back_own[rows:, :], back_other[rows:, :], back_ring[rows:, :]), rows
-    )
-    mean_term = jnp.sum(gates * grad_gates, axis=0, keepdims=True)
-    logits = low(gates * (grad_gates - mean_term))
-    logits_grad[...] = logits
-    total = jnp.zeros(gain_grad.shape, jnp.float32)
-    for start in range(0, rows, HEAD_SIZE):
-        at = pl.ds(start, HEAD_SIZE)
-        grad = sum_blocks(back_own[at, :], back_other[at, :], back_ring[at, :])
-        grad = grad + matmul(logits[:, start : start + HEAD_SIZE], router_ref[...], FIRST_WITH_FIRST)
-        middle, scale = middle_ref[at, :], scale_ref[at, :]
-        scaled = grad * gain_ref[...]
-        mean = jnp.mean(scaled * middle, axis=1, keepdims=True)
-        out = ct_ref[at, :].astype(jnp.float32) + scale * scaled - middle * (scale**3 * mean)
-        total = total + jnp.sum(middle * scale * grad, axis=0, keepdims=True)
-        grad_ref[at, :] = out
-        low_ref[at, :] = low(out)
-    gain_grad[...] = total
-    pltpu.make_async_copy(weight_ref, weight_here, weight_sem).wait()
-    for start in range(0, weight_here.shape[0], 256):
-        at = pl.ds(start, 256)
-        mix_ref[:, at] = low(matmul(low_ref[...], weight_here[at, :], LAST_WITH_LAST))
+    step, tile = pl.program_id(0), middle_ref.shape[0]
+    at = pl.multiple_of(step * tile, tile)
+    copy = pltpu.make_async_copy(weight_ref, weight_here, weight_sem)
+
+    @pl.when(step == 0)
+    def _():
+        copy.start()
+        gates = gates_ref[...]
+        grad_gates = sum_blocks(extra_own[...], extra_other[...], extra_ring[...])
+        grad_gates = unpacked(grad_gates, gates.shape[1])
+        mean_term = jnp.sum(gates * grad_gates, axis=0, keepdims=True)
+        logits_ref[...] = low(gates * (grad_gates - mean_term))
+        gain_grad[...] = jnp.zeros(gain_grad.shape, jnp.float32)
+
+    grad = sum_blocks(back_own[...], back_other[...], back_ring[...])
+    grad = grad + matmul(logits_ref[:, pl.ds(at, tile)], router_ref[...], FIRST_WITH_FIRST)
+    middle, scale = middle_ref[...], scale_ref[...]
+    scaled = grad * gain_ref[...]
+    mean = jnp.mean(scaled * middle, axis=1, keepdims=True)
+    out = ct_ref[...].astype(jnp.float32) + scale * scaled - middle * (scale**3 * mean)
+    gain_grad[...] += jnp.sum(middle * scale * grad, axis=0, keepdims=True)
+    grad_ref[...] = out
+    unit_ref[pl.ds(at, tile), :] = low(out)
+
+    @pl.when(step == pl.num_programs(0) - 1)
+    def _():
+        count, columns = unit_ref.shape[0] - EXTRA, unit_ref.shape[1]
+        gain = gain_grad[...]
+        high = low(gain).astype(jnp.float32)
+        logits = logits_ref[...].astype(jnp.float32)
+        experts = logits.shape[0]
+        pad = jnp.zeros((experts, columns - logits.shape[1]), jnp.float32)
+        behind = jnp.concatenate([logits, pad], axis=1)
+        behind = jnp.concatenate([jnp.zeros((EXTRA - experts, columns), jnp.float32), behind])
+        row = lax.broadcasted_iota(jnp.int32, behind.shape, 0)
+        behind = jnp.where(row == 0, high, jnp.where(row == 1, gain - high, behind))
+        unit_ref[count:, :] = low(behind)
+        copy.wait()
+        for start in range(0, weight_here.shape[0], 256):
+            part = pl.ds(start, 256)
+            mix_ref[:, part] = low(
+                matmul(unit_ref[:count, :], weight_here[part, :], LAST_WITH_LAST)
+            )
 
 
 def middle_back(back, gates, router, middle, scale, gain, upstream, out_weight):
-    rows, model_width = middle.shape
+    rows, columns = middle.shape
+    tile = HEAD_SIZE
+
+    def whole(*shape):
+        return pl.BlockSpec(shape, lambda i: (0, 0))
+
+    def cut(width):
+        return pl.BlockSpec((tile, width), lambda i: (i, 0))
+
+    extra = pl.BlockSpec((EXTRA, columns), lambda i: (rows // EXTRA, 0))
     shapes = [
-        ((rows, model_width), jnp.float32),
-        ((rows, model_width), jnp.bfloat16),
+        ((rows, columns), jnp.float32),
+        ((rows + EXTRA, columns), jnp.bfloat16),
         ((rows, out_weight.shape[0]), jnp.bfloat16),
-        ((1, model_width), jnp.float32),
-        (gates.shape, jnp.bfloat16),
     ]
     return pl.pallas_call(
         middle_back_kernel,
-        in_specs=[pl.BlockSpec(memory_space=pltpu.VMEM)] * 9 + [pl.BlockSpec(memory_space=pl.ANY)],
+        grid=(rows // tile,),
+        in_specs=[
+            *[cut(columns)] * 3,
+            *[extra] * 3,
+            whole(*gates.shape),
+            whole(*router.shape),
+            cut(columns),
+            cut(1),
+            whole(*gain.shape),
+            cut(columns),
+            pl.BlockSpec(memory_space=pl.ANY),
+        ],
+        out_specs=[
+            cut(columns),
+            whole(rows + EXTRA, columns),
+            whole(rows, out_weight.shape[0]),
+        ],
         out_shape=[jax.ShapeDtypeStruct(*shape) for shape in shapes],
-        scratch_shapes=[pltpu.VMEM(out_weight.shape, jnp.bfloat16), pltpu.SemaphoreType.DMA],
+        scratch_shapes=[
+            pltpu.VMEM((1, columns), jnp.float32),
+            pltpu.VMEM(gates.shape, jnp.bfloat16),
+            pltpu.VMEM(out_weight.shape, jnp.bfloat16),
+            pltpu.SemaphoreType.DMA,
+        ],
         compiler_params=pltpu.CompilerParams(vmem_limit_bytes=60 * 2**20),
         cost_estimate=SHORT,
-    )(*back, gates, router, middle, scale, gain, upstream, out_weight)
+    )(*back, *back, gates, router, middle, scale, gain, upstream, out_weight)
 
 
 def middle_kernel(
@@ -792,77 +834,102 @@
     )(grad_projected, qkv_weight, tokens, scale, gain, grad_middle)
 
 
-def halves_kernel(fill, core_ref, *refs):
-    theirs_ref, mine_ref = refs[-2:]
-
-    @pl.when(pl.program_id(0) == 0)
+def put_pieces(half, place_ref, field, pieces):
+    rows = field.shape[0] // 2
+    stays, sent = pieces[2 * half : 2 * half + 2]
+
+    @pl.when((pl.program_id(0) == half) & (place_ref[half] == 0))
     def _():
-        fill(*refs[:-2], theirs_ref)
-
-    @pl.when(pl.program_id(0) == 1)
+        stays[...], sent[...] = field[:rows], field[rows:]
+
+    @pl.when((pl.program_id(0) == half) & (place_ref[half] == 1))
     def _():
-        fill(*refs[:-2], mine_ref)
-
-
-def in_halves(fill, core, tiled, whole, total):
-    columns = tiled[0].shape[1]
-    tile = columns // 4
-
-    def chosen(half, i, core_ref):
-        return jnp.where(half == 1, core_ref[0], 1 - core_ref[0]) * 2 + i
-
-    def cut(field):
-        return pl.BlockSpec(
-            (field.shape[0], tile), lambda half, i, core_ref: (0, chosen(half, i, core_ref))
-        )
-
-    def kept(field):
-        return pl.BlockSpec(field.shape, lambda half, i, core_ref: (0, 0))
-
-    return pl.pallas_call(
-        functools.partial(halves_kernel, fill),
+        stays[...], sent[...] = field[rows:], field[:rows]
+
+
+def qkv_grads_kernel(place_ref, left_own, left_other, right_own, right_other, *pieces):
+    field = matmul(left_own[...], right_own[...], FIRST_WITH_FIRST)
+    field = low(field + matmul(left_other[...], right_other[...], FIRST_WITH_FIRST))
+    for half in range(2):
+        put_pieces(half, place_ref, field, pieces)
+
+
+def out_grads_kernel(place_ref, *refs):
+    field = small = gain = 0.0
+    for mix, rows, grad, logits, behind in (refs[0:5], refs[5:10]):
+        field = field + matmul(mix[...], grad[...], FIRST_WITH_FIRST)
+        experts = EXTRA // 2
+        chosen = logits[...][EXTRA - experts :]
+        pad = [jnp.zeros_like(chosen)] * (HEAD_SIZE // experts - 1)
+        chosen = jnp.concatenate([chosen] + pad)
+        small = small + matmul(rows[...], chosen, (((0,), (1,)), ((), ())))
+        behind = behind[...].astype(jnp.float32)
+        gain = gain + behind[0:1] + behind[1:2]
+    lane = lax.broadcasted_iota(jnp.int32, small.shape, 1)
+    gain = jnp.broadcast_to(gain, (HEAD_SIZE, small.shape[0])).T
+    small = jnp.where(lane == EXTRA // 2, gain, small)
+    field = low(jnp.concatenate([field, small], axis=1))
+    for half in range(2):
+        put_pieces(half, place_ref, field, refs[10:])
+
+
+def chip_grads(kernel, place, operands, total):
+    dp, x, _, core = place
+    tile = operands[0][0].shape[1] // 4
+
+    def spec(field, rows, at, is_cut):
+        if is_cut:
+            return pl.BlockSpec((rows, tile), lambda i, place_ref: (at, 2 * place_ref[2] + i))
+        columns = operands[0][0].shape[0] if rows == EXTRA else field.shape[1]
+        return pl.BlockSpec((rows, columns), lambda i, place_ref: (at, 0))
+
+    piece = (tile // 2, total)
+    pieces = pl.pallas_call(
+        kernel,
         grid_spec=pltpu.PrefetchScalarGridSpec(
             num_scalar_prefetch=1,
-            grid=(2, 2),
-            in_specs=[cut(field) for field in tiled] + [kept(field) for field in whole],
-            out_specs=[
-                pl.BlockSpec((tile, total), lambda half, i, core_ref: (jnp.where(half == 0, i, 1), 0)),
-                pl.BlockSpec((tile, total), lambda half, i, core_ref: (jnp.where(half == 1, i, 0), 0)),
-            ],
+            grid=(2,),
+            in_specs=[spec(*operand) for operand in operands],
+            out_specs=[pl.BlockSpec(piece, lambda i, place_ref: (0, 0))] * 4,
         ),
-        out_shape=[jax.ShapeDtypeStruct((columns // 2, total), jnp.bfloat16)] * 2,
+        out_shape=[jax.ShapeDtypeStruct(piece, jnp.bfloat16)] * 4,
         compiler_params=pltpu.CompilerParams(vmem_limit_bytes=24 * 2**20),
         cost_estimate=SHORT,
-    )(core[None].astype(jnp.int32), *tiled, *whole)
-
-
-def fill_product(left_ref, right_ref, out_ref):
-    out_ref[...] = low(matmul(left_ref[...], right_ref[...], FIRST_WITH_FIRST))
-
-
-def product(left, right, core):
-    return in_halves(fill_product, core, [left], [right], right.shape[1])
-
-
-def fill_out_grads(mix_ref, rows_ref, gain_ref, grad_out, logits_ref, out_ref):
-    rows, width = grad_out.shape
-    out_ref[:, :width] = low(matmul(mix_ref[...], grad_out[...], FIRST_WITH_FIRST))
-    logits = logits_ref[...]
-    experts = logits.shape[0]
-    logits = jnp.concatenate([logits] + [jnp.zeros_like(logits)] * (HEAD_SIZE // experts - 1))
-    small = matmul(rows_ref[:rows, :], logits, (((0,), (1,)), ((), ())))
-    lane = lax.broadcasted_iota(jnp.int32, small.shape, 1)
-    gain = jnp.broadcast_to(gain_ref[...], (HEAD_SIZE, small.shape[0])).T
-    out_ref[:, width:] = low(jnp.where(lane == experts, gain, small))
-
-
-def out_grads(mix, grad_out, unit, logits, gain, core):
-    total = grad_out.shape[1] + HEAD_SIZE
-    return in_halves(fill_out_grads, core, [mix, unit, gain], [grad_out, logits], total)
-
-
-def finish_kernel(place_ref, own_0, got_0, own_1, got_1, weight_ref, gain_ref, out_ref, grad_ref):
+    )(jnp.stack([x, dp, core]).astype(jnp.int32), *[operand[0] for operand in operands])
+    return pieces[0:2], pieces[2:4]
+
+
+def qkv_grads(normed, grads, place):
+    rows = grads[0].shape[0]
+    operands = [(field, rows, 0, True) for field in normed]
+    operands += [(field, rows, 0, False) for field in grads]
+    return chip_grads(qkv_grads_kernel, place, operands, grads[0].shape[1])
+
+
+def out_grads(mixes, units, grads, place):
+    rows = mixes[0].shape[0]
+    operands = []
+    for mix, unit, grad in zip(mixes, units, grads):
+        operands += [
+            (mix, rows, 0, True),
+            (unit, rows, 0, True),
+            (grad, rows, 0, False),
+            (grad, EXTRA, rows // EXTRA, False),
+            (grad, EXTRA, rows // EXTRA, True),
+        ]
+    return chip_grads(out_grads_kernel, place, operands, grads[0].shape[1] + HEAD_SIZE)
+
+
+def from_pieces(put, place_ref, pieces):
     step = pl.program_id(0)
+    for half in range(2):
+        here = 2 * half + place_ref[half]
+        pl.when(step == here)(functools.partial(put, pieces[2 * half]))
+        pl.when(step == 4 * half + 1 - here)(functools.partial(put, pieces[2 * half + 1]))
+
+
+def finish_qkv_kernel(place_ref, *refs):
+    weight_ref, gain_ref, out_ref, grad_ref = refs[4:]
 
     def put(field):
         field = field[...].astype(jnp.float32)
@@ -870,37 +937,41 @@
         total = jnp.sum(field * weight_ref[...].astype(jnp.float32), axis=1, keepdims=True)
         grad_ref[...] = total / gain_ref[...]
 
-    for half, (own, got) in enumerate(((own_0, got_0), (own_1, got_1))):
-        here = 2 * half + place_ref[half]
-        pl.when(step == here)(functools.partial(put, own))
-        pl.when(step == 4 * half + 1 - here)(functools.partial(put, got))
-
-
-def finish(fields, place, weight, gain):
+    from_pieces(put, place_ref, refs[:4])
+
+
+def finish_out_kernel(place_ref, *refs):
+    out_ref, small_ref = refs[4:]
+    width = out_ref.shape[1]
+
+    def put(field):
+        out_ref[...] = field[:, :width].astype(jnp.float32)
+        small_ref[...] = field[:, width:].astype(jnp.float32)
+
+    from_pieces(put, place_ref, refs[:4])
+
+
+def finish(kernel, fields, place, extras, widths):
     dp, x, _, _ = place
-    (own_0, got_0), (own_1, got_1) = fields
-    rows, columns = own_0.shape
-    whole = pl.BlockSpec((rows, columns), lambda i: (0, 0))
+    pieces = [*fields[0], *fields[1]]
+    rows = pieces[0].shape[0]
+
+    def cut(width):
+        return pl.BlockSpec((rows, width), lambda i: (i, 0))
+
     return pl.pallas_call(
-        finish_kernel,
+        kernel,
         grid=(4,),
         in_specs=[
             pl.BlockSpec(memory_space=pltpu.SMEM),
-            *[whole] * 4,
-            pl.BlockSpec((rows, columns), lambda i: (i, 0)),
-            pl.BlockSpec((rows, 1), lambda i: (i, 0)),
+            *[pl.BlockSpec(piece.shape, lambda i: (0, 0)) for piece in pieces],
+            *[cut(extra.shape[1]) for extra in extras],
         ],
-        out_specs=[
-            pl.BlockSpec((rows, columns), lambda i: (i, 0)),
-            pl.BlockSpec((rows, 1), lambda i: (i, 0)),
-        ],
-        out_shape=[
-            jax.ShapeDtypeStruct((4 * rows, columns), jnp.float32),
-            jax.ShapeDtypeStruct((4 * rows, 1), jnp.float32),
-        ],
+        out_specs=[cut(width) for width in widths],
+        out_shape=[jax.ShapeDtypeStruct((4 * rows, width), jnp.float32) for width in widths],
         compiler_params=pltpu.CompilerParams(vmem_limit_bytes=24 * 2**20),
         cost_estimate=SHORT,
-    )(jnp.stack([x, dp]).astype(jnp.int32), own_0, got_0, own_1, got_1, weight, gain)
+    )(jnp.stack([x, dp]).astype(jnp.int32), *pieces, *extras)
 
 
 def turn(field, cosine, sine):
@@ -928,9 +999,12 @@
 
 def probabilities(query, key, seg_row, seg_column):
     scores = matmul(key, query, LAST_WITH_LAST) * HEAD_SIZE ** (-0.5)
-    key_at = lax.broadcasted_iota(jnp.int32, scores.shape, 0)
-    query_at = lax.broadcasted_iota(jnp.int32, scores.shape, 1)
-    scores = jnp.where((seg_row == seg_column) & (key_at <= query_at), scores, -1e30)
+    square = key.shape[0], key.shape[0]
+    key_at = lax.broadcasted_iota(jnp.int32, square, 0)
+    query_at = lax.broadcasted_iota(jnp.int32, square, 1)
+    hidden = jnp.where((seg_row == seg_column) & (key_at <= query_at), 0.0, -1e30)
+    hidden = jnp.concatenate([hidden] * (scores.shape[1] // key.shape[0]), axis=1)
+    scores = jnp.where(hidden < 0.0, -1e30, scores)
     raised = jnp.exp(scores - jnp.max(scores, axis=0, keepdims=True))
     return raised / jnp.sum(raised, axis=0, keepdims=True)
 
@@ -988,19 +1062,24 @@
         at = pl.multiple_of(head * HEAD_SIZE, HEAD_SIZE)
         out_ref[:, pl.ds(at, HEAD_SIZE)] = low(field)
 
-    grad_key = grad_value = 0.0
-    for half in range(HEADS_AT_ONCE):
-        columns = slice(half * HEAD_SIZE, (half + 1) * HEAD_SIZE)
-        query, grad_mix = query_ref[:, columns], grad_ref[:, columns]
-        probs = probabilities(query, key, seg_row[...], seg_column[...])
-        grad_probs = matmul(value, grad_mix, LAST_WITH_LAST)
-        grad_scores = low(
-            probs * (grad_probs - jnp.sum(probs * grad_probs, axis=0, keepdims=True))
+    def stacked(ref):
+        return jnp.concatenate(
+            [ref[:, at * HEAD_SIZE : (at + 1) * HEAD_SIZE] for at in range(HEADS_AT_ONCE)]
         )
-        grad_query = matmul(grad_scores, key, FIRST_WITH_FIRST) * HEAD_SIZE ** (-0.5)
-        put(step * HEADS_AT_ONCE + half, turn(grad_query, cosine, sine))
-        grad_key = grad_key + matmul(grad_scores, query) * HEAD_SIZE ** (-0.5)
-        grad_value = grad_value + matmul(low(probs), grad_mix)
+
+    query, grad_mix = stacked(query_ref), stacked(grad_ref)
+    rows = key.shape[0]
+    probs = probabilities(query, key, seg_row[...], seg_column[...])
+    grad_probs = matmul(value, grad_mix, LAST_WITH_LAST)
+    grad_scores = low(
+        probs * (grad_probs - jnp.sum(probs * grad_probs, axis=0, keepdims=True))
+    )
+    grad_query = matmul(grad_scores, key, FIRST_WITH_FIRST) * HEAD_SIZE ** (-0.5)
+    for at in range(HEADS_AT_ONCE):
+        head = grad_query[at * rows : (at + 1) * rows]
+        put(step * HEADS_AT_ONCE + at, turn(head, cosine, sine))
+    grad_key = matmul(grad_scores, query) * HEAD_SIZE ** (-0.5)
+    grad_value = matmul(low(probs), grad_mix)
 
     @pl.when(place == 0)
     def _():
@@ -1163,8 +1242,11 @@
     normed_2 = ring_z(normed_1[0])
     ct_3 = sent_dealt(ct_3)
     ct_2 = swapped(arrange(*ct_2))
+    mixes, normeds = swapped(attn_mix), swapped(normed_attn)
     sums_1, back_1, kept = expert_step(1, choice, normed_1, ct_1, matrices, kept)
-    normed_2, ct_3, ct_2, back_1, kept = part(normed_2, ct_3, ct_2, back_1, kept)
+    normed_2, ct_3, ct_2, back_1, kept, mixes, normeds = part(
+        normed_2, ct_3, ct_2, back_1, kept, mixes, normeds
+    )
 
     normed_3 = ring_z(normed_2)
     normed_2, back_1_other = swapped(normed_2), other_core(back_1[1])
@@ -1194,15 +1276,17 @@
     down_second = low(matmul(all_hidden.T, all_grad_out[:, half_width:]))
     sums_1 = low(sum_blocks(sums_1[0], sums_1_other))
     sums_2_other = other_core(sums_2[1])
+    up_second = block(up_second, dp, 2), block(up_second, 1 - dp, 2)
+    down_second = block(down_second, dp, 2), block(down_second, 1 - dp, 2)
     back_3, up_first, up_second, down_first, down_second, sums_1, sums_2_other = part(
         back_3, up_first, up_second, down_first, down_second, sums_1, sums_2_other
     )
 
     sums_1 = ring_z(sums_1)
     up_first = up_first, to_owner(up_first)
-    up_second = block(up_second, dp, 2), other_dp(block(up_second, 1 - dp, 2))
-    sums_3_other = other_core(sums_3[1])
-    grad_middle, grad_attn_out, grad_mix, term_gain_second, grad_logits = middle_back(
+    up_second = up_second[0], other_dp(up_second[1])
+    sums_0_other, sums_3_other = other_core(sums_0[1]), other_core(sums_3[1])
+    grad_middle, grad_unit, grad_mix = middle_back(
         (back_0[0], back_0_other, back_3),
         gates,
         router,
@@ -1212,84 +1296,106 @@
         ct_0[0],
         full_out,
     )
-    out = out_grads(attn_mix, grad_attn_out, unit_0, grad_logits, term_gain_second, core)
     grad_projected = attend_back(query, key, value, grad_mix, cosine, sine, segment)
-    qkv = product(normed_attn, grad_projected, core)
-    sums_1, sums_3_other, out, qkv, grad_projected, up_first, up_second = part(
-        sums_1, sums_3_other, out, qkv, grad_projected, up_first, up_second
-    )
-
-    sums_2 = ring_z(low(sum_blocks(sums_2[0], sums_2_other, sums_1)))
-    out, qkv = chip_send(*out), chip_send(*qkv)
+    (
+        sums_0_other,
+        sums_1,
+        sums_3_other,
+        grad_projected,
+        grad_unit,
+        up_first,
+        up_second,
+        down_first,
+        down_second,
+    ) = part(
+        sums_0_other,
+        sums_1,
+        sums_3_other,
+        grad_projected,
+        grad_unit,
+        up_first,
+        up_second,
+        down_first,
+        down_second,
+    )
+
+    grads_projected, grad_units = swapped(grad_projected), swapped(grad_unit)
     down_first = down_first, to_owner(down_first)
-    down_second = block(down_second, dp, 2), other_dp(block(down_second, 1 - dp, 2))
+    down_second = down_second[0], other_dp(down_second[1])
     up_first, up_second = low(sum_blocks(*up_first)), low(sum_blocks(*up_second))
-    sums_2, out, qkv, down_first, down_second, up_first, up_second, grad_projected = part(
-        sums_2, out, qkv, down_first, down_second, up_first, up_second, grad_projected
-    )
-
-    sums_3 = ring_z(low(sum_blocks(sums_3[0], sums_3_other, sums_2)))
-    out = slab_send(out, place)
-    up_first = block(up_first, dp, 2), owners_dp(block(up_first, 1 - dp, 2))
+    up_first = block(up_first, dp, 2), block(up_first, 1 - dp, 2)
+    sums_2 = low(sum_blocks(sums_2[0], sums_2_other, sums_1))
+    qkv = qkv_grads(normeds, grads_projected, place)
+    sums_2, grad_units, qkv, down_first, down_second, up_first, up_second, grad_projected = part(
+        sums_2, grad_units, qkv, down_first, down_second, up_first, up_second, grad_projected
+    )
+
+    sums_2 = ring_z(sums_2)
+    qkv = slab_sum(qkv, place)
+    up_first = up_first[0], owners_dp(up_first[1])
     up_second = up_second, to_owner(up_second)
-    qkv = low(sum_blocks(*qkv))
+    down_first, down_second, qkv = part(down_first, down_second, qkv)
     down_first, down_second = low(sum_blocks(*down_first)), low(sum_blocks(*down_second))
+    down_first = block(down_first, dp, 2), block(down_first, 1 - dp, 2)
     grad_tokens = tokens_back(
         grad_projected, full_qkv, tokens, inv_first, gain_first, grad_middle
     )
+    out = out_grads(mixes, normed_0, grad_units, place)
+    sums_3 = low(sum_blocks(sums_3[0], sums_3_other, after(sums_2, qkv)))
     sums_3, out, qkv, up_first, up_second, down_first, down_second, grad_tokens = part(
         sums_3, out, qkv, up_first, up_second, down_first, down_second, grad_tokens
     )
 
-    out = slab_send_on(out, place)
-    down_first = block(down_first, dp, 2), owners_dp(block(down_first, 1 - dp, 2))
+    sums_3 = ring_z(sums_3)
+    qkv = slab_sum_on(qkv, place)
+    down_first = down_first[0], owners_dp(down_first[1])
     down_second = down_second, to_owner(down_second)
-    sums_0_other = other_core(sums_0[1])
+    input_gradient = to_dealt(grad_tokens)
     up_grad = low(jnp.concatenate([sum_blocks(*up_first), sum_blocks(*up_second)], axis=1))
-    out, qkv, down_first, down_second, sums_0_other, up_grad, grad_tokens = part(
-        out, qkv, down_first, down_second, sums_0_other, up_grad, grad_tokens
-    )
-
-    out, qkv = line_send(out, z), slab_send((qkv,), place)
-    layer_out = low(middle + sum_blocks(sums_0[0], sums_0_other, sums_3))
+    up_grad = block(up_grad, core, 2), block(up_grad, 1 - core, 2)
+    layer_out = low(middle + sum_blocks(sums_0[0], sums_0_other, after(sums_3, qkv)))
+    out, qkv, up_grad, down_first, down_second, layer_out, input_gradient = part(
+        out, qkv, up_grad, down_first, down_second, layer_out, input_gradient
+    )
+
+    qkv, out = line_sum(qkv), slab_sum(out, place)
     down_grad = low(jnp.concatenate([sum_blocks(*down_first), sum_blocks(*down_second)], axis=1))
-    out, qkv, layer_out, down_grad, grad_tokens, up_grad = part(
-        out, qkv, layer_out, down_grad, grad_tokens, up_grad
-    )
-
-    out, qkv = line_spread(out), slab_send_on(qkv, place)
+    down_grad = block(down_grad, core, 2), block(down_grad, 1 - core, 2)
+    out, qkv, up_grad, down_grad, layer_out = part(out, qkv, up_grad, down_grad, layer_out)
+
+    qkv, out = line_spread(qkv, place), slab_sum_on(out, place)
     layer_out = to_dealt(layer_out)
-    out, qkv, layer_out, grad_tokens, up_grad = part(out, qkv, layer_out, grad_tokens, up_grad)
-
-    out, qkv = slab_spread(out, z), line_send(qkv, z)
-    input_gradient = to_dealt(grad_tokens)
-    out, qkv, input_gradient, up_grad, down_grad = part(
-        out, qkv, input_gradient, up_grad, down_grad
-    )
-
-    out, qkv = slab_spread_on(out, place), line_spread(qkv)
-    up_grad = up_grad, other_core(block(up_grad, 1 - core, 2))
+    out, qkv, layer_out, up_grad, down_grad = part(out, qkv, layer_out, up_grad, down_grad)
+
+    qkv, out = slab_spread(qkv, place), line_sum(out)
     out, qkv, up_grad, down_grad = part(out, qkv, up_grad, down_grad)
 
-    qkv = slab_spread(qkv, z)
-    down_grad = down_grad, other_core(block(down_grad, 1 - core, 2))
-    out = whole_of(out, place).astype(jnp.float32)
-    qkv, out, up_grad, down_grad = part(qkv, out, up_grad, down_grad)
-    qkv = slab_spread_on(qkv, place)
-    gate_up_grad, down_grad = (
-        jnp.where(core == x, block(field, core, 2), received)[None].astype(jnp.float32)
-        for field, received in (up_grad, down_grad)
+    qkv, out = slab_spread_on(qkv), line_spread(out, place)
+    out, qkv, up_grad, down_grad = part(out, qkv, up_grad, down_grad)
+
+    out = slab_spread(out, place)
+    up_grad, down_grad = (
+        jnp.where(core == x, field[0], other_core(field[1])) for field in (up_grad, down_grad)
     )
     gain = attention_gain.astype(jnp.float32)[:, None]
-    qkv_grad, gain_first_grad = finish(qkv, place, qkv_weight, gain)
+    qkv_grad, gain_first_grad = finish(
+        finish_qkv_kernel, qkv, place, [qkv_weight, gain], [qkv_weight.shape[1], 1]
+    )
+    out, qkv_grad, gain_first_grad, up_grad, down_grad = part(
+        out, qkv_grad, gain_first_grad, up_grad, down_grad
+    )
+
+    out = slab_spread_on(out)
+    gate_up_grad, down_grad = (field[None].astype(jnp.float32) for field in (up_grad, down_grad))
+    out_grad, small_grad = finish(finish_out_kernel, out, place, [], [model_width, HEAD_SIZE])
     return (
         layer_out,
         input_gradient,
         gain_first_grad[:, 0],
-        out[:, model_width + expert_count],
+        small_grad[:, expert_count],
         qkv_grad,
-        out[:, :model_width],
-        out[:, model_width : model_width + expert_count],
+        out_grad,
+        small_grad[:, :expert_count],
         gate_up_grad,
         down_grad,
     )

time: 552 us -> 534 us (0.967)
  the two profiles are of different devices: /device:TPU:8 before, /device:TPU:0 now
where the time goes in v4:
time: 534 us; the launch traced here: 525 us
  waiting for transfers between devices  161 us (30%)
  Pallas kernels  133 us (25%)
  starting transfers between devices  82 us (15%)
  other arithmetic  60.1 us (11%)
  matrix products  44.7 us (8%)
  local copies, waits for them, and re-layouts  41.5 us (8%)
    pallas_call x4, Pallas kernels, expert_step(): pl.pallas_call(functools.partial(expert_kernel, columns=256), grid=(2,),...  83.2 us
    ppermute x12, waiting for transfers between devices, ring_z(): return lax.ppermute(field, 'expert', pairs)  63.7 us
    dot_general x12, matrix products, matmul(): lax.dot_general(left, right, dims, preferred_element_type=jnp.float32)  44.7 us
    ppermute x17, waiting for transfers between devices, other_dp(): return lax.ppermute(field, 'dp', [(0, 1), (1, 0)])  38.6 us
    ppermute x12, waiting for transfers between devices, across_z(): lax.ppermute(field, 'expert', [(i, i ^ 2 * distance) for i in range(8)])  33.4 us
    convert_element_type x18, other arithmetic, low(): return field.astype(jnp.bfloat16)  26.1 us
    unnamed x219, local copies, waits for them, and re-layouts  24.3 us
    ppermute x8, waiting for transfers between devices, across_x(): return lax.ppermute(field, 'expert', [(i, i ^ 1) for i in range(8)])  19.2 us
  transfers between devices with their start and end apart: 82, of which 30 were waited for; matrix products, arithmetic and copies ran while one was open for 22% of the time, Pallas kernels for 25%

profile of v4, /device:TPU:0, one launch (start us, length us, event | category | flops | bytes accessed | tf_op | source)
XLA Modules:
  0.0 524.8 jit_solution(7806063770384584295)
XLA Ops:
  2.1 2.4 pad_maximum_fusion
  5.1 2.6 collective-permute-start.2
  9.4 5.5 %collective-permute-start.7 = (bf16[1536,1536]{1,0:T(8,128)(2,1)}, bf16[1536,1536]{1,0:T(8,128)(2,1)}, u32[]{:S(2)}, u32[]{:S(2)}) collective-permute-start(bf16[1536,1536]{1,0:T(8,128)(2,1)} %bitcast.64), channel_id=1, source_target_pairs={{0,2},{3,1},{4,6},{7,5},{8,10},{11,9},{12,14},{15,13},{16,18},{19,... | collective-permute-start | bytes 14155784 | tf_op jit(solution)/shard_map/ppermute | solution.py:398
  18.2 8.2 %maximum_select_fusion.weight_ref = bf16[1536,2048]{1,0:T(8,128)(2,1)} fusion(bf16[768,2048]{1,0:T(8,128)(2,1)} %collective-permute-done.1, bf16[768,2048]{1,0:T(8,128)(2,1)} %refs_4_.1, pred[]{:T(512)S(6)} %eq.192), kind=kLoop, calls=%fused_computation | loop fusion | flops 28311552 | bytes 12582913 | tf_op jit(solution)/shard_map/jit(_where)/select_n | solution.py:402
  29.3 2.6 fusion.84.query_in.key_in.value_in
  31.9 6.1 %collective-permute-done = bf16[400,1536]{1,0:T(8,128)(2,1)} collective-permute-done((bf16[400,1536]{1,0:T(8,128)(2,1)}, bf16[400,1536]{1,0:T(8,128)(2,1)}, u32[]{:S(2)}, u32[]{:S(2)}) %collective-permute-start) | collective-permute-done | bytes 1228832 | tf_op jit(solution)/shard_map/ppermute | solution.py:388
  41.4 3.5 collective-permute-start.12
  45.0 7.4 %shard_map.187 = (bf16[384,1536]{1,0:T(8,128)(2,1)S(1)}, bf16[384,256]{1,0:T(8,128)(2,1)S(1)}, bf16[384,256]{1,0:T(8,128)(2,1)S(1)}, bf16[384,1536]{1,0:T(8,128)(2,1)S(1)}) custom-call(f32[384,2048]{1,0:T(8,128)S(1)} %fusion.84.query_in.key_in.value_in, f32[384,2048]{1,0:T(8,128)S(1)} %fusion.84.query_in.key_in.value_in, ...), custom_call_target="tpu_custom_call" | custom-call | flops 1000 | bytes 1000 | tf_op jit(solution)/shard_map/pallas_call | solution.py:1031
  52.5 4.9 maximum_select_fusion.1.weight_ref
  57.5 2.7 shard_map.188
  62.4 5.1 collective-permute-done.5
  72.4 14.3 %collective-permute-done.11 = bf16[192,1536]{1,0:T(8,128)(2,1)S(1)} collective-permute-done((bf16[192,1536]{1,0:T(8,128)(2,1)S(1)}, bf16[192,1536]{1,0:T(8,128)(2,1)S(1)}, u32[]{:S(2)}, u32[]{:S(2)}) %collective-permute-start.11) | collective-permute-done | bytes 589856 | tf_op jit(solution)/shard_map/ppermute | solution.py:363
  86.7 3.3 collective-permute-done.12.down_other
  90.0 5.8 %collective-permute-done.8.own_rows = bf16[400,1536]{1,0:T(8,128)(2,1)} collective-permute-done((bf16[400,1536]{1,0:T(8,128)(2,1)S(1)}, bf16[400,1536]{1,0:T(8,128)(2,1)}, u32[]{:S(2)}, u32[]{:S(2)}) %collective-permute-start.8) | collective-permute-done | bytes 1228832 | tf_op jit(solution)/shard_map/ppermute | solution.py:388
  99.4 2.3 constant_dynamic-slice_fusion.18
  102.4 20.9 %shard_map.189 = (bf16[384,1536]{1,0:T(8,128)(2,1)S(1)}, bf16[384,1536]{1,0:T(8,128)(2,1)}, bf16[400,1536]{1,0:T(8,128)(2,1)}, bf16[400,1536]{1,0:T(8,128)(2,1)}...) custom-call(s32[2]{0:T(128)S(1)} %pad_add_fusion.choice, ...), custom_call_target="tpu_custom_call" | custom-call | flops 1000 | bytes 1000 | tf_op jit(solution)/shard_map/pallas_call | solution.py:623
  124.6 3.6 collective-permute-start.17
  133.1 21.1 %shard_map.190 = (bf16[384,1536]{1,0:T(8,128)(2,1)S(1)}, bf16[384,1536]{1,0:T(8,128)(2,1)}, bf16[400,1536]{1,0:T(8,128)(2,1)}, bf16[400,1536]{1,0:T(8,128)(2,1)}...) custom-call(s32[2]{0:T(128)S(1)} %pad_add_fusion.choice, ...), custom_call_target="tpu_custom_call", output_to_operand_aliasing={{4}: (9, {}), {5}: (10, {}), {6}: (11, {}), {7}: (12, {})} | custom-call | flops 1000 | bytes 1000 | tf_op jit(solution)/shard_map/pallas_call | solution.py:623
  161.5 20.4 %shard_map.191 = (bf16[384,1536]{1,0:T(8,128)(2,1)S(1)}, bf16[384,1536]{1,0:T(8,128)(2,1)S(1)}, bf16[400,1536]{1,0:T(8,128)(2,1)}, bf16[400,1536]{1,0:T(8,128)(2...) custom-call(s32[2]{0:T(128)S(1)} %pad_add_fusion.choice, ...), custom_call_target="tpu_custom_call", output_to_operand_aliasing={{4}: (9, {}), {5}: (10, {}), {6}: (11, {}), {7}: (12, {})} | custom-call | flops 1000 | bytes 1000 | tf_op jit(solution)/shard_map/pallas_call | solution.py:623
  183.7 4.4 collective-permute-done.22.own_rows
  192.5 20.8 %shard_map.192 = (bf16[384,1536]{1,0:T(8,128)(2,1)S(1)}, bf16[384,1536]{1,0:T(8,128)(2,1)}, bf16[400,1536]{1,0:T(8,128)(2,1)}, bf16[400,1536]{1,0:T(8,128)(2,1)}...) custom-call(s32[2]{0:T(128)S(1)} %pad_add_fusion.choice, ...), custom_call_target="tpu_custom_call", output_to_operand_aliasing={{4}: (9, {}), {5}: (10, {}), {6}: (11, {}), {7}: (12, {})} | custom-call | flops 1000 | bytes 1000 | tf_op jit(solution)/shard_map/pallas_call | solution.py:623
  213.3 5.6 %collective-permute-done.28 = bf16[400,1536]{1,0:T(8,128)(2,1)} collective-permute-done((bf16[400,1536]{1,0:T(8,128)(2,1)}, bf16[400,1536]{1,0:T(8,128)(2,1)}, u32[]{:S(2)}, u32[]{:S(2)}) %collective-permute-start.28) | collective-permute-done | bytes 1228832 | tf_op jit(solution)/shard_map/ppermute | solution.py:388
  219.0 3.3 add_convert_fusion.2
  222.7 13.0 %fusion.11 = bf16[1536,768]{1,0:T(8,128)(2,1)} fusion(bf16[3072,1536]{1,0:T(8,128)(2,1)} %get-tuple-element.374, bf16[3072,1536]{1,0:T(8,128)(2,1)} %get-tuple-element.375), kind=kOutput, calls=%fused_computation.12 | convolution fusion | flops 7248936960 | bytes 16515072 | tf_op jit(solution)/shard_map/dot_general | solution.py:477
  235.8 8.9 %fusion.8 = bf16[1536,768]{1,0:T(8,128)(2,1)} fusion(bf16[3072,1536]{1,0:T(8,128)(2,1)S(1)} %bitcast.63, bf16[3072,1536]{1,0:T(8,128)(2,1)S(1)} %bitcast.61), kind=kOutput, calls=%fused_computation.11 | convolution fusion | flops 7248936960 | bytes 16515072 | tf_op jit(solution)/shard_map/dot_general | solution.py:477
  244.8 7.7 %collective-permute-done.30 = bf16[400,1536]{1,0:T(8,128)(2,1)} collective-permute-done((bf16[400,1536]{1,0:T(8,128)(2,1)}, bf16[400,1536]{1,0:T(8,128)(2,1)}, u32[]{:S(2)}, u32[]{:S(2)}) %collective-permute-start.30) | collective-permute-done | bytes 1228832 | tf_op jit(solution)/shard_map/ppermute | solution.py:388
  254.7 2.7 add_convert_fusion.11
  257.4 6.3 %fusion.20 = bf16[768,768]{1,0:T(8,128)(2,1)S(1)} fusion(bf16[3072,768]{1,0:T(8,128)(2,1)} %get-tuple-element.381, bf16[3072,1536]{1,0:T(8,128)(2,1)S(1)} %bitcast.59), kind=kOutput, calls=%fused_computation.43 | convolution fusion | flops 3624468480 | bytes 10616832 | tf_op jit(solution)/shard_map/dot_general | solution.py:477
  267.4 4.9 fusion.17
  272.3 11.0 %collective-permute-done.34.back_ring.extra_ring = bf16[400,1536]{1,0:T(8,128)(2,1)S(1)} collective-permute-done((bf16[400,1536]{1,0:T(8,128)(2,1)S(1)}, bf16[400,1536]{1,0:T(8,128)(2,1)S(1)}, u32[]{:S(2)}, u32[]{:S(2)}) %collective-permute-start.34) | collective-permute-done | bytes 1228832 | tf_op jit(solution)/shard_map/ppermute | solution.py:388
  286.4 9.7 %shard_map.193 = (f32[384,1536]{1,0:T(8,128)}, bf16[400,1536]{1,0:T(8,128)(2,1)}, bf16[384,1536]{1,0:T(8,128)(2,1)}) custom-call(bf16[400,1536]{1,0:T(8,128)(2,1)} %get-tuple-element.391.back_own.extra_own, bf16[400,1536]{1,0:T(8,128)(2,1)} %collective-permute-done.32.back_other.extra_other, bf16[400,1536]{1,0:T(8,128)(2,1)} %copy-done.61, ...), custom_call_target="tpu_custom_call" | custom-call | flops 1000 | bytes 1000 | tf_op jit(solution)/shard_map/pallas_call | solution.py:734
  298.7 8.8 %shard_map.194.right_own.grad_ref = bf16[384,2048]{1,0:T(8,128)(2,1)S(1)} custom-call(bf16[384,1536]{1,0:T(8,128)(2,1)S(1)} %copy-done.36, bf16[384,256]{1,0:T(8,128)(2,1)S(1)} %copy-done.51, bf16[384,256]{1,0:T(8,128)(2,1)S(1)} %copy-done.53, bf16[384,1536]{1,0:T(8,128)(2,1)S(1)} %copy-done.43, f32[384,128]{1,0:T(8,128)S(1)} %get-tuple-element.283.cos_ref, ...), custom_call_target="tpu_custom_call" | custom-call | flops 1000 | bytes 1000 | tf_op jit(solution)/shard_map/pallas_call | solution.py:1111
  307.6 7.8 %collective-permute-done.36 = bf16[384,1536]{1,0:T(8,128)(2,1)} collective-permute-done((bf16[384,1536]{1,0:T(8,128)(2,1)}, bf16[384,1536]{1,0:T(8,128)(2,1)}, u32[]{:S(2)}, u32[]{:S(2)}) %collective-permute-start.36) | collective-permute-done | bytes 1179680 | tf_op jit(solution)/shard_map/ppermute | solution.py:388
  318.0 3.0 add_convert_fusion
  322.6 2.7 add_convert_fusion.9
  325.3 3.2 add_convert_fusion.10
  328.5 5.9 %shard_map.195 = (bf16[192,2048]{1,0:T(8,128)(2,1)S(1)}, bf16[192,2048]{1,0:T(8,128)(2,1)}, bf16[192,2048]{1,0:T(8,128)(2,1)S(1)}, bf16[192,2048]{1,0:T(8,128)(2,1)}) custom-call(s32[3]{0:T(128)S(1)} %pad_add_fusion.1.place_ref, bf16[384,1536]{1,0:T(8,128)(2,1)S(1)} %copy-done.23, bf16[384,1536]{1,0:T(8,128)(2,1)S(1)} %copy-done.40, ...), custom_call_target="tpu_custom_call" | custom-call | flops 1000 | bytes 1000 | tf_op jit(solution)/shard_map/pallas_call | solution.py:887
  339.8 3.0 collective-permute-start.45
  343.3 3.4 collective-permute-start.47
  348.0 2.8 copy-done.4
  353.7 3.3 shard_map.197
  357.1 4.4 shard_map.196
  367.8 4.0 collective-permute-done.44
  377.5 3.4 collective-permute-start.51
  382.9 2.6 collective-permute-done.50
  386.9 10.7 %collective-permute-done.49 = bf16[96,2048]{1,0:T(8,128)(2,1)S(1)} collective-permute-done((bf16[96,2048]{1,0:T(8,128)(2,1)S(1)}, bf16[96,2048]{1,0:T(8,128)(2,1)S(1)}, u32[]{:S(2)}, u32[]{:S(2)}) %collective-permute-start.49) | collective-permute-done | bytes 393248 | tf_op jit(solution)/shard_map/ppermute | solution.py:363
  399.7 6.3 %collective-permute-done.53 = bf16[384,1536]{1,0:T(8,128)(2,1)S(1)} collective-permute-done((bf16[384,1536]{1,0:T(8,128)(2,1)S(1)}, bf16[384,1536]{1,0:T(8,128)(2,1)S(1)}, u32[]{:S(2)}, u32[]{:S(2)}) %collective-permute-start.53) | collective-permute-done | bytes 1179680 | tf_op jit(solution)/shard_map/ppermute | solution.py:388
  409.4 2.9 collective-permute-start.59
  414.5 2.8 collective-permute-done.57
  417.3 7.9 %collective-permute-done.58 = bf16[48,2048]{1,0:T(8,128)(2,1)S(1)} collective-permute-done((bf16[48,2048]{1,0:T(8,128)(2,1)S(1)}, bf16[48,2048]{1,0:T(8,128)(2,1)S(1)}, u32[]{:S(2)}, u32[]{:S(2)}) %collective-permute-start.58) | collective-permute-done | bytes 196640 | tf_op jit(solution)/shard_map/ppermute | solution.py:383
  435.3 3.1 collective-permute-start.60
  438.4 6.6 %collective-permute-done.63 = bf16[48,2048]{1,0:T(8,128)(2,1)S(1)} collective-permute-done((bf16[48,2048]{1,0:T(8,128)(2,1)S(1)}, bf16[48,2048]{1,0:T(8,128)(2,1)S(1)}, u32[]{:S(2)}, u32[]{:S(2)}) %collective-permute-start.63) | collective-permute-done | bytes 196640 | tf_op jit(solution)/shard_map/ppermute | solution.py:383
  445.3 7.0 %collective-permute-done.60 = bf16[96,1664]{1,0:T(8,128)(2,1)S(1)} collective-permute-done((bf16[96,1664]{1,0:T(8,128)(2,1)S(1)}, bf16[96,1664]{1,0:T(8,128)(2,1)S(1)}, u32[]{:S(2)}, u32[]{:S(2)}) %collective-permute-start.60) | collective-permute-done | bytes 319520 | tf_op jit(solution)/shard_map/ppermute | solution.py:363
  459.8 2.7 collective-permute-done.66
  462.4 4.1 collective-permute-done.67
  467.0 2.9 collective-permute-start.71
  470.0 2.4 collective-permute-start.73
  474.5 8.4 %collective-permute-done.72 = bf16[48,1664]{1,0:T(8,128)(2,1)S(1)} collective-permute-done((bf16[48,1664]{1,0:T(8,128)(2,1)S(1)}, bf16[48,1664]{1,0:T(8,128)(2,1)S(1)}, u32[]{:S(2)}, u32[]{:S(2)}) %collective-permute-start.72) | collective-permute-done | bytes 159776 | tf_op jit(solution)/shard_map/ppermute | solution.py:383
  483.2 7.0 %collective-permute-done.74.refs_1_ = bf16[192,2048]{1,0:T(8,128)(2,1)S(1)} collective-permute-done((bf16[192,2048]{1,0:T(8,128)(2,1)S(1)}, bf16[192,2048]{1,0:T(8,128)(2,1)S(1)}, u32[]{:S(2)}, u32[]{:S(2)}) %collective-permute-start.74) | collective-permute-done | bytes 786464 | tf_op jit(solution)/shard_map/ppermute | solution.py:374
  493.4 4.0 shard_map.198
  497.4 4.7 collective-permute-done.76
  506.4 3.1 bitcast_convert_fusion
  509.5 9.6 %collective-permute-done.80.refs_1_ = bf16[192,1664]{1,0:T(8,128)(2,1)S(1)} collective-permute-done((bf16[192,1664]{1,0:T(8,128)(2,1)S(1)}, bf16[192,1664]{1,0:T(8,128)(2,1)S(1)}, u32[]{:S(2)}, u32[]{:S(2)}) %collective-permute-start.80) | collective-permute-done | bytes 639008 | tf_op jit(solution)/shard_map/ppermute | solution.py:374
  519.2 3.7 shard_map.199
  (453 shorter events, 122.7 us)
Async XLA Ops:
  4.6 13.6 %collective-permute-start.1 = (bf16[768,2048]{1,0:T(8,128)(2,1)}, bf16[768,2048]{1,0:T(8,128)(2,1)}, u32[]{:S(2)}, u32[]{:S(2)}) collective-permute-start(bf16[768,2048]{1,0:T(8,128)(2,1)} %refs_4_.1), channel_id=1, source_target_pairs={{0,1},{1,0},{2,3},{3,2},{4,5},{5,4},{6,7},{7,6},{8,9},{9,8},{10,11... | collective-permute-start | bytes 9437192 | tf_op jit(solution)/shard_map/ppermute | solution.py:359
  5.1 21.3 %collective-permute-start.2 = (bf16[192,1536]{1,0:T(8,128)(2,1)S(1)}, bf16[192,1536]{1,0:T(8,128)(2,1)S(1)}, u32[]{:S(2)}, u32[]{:S(2)}) collective-permute-start(bf16[192,1536]{1,0:T(8,128)(2,1)S(1)} %constant_dynamic-slice_fusion.24), channel_id=1, source_target_pairs={{0,16},{16,0},{1,17},{17,1},{2,18},{18,2},{3,19},{19,3},{4,20},{20... | collective-permute-start | bytes 1769480 | tf_op jit(solution)/shard_map/ppermute | solution.py:363
  7.7 30.3 %collective-permute-start = (bf16[400,1536]{1,0:T(8,128)(2,1)}, bf16[400,1536]{1,0:T(8,128)(2,1)}, u32[]{:S(2)}, u32[]{:S(2)}) collective-permute-start(bf16[400,1536]{1,0:T(8,128)(2,1)} %pad_maximum_fusion), channel_id=1, source_target_pairs={{0,4},{2,6},{4,12},{6,14},{8,0},{10,2},{12,8},{14,10},{1,5},{3,7},... | collective-permute-start | bytes 3686408 | tf_op jit(solution)/shard_map/ppermute | solution.py:388
  9.4 58.1 %collective-permute-start.7 = (bf16[1536,1536]{1,0:T(8,128)(2,1)}, bf16[1536,1536]{1,0:T(8,128)(2,1)}, u32[]{:S(2)}, u32[]{:S(2)}) collective-permute-start(bf16[1536,1536]{1,0:T(8,128)(2,1)} %bitcast.64), channel_id=1, source_target_pairs={{0,2},{3,1},{4,6},{7,5},{8,10},{11,9},{12,14},{15,13},{16,18},{19,... | collective-permute-start | bytes 14155784 | tf_op jit(solution)/shard_map/ppermute | solution.py:398
  17.5 20.5 %collective-permute-start.4 = (bf16[768,1536]{1,0:T(8,128)(2,1)}, bf16[768,1536]{1,0:T(8,128)(2,1)}, u32[]{:S(2)}, u32[]{:S(2)}) collective-permute-start(bf16[768,1536]{1,0:T(8,128)(2,1)} %param.20), channel_id=1, source_target_pairs={{0,1},{1,0},{2,3},{3,2},{4,5},{5,4},{6,7},{7,6},{8,9},{9,8},{10,11... | collective-permute-start | bytes 7077896 | tf_op jit(solution)/shard_map/ppermute | solution.py:359
  38.0 29.5 %collective-permute-start.5 = (bf16[400,1536]{1,0:T(8,128)(2,1)}, bf16[400,1536]{1,0:T(8,128)(2,1)}, u32[]{:S(2)}, u32[]{:S(2)}) collective-permute-start(bf16[400,1536]{1,0:T(8,128)(2,1)} %collective-permute-done), channel_id=1, source_target_pairs={{0,4},{2,6},{4,12},{6,14},{8,0},{10,2},{12,8},{14,10},{1,5},{3,7},... | collective-permute-start | bytes 3686408 | tf_op jit(solution)/shard_map/ppermute | solution.py:388
  40.8 21.5 %collective-permute-start.6 = (bf16[192,1536]{1,0:T(8,128)(2,1)S(1)}, bf16[192,1536]{1,0:T(8,128)(2,1)S(1)}, u32[]{:S(2)}, u32[]{:S(2)}) collective-permute-start(bf16[192,1536]{1,0:T(8,128)(2,1)S(1)} %get-tuple-element.582), channel_id=1, source_target_pairs={{0,16},{16,0},{1,17},{17,1},{2,18},{18,2},{3,19},{19,3},{4,20},{20... | collective-permute-start | bytes 1769480 | tf_op jit(solution)/shard_map/ppermute | solution.py:363
  41.4 48.6 %collective-permute-start.12 = (bf16[768,1536]{1,0:T(8,128)(2,1)}, bf16[768,1536]{1,0:T(8,128)(2,1)S(1)}, u32[]{:S(2)}, u32[]{:S(2)}) collective-permute-start(bf16[768,1536]{1,0:T(8,128)(2,1)} %bitcast.71), channel_id=1, source_target_pairs={{0,2},{3,1},{4,6},{7,5},{8,10},{11,9},{12,14},{15,13},{16,18},{19,... | collective-permute-start | bytes 7077896 | tf_op jit(solution)/shard_map/ppermute | solution.py:398
  67.5 28.3 %collective-permute-start.8 = (bf16[400,1536]{1,0:T(8,128)(2,1)S(1)}, bf16[400,1536]{1,0:T(8,128)(2,1)}, u32[]{:S(2)}, u32[]{:S(2)}) collective-permute-start(bf16[400,1536]{1,0:T(8,128)(2,1)S(1)} %get-tuple-element.304.own_rows.refs_1_), channel_id=1, source_target_pairs={{0,4},{2,6},{4,12},{6,14},{8,0},{10,2},{12,8},{14,10},{1,5},{3,7},... | collective-permute-start | bytes 3686408 | tf_op jit(solution)/shard_map/ppermute | solution.py:388
  68.3 27.6 %collective-permute-start.9 = (bf16[400,1536]{1,0:T(8,128)(2,1)S(1)}, bf16[400,1536]{1,0:T(8,128)(2,1)S(1)}, u32[]{:S(2)}, u32[]{:S(2)}) collective-permute-start(bf16[400,1536]{1,0:T(8,128)(2,1)S(1)} %get-tuple-element.304.own_rows.refs_1_), channel_id=1, source_target_pairs={{0,1},{1,0},{2,3},{3,2},{4,5},{5,4},{6,7},{7,6},{8,9},{9,8},{10,11... | collective-permute-start | bytes 3686408 | tf_op jit(solution)/shard_map/ppermute | solution.py:359
  69.1 20.9 %collective-permute-start.10 = (bf16[384,1536]{1,0:T(8,128)(2,1)S(1)}, bf16[384,1536]{1,0:T(8,128)(2,1)S(1)}, u32[]{:S(2)}, u32[]{:S(2)}) collective-permute-start(bf16[384,1536]{1,0:T(8,128)(2,1)S(1)} %convolution_convert_fusion.5.own_ct.ct_ref), channel_id=1, source_target_pairs={{0,1},{1,0},{2,3},{3,2},{4,5},{5,4},{6,7},{7,6},{8,9},{9,8},{10,11... | collective-permute-start | bytes 3538952 | tf_op jit(solution)/shard_map/ppermute | solution.py:359
  71.0 15.7 %collective-permute-start.11 = (bf16[192,1536]{1,0:T(8,128)(2,1)S(1)}, bf16[192,1536]{1,0:T(8,128)(2,1)S(1)}, u32[]{:S(2)}, u32[]{:S(2)}) collective-permute-start(bf16[192,1536]{1,0:T(8,128)(2,1)S(1)} %get-tuple-element.580), channel_id=1, source_target_pairs={{0,16},{16,0},{1,17},{17,1},{2,18},{18,2},{3,19},{19,3},{4,20},{20... | collective-permute-start | bytes 1769480 | tf_op jit(solution)/shard_map/ppermute | solution.py:363
  95.8 28.8 %collective-permute-start.13 = (bf16[400,1536]{1,0:T(8,128)(2,1)}, bf16[400,1536]{1,0:T(8,128)(2,1)}, u32[]{:S(2)}, u32[]{:S(2)}) collective-permute-start(bf16[400,1536]{1,0:T(8,128)(2,1)} %collective-permute-done.5), channel_id=1, source_target_pairs={{0,4},{2,6},{4,12},{6,14},{8,0},{10,2},{12,8},{14,10},{1,5},{3,7},... | collective-permute-start | bytes 3686408 | tf_op jit(solution)/shard_map/ppermute | solution.py:388
  97.0 27.6 %collective-permute-start.15 = (bf16[400,1536]{1,0:T(8,128)(2,1)}, bf16[400,1536]{1,0:T(8,128)(2,1)}, u32[]{:S(2)}, u32[]{:S(2)}) collective-permute-start(bf16[400,1536]{1,0:T(8,128)(2,1)} %collective-permute-done.8.own_rows), channel_id=1, source_target_pairs={{0,1},{1,0},{2,3},{3,2},{4,5},{5,4},{6,7},{7,6},{8,9},{9,8},{10,11... | collective-permute-start | bytes 3686408 | tf_op jit(solution)/shard_map/ppermute | solution.py:359
  98.9 25.8 %collective-permute-start.14 = (bf16[384,1536]{1,0:T(8,128)(2,1)}, bf16[384,1536]{1,0:T(8,128)(2,1)}, u32[]{:S(2)}, u32[]{:S(2)}) collective-permute-start(bf16[384,1536]{1,0:T(8,128)(2,1)} %convolution_convert_fusion.4.own_ct), channel_id=1, source_target_pairs={{0,1},{1,0},{2,3},{3,2},{4,5},{5,4},{6,7},{7,6},{8,9},{9,8},{10,11... | collective-permute-start | bytes 3538952 | tf_op jit(solution)/shard_map/ppermute | solution.py:359
  101.8 22.4 %collective-permute-start.16 = (bf16[192,1536]{1,0:T(8,128)(2,1)}, bf16[192,1536]{1,0:T(8,128)(2,1)}, u32[]{:S(2)}, u32[]{:S(2)}) collective-permute-start(bf16[192,1536]{1,0:T(8,128)(2,1)} %get-tuple-element.578), channel_id=1, source_target_pairs={{0,16},{16,0},{1,17},{17,1},{2,18},{18,2},{3,19},{19,3},{4,20},{20... | collective-permute-start | bytes 1769480 | tf_op jit(solution)/shard_map/ppermute | solution.py:363
  102.3 52.8 %collective-permute-start.20 = (bf16[384,1536]{1,0:T(8,128)(2,1)S(1)}, bf16[384,1536]{1,0:T(8,128)(2,1)S(1)}, u32[]{:S(2)}, u32[]{:S(2)}) collective-permute-start(bf16[384,1536]{1,0:T(8,128)(2,1)S(1)} %copy-done.19), channel_id=1, source_target_pairs={{0,1},{1,0},{2,3},{3,2},{4,5},{5,4},{6,7},{7,6},{8,9},{9,8},{10,11... | collective-permute-start | bytes 3538952 | tf_op jit(solution)/shard_map/ppermute | solution.py:359
  124.2 31.0 %collective-permute-start.21 = (bf16[384,1536]{1,0:T(8,128)(2,1)S(1)}, bf16[384,1536]{1,0:T(8,128)(2,1)S(1)}, u32[]{:S(2)}, u32[]{:S(2)}) collective-permute-start(bf16[384,1536]{1,0:T(8,128)(2,1)S(1)} %copy-done.22), channel_id=1, source_target_pairs={{0,1},{1,0},{2,3},{3,2},{4,5},{5,4},{6,7},{7,6},{8,9},{9,8},{10,11... | collective-permute-start | bytes 3538952 | tf_op jit(solution)/shard_map/ppermute | solution.py:359
  124.6 31.6 %collective-permute-start.17 = (bf16[400,1536]{1,0:T(8,128)(2,1)}, bf16[400,1536]{1,0:T(8,128)(2,1)S(1)}, u32[]{:S(2)}, u32[]{:S(2)}) collective-permute-start(bf16[400,1536]{1,0:T(8,128)(2,1)} %collective-permute-done.8.own_rows), channel_id=1, source_target_pairs={{0,4},{2,6},{4,12},{6,14},{8,0},{10,2},{12,8},{14,10},{1,5},{3,7},... | collective-permute-start | bytes 3686408 | tf_op jit(solution)/shard_map/ppermute | solution.py:388
  130.1 26.1 %collective-permute-start.19 = (bf16[384,1536]{1,0:T(8,128)(2,1)S(1)}, bf16[384,1536]{1,0:T(8,128)(2,1)S(1)}, u32[]{:S(2)}, u32[]{:S(2)}) collective-permute-start(bf16[384,1536]{1,0:T(8,128)(2,1)S(1)} %convolution_convert_fusion.3.own_ct), channel_id=1, source_target_pairs={{0,1},{1,0},{2,3},{3,2},{4,5},{5,4},{6,7},{7,6},{8,9},{9,8},{10,11... | collective-permute-start | bytes 3538952 | tf_op jit(solution)/shard_map/ppermute | solution.py:359
  131.5 24.7 %collective-permute-start.18 = (bf16[192,1536]{1,0:T(8,128)(2,1)S(1)}, bf16[192,1536]{1,0:T(8,128)(2,1)S(1)}, u32[]{:S(2)}, u32[]{:S(2)}) collective-permute-start(bf16[192,1536]{1,0:T(8,128)(2,1)S(1)} %get-tuple-element.576), channel_id=1, source_target_pairs={{0,16},{16,0},{1,17},{17,1},{2,18},{18,2},{3,19},{19,3},{4,20},{20... | collective-permute-start | bytes 1769480 | tf_op jit(solution)/shard_map/ppermute | solution.py:363
  157.3 24.6 %collective-permute-start.23 = (bf16[400,1536]{1,0:T(8,128)(2,1)}, bf16[400,1536]{1,0:T(8,128)(2,1)S(1)}, u32[]{:S(2)}, u32[]{:S(2)}) collective-permute-start(bf16[400,1536]{1,0:T(8,128)(2,1)} %get-tuple-element.334), channel_id=1, source_target_pairs={{0,1},{1,0},{2,3},{3,2},{4,5},{5,4},{6,7},{7,6},{8,9},{9,8},{10,11... | collective-permute-start | bytes 3686408 | tf_op jit(solution)/shard_map/ppermute | solution.py:359
  157.6 30.6 %collective-permute-start.22 = (bf16[400,1536]{1,0:T(8,128)(2,1)S(1)}, bf16[400,1536]{1,0:T(8,128)(2,1)}, u32[]{:S(2)}, u32[]{:S(2)}) collective-permute-start(bf16[400,1536]{1,0:T(8,128)(2,1)S(1)} %collective-permute-done.17.own_rows), channel_id=1, source_target_pairs={{0,4},{2,6},{4,12},{6,14},{8,0},{10,2},{12,8},{14,10},{1,5},{3,7},... | collective-permute-start | bytes 3686408 | tf_op jit(solution)/shard_map/ppermute | solution.py:388
  160.4 23.4 %collective-permute-start.24 = (bf16[384,1536]{1,0:T(8,128)(2,1)S(1)}, bf16[384,1536]{1,0:T(8,128)(2,1)S(1)}, u32[]{:S(2)}, u32[]{:S(2)}) collective-permute-start(bf16[384,1536]{1,0:T(8,128)(2,1)S(1)} %convolution_convert_fusion.2.own_ct), channel_id=1, source_target_pairs={{0,1},{1,0},{2,3},{3,2},{4,5},{5,4},{6,7},{7,6},{8,9},{9,8},{10,11... | collective-permute-start | bytes 3538952 | tf_op jit(solution)/shard_map/ppermute | solution.py:359
  188.1 30.8 %collective-permute-start.28 = (bf16[400,1536]{1,0:T(8,128)(2,1)}, bf16[400,1536]{1,0:T(8,128)(2,1)}, u32[]{:S(2)}, u32[]{:S(2)}) collective-permute-start(bf16[400,1536]{1,0:T(8,128)(2,1)} %add_convert_fusion.3), channel_id=1, source_target_pairs={{0,4},{2,6},{4,12},{6,14},{8,0},{10,2},{12,8},{14,10},{1,5},{3,7},... | collective-permute-start | bytes 3686408 | tf_op jit(solution)/shard_map/ppermute | solution.py:388
  188.3 30.6 %collective-permute-start.29 = (bf16[400,1536]{1,0:T(8,128)(2,1)}, bf16[400,1536]{1,0:T(8,128)(2,1)}, u32[]{:S(2)}, u32[]{:S(2)}) collective-permute-start(bf16[400,1536]{1,0:T(8,128)(2,1)} %get-tuple-element.360), channel_id=1, source_target_pairs={{0,1},{1,0},{2,3},{3,2},{4,5},{5,4},{6,7},{7,6},{8,9},{9,8},{10,11... | collective-permute-start | bytes 3686408 | tf_op jit(solution)/shard_map/ppermute | solution.py:359
  188.9 55.9 %collective-permute-start.32 = (bf16[400,1536]{1,0:T(8,128)(2,1)}, bf16[400,1536]{1,0:T(8,128)(2,1)}, u32[]{:S(2)}, u32[]{:S(2)}) collective-permute-start(bf16[400,1536]{1,0:T(8,128)(2,1)} %get-tuple-element.372), channel_id=1, source_target_pairs={{0,1},{1,0},{2,3},{3,2},{4,5},{5,4},{6,7},{7,6},{8,9},{9,8},{10,11... | collective-permute-start | bytes 3686408 | tf_op jit(solution)/shard_map/ppermute | solution.py:359
  189.0 55.8 %collective-permute-start.33 = (bf16[384,1536]{1,0:T(8,128)(2,1)}, bf16[384,1536]{1,0:T(8,128)(2,1)}, u32[]{:S(2)}, u32[]{:S(2)}) collective-permute-start(bf16[384,1536]{1,0:T(8,128)(2,1)} %get-tuple-element.373), channel_id=1, source_target_pairs={{0,1},{1,0},{2,3},{3,2},{4,5},{5,4},{6,7},{7,6},{8,9},{9,8},{10,11... | collective-permute-start | bytes 3538952 | tf_op jit(solution)/shard_map/ppermute | solution.py:359
  192.3 80.0 %collective-permute-start.35 = (bf16[384,1536]{1,0:T(8,128)(2,1)}, bf16[384,1536]{1,0:T(8,128)(2,1)}, u32[]{:S(2)}, u32[]{:S(2)}) collective-permute-start(bf16[384,1536]{1,0:T(8,128)(2,1)} %copy-done.59), channel_id=1, source_target_pairs={{0,1},{1,0},{2,3},{3,2},{4,5},{5,4},{6,7},{7,6},{8,9},{9,8},{10,11... | collective-permute-start | bytes 3538952 | tf_op jit(solution)/shard_map/ppermute | solution.py:359
  222.3 30.1 %collective-permute-start.30 = (bf16[400,1536]{1,0:T(8,128)(2,1)}, bf16[400,1536]{1,0:T(8,128)(2,1)}, u32[]{:S(2)}, u32[]{:S(2)}) collective-permute-start(bf16[400,1536]{1,0:T(8,128)(2,1)} %add_convert_fusion.2), channel_id=1, source_target_pairs={{0,4},{2,6},{4,12},{6,14},{8,0},{10,2},{12,8},{14,10},{1,5},{3,7},... | collective-permute-start | bytes 3686408 | tf_op jit(solution)/shard_map/ppermute | solution.py:388
  222.6 29.9 %collective-permute-start.31 = (bf16[400,1536]{1,0:T(8,128)(2,1)}, bf16[400,1536]{1,0:T(8,128)(2,1)S(1)}, u32[]{:S(2)}, u32[]{:S(2)}) collective-permute-start(bf16[400,1536]{1,0:T(8,128)(2,1)} %get-tuple-element.371), channel_id=1, source_target_pairs={{0,1},{1,0},{2,3},{3,2},{4,5},{5,4},{6,7},{7,6},{8,9},{9,8},{10,11... | collective-permute-start | bytes 3686408 | tf_op jit(solution)/shard_map/ppermute | solution.py:359
  254.2 29.1 %collective-permute-start.34 = (bf16[400,1536]{1,0:T(8,128)(2,1)S(1)}, bf16[400,1536]{1,0:T(8,128)(2,1)S(1)}, u32[]{:S(2)}, u32[]{:S(2)}) collective-permute-start(bf16[400,1536]{1,0:T(8,128)(2,1)S(1)} %add_convert_fusion.1), channel_id=1, source_target_pairs={{0,4},{2,6},{4,12},{6,14},{8,0},{10,2},{12,8},{14,10},{1,5},{3,7},... | collective-permute-start | bytes 3686408 | tf_op jit(solution)/shard_map/ppermute | solution.py:388
  283.3 32.1 %collective-permute-start.38 = (bf16[1536,768]{1,0:T(8,128)(2,1)}, bf16[1536,768]{1,0:T(8,128)(2,1)}, u32[]{:S(2)}, u32[]{:S(2)}) collective-permute-start(bf16[1536,768]{1,0:T(8,128)(2,1)} %fusion.8), channel_id=1, source_target_pairs={{1,3},{2,0},{5,7},{6,4},{9,11},{10,8},{13,15},{14,12},{17,19},{18,... | collective-permute-start | bytes 7077896 | tf_op jit(solution)/shard_map/ppermute | solution.py:393
  284.6 23.0 %collective-permute-start.27 = (bf16[384,1536]{1,0:T(8,128)(2,1)}, bf16[384,1536]{1,0:T(8,128)(2,1)}, u32[]{:S(2)}, u32[]{:S(2)}) collective-permute-start(bf16[384,1536]{1,0:T(8,128)(2,1)} %get-tuple-element.358), channel_id=1, source_target_pairs={{0,1},{1,0},{2,3},{3,2},{4,5},{5,4},{6,7},{7,6},{8,9},{9,8},{10,11... | collective-permute-start | bytes 3538952 | tf_op jit(solution)/shard_map/ppermute | solution.py:359
  285.8 21.8 %collective-permute-start.37 = (bf16[384,1536]{1,0:T(8,128)(2,1)}, bf16[384,1536]{1,0:T(8,128)(2,1)}, u32[]{:S(2)}, u32[]{:S(2)}) collective-permute-start(bf16[384,1536]{1,0:T(8,128)(2,1)} %get-tuple-element.387), channel_id=1, source_target_pairs={{0,1},{1,0},{2,3},{3,2},{4,5},{5,4},{6,7},{7,6},{8,9},{9,8},{10,11... | collective-permute-start | bytes 3538952 | tf_op jit(solution)/shard_map/ppermute | solution.py:359
  285.8 29.6 %collective-permute-start.36 = (bf16[384,1536]{1,0:T(8,128)(2,1)}, bf16[384,1536]{1,0:T(8,128)(2,1)}, u32[]{:S(2)}, u32[]{:S(2)}) collective-permute-start(bf16[384,1536]{1,0:T(8,128)(2,1)} %add_convert_fusion.11), channel_id=1, source_target_pairs={{0,4},{2,6},{4,12},{6,14},{8,0},{10,2},{12,8},{14,10},{1,5},{3,7},... | collective-permute-start | bytes 3538952 | tf_op jit(solution)/shard_map/ppermute | solution.py:388
  285.8 29.6 %collective-permute-start.39 = (bf16[768,768]{1,0:T(8,128)(2,1)}, bf16[768,768]{1,0:T(8,128)(2,1)}, u32[]{:S(2)}, u32[]{:S(2)}) collective-permute-start(bf16[768,768]{1,0:T(8,128)(2,1)} %get-tuple-element.401), channel_id=1, source_target_pairs={{0,16},{16,0},{1,17},{17,1},{2,18},{18,2},{3,19},{19,3},{4,20},{20... | collective-permute-start | bytes 3538952 | tf_op jit(solution)/shard_map/ppermute | solution.py:363
  315.4 13.1 %collective-permute-start.41 = (bf16[384,2048]{1,0:T(8,128)(2,1)S(1)}, bf16[384,2048]{1,0:T(8,128)(2,1)S(1)}, u32[]{:S(2)}, u32[]{:S(2)}) collective-permute-start(bf16[384,2048]{1,0:T(8,128)(2,1)S(1)} %shard_map.194.right_own.grad_ref), channel_id=1, source_target_pairs={{0,1},{1,0},{2,3},{3,2},{4,5},{5,4},{6,7},{7,6},{8,9},{9,8},{10,11... | collective-permute-start | bytes 4718600 | tf_op jit(solution)/shard_map/ppermute | solution.py:359
  315.4 20.8 %collective-permute-start.40 = (bf16[400,1536]{1,0:T(8,128)(2,1)S(1)}, bf16[400,1536]{1,0:T(8,128)(2,1)S(1)}, u32[]{:S(2)}, u32[]{:S(2)}) collective-permute-start(bf16[400,1536]{1,0:T(8,128)(2,1)S(1)} %copy-done.6), channel_id=1, source_target_pairs={{0,1},{1,0},{2,3},{3,2},{4,5},{5,4},{6,7},{7,6},{8,9},{9,8},{10,11... | collective-permute-start | bytes 3686408 | tf_op jit(solution)/shard_map/ppermute | solution.py:359
  315.9 20.3 %collective-permute-start.42 = (bf16[768,768]{1,0:T(8,128)(2,1)S(1)}, bf16[768,768]{1,0:T(8,128)(2,1)S(1)}, u32[]{:S(2)}, u32[]{:S(2)}) collective-permute-start(bf16[768,768]{1,0:T(8,128)(2,1)S(1)} %copy-done.78), channel_id=1, source_target_pairs={{1,3},{2,0},{5,7},{6,4},{9,11},{10,8},{13,15},{14,12},{17,19},{18,... | collective-permute-start | bytes 3538952 | tf_op jit(solution)/shard_map/ppermute | solution.py:393
  317.4 18.8 %collective-permute-start.43 = (bf16[384,768]{1,0:T(8,128)(2,1)S(1)}, bf16[384,768]{1,0:T(8,128)(2,1)S(1)}, u32[]{:S(2)}, u32[]{:S(2)}) collective-permute-start(bf16[384,768]{1,0:T(8,128)(2,1)S(1)} %copy-done.86), channel_id=1, source_target_pairs={{0,16},{16,0},{1,17},{17,1},{2,18},{18,2},{3,19},{19,3},{4,20},{20... | collective-permute-start | bytes 1769480 | tf_op jit(solution)/shard_map/ppermute | solution.py:363
  338.3 23.2 %collective-permute-start.46 = (bf16[192,2048]{1,0:T(8,128)(2,1)}, bf16[192,2048]{1,0:T(8,128)(2,1)}, u32[]{:S(2)}, u32[]{:S(2)}) collective-permute-start(bf16[192,2048]{1,0:T(8,128)(2,1)} %get-tuple-element.432), channel_id=1, source_target_pairs={{0,16},{16,0},{1,17},{17,1},{2,18},{18,2},{3,19},{19,3},{4,20},{20... | collective-permute-start | bytes 2359304 | tf_op jit(solution)/shard_map/ppermute | solution.py:363
  339.8 23.2 %collective-permute-start.45 = (bf16[192,2048]{1,0:T(8,128)(2,1)}, bf16[192,2048]{1,0:T(8,128)(2,1)}, u32[]{:S(2)}, u32[]{:S(2)}) collective-permute-start(bf16[192,2048]{1,0:T(8,128)(2,1)} %get-tuple-element.430), channel_id=1, source_target_pairs={{0,2},{2,0},{4,6},{6,4},{8,10},{10,8},{12,14},{14,12},{1,3},{3,1},... | collective-permute-start | bytes 2359304 | tf_op jit(solution)/shard_map/ppermute | solution.py:374
  342.9 28.9 %collective-permute-start.44 = (bf16[384,1536]{1,0:T(8,128)(2,1)}, bf16[384,1536]{1,0:T(8,128)(2,1)S(1)}, u32[]{:S(2)}, u32[]{:S(2)}) collective-permute-start(bf16[384,1536]{1,0:T(8,128)(2,1)} %add_convert_fusion.10), channel_id=1, source_target_pairs={{0,4},{2,6},{4,12},{6,14},{8,0},{10,2},{12,8},{14,10},{1,5},{3,7},... | collective-permute-start | bytes 3538952 | tf_op jit(solution)/shard_map/ppermute | solution.py:388
  343.3 30.3 %collective-permute-start.47 = (bf16[768,768]{1,0:T(8,128)(2,1)}, bf16[768,768]{1,0:T(8,128)(2,1)S(1)}, u32[]{:S(2)}, u32[]{:S(2)}) collective-permute-start(bf16[768,768]{1,0:T(8,128)(2,1)} %get-tuple-element.447), channel_id=1, source_target_pairs={{0,16},{3,19},{4,20},{7,23},{8,24},{11,27},{12,28},{15,31},{16,0},... | collective-permute-start | bytes 3538952 | tf_op jit(solution)/shard_map/ppermute | solution.py:370
  346.7 27.4 %collective-permute-start.48 = (bf16[768,768]{1,0:T(8,128)(2,1)}, bf16[768,768]{1,0:T(8,128)(2,1)S(1)}, u32[]{:S(2)}, u32[]{:S(2)}) collective-permute-start(bf16[768,768]{1,0:T(8,128)(2,1)} %add_convert_fusion.9), channel_id=1, source_target_pairs={{1,3},{2,0},{5,7},{6,4},{9,11},{10,8},{13,15},{14,12},{17,19},{18,... | collective-permute-start | bytes 3538952 | tf_op jit(solution)/shard_map/ppermute | solution.py:393
  374.9 23.4 %collective-permute-start.54 = (bf16[192,1536]{1,0:T(8,128)(2,1)S(1)}, bf16[192,1536]{1,0:T(8,128)(2,1)S(1)}, u32[]{:S(2)}, u32[]{:S(2)}) collective-permute-start(bf16[192,1536]{1,0:T(8,128)(2,1)S(1)} %get-tuple-element.589), channel_id=1, source_target_pairs={{0,16},{16,0},{1,17},{17,1},{2,18},{18,2},{3,19},{19,3},{4,20},{20... | collective-permute-start | bytes 1769480 | tf_op jit(solution)/shard_map/ppermute | solution.py:363
  375.6 22.0 %collective-permute-start.49 = (bf16[96,2048]{1,0:T(8,128)(2,1)S(1)}, bf16[96,2048]{1,0:T(8,128)(2,1)S(1)}, u32[]{:S(2)}, u32[]{:S(2)}) collective-permute-start(bf16[96,2048]{1,0:T(8,128)(2,1)S(1)} %get-tuple-element.460), channel_id=1, source_target_pairs={{0,16},{16,0},{1,17},{17,1},{2,18},{18,2},{3,19},{19,3},{4,20},{20... | collective-permute-start | bytes 1179656 | tf_op jit(solution)/shard_map/ppermute | solution.py:363
  377.1 28.9 %collective-permute-start.53 = (bf16[384,1536]{1,0:T(8,128)(2,1)S(1)}, bf16[384,1536]{1,0:T(8,128)(2,1)S(1)}, u32[]{:S(2)}, u32[]{:S(2)}) collective-permute-start(bf16[384,1536]{1,0:T(8,128)(2,1)S(1)} %add_convert_fusion.8), channel_id=1, source_target_pairs={{0,4},{2,6},{4,12},{6,14},{8,0},{10,2},{12,8},{14,10},{1,5},{3,7},... | collective-permute-start | bytes 3538952 | tf_op jit(solution)/shard_map/ppermute | solution.py:388
  377.5 30.4 %collective-permute-start.51 = (bf16[384,768]{1,0:T(8,128)(2,1)S(1)}, bf16[384,768]{1,0:T(8,128)(2,1)S(1)}, u32[]{:S(2)}, u32[]{:S(2)}) collective-permute-start(bf16[384,768]{1,0:T(8,128)(2,1)S(1)} %get-tuple-element.468), channel_id=1, source_target_pairs={{0,16},{3,19},{4,20},{7,23},{8,24},{11,27},{12,28},{15,31},{16,0},... | collective-permute-start | bytes 1769480 | tf_op jit(solution)/shard_map/ppermute | solution.py:370
  385.5 22.4 %collective-permute-start.52 = (bf16[384,768]{1,0:T(8,128)(2,1)S(1)}, bf16[384,768]{1,0:T(8,128)(2,1)S(1)}, u32[]{:S(2)}, u32[]{:S(2)}) collective-permute-start(bf16[384,768]{1,0:T(8,128)(2,1)S(1)} %add_convert_fusion.18), channel_id=1, source_target_pairs={{1,3},{2,0},{5,7},{6,4},{9,11},{10,8},{13,15},{14,12},{17,19},{18,... | collective-permute-start | bytes 1769480 | tf_op jit(solution)/shard_map/ppermute | solution.py:393
  408.0 17.2 %collective-permute-start.58 = (bf16[48,2048]{1,0:T(8,128)(2,1)S(1)}, bf16[48,2048]{1,0:T(8,128)(2,1)S(1)}, u32[]{:S(2)}, u32[]{:S(2)}) collective-permute-start(bf16[48,2048]{1,0:T(8,128)(2,1)S(1)} %get-tuple-element.481), channel_id=1, source_target_pairs={{0,8},{2,10},{4,12},{6,14},{8,0},{10,2},{12,4},{14,6},{1,9},{3,11}... | collective-permute-start | bytes 589832 | tf_op jit(solution)/shard_map/ppermute | solution.py:383
  409.4 15.8 %collective-permute-start.59 = (bf16[48,2048]{1,0:T(8,128)(2,1)S(1)}, bf16[48,2048]{1,0:T(8,128)(2,1)S(1)}, u32[]{:S(2)}, u32[]{:S(2)}) collective-permute-start(bf16[48,2048]{1,0:T(8,128)(2,1)S(1)} %get-tuple-element.482), channel_id=1, source_target_pairs={{0,12},{2,14},{4,8},{6,10},{8,4},{10,6},{12,0},{14,2},{1,13},{3,15... | collective-permute-start | bytes 589832 | tf_op jit(solution)/shard_map/ppermute | solution.py:383
  412.4 14.8 %collective-permute-start.56 = (bf16[192,1664]{1,0:T(8,128)(2,1)S(1)}, bf16[192,1664]{1,0:T(8,128)(2,1)S(1)}, u32[]{:S(2)}, u32[]{:S(2)}) collective-permute-start(bf16[192,1664]{1,0:T(8,128)(2,1)S(1)} %get-tuple-element.478), channel_id=1, source_target_pairs={{0,16},{16,0},{1,17},{17,1},{2,18},{18,2},{3,19},{19,3},{4,20},{20... | collective-permute-start | bytes 1916936 | tf_op jit(solution)/shard_map/ppermute | solution.py:363
  412.9 14.5 %collective-permute-start.55 = (bf16[192,1664]{1,0:T(8,128)(2,1)S(1)}, bf16[192,1664]{1,0:T(8,128)(2,1)S(1)}, u32[]{:S(2)}, u32[]{:S(2)}) collective-permute-start(bf16[192,1664]{1,0:T(8,128)(2,1)S(1)} %get-tuple-element.476), channel_id=1, source_target_pairs={{0,2},{2,0},{4,6},{6,4},{8,10},{10,8},{12,14},{14,12},{1,3},{3,1},... | collective-permute-start | bytes 1916936 | tf_op jit(solution)/shard_map/ppermute | solution.py:374
  429.1 15.9 %collective-permute-start.63 = (bf16[48,2048]{1,0:T(8,128)(2,1)S(1)}, bf16[48,2048]{1,0:T(8,128)(2,1)S(1)}, u32[]{:S(2)}, u32[]{:S(2)}) collective-permute-start(bf16[48,2048]{1,0:T(8,128)(2,1)S(1)} %add_convert_fusion.23), channel_id=1, source_target_pairs={{0,8},{2,10},{4,12},{6,14},{8,0},{10,2},{12,4},{14,6},{1,9},{3,11}... | collective-permute-start | bytes 589832 | tf_op jit(solution)/shard_map/ppermute | solution.py:383
  429.9 15.1 %collective-permute-start.64 = (bf16[48,2048]{1,0:T(8,128)(2,1)S(1)}, bf16[48,2048]{1,0:T(8,128)(2,1)S(1)}, u32[]{:S(2)}, u32[]{:S(2)}) collective-permute-start(bf16[48,2048]{1,0:T(8,128)(2,1)S(1)} %add_convert_fusion.23), channel_id=1, source_target_pairs={{0,12},{2,14},{4,8},{6,10},{8,4},{10,6},{12,0},{14,2},{1,13},{3,15... | collective-permute-start | bytes 589832 | tf_op jit(solution)/shard_map/ppermute | solution.py:383
  433.0 20.0 %collective-permute-start.65 = (bf16[192,1536]{1,0:T(8,128)(2,1)S(1)}, bf16[192,1536]{1,0:T(8,128)(2,1)S(1)}, u32[]{:S(2)}, u32[]{:S(2)}) collective-permute-start(bf16[192,1536]{1,0:T(8,128)(2,1)S(1)} %get-tuple-element.585), channel_id=1, source_target_pairs={{0,16},{16,0},{1,17},{17,1},{2,18},{18,2},{3,19},{19,3},{4,20},{20... | collective-permute-start | bytes 1769480 | tf_op jit(solution)/shard_map/ppermute | solution.py:363
  435.3 17.1 %collective-permute-start.60 = (bf16[96,1664]{1,0:T(8,128)(2,1)S(1)}, bf16[96,1664]{1,0:T(8,128)(2,1)S(1)}, u32[]{:S(2)}, u32[]{:S(2)}) collective-permute-start(bf16[96,1664]{1,0:T(8,128)(2,1)S(1)} %get-tuple-element.491), channel_id=1, source_target_pairs={{0,16},{16,0},{1,17},{17,1},{2,18},{18,2},{3,19},{19,3},{4,20},{20... | collective-permute-start | bytes 958472 | tf_op jit(solution)/shard_map/ppermute | solution.py:363
  469.9 13.0 %collective-permute-start.72 = (bf16[48,1664]{1,0:T(8,128)(2,1)S(1)}, bf16[48,1664]{1,0:T(8,128)(2,1)S(1)}, u32[]{:S(2)}, u32[]{:S(2)}) collective-permute-start(bf16[48,1664]{1,0:T(8,128)(2,1)S(1)} %add_convert_fusion.24), channel_id=1, source_target_pairs={{0,8},{2,10},{4,12},{6,14},{8,0},{10,2},{12,4},{14,6},{1,9},{3,11}... | collective-permute-start | bytes 479240 | tf_op jit(solution)/shard_map/ppermute | solution.py:383
  472.3 17.8 %collective-permute-start.74 = (bf16[192,2048]{1,0:T(8,128)(2,1)S(1)}, bf16[192,2048]{1,0:T(8,128)(2,1)S(1)}, u32[]{:S(2)}, u32[]{:S(2)}) collective-permute-start(bf16[192,2048]{1,0:T(8,128)(2,1)S(1)} %maximum_select_fusion.4.refs_0_), channel_id=1, source_target_pairs={{0,2},{2,0},{4,6},{6,4},{8,10},{10,8},{12,14},{14,12},{1,3},{3,1},... | collective-permute-start | bytes 2359304 | tf_op jit(solution)/shard_map/ppermute | solution.py:374
  473.4 16.7 %collective-permute-start.75 = (bf16[192,2048]{1,0:T(8,128)(2,1)S(1)}, bf16[192,2048]{1,0:T(8,128)(2,1)S(1)}, u32[]{:S(2)}, u32[]{:S(2)}) collective-permute-start(bf16[192,2048]{1,0:T(8,128)(2,1)S(1)} %maximum_select_fusion.5.refs_2_), channel_id=1, source_target_pairs={{0,16},{16,0},{1,17},{17,1},{2,18},{18,2},{3,19},{19,3},{4,20},{20... | collective-permute-start | bytes 2359304 | tf_op jit(solution)/shard_map/ppermute | solution.py:363
  503.6 15.5 %collective-permute-start.80 = (bf16[192,1664]{1,0:T(8,128)(2,1)S(1)}, bf16[192,1664]{1,0:T(8,128)(2,1)S(1)}, u32[]{:S(2)}, u32[]{:S(2)}) collective-permute-start(bf16[192,1664]{1,0:T(8,128)(2,1)S(1)} %maximum_select_fusion.6.refs_0_), channel_id=1, source_target_pairs={{0,2},{2,0},{4,6},{6,4},{8,10},{10,8},{12,14},{14,12},{1,3},{3,1},... | collective-permute-start | bytes 1916936 | tf_op jit(solution)/shard_map/ppermute | solution.py:374
  503.8 15.3 %collective-permute-start.81 = (bf16[192,1664]{1,0:T(8,128)(2,1)S(1)}, bf16[192,1664]{1,0:T(8,128)(2,1)}, u32[]{:S(2)}, u32[]{:S(2)}) collective-permute-start(bf16[192,1664]{1,0:T(8,128)(2,1)S(1)} %maximum_select_fusion.7.refs_2_), channel_id=1, source_target_pairs={{0,16},{16,0},{1,17},{17,1},{2,18},{18,2},{3,19},{19,3},{4,20},{20... | collective-permute-start | bytes 1916936 | tf_op jit(solution)/shard_map/ppermute | solution.py:363
  (127 other events, 1038.0 us)

commit v5 on v4

--- a/solution.py
+++ b/solution.py
@@ -920,6 +920,50 @@
     return chip_grads(out_grads_kernel, place, operands, grads[0].shape[1] + HEAD_SIZE)
 
 
+def dealt_kernel(rows_ref, order_ref, out_ref):
+    count, columns = rows_ref.shape
+    half = count // 2
+    order = order_ref[...]
+    second = order >= half
+    place = jnp.where(second, order - half, order).astype(jnp.float32)
+    pad = jnp.zeros((1, columns - count), jnp.float32)
+    place = jnp.concatenate([place, pad], axis=1)
+    second = jnp.concatenate([jnp.where(second, 1.0, 0.0), pad], axis=1)
+    row = lax.broadcasted_iota(jnp.int32, (EXTRA, columns), 0)
+    out_ref[:count, :] = rows_ref[...]
+    out_ref[count:, :] = low(jnp.where(row == 0, place, jnp.where(row == 1, second, 0.0)))
+
+
+def dealt_unit(rows, order):
+    count, columns = rows.shape
+    return pl.pallas_call(
+        dealt_kernel,
+        out_shape=jax.ShapeDtypeStruct((count + EXTRA, columns), rows.dtype),
+        compiler_params=pltpu.CompilerParams(vmem_limit_bytes=16 * 2**20),
+        cost_estimate=SHORT,
+    )(rows, order)
+
+
+def settle_kernel(held_ref, middle_ref, own_ref, other_ref, ring_ref, first_ref, second_ref):
+    field = low(middle_ref[...] + sum_blocks(own_ref[...], other_ref[...], ring_ref[...]))
+    rows = field.shape[0]
+    place = lax.broadcasted_iota(jnp.int32, (rows, rows), 0)
+    chosen = low(jnp.where(held_ref[...] == place, 1.0, 0.0))
+    dealt = low(matmul(chosen, field))
+    first_ref[...], second_ref[...] = dealt[: rows // 2], dealt[rows // 2 :]
+
+
+def settle(held_at, middle, *sums):
+    rows, columns = middle.shape
+    half = jax.ShapeDtypeStruct((rows // 2, columns), jnp.bfloat16)
+    return pl.pallas_call(
+        settle_kernel,
+        out_shape=[half] * 2,
+        compiler_params=pltpu.CompilerParams(vmem_limit_bytes=24 * 2**20),
+        cost_estimate=SHORT,
+    )(held_at, middle, *sums)
+
+
 def from_pieces(put, place_ref, pieces):
     step = pl.program_id(0)
     for half in range(2):
@@ -940,15 +984,41 @@
     from_pieces(put, place_ref, refs[:4])
 
 
-def finish_out_kernel(place_ref, *refs):
-    out_ref, small_ref = refs[4:]
+def finish_out_kernel(place_ref, first, second, *refs):
+    out_ref, small_ref = refs[-2:]
     width = out_ref.shape[1]
 
     def put(field):
         out_ref[...] = field[:, :width].astype(jnp.float32)
         small_ref[...] = field[:, width:].astype(jnp.float32)
 
-    from_pieces(put, place_ref, refs[:4])
+    pl.when(pl.program_id(0) == 0)(functools.partial(put, first))
+    pl.when(pl.program_id(0) == 1)(functools.partial(put, second))
+
+
+def finish_out(pieces, place, is_own, kept):
+    dp, x, _, _ = place
+    at = jnp.stack([x, dp]).astype(jnp.int32)
+    at = at if is_own else 1 - at
+    rows, total = pieces[0].shape
+    widths = total - HEAD_SIZE, HEAD_SIZE
+    whole = pl.BlockSpec((rows, total), lambda i, place_ref: (0, 0))
+    return pl.pallas_call(
+        finish_out_kernel,
+        grid_spec=pltpu.PrefetchScalarGridSpec(
+            num_scalar_prefetch=1,
+            grid=(2,),
+            in_specs=[whole] * 2 + [pl.BlockSpec(memory_space=pl.ANY)] * len(kept),
+            out_specs=[
+                pl.BlockSpec((rows, width), lambda i, place_ref: (2 * i + place_ref[i], 0))
+                for width in widths
+            ],
+        ),
+        out_shape=[jax.ShapeDtypeStruct((4 * rows, width), jnp.float32) for width in widths],
+        input_output_aliases={3 + i: i for i in range(len(kept))},
+        compiler_params=pltpu.CompilerParams(vmem_limit_bytes=24 * 2**20),
+        cost_estimate=SHORT,
+    )(at, *pieces, *kept)
 
 
 def finish(kernel, fields, place, extras, widths):
@@ -1167,16 +1237,17 @@
     def swapped(field):
         return field, other_core(field)
 
-    def to_dealt(field):
-        held_at = jnp.where(deal_order[0] // half_rows == dp, 0, half_rows)
-        held_at = held_at + deal_order[0] % half_rows
-        chosen = low(held_at[None, :] == row_ids[:, None])
-        field = low(matmul(chosen, field))
-        return in_order(dp == 0, field[:half_rows], other_dp(field[half_rows:]))
-
-    order = jnp.concatenate([deal_order % half_rows, deal_order // half_rows])
-    order = jnp.pad(low(order), ((0, EXTRA - 2), (0, model_width - count_of_rows)))
-    ct_0 = jnp.concatenate([cotangent, order])
+    held_at = jnp.where(deal_order // half_rows == dp, 0, half_rows) + deal_order % half_rows
+
+    def deal(field):
+        field = low(matmul(low(held_at == row_ids[:, None]), field))
+        return field[:half_rows], field[half_rows:]
+
+    def to_dealt(halves):
+        return in_order(dp == 0, halves[0], other_dp(halves[1]))
+
+    ct_0 = dealt_unit(cotangent, deal_order)
+    order = ct_0[count_of_rows:]
     ct_1 = ring_z(ct_0)
     hidden_out = half_of(after(hidden_in, ct_0), 1 - dp)
     hidden_arrived = other_dp(hidden_out)
@@ -1341,7 +1412,8 @@
         grad_projected, full_qkv, tokens, inv_first, gain_first, grad_middle
     )
     out = out_grads(mixes, normed_0, grad_units, place)
-    sums_3 = low(sum_blocks(sums_3[0], sums_3_other, after(sums_2, qkv)))
+    grad_tokens = deal(grad_tokens)
+    sums_3 = low(sum_blocks(sums_3[0], sums_3_other, sums_2))
     sums_3, out, qkv, up_first, up_second, down_first, down_second, grad_tokens = part(
         sums_3, out, qkv, up_first, up_second, down_first, down_second, grad_tokens
     )
@@ -1353,14 +1425,14 @@
     input_gradient = to_dealt(grad_tokens)
     up_grad = low(jnp.concatenate([sum_blocks(*up_first), sum_blocks(*up_second)], axis=1))
     up_grad = block(up_grad, core, 2), block(up_grad, 1 - core, 2)
-    layer_out = low(middle + sum_blocks(sums_0[0], sums_0_other, after(sums_3, qkv)))
-    out, qkv, up_grad, down_first, down_second, layer_out, input_gradient = part(
-        out, qkv, up_grad, down_first, down_second, layer_out, input_gradient
+    out, qkv, up_grad, down_first, down_second, sums_3, input_gradient = part(
+        out, qkv, up_grad, down_first, down_second, sums_3, input_gradient
     )
 
     qkv, out = line_sum(qkv), slab_sum(out, place)
     down_grad = low(jnp.concatenate([sum_blocks(*down_first), sum_blocks(*down_second)], axis=1))
     down_grad = block(down_grad, core, 2), block(down_grad, 1 - core, 2)
+    layer_out = settle(held_at, middle, sums_0[0], sums_0_other, sums_3)
     out, qkv, up_grad, down_grad, layer_out = part(out, qkv, up_grad, down_grad, layer_out)
 
     qkv, out = line_spread(qkv, place), slab_sum_on(out, place)
@@ -1385,9 +1457,10 @@
         out, qkv_grad, gain_first_grad, up_grad, down_grad
     )
 
-    out = slab_spread_on(out)
+    out_grad, small_grad = finish_out(out, place, True, [])
+    (_, first), (_, second) = slab_spread_on(out)
+    out_grad, small_grad = finish_out([first, second], place, False, [out_grad, small_grad])
     gate_up_grad, down_grad = (field[None].astype(jnp.float32) for field in (up_grad, down_grad))
-    out_grad, small_grad = finish(finish_out_kernel, out, place, [], [model_width, HEAD_SIZE])
     return (
         layer_out,
         input_gradient,

time: 534 us -> 523 us (0.979)
  waiting for transfers between devices: 161 us -> 152 us
    ppermute x12, waiting for transfers between devices: 63.7 us -> 54.9 us  [ring_z(): return lax.ppermute(field, 'expert', pairs)]
    pallas_call x0 -> x4, Pallas kernels: none -> 7.44 us  [the longest x2 4.12 us: finish_out(): pl.pallas_call(finish_out_kernel, grid_spec=pltpu.PrefetchScalarGridSpec(...]
    unnamed x219 -> x205, local copies, waits for them, and re-layouts: 24.3 us -> 21.9 us
    convert_element_type x18 -> x17, other arithmetic: 26.1 us -> 23.7 us  [low(): return field.astype(jnp.bfloat16)]
    dot_general x12 -> x11, matrix products: 44.7 us -> 44.1 us  [matmul(): lax.dot_general(left, right, dims, preferred_element_type=jnp.float32)]
  transfers between devices with their start and end apart: 82 -> 82, of which waited for: 30 -> 33; matrix products, arithmetic and copies ran while one was open for 22% -> 23% of each run, Pallas kernels for 25% -> 26%
where the time goes in v5:
time: 523 us; the launch traced here: 514 us
  waiting for transfers between devices  152 us (29%)
  Pallas kernels  136 us (26%)
  starting transfers between devices  81.7 us (16%)
  other arithmetic  57.8 us (11%)
  matrix products  44.1 us (8%)
  local copies, waits for them, and re-layouts  40.5 us (8%)
    pallas_call x4, Pallas kernels, expert_step(): pl.pallas_call(functools.partial(expert_kernel, columns=256), grid=(2,),...  83.1 us
    ppermute x12, waiting for transfers between devices, ring_z(): return lax.ppermute(field, 'expert', pairs)  54.9 us
    dot_general x11, matrix products, matmul(): lax.dot_general(left, right, dims, preferred_element_type=jnp.float32)  44.1 us
    ppermute x17, waiting for transfers between devices, other_dp(): return lax.ppermute(field, 'dp', [(0, 1), (1, 0)])  41.9 us
    ppermute x12, waiting for transfers between devices, across_z(): lax.ppermute(field, 'expert', [(i, i ^ 2 * distance) for i in range(8)])  28.9 us
    convert_element_type x17, other arithmetic, low(): return field.astype(jnp.bfloat16)  23.7 us
    unnamed x205, local copies, waits for them, and re-layouts  21.9 us
    ppermute x12, starting transfers between devices, across_z(): lax.ppermute(field, 'expert', [(i, i ^ 2 * distance) for i in range(8)])  17.7 us
  transfers between devices with their start and end apart: 82, of which 33 were waited for; matrix products, arithmetic and copies ran while one was open for 23% of the time, Pallas kernels for 26%

profile of v5, /device:TPU:0, one launch (start us, length us, event | category | flops | bytes accessed | tf_op | source)
XLA Modules:
  0.0 513.9 jit_solution(14519812458938762888)
XLA Ops:
  4.4 2.6 collective-permute-start.2
  8.7 5.6 %collective-permute-start.7 = (bf16[1536,1536]{1,0:T(8,128)(2,1)}, bf16[1536,1536]{1,0:T(8,128)(2,1)}, u32[]{:S(2)}, u32[]{:S(2)}) collective-permute-start(bf16[1536,1536]{1,0:T(8,128)(2,1)} %bitcast.61), channel_id=1, source_target_pairs={{0,2},{3,1},{4,6},{7,5},{8,10},{11,9},{12,14},{15,13},{16,18},{19,... | collective-permute-start | bytes 14155784 | tf_op jit(solution)/shard_map/ppermute | solution.py:398
  18.4 8.3 %maximum_select_fusion.weight_ref = bf16[1536,2048]{1,0:T(8,128)(2,1)} fusion(bf16[768,2048]{1,0:T(8,128)(2,1)} %collective-permute-done.1, bf16[768,2048]{1,0:T(8,128)(2,1)} %refs_4_.1, pred[]{:T(512)S(6)} %eq.179), kind=kLoop, calls=%fused_computation | loop fusion | flops 28311552 | bytes 12582913 | tf_op jit(solution)/shard_map/jit(_where)/select_n | solution.py:402
  29.5 2.6 fusion.77.query_in.key_in.value_in
  32.2 5.2 %collective-permute-done = bf16[400,1536]{1,0:T(8,128)(2,1)} collective-permute-done((bf16[400,1536]{1,0:T(8,128)(2,1)}, bf16[400,1536]{1,0:T(8,128)(2,1)}, u32[]{:S(2)}, u32[]{:S(2)}) %collective-permute-start) | collective-permute-done | bytes 1228832 | tf_op jit(solution)/shard_map/ppermute | solution.py:388
  40.8 3.5 collective-permute-start.12
  44.4 7.4 %shard_map.188 = (bf16[384,1536]{1,0:T(8,128)(2,1)S(1)}, bf16[384,256]{1,0:T(8,128)(2,1)S(1)}, bf16[384,256]{1,0:T(8,128)(2,1)S(1)}, bf16[384,1536]{1,0:T(8,128)(2,1)S(1)}) custom-call(f32[384,2048]{1,0:T(8,128)S(1)} %fusion.77.query_in.key_in.value_in, f32[384,2048]{1,0:T(8,128)S(1)} %fusion.77.query_in.key_in.value_in, ...), custom_call_target="tpu_custom_call" | custom-call | flops 1000 | bytes 1000 | tf_op jit(solution)/shard_map/pallas_call | solution.py:1101
  51.8 4.8 maximum_select_fusion.1.weight_ref
  56.8 2.7 shard_map.189
  61.7 5.1 collective-permute-done.5
  71.7 14.3 %collective-permute-done.11 = bf16[192,1536]{1,0:T(8,128)(2,1)S(1)} collective-permute-done((bf16[192,1536]{1,0:T(8,128)(2,1)S(1)}, bf16[192,1536]{1,0:T(8,128)(2,1)S(1)}, u32[]{:S(2)}, u32[]{:S(2)}) %collective-permute-start.11) | collective-permute-done | bytes 589856 | tf_op jit(solution)/shard_map/ppermute | solution.py:363
  86.0 3.3 collective-permute-done.12.down_other
  89.4 5.8 %collective-permute-done.8.own_rows = bf16[400,1536]{1,0:T(8,128)(2,1)} collective-permute-done((bf16[400,1536]{1,0:T(8,128)(2,1)S(1)}, bf16[400,1536]{1,0:T(8,128)(2,1)}, u32[]{:S(2)}, u32[]{:S(2)}) %collective-permute-start.8) | collective-permute-done | bytes 1228832 | tf_op jit(solution)/shard_map/ppermute | solution.py:388
  98.7 2.5 constant_dynamic-slice_fusion.18
  103.2 20.9 %shard_map.190 = (bf16[384,1536]{1,0:T(8,128)(2,1)S(1)}, bf16[384,1536]{1,0:T(8,128)(2,1)}, bf16[400,1536]{1,0:T(8,128)(2,1)}, bf16[400,1536]{1,0:T(8,128)(2,1)}...) custom-call(s32[2]{0:T(128)S(1)} %pad_add_fusion.choice, ...), custom_call_target="tpu_custom_call" | custom-call | flops 1000 | bytes 1000 | tf_op jit(solution)/shard_map/pallas_call | solution.py:623
  125.5 3.6 collective-permute-start.17
  133.9 20.8 %shard_map.191 = (bf16[384,1536]{1,0:T(8,128)(2,1)S(1)}, bf16[384,1536]{1,0:T(8,128)(2,1)S(1)}, bf16[400,1536]{1,0:T(8,128)(2,1)}, bf16[400,1536]{1,0:T(8,128)(2...) custom-call(s32[2]{0:T(128)S(1)} %pad_add_fusion.choice, ...), custom_call_target="tpu_custom_call", output_to_operand_aliasing={{4}: (9, {}), {5}: (10, {}), {6}: (11, {}), {7}: (12, {})} | custom-call | flops 1000 | bytes 1000 | tf_op jit(solution)/shard_map/pallas_call | solution.py:623
  162.4 20.5 %shard_map.192 = (bf16[384,1536]{1,0:T(8,128)(2,1)S(1)}, bf16[384,1536]{1,0:T(8,128)(2,1)S(1)}, bf16[400,1536]{1,0:T(8,128)(2,1)}, bf16[400,1536]{1,0:T(8,128)(2...) custom-call(s32[2]{0:T(128)S(1)} %pad_add_fusion.choice, ...), custom_call_target="tpu_custom_call", output_to_operand_aliasing={{4}: (9, {}), {5}: (10, {}), {6}: (11, {}), {7}: (12, {})} | custom-call | flops 1000 | bytes 1000 | tf_op jit(solution)/shard_map/pallas_call | solution.py:623
  182.9 3.5 add_convert_fusion.3
  186.4 2.5 collective-permute-done.22.own_rows
  190.1 2.0 collective-permute-done.26.other_rows
  193.6 20.9 %shard_map.193 = (bf16[384,1536]{1,0:T(8,128)(2,1)S(1)}, bf16[384,1536]{1,0:T(8,128)(2,1)}, bf16[400,1536]{1,0:T(8,128)(2,1)}, bf16[400,1536]{1,0:T(8,128)(2,1)}...) custom-call(s32[2]{0:T(128)S(1)} %pad_add_fusion.choice, ...), custom_call_target="tpu_custom_call", output_to_operand_aliasing={{4}: (9, {}), {5}: (10, {}), {6}: (11, {}), {7}: (12, {})} | custom-call | flops 1000 | bytes 1000 | tf_op jit(solution)/shard_map/pallas_call | solution.py:623
  214.5 5.2 %collective-permute-done.28 = bf16[400,1536]{1,0:T(8,128)(2,1)} collective-permute-done((bf16[400,1536]{1,0:T(8,128)(2,1)}, bf16[400,1536]{1,0:T(8,128)(2,1)}, u32[]{:S(2)}, u32[]{:S(2)}) %collective-permute-start.28) | collective-permute-done | bytes 1228832 | tf_op jit(solution)/shard_map/ppermute | solution.py:388
  219.7 2.2 add_convert_fusion.2
  222.3 11.7 %fusion.11 = bf16[1536,768]{1,0:T(8,128)(2,1)S(1)} fusion(bf16[3072,1536]{1,0:T(8,128)(2,1)} %get-tuple-element.378, bf16[3072,1536]{1,0:T(8,128)(2,1)} %get-tuple-element.379), kind=kOutput, calls=%fused_computation.12 | convolution fusion | flops 7248936960 | bytes 16515072 | tf_op jit(solution)/shard_map/dot_general | solution.py:477
  234.1 12.8 %fusion.8 = bf16[1536,768]{1,0:T(8,128)(2,1)} fusion(bf16[3072,1536]{1,0:T(8,128)(2,1)} %get-tuple-element.378, bf16[3072,1536]{1,0:T(8,128)(2,1)} %get-tuple-element.379), kind=kOutput, calls=%fused_computation.11 | convolution fusion | flops 7248936960 | bytes 16515072 | tf_op jit(solution)/shard_map/dot_general | solution.py:477
  246.9 4.8 collective-permute-done.30
  252.5 2.6 add_convert_fusion.10
  255.2 4.0 fusion.20
  261.8 5.0 fusion.17
  266.8 14.5 %collective-permute-done.34.back_ring.extra_ring = bf16[400,1536]{1,0:T(8,128)(2,1)} collective-permute-done((bf16[400,1536]{1,0:T(8,128)(2,1)S(1)}, bf16[400,1536]{1,0:T(8,128)(2,1)}, u32[]{:S(2)}, u32[]{:S(2)}) %collective-permute-start.34) | collective-permute-done | bytes 1228832 | tf_op jit(solution)/shard_map/ppermute | solution.py:388
  286.4 9.7 %shard_map.194 = (f32[384,1536]{1,0:T(8,128)}, bf16[400,1536]{1,0:T(8,128)(2,1)}, bf16[384,1536]{1,0:T(8,128)(2,1)}) custom-call(bf16[400,1536]{1,0:T(8,128)(2,1)} %get-tuple-element.395.back_own.extra_own, bf16[400,1536]{1,0:T(8,128)(2,1)} %copy-done.62, bf16[400,1536]{1,0:T(8,128)(2,1)} %collective-permute-done.34.back_ring.extra_ring, ...), custom_call_target="tpu_custom_call" | custom-call | flops 1000 | bytes 1000 | tf_op jit(solution)/shard_map/pallas_call | solution.py:734
  301.4 8.8 %shard_map.195.right_own.grad_ref = bf16[384,2048]{1,0:T(8,128)(2,1)S(1)} custom-call(bf16[384,1536]{1,0:T(8,128)(2,1)S(1)} %copy-done.37, bf16[384,256]{1,0:T(8,128)(2,1)S(1)} %copy-done.49, bf16[384,256]{1,0:T(8,128)(2,1)S(1)} %copy-done.51, bf16[384,1536]{1,0:T(8,128)(2,1)S(1)} %copy-done.44, f32[384,128]{1,0:T(8,128)S(1)} %copy-done.24, ...), custom_call_target="tpu_custom_call" | custom-call | flops 1000 | bytes 1000 | tf_op jit(solution)/shard_map/pallas_call | solution.py:1181
  310.3 3.5 collective-permute-done.36
  316.2 3.0 add_convert_fusion
  320.8 2.7 add_convert_fusion.8
  323.5 3.2 add_convert_fusion.9
  326.8 4.7 shard_map.196
  333.2 2.9 collective-permute-start.45
  336.5 3.4 collective-permute-start.47
  341.5 3.3 shard_map.198
  344.8 4.4 shard_map.197
  350.1 2.0 collective-permute-done.46
  358.7 6.3 %collective-permute-done.44 = bf16[384,1536]{1,0:T(8,128)(2,1)} collective-permute-done((bf16[384,1536]{1,0:T(8,128)(2,1)}, bf16[384,1536]{1,0:T(8,128)(2,1)}, u32[]{:S(2)}, u32[]{:S(2)}) %collective-permute-start.44) | collective-permute-done | bytes 1179680 | tf_op jit(solution)/shard_map/ppermute | solution.py:388
  365.1 2.1 add_convert_fusion.7
  369.8 3.3 collective-permute-start.51
  379.8 10.1 %collective-permute-done.49 = bf16[96,2048]{1,0:T(8,128)(2,1)S(1)} collective-permute-done((bf16[96,2048]{1,0:T(8,128)(2,1)S(1)}, bf16[96,2048]{1,0:T(8,128)(2,1)S(1)}, u32[]{:S(2)}, u32[]{:S(2)}) %collective-permute-start.49) | collective-permute-done | bytes 393248 | tf_op jit(solution)/shard_map/ppermute | solution.py:363
  392.0 4.2 collective-permute-done.51
  396.2 2.0 collective-permute-done.53.ring_ref
  399.8 2.8 collective-permute-start.59
  405.4 2.2 shard_map.199
  408.7 6.6 %collective-permute-done.58 = bf16[48,2048]{1,0:T(8,128)(2,1)S(1)} collective-permute-done((bf16[48,2048]{1,0:T(8,128)(2,1)S(1)}, bf16[48,2048]{1,0:T(8,128)(2,1)S(1)}, u32[]{:S(2)}, u32[]{:S(2)}) %collective-permute-start.58) | collective-permute-done | bytes 196640 | tf_op jit(solution)/shard_map/ppermute | solution.py:383
  425.7 8.8 %collective-permute-done.63 = bf16[48,2048]{1,0:T(8,128)(2,1)S(1)} collective-permute-done((bf16[48,2048]{1,0:T(8,128)(2,1)S(1)}, bf16[48,2048]{1,0:T(8,128)(2,1)S(1)}, u32[]{:S(2)}, u32[]{:S(2)}) %collective-permute-start.63) | collective-permute-done | bytes 196640 | tf_op jit(solution)/shard_map/ppermute | solution.py:383
  434.9 6.5 %collective-permute-done.60 = bf16[96,1664]{1,0:T(8,128)(2,1)S(1)} collective-permute-done((bf16[96,1664]{1,0:T(8,128)(2,1)S(1)}, bf16[96,1664]{1,0:T(8,128)(2,1)S(1)}, u32[]{:S(2)}, u32[]{:S(2)}) %collective-permute-start.60) | collective-permute-done | bytes 319520 | tf_op jit(solution)/shard_map/ppermute | solution.py:363
  444.0 2.4 collective-permute-start.67
  451.2 4.8 collective-permute-done.67
  464.4 7.8 %collective-permute-done.72 = bf16[48,1664]{1,0:T(8,128)(2,1)S(1)} collective-permute-done((bf16[48,1664]{1,0:T(8,128)(2,1)S(1)}, bf16[48,1664]{1,0:T(8,128)(2,1)S(1)}, u32[]{:S(2)}, u32[]{:S(2)}) %collective-permute-start.72) | collective-permute-done | bytes 159776 | tf_op jit(solution)/shard_map/ppermute | solution.py:383
  472.5 7.0 %collective-permute-done.74.refs_1_ = bf16[192,2048]{1,0:T(8,128)(2,1)S(1)} collective-permute-done((bf16[192,2048]{1,0:T(8,128)(2,1)S(1)}, bf16[192,2048]{1,0:T(8,128)(2,1)S(1)}, u32[]{:S(2)}, u32[]{:S(2)}) %collective-permute-start.74) | collective-permute-done | bytes 786464 | tf_op jit(solution)/shard_map/ppermute | solution.py:374
  483.0 4.0 shard_map.200
  488.1 3.7 collective-permute-done.76
  496.6 2.1 shard_map.201
  499.4 3.0 bitcast_convert_fusion
  502.4 6.4 %collective-permute-done.80.first = bf16[192,1664]{1,0:T(8,128)(2,1)S(1)} collective-permute-done((bf16[192,1664]{1,0:T(8,128)(2,1)S(1)}, bf16[192,1664]{1,0:T(8,128)(2,1)S(1)}, u32[]{:S(2)}, u32[]{:S(2)}) %collective-permute-start.80) | collective-permute-done | bytes 639008 | tf_op jit(solution)/shard_map/ppermute | solution.py:374
  510.0 2.1 shard_map.202
  (435 shorter events, 130.4 us)
Async XLA Ops:
  3.9 14.5 %collective-permute-start.1 = (bf16[768,2048]{1,0:T(8,128)(2,1)}, bf16[768,2048]{1,0:T(8,128)(2,1)}, u32[]{:S(2)}, u32[]{:S(2)}) collective-permute-start(bf16[768,2048]{1,0:T(8,128)(2,1)} %refs_4_.1), channel_id=1, source_target_pairs={{0,1},{1,0},{2,3},{3,2},{4,5},{5,4},{6,7},{7,6},{8,9},{9,8},{10,11... | collective-permute-start | bytes 9437192 | tf_op jit(solution)/shard_map/ppermute | solution.py:359
  4.4 22.2 %collective-permute-start.2 = (bf16[192,1536]{1,0:T(8,128)(2,1)S(1)}, bf16[192,1536]{1,0:T(8,128)(2,1)S(1)}, u32[]{:S(2)}, u32[]{:S(2)}) collective-permute-start(bf16[192,1536]{1,0:T(8,128)(2,1)S(1)} %constant_dynamic-slice_fusion.24), channel_id=1, source_target_pairs={{0,16},{16,0},{1,17},{17,1},{2,18},{18,2},{3,19},{19,3},{4,20},{20... | collective-permute-start | bytes 1769480 | tf_op jit(solution)/shard_map/ppermute | solution.py:363
  7.0 30.3 %collective-permute-start = (bf16[400,1536]{1,0:T(8,128)(2,1)}, bf16[400,1536]{1,0:T(8,128)(2,1)}, u32[]{:S(2)}, u32[]{:S(2)}) collective-permute-start(bf16[400,1536]{1,0:T(8,128)(2,1)} %shard_map.187), channel_id=1, source_target_pairs={{0,4},{2,6},{4,12},{6,14},{8,0},{10,2},{12,8},{14,10},{1,5},{3,7},... | collective-permute-start | bytes 3686408 | tf_op jit(solution)/shard_map/ppermute | solution.py:388
  8.7 58.1 %collective-permute-start.7 = (bf16[1536,1536]{1,0:T(8,128)(2,1)}, bf16[1536,1536]{1,0:T(8,128)(2,1)}, u32[]{:S(2)}, u32[]{:S(2)}) collective-permute-start(bf16[1536,1536]{1,0:T(8,128)(2,1)} %bitcast.61), channel_id=1, source_target_pairs={{0,2},{3,1},{4,6},{7,5},{8,10},{11,9},{12,14},{15,13},{16,18},{19,... | collective-permute-start | bytes 14155784 | tf_op jit(solution)/shard_map/ppermute | solution.py:398
  17.6 19.7 %collective-permute-start.4 = (bf16[768,1536]{1,0:T(8,128)(2,1)}, bf16[768,1536]{1,0:T(8,128)(2,1)}, u32[]{:S(2)}, u32[]{:S(2)}) collective-permute-start(bf16[768,1536]{1,0:T(8,128)(2,1)} %param.20), channel_id=1, source_target_pairs={{0,1},{1,0},{2,3},{3,2},{4,5},{5,4},{6,7},{7,6},{8,9},{9,8},{10,11... | collective-permute-start | bytes 7077896 | tf_op jit(solution)/shard_map/ppermute | solution.py:359
  37.3 29.5 %collective-permute-start.5 = (bf16[400,1536]{1,0:T(8,128)(2,1)}, bf16[400,1536]{1,0:T(8,128)(2,1)}, u32[]{:S(2)}, u32[]{:S(2)}) collective-permute-start(bf16[400,1536]{1,0:T(8,128)(2,1)} %collective-permute-done), channel_id=1, source_target_pairs={{0,4},{2,6},{4,12},{6,14},{8,0},{10,2},{12,8},{14,10},{1,5},{3,7},... | collective-permute-start | bytes 3686408 | tf_op jit(solution)/shard_map/ppermute | solution.py:388
  40.2 21.5 %collective-permute-start.6 = (bf16[192,1536]{1,0:T(8,128)(2,1)S(1)}, bf16[192,1536]{1,0:T(8,128)(2,1)S(1)}, u32[]{:S(2)}, u32[]{:S(2)}) collective-permute-start(bf16[192,1536]{1,0:T(8,128)(2,1)S(1)} %get-tuple-element.590), channel_id=1, source_target_pairs={{0,16},{16,0},{1,17},{17,1},{2,18},{18,2},{3,19},{19,3},{4,20},{20... | collective-permute-start | bytes 1769480 | tf_op jit(solution)/shard_map/ppermute | solution.py:363
  40.8 48.6 %collective-permute-start.12 = (bf16[768,1536]{1,0:T(8,128)(2,1)}, bf16[768,1536]{1,0:T(8,128)(2,1)S(1)}, u32[]{:S(2)}, u32[]{:S(2)}) collective-permute-start(bf16[768,1536]{1,0:T(8,128)(2,1)} %bitcast.68), channel_id=1, source_target_pairs={{0,2},{3,1},{4,6},{7,5},{8,10},{11,9},{12,14},{15,13},{16,18},{19,... | collective-permute-start | bytes 7077896 | tf_op jit(solution)/shard_map/ppermute | solution.py:398
  66.8 28.3 %collective-permute-start.8 = (bf16[400,1536]{1,0:T(8,128)(2,1)S(1)}, bf16[400,1536]{1,0:T(8,128)(2,1)}, u32[]{:S(2)}, u32[]{:S(2)}) collective-permute-start(bf16[400,1536]{1,0:T(8,128)(2,1)S(1)} %get-tuple-element.308.own_rows.refs_1_), channel_id=1, source_target_pairs={{0,4},{2,6},{4,12},{6,14},{8,0},{10,2},{12,8},{14,10},{1,5},{3,7},... | collective-permute-start | bytes 3686408 | tf_op jit(solution)/shard_map/ppermute | solution.py:388
  67.6 27.6 %collective-permute-start.9 = (bf16[400,1536]{1,0:T(8,128)(2,1)S(1)}, bf16[400,1536]{1,0:T(8,128)(2,1)S(1)}, u32[]{:S(2)}, u32[]{:S(2)}) collective-permute-start(bf16[400,1536]{1,0:T(8,128)(2,1)S(1)} %get-tuple-element.308.own_rows.refs_1_), channel_id=1, source_target_pairs={{0,1},{1,0},{2,3},{3,2},{4,5},{5,4},{6,7},{7,6},{8,9},{9,8},{10,11... | collective-permute-start | bytes 3686408 | tf_op jit(solution)/shard_map/ppermute | solution.py:359
  68.5 20.9 %collective-permute-start.10 = (bf16[384,1536]{1,0:T(8,128)(2,1)S(1)}, bf16[384,1536]{1,0:T(8,128)(2,1)S(1)}, u32[]{:S(2)}, u32[]{:S(2)}) collective-permute-start(bf16[384,1536]{1,0:T(8,128)(2,1)S(1)} %convolution_convert_fusion.4.own_ct.ct_ref), channel_id=1, source_target_pairs={{0,1},{1,0},{2,3},{3,2},{4,5},{5,4},{6,7},{7,6},{8,9},{9,8},{10,11... | collective-permute-start | bytes 3538952 | tf_op jit(solution)/shard_map/ppermute | solution.py:359
  70.3 15.7 %collective-permute-start.11 = (bf16[192,1536]{1,0:T(8,128)(2,1)S(1)}, bf16[192,1536]{1,0:T(8,128)(2,1)S(1)}, u32[]{:S(2)}, u32[]{:S(2)}) collective-permute-start(bf16[192,1536]{1,0:T(8,128)(2,1)S(1)} %get-tuple-element.588), channel_id=1, source_target_pairs={{0,16},{16,0},{1,17},{17,1},{2,18},{18,2},{3,19},{19,3},{4,20},{20... | collective-permute-start | bytes 1769480 | tf_op jit(solution)/shard_map/ppermute | solution.py:363
  95.2 30.3 %collective-permute-start.13 = (bf16[400,1536]{1,0:T(8,128)(2,1)}, bf16[400,1536]{1,0:T(8,128)(2,1)}, u32[]{:S(2)}, u32[]{:S(2)}) collective-permute-start(bf16[400,1536]{1,0:T(8,128)(2,1)} %collective-permute-done.5), channel_id=1, source_target_pairs={{0,4},{2,6},{4,12},{6,14},{8,0},{10,2},{12,8},{14,10},{1,5},{3,7},... | collective-permute-start | bytes 3686408 | tf_op jit(solution)/shard_map/ppermute | solution.py:388
  96.3 29.1 %collective-permute-start.15 = (bf16[400,1536]{1,0:T(8,128)(2,1)}, bf16[400,1536]{1,0:T(8,128)(2,1)}, u32[]{:S(2)}, u32[]{:S(2)}) collective-permute-start(bf16[400,1536]{1,0:T(8,128)(2,1)} %collective-permute-done.8.own_rows), channel_id=1, source_target_pairs={{0,1},{1,0},{2,3},{3,2},{4,5},{5,4},{6,7},{7,6},{8,9},{9,8},{10,11... | collective-permute-start | bytes 3686408 | tf_op jit(solution)/shard_map/ppermute | solution.py:359
  98.2 27.3 %collective-permute-start.14 = (bf16[384,1536]{1,0:T(8,128)(2,1)}, bf16[384,1536]{1,0:T(8,128)(2,1)}, u32[]{:S(2)}, u32[]{:S(2)}) collective-permute-start(bf16[384,1536]{1,0:T(8,128)(2,1)} %convolution_convert_fusion.3.own_ct), channel_id=1, source_target_pairs={{0,1},{1,0},{2,3},{3,2},{4,5},{5,4},{6,7},{7,6},{8,9},{9,8},{10,11... | collective-permute-start | bytes 3538952 | tf_op jit(solution)/shard_map/ppermute | solution.py:359
  101.2 23.7 %collective-permute-start.16 = (bf16[192,1536]{1,0:T(8,128)(2,1)}, bf16[192,1536]{1,0:T(8,128)(2,1)}, u32[]{:S(2)}, u32[]{:S(2)}) collective-permute-start(bf16[192,1536]{1,0:T(8,128)(2,1)} %get-tuple-element.586), channel_id=1, source_target_pairs={{0,16},{16,0},{1,17},{17,1},{2,18},{18,2},{3,19},{19,3},{4,20},{20... | collective-permute-start | bytes 1769480 | tf_op jit(solution)/shard_map/ppermute | solution.py:363
  101.8 53.9 %collective-permute-start.20 = (bf16[384,1536]{1,0:T(8,128)(2,1)S(1)}, bf16[384,1536]{1,0:T(8,128)(2,1)S(1)}, u32[]{:S(2)}, u32[]{:S(2)}) collective-permute-start(bf16[384,1536]{1,0:T(8,128)(2,1)S(1)} %copy-done.15), channel_id=1, source_target_pairs={{0,1},{1,0},{2,3},{3,2},{4,5},{5,4},{6,7},{7,6},{8,9},{9,8},{10,11... | collective-permute-start | bytes 3538952 | tf_op jit(solution)/shard_map/ppermute | solution.py:359
  125.0 30.7 %collective-permute-start.21 = (bf16[384,1536]{1,0:T(8,128)(2,1)S(1)}, bf16[384,1536]{1,0:T(8,128)(2,1)S(1)}, u32[]{:S(2)}, u32[]{:S(2)}) collective-permute-start(bf16[384,1536]{1,0:T(8,128)(2,1)S(1)} %copy-done.17), channel_id=1, source_target_pairs={{0,1},{1,0},{2,3},{3,2},{4,5},{5,4},{6,7},{7,6},{8,9},{9,8},{10,11... | collective-permute-start | bytes 3538952 | tf_op jit(solution)/shard_map/ppermute | solution.py:359
  125.5 31.3 %collective-permute-start.17 = (bf16[400,1536]{1,0:T(8,128)(2,1)}, bf16[400,1536]{1,0:T(8,128)(2,1)S(1)}, u32[]{:S(2)}, u32[]{:S(2)}) collective-permute-start(bf16[400,1536]{1,0:T(8,128)(2,1)} %collective-permute-done.8.own_rows), channel_id=1, source_target_pairs={{0,4},{2,6},{4,12},{6,14},{8,0},{10,2},{12,8},{14,10},{1,5},{3,7},... | collective-permute-start | bytes 3686408 | tf_op jit(solution)/shard_map/ppermute | solution.py:388
  130.9 25.8 %collective-permute-start.19 = (bf16[384,1536]{1,0:T(8,128)(2,1)S(1)}, bf16[384,1536]{1,0:T(8,128)(2,1)S(1)}, u32[]{:S(2)}, u32[]{:S(2)}) collective-permute-start(bf16[384,1536]{1,0:T(8,128)(2,1)S(1)} %convolution_convert_fusion.2.own_ct), channel_id=1, source_target_pairs={{0,1},{1,0},{2,3},{3,2},{4,5},{5,4},{6,7},{7,6},{8,9},{9,8},{10,11... | collective-permute-start | bytes 3538952 | tf_op jit(solution)/shard_map/ppermute | solution.py:359
  132.3 24.4 %collective-permute-start.18 = (bf16[192,1536]{1,0:T(8,128)(2,1)S(1)}, bf16[192,1536]{1,0:T(8,128)(2,1)}, u32[]{:S(2)}, u32[]{:S(2)}) collective-permute-start(bf16[192,1536]{1,0:T(8,128)(2,1)S(1)} %get-tuple-element.584), channel_id=1, source_target_pairs={{0,16},{16,0},{1,17},{17,1},{2,18},{18,2},{3,19},{19,3},{4,20},{20... | collective-permute-start | bytes 1769480 | tf_op jit(solution)/shard_map/ppermute | solution.py:363
  158.0 24.9 %collective-permute-start.23 = (bf16[400,1536]{1,0:T(8,128)(2,1)}, bf16[400,1536]{1,0:T(8,128)(2,1)}, u32[]{:S(2)}, u32[]{:S(2)}) collective-permute-start(bf16[400,1536]{1,0:T(8,128)(2,1)} %get-tuple-element.338), channel_id=1, source_target_pairs={{0,1},{1,0},{2,3},{3,2},{4,5},{5,4},{6,7},{7,6},{8,9},{9,8},{10,11... | collective-permute-start | bytes 3686408 | tf_op jit(solution)/shard_map/ppermute | solution.py:359
  158.3 30.6 %collective-permute-start.22 = (bf16[400,1536]{1,0:T(8,128)(2,1)S(1)}, bf16[400,1536]{1,0:T(8,128)(2,1)}, u32[]{:S(2)}, u32[]{:S(2)}) collective-permute-start(bf16[400,1536]{1,0:T(8,128)(2,1)S(1)} %collective-permute-done.17.own_rows), channel_id=1, source_target_pairs={{0,4},{2,6},{4,12},{6,14},{8,0},{10,2},{12,8},{14,10},{1,5},{3,7},... | collective-permute-start | bytes 3686408 | tf_op jit(solution)/shard_map/ppermute | solution.py:388
  161.2 25.2 %collective-permute-start.24 = (bf16[384,1536]{1,0:T(8,128)(2,1)S(1)}, bf16[384,1536]{1,0:T(8,128)(2,1)}, u32[]{:S(2)}, u32[]{:S(2)}) collective-permute-start(bf16[384,1536]{1,0:T(8,128)(2,1)S(1)} %convolution_convert_fusion.1.own_ct), channel_id=1, source_target_pairs={{0,1},{1,0},{2,3},{3,2},{4,5},{5,4},{6,7},{7,6},{8,9},{9,8},{10,11... | collective-permute-start | bytes 3538952 | tf_op jit(solution)/shard_map/ppermute | solution.py:359
  188.9 30.8 %collective-permute-start.28 = (bf16[400,1536]{1,0:T(8,128)(2,1)}, bf16[400,1536]{1,0:T(8,128)(2,1)}, u32[]{:S(2)}, u32[]{:S(2)}) collective-permute-start(bf16[400,1536]{1,0:T(8,128)(2,1)} %add_convert_fusion.3), channel_id=1, source_target_pairs={{0,4},{2,6},{4,12},{6,14},{8,0},{10,2},{12,8},{14,10},{1,5},{3,7},... | collective-permute-start | bytes 3686408 | tf_op jit(solution)/shard_map/ppermute | solution.py:388
  189.1 30.6 %collective-permute-start.29 = (bf16[400,1536]{1,0:T(8,128)(2,1)}, bf16[400,1536]{1,0:T(8,128)(2,1)}, u32[]{:S(2)}, u32[]{:S(2)}) collective-permute-start(bf16[400,1536]{1,0:T(8,128)(2,1)} %get-tuple-element.364), channel_id=1, source_target_pairs={{0,1},{1,0},{2,3},{3,2},{4,5},{5,4},{6,7},{7,6},{8,9},{9,8},{10,11... | collective-permute-start | bytes 3686408 | tf_op jit(solution)/shard_map/ppermute | solution.py:359
  189.6 57.2 %collective-permute-start.32 = (bf16[400,1536]{1,0:T(8,128)(2,1)}, bf16[400,1536]{1,0:T(8,128)(2,1)S(1)}, u32[]{:S(2)}, u32[]{:S(2)}) collective-permute-start(bf16[400,1536]{1,0:T(8,128)(2,1)} %get-tuple-element.376), channel_id=1, source_target_pairs={{0,1},{1,0},{2,3},{3,2},{4,5},{5,4},{6,7},{7,6},{8,9},{9,8},{10,11... | collective-permute-start | bytes 3686408 | tf_op jit(solution)/shard_map/ppermute | solution.py:359
  189.7 57.2 %collective-permute-start.33 = (bf16[384,1536]{1,0:T(8,128)(2,1)}, bf16[384,1536]{1,0:T(8,128)(2,1)}, u32[]{:S(2)}, u32[]{:S(2)}) collective-permute-start(bf16[384,1536]{1,0:T(8,128)(2,1)} %copy-done.59), channel_id=1, source_target_pairs={{0,1},{1,0},{2,3},{3,2},{4,5},{5,4},{6,7},{7,6},{8,9},{9,8},{10,11... | collective-permute-start | bytes 3538952 | tf_op jit(solution)/shard_map/ppermute | solution.py:359
  192.2 74.7 %collective-permute-start.35 = (bf16[384,1536]{1,0:T(8,128)(2,1)}, bf16[384,1536]{1,0:T(8,128)(2,1)}, u32[]{:S(2)}, u32[]{:S(2)}) collective-permute-start(bf16[384,1536]{1,0:T(8,128)(2,1)} %copy-done.60), channel_id=1, source_target_pairs={{0,1},{1,0},{2,3},{3,2},{4,5},{5,4},{6,7},{7,6},{8,9},{9,8},{10,11... | collective-permute-start | bytes 3538952 | tf_op jit(solution)/shard_map/ppermute | solution.py:359
  221.9 29.8 %collective-permute-start.30 = (bf16[400,1536]{1,0:T(8,128)(2,1)S(1)}, bf16[400,1536]{1,0:T(8,128)(2,1)S(1)}, u32[]{:S(2)}, u32[]{:S(2)}) collective-permute-start(bf16[400,1536]{1,0:T(8,128)(2,1)S(1)} %add_convert_fusion.2), channel_id=1, source_target_pairs={{0,4},{2,6},{4,12},{6,14},{8,0},{10,2},{12,8},{14,10},{1,5},{3,7},... | collective-permute-start | bytes 3686408 | tf_op jit(solution)/shard_map/ppermute | solution.py:388
  222.2 29.5 %collective-permute-start.31 = (bf16[400,1536]{1,0:T(8,128)(2,1)S(1)}, bf16[400,1536]{1,0:T(8,128)(2,1)S(1)}, u32[]{:S(2)}, u32[]{:S(2)}) collective-permute-start(bf16[400,1536]{1,0:T(8,128)(2,1)S(1)} %copy-done.93), channel_id=1, source_target_pairs={{0,1},{1,0},{2,3},{3,2},{4,5},{5,4},{6,7},{7,6},{8,9},{9,8},{10,11... | collective-permute-start | bytes 3686408 | tf_op jit(solution)/shard_map/ppermute | solution.py:359
  252.2 29.1 %collective-permute-start.34 = (bf16[400,1536]{1,0:T(8,128)(2,1)S(1)}, bf16[400,1536]{1,0:T(8,128)(2,1)}, u32[]{:S(2)}, u32[]{:S(2)}) collective-permute-start(bf16[400,1536]{1,0:T(8,128)(2,1)S(1)} %add_convert_fusion.1), channel_id=1, source_target_pairs={{0,4},{2,6},{4,12},{6,14},{8,0},{10,2},{12,8},{14,10},{1,5},{3,7},... | collective-permute-start | bytes 3686408 | tf_op jit(solution)/shard_map/ppermute | solution.py:388
  281.3 32.5 %collective-permute-start.38 = (bf16[1536,768]{1,0:T(8,128)(2,1)}, bf16[1536,768]{1,0:T(8,128)(2,1)}, u32[]{:S(2)}, u32[]{:S(2)}) collective-permute-start(bf16[1536,768]{1,0:T(8,128)(2,1)} %fusion.8), channel_id=1, source_target_pairs={{1,3},{2,0},{5,7},{6,4},{9,11},{10,8},{13,15},{14,12},{17,19},{18,... | collective-permute-start | bytes 7077896 | tf_op jit(solution)/shard_map/ppermute | solution.py:393
  282.6 27.7 %collective-permute-start.27 = (bf16[384,1536]{1,0:T(8,128)(2,1)}, bf16[384,1536]{1,0:T(8,128)(2,1)}, u32[]{:S(2)}, u32[]{:S(2)}) collective-permute-start(bf16[384,1536]{1,0:T(8,128)(2,1)} %get-tuple-element.362), channel_id=1, source_target_pairs={{0,1},{1,0},{2,3},{3,2},{4,5},{5,4},{6,7},{7,6},{8,9},{9,8},{10,11... | collective-permute-start | bytes 3538952 | tf_op jit(solution)/shard_map/ppermute | solution.py:359
  283.8 26.5 %collective-permute-start.37 = (bf16[384,1536]{1,0:T(8,128)(2,1)}, bf16[384,1536]{1,0:T(8,128)(2,1)}, u32[]{:S(2)}, u32[]{:S(2)}) collective-permute-start(bf16[384,1536]{1,0:T(8,128)(2,1)} %get-tuple-element.391), channel_id=1, source_target_pairs={{0,1},{1,0},{2,3},{3,2},{4,5},{5,4},{6,7},{7,6},{8,9},{9,8},{10,11... | collective-permute-start | bytes 3538952 | tf_op jit(solution)/shard_map/ppermute | solution.py:359
  283.8 30.0 %collective-permute-start.36 = (bf16[384,1536]{1,0:T(8,128)(2,1)}, bf16[384,1536]{1,0:T(8,128)(2,1)}, u32[]{:S(2)}, u32[]{:S(2)}) collective-permute-start(bf16[384,1536]{1,0:T(8,128)(2,1)} %add_convert_fusion.10), channel_id=1, source_target_pairs={{0,4},{2,6},{4,12},{6,14},{8,0},{10,2},{12,8},{14,10},{1,5},{3,7},... | collective-permute-start | bytes 3538952 | tf_op jit(solution)/shard_map/ppermute | solution.py:388
  284.2 29.6 %collective-permute-start.39 = (bf16[768,768]{1,0:T(8,128)(2,1)}, bf16[768,768]{1,0:T(8,128)(2,1)}, u32[]{:S(2)}, u32[]{:S(2)}) collective-permute-start(bf16[768,768]{1,0:T(8,128)(2,1)} %get-tuple-element.405), channel_id=1, source_target_pairs={{0,16},{16,0},{1,17},{17,1},{2,18},{18,2},{3,19},{19,3},{4,20},{20... | collective-permute-start | bytes 3538952 | tf_op jit(solution)/shard_map/ppermute | solution.py:363
  313.8 12.9 %collective-permute-start.41 = (bf16[384,2048]{1,0:T(8,128)(2,1)S(1)}, bf16[384,2048]{1,0:T(8,128)(2,1)S(1)}, u32[]{:S(2)}, u32[]{:S(2)}) collective-permute-start(bf16[384,2048]{1,0:T(8,128)(2,1)S(1)} %shard_map.195.right_own.grad_ref), channel_id=1, source_target_pairs={{0,1},{1,0},{2,3},{3,2},{4,5},{5,4},{6,7},{7,6},{8,9},{9,8},{10,11... | collective-permute-start | bytes 4718600 | tf_op jit(solution)/shard_map/ppermute | solution.py:359
  313.8 18.9 %collective-permute-start.40 = (bf16[400,1536]{1,0:T(8,128)(2,1)S(1)}, bf16[400,1536]{1,0:T(8,128)(2,1)S(1)}, u32[]{:S(2)}, u32[]{:S(2)}) collective-permute-start(bf16[400,1536]{1,0:T(8,128)(2,1)S(1)} %copy-done.5), channel_id=1, source_target_pairs={{0,1},{1,0},{2,3},{3,2},{4,5},{5,4},{6,7},{7,6},{8,9},{9,8},{10,11... | collective-permute-start | bytes 3686408 | tf_op jit(solution)/shard_map/ppermute | solution.py:359
  314.3 18.4 %collective-permute-start.42 = (bf16[768,768]{1,0:T(8,128)(2,1)S(1)}, bf16[768,768]{1,0:T(8,128)(2,1)S(1)}, u32[]{:S(2)}, u32[]{:S(2)}) collective-permute-start(bf16[768,768]{1,0:T(8,128)(2,1)S(1)} %copy-done.76), channel_id=1, source_target_pairs={{1,3},{2,0},{5,7},{6,4},{9,11},{10,8},{13,15},{14,12},{17,19},{18,... | collective-permute-start | bytes 3538952 | tf_op jit(solution)/shard_map/ppermute | solution.py:393
  315.6 15.9 %collective-permute-start.43 = (bf16[384,768]{1,0:T(8,128)(2,1)S(1)}, bf16[384,768]{1,0:T(8,128)(2,1)S(1)}, u32[]{:S(2)}, u32[]{:S(2)}) collective-permute-start(bf16[384,768]{1,0:T(8,128)(2,1)S(1)} %copy-done.84), channel_id=1, source_target_pairs={{0,16},{16,0},{1,17},{17,1},{2,18},{18,2},{3,19},{19,3},{4,20},{20... | collective-permute-start | bytes 1769480 | tf_op jit(solution)/shard_map/ppermute | solution.py:363
  332.7 19.4 %collective-permute-start.46 = (bf16[192,2048]{1,0:T(8,128)(2,1)S(1)}, bf16[192,2048]{1,0:T(8,128)(2,1)}, u32[]{:S(2)}, u32[]{:S(2)}) collective-permute-start(bf16[192,2048]{1,0:T(8,128)(2,1)S(1)} %get-tuple-element.444), channel_id=1, source_target_pairs={{0,16},{16,0},{1,17},{17,1},{2,18},{18,2},{3,19},{19,3},{4,20},{20... | collective-permute-start | bytes 2359304 | tf_op jit(solution)/shard_map/ppermute | solution.py:363
  333.2 20.8 %collective-permute-start.45 = (bf16[192,2048]{1,0:T(8,128)(2,1)S(1)}, bf16[192,2048]{1,0:T(8,128)(2,1)}, u32[]{:S(2)}, u32[]{:S(2)}) collective-permute-start(bf16[192,2048]{1,0:T(8,128)(2,1)S(1)} %get-tuple-element.442), channel_id=1, source_target_pairs={{0,2},{2,0},{4,6},{6,4},{8,10},{10,8},{12,14},{14,12},{1,3},{3,1},... | collective-permute-start | bytes 2359304 | tf_op jit(solution)/shard_map/ppermute | solution.py:374
  336.1 28.9 %collective-permute-start.44 = (bf16[384,1536]{1,0:T(8,128)(2,1)}, bf16[384,1536]{1,0:T(8,128)(2,1)}, u32[]{:S(2)}, u32[]{:S(2)}) collective-permute-start(bf16[384,1536]{1,0:T(8,128)(2,1)} %add_convert_fusion.9), channel_id=1, source_target_pairs={{0,4},{2,6},{4,12},{6,14},{8,0},{10,2},{12,8},{14,10},{1,5},{3,7},... | collective-permute-start | bytes 3538952 | tf_op jit(solution)/shard_map/ppermute | solution.py:388
  336.5 30.7 %collective-permute-start.47 = (bf16[768,768]{1,0:T(8,128)(2,1)}, bf16[768,768]{1,0:T(8,128)(2,1)}, u32[]{:S(2)}, u32[]{:S(2)}) collective-permute-start(bf16[768,768]{1,0:T(8,128)(2,1)} %get-tuple-element.450), channel_id=1, source_target_pairs={{0,16},{3,19},{4,20},{7,23},{8,24},{11,27},{12,28},{15,31},{16,0},... | collective-permute-start | bytes 3538952 | tf_op jit(solution)/shard_map/ppermute | solution.py:370
  339.9 27.4 %collective-permute-start.48 = (bf16[768,768]{1,0:T(8,128)(2,1)}, bf16[768,768]{1,0:T(8,128)(2,1)}, u32[]{:S(2)}, u32[]{:S(2)}) collective-permute-start(bf16[768,768]{1,0:T(8,128)(2,1)} %add_convert_fusion.8), channel_id=1, source_target_pairs={{1,3},{2,0},{5,7},{6,4},{9,11},{10,8},{13,15},{14,12},{17,19},{18,... | collective-permute-start | bytes 3538952 | tf_op jit(solution)/shard_map/ppermute | solution.py:393
  367.3 23.4 %collective-permute-start.54 = (bf16[192,1536]{1,0:T(8,128)(2,1)S(1)}, bf16[192,1536]{1,0:T(8,128)(2,1)S(1)}, u32[]{:S(2)}, u32[]{:S(2)}) collective-permute-start(bf16[192,1536]{1,0:T(8,128)(2,1)S(1)} %get-tuple-element.475), channel_id=1, source_target_pairs={{0,16},{16,0},{1,17},{17,1},{2,18},{18,2},{3,19},{19,3},{4,20},{20... | collective-permute-start | bytes 1769480 | tf_op jit(solution)/shard_map/ppermute | solution.py:363
  368.5 21.4 %collective-permute-start.49 = (bf16[96,2048]{1,0:T(8,128)(2,1)S(1)}, bf16[96,2048]{1,0:T(8,128)(2,1)S(1)}, u32[]{:S(2)}, u32[]{:S(2)}) collective-permute-start(bf16[96,2048]{1,0:T(8,128)(2,1)S(1)} %get-tuple-element.463), channel_id=1, source_target_pairs={{0,16},{16,0},{1,17},{17,1},{2,18},{18,2},{3,19},{19,3},{4,20},{20... | collective-permute-start | bytes 1179656 | tf_op jit(solution)/shard_map/ppermute | solution.py:363
  369.8 28.5 %collective-permute-start.53 = (bf16[384,1536]{1,0:T(8,128)(2,1)S(1)}, bf16[384,1536]{1,0:T(8,128)(2,1)S(1)}, u32[]{:S(2)}, u32[]{:S(2)}) collective-permute-start(bf16[384,1536]{1,0:T(8,128)(2,1)S(1)} %add_convert_fusion.7), channel_id=1, source_target_pairs={{0,4},{2,6},{4,12},{6,14},{8,0},{10,2},{12,8},{14,10},{1,5},{3,7},... | collective-permute-start | bytes 3538952 | tf_op jit(solution)/shard_map/ppermute | solution.py:388
  369.8 26.4 %collective-permute-start.51 = (bf16[384,768]{1,0:T(8,128)(2,1)S(1)}, bf16[384,768]{1,0:T(8,128)(2,1)S(1)}, u32[]{:S(2)}, u32[]{:S(2)}) collective-permute-start(bf16[384,768]{1,0:T(8,128)(2,1)S(1)} %get-tuple-element.471), channel_id=1, source_target_pairs={{0,16},{3,19},{4,20},{7,23},{8,24},{11,27},{12,28},{15,31},{16,0},... | collective-permute-start | bytes 1769480 | tf_op jit(solution)/shard_map/ppermute | solution.py:370
  378.2 18.0 %collective-permute-start.52 = (bf16[384,768]{1,0:T(8,128)(2,1)S(1)}, bf16[384,768]{1,0:T(8,128)(2,1)S(1)}, u32[]{:S(2)}, u32[]{:S(2)}) collective-permute-start(bf16[384,768]{1,0:T(8,128)(2,1)S(1)} %add_convert_fusion.17), channel_id=1, source_target_pairs={{1,3},{2,0},{5,7},{6,4},{9,11},{10,8},{13,15},{14,12},{17,19},{18,... | collective-permute-start | bytes 1769480 | tf_op jit(solution)/shard_map/ppermute | solution.py:393
  398.2 17.1 %collective-permute-start.58 = (bf16[48,2048]{1,0:T(8,128)(2,1)S(1)}, bf16[48,2048]{1,0:T(8,128)(2,1)S(1)}, u32[]{:S(2)}, u32[]{:S(2)}) collective-permute-start(bf16[48,2048]{1,0:T(8,128)(2,1)S(1)} %get-tuple-element.482), channel_id=1, source_target_pairs={{0,8},{2,10},{4,12},{6,14},{8,0},{10,2},{12,4},{14,6},{1,9},{3,11}... | collective-permute-start | bytes 589832 | tf_op jit(solution)/shard_map/ppermute | solution.py:383
  399.8 15.5 %collective-permute-start.59 = (bf16[48,2048]{1,0:T(8,128)(2,1)S(1)}, bf16[48,2048]{1,0:T(8,128)(2,1)S(1)}, u32[]{:S(2)}, u32[]{:S(2)}) collective-permute-start(bf16[48,2048]{1,0:T(8,128)(2,1)S(1)} %get-tuple-element.483), channel_id=1, source_target_pairs={{0,12},{2,14},{4,8},{6,10},{8,4},{10,6},{12,0},{14,2},{1,13},{3,15... | collective-permute-start | bytes 589832 | tf_op jit(solution)/shard_map/ppermute | solution.py:383
  402.6 14.2 %collective-permute-start.56 = (bf16[192,1664]{1,0:T(8,128)(2,1)S(1)}, bf16[192,1664]{1,0:T(8,128)(2,1)S(1)}, u32[]{:S(2)}, u32[]{:S(2)}) collective-permute-start(bf16[192,1664]{1,0:T(8,128)(2,1)S(1)} %get-tuple-element.479), channel_id=1, source_target_pairs={{0,16},{16,0},{1,17},{17,1},{2,18},{18,2},{3,19},{19,3},{4,20},{20... | collective-permute-start | bytes 1916936 | tf_op jit(solution)/shard_map/ppermute | solution.py:363
  403.1 14.0 %collective-permute-start.55 = (bf16[192,1664]{1,0:T(8,128)(2,1)S(1)}, bf16[192,1664]{1,0:T(8,128)(2,1)S(1)}, u32[]{:S(2)}, u32[]{:S(2)}) collective-permute-start(bf16[192,1664]{1,0:T(8,128)(2,1)S(1)} %get-tuple-element.477), channel_id=1, source_target_pairs={{0,2},{2,0},{4,6},{6,4},{8,10},{10,8},{12,14},{14,12},{1,3},{3,1},... | collective-permute-start | bytes 1916936 | tf_op jit(solution)/shard_map/ppermute | solution.py:374
  418.7 15.9 %collective-permute-start.63 = (bf16[48,2048]{1,0:T(8,128)(2,1)S(1)}, bf16[48,2048]{1,0:T(8,128)(2,1)S(1)}, u32[]{:S(2)}, u32[]{:S(2)}) collective-permute-start(bf16[48,2048]{1,0:T(8,128)(2,1)S(1)} %add_convert_fusion.22), channel_id=1, source_target_pairs={{0,8},{2,10},{4,12},{6,14},{8,0},{10,2},{12,4},{14,6},{1,9},{3,11}... | collective-permute-start | bytes 589832 | tf_op jit(solution)/shard_map/ppermute | solution.py:383
  419.9 14.6 %collective-permute-start.64 = (bf16[48,2048]{1,0:T(8,128)(2,1)S(1)}, bf16[48,2048]{1,0:T(8,128)(2,1)S(1)}, u32[]{:S(2)}, u32[]{:S(2)}) collective-permute-start(bf16[48,2048]{1,0:T(8,128)(2,1)S(1)} %add_convert_fusion.22), channel_id=1, source_target_pairs={{0,12},{2,14},{4,8},{6,10},{8,4},{10,6},{12,0},{14,2},{1,13},{3,15... | collective-permute-start | bytes 589832 | tf_op jit(solution)/shard_map/ppermute | solution.py:383
  421.8 20.2 %collective-permute-start.65 = (bf16[192,1536]{1,0:T(8,128)(2,1)S(1)}, bf16[192,1536]{1,0:T(8,128)(2,1)S(1)}, u32[]{:S(2)}, u32[]{:S(2)}) collective-permute-start(bf16[192,1536]{1,0:T(8,128)(2,1)S(1)} %get-tuple-element.501), channel_id=1, source_target_pairs={{0,16},{16,0},{1,17},{17,1},{2,18},{18,2},{3,19},{19,3},{4,20},{20... | collective-permute-start | bytes 1769480 | tf_op jit(solution)/shard_map/ppermute | solution.py:363
  424.7 16.7 %collective-permute-start.60 = (bf16[96,1664]{1,0:T(8,128)(2,1)S(1)}, bf16[96,1664]{1,0:T(8,128)(2,1)S(1)}, u32[]{:S(2)}, u32[]{:S(2)}) collective-permute-start(bf16[96,1664]{1,0:T(8,128)(2,1)S(1)} %get-tuple-element.496), channel_id=1, source_target_pairs={{0,16},{16,0},{1,17},{17,1},{2,18},{18,2},{3,19},{19,3},{4,20},{20... | collective-permute-start | bytes 958472 | tf_op jit(solution)/shard_map/ppermute | solution.py:363
  458.9 13.4 %collective-permute-start.72 = (bf16[48,1664]{1,0:T(8,128)(2,1)S(1)}, bf16[48,1664]{1,0:T(8,128)(2,1)S(1)}, u32[]{:S(2)}, u32[]{:S(2)}) collective-permute-start(bf16[48,1664]{1,0:T(8,128)(2,1)S(1)} %add_convert_fusion.23), channel_id=1, source_target_pairs={{0,8},{2,10},{4,12},{6,14},{8,0},{10,2},{12,4},{14,6},{1,9},{3,11}... | collective-permute-start | bytes 479240 | tf_op jit(solution)/shard_map/ppermute | solution.py:383
  462.2 17.4 %collective-permute-start.74 = (bf16[192,2048]{1,0:T(8,128)(2,1)S(1)}, bf16[192,2048]{1,0:T(8,128)(2,1)S(1)}, u32[]{:S(2)}, u32[]{:S(2)}) collective-permute-start(bf16[192,2048]{1,0:T(8,128)(2,1)S(1)} %maximum_select_fusion.4.refs_0_), channel_id=1, source_target_pairs={{0,2},{2,0},{4,6},{6,4},{8,10},{10,8},{12,14},{14,12},{1,3},{3,1},... | collective-permute-start | bytes 2359304 | tf_op jit(solution)/shard_map/ppermute | solution.py:374
  463.8 17.2 %collective-permute-start.75 = (bf16[192,2048]{1,0:T(8,128)(2,1)S(1)}, bf16[192,2048]{1,0:T(8,128)(2,1)S(1)}, u32[]{:S(2)}, u32[]{:S(2)}) collective-permute-start(bf16[192,2048]{1,0:T(8,128)(2,1)S(1)} %maximum_select_fusion.5.refs_2_), channel_id=1, source_target_pairs={{0,16},{16,0},{1,17},{17,1},{2,18},{18,2},{3,19},{19,3},{4,20},{20... | collective-permute-start | bytes 2359304 | tf_op jit(solution)/shard_map/ppermute | solution.py:363
  493.2 15.5 %collective-permute-start.80 = (bf16[192,1664]{1,0:T(8,128)(2,1)S(1)}, bf16[192,1664]{1,0:T(8,128)(2,1)S(1)}, u32[]{:S(2)}, u32[]{:S(2)}) collective-permute-start(bf16[192,1664]{1,0:T(8,128)(2,1)S(1)} %maximum_select_fusion.6.first), channel_id=1, source_target_pairs={{0,2},{2,0},{4,6},{6,4},{8,10},{10,8},{12,14},{14,12},{1,3},{3,1},... | collective-permute-start | bytes 1916936 | tf_op jit(solution)/shard_map/ppermute | solution.py:374
  494.7 15.2 %collective-permute-start.81 = (bf16[192,1664]{1,0:T(8,128)(2,1)S(1)}, bf16[192,1664]{1,0:T(8,128)(2,1)S(1)}, u32[]{:S(2)}, u32[]{:S(2)}) collective-permute-start(bf16[192,1664]{1,0:T(8,128)(2,1)S(1)} %maximum_select_fusion.7.second), channel_id=1, source_target_pairs={{0,16},{16,0},{1,17},{17,1},{2,18},{18,2},{3,19},{19,3},{4,20},{20... | collective-permute-start | bytes 1916936 | tf_op jit(solution)/shard_map/ppermute | solution.py:363
  (120 other events, 1075.7 us)

commit v6 on v5

--- a/solution.py
+++ b/solution.py
@@ -964,6 +964,38 @@
     )(held_at, middle, *sums)
 
 
+def add_cut_kernel(dp_ref, own_ref, got_ref, sent_ref, kept_ref):
+    field = low(sum_blocks(own_ref[...], got_ref[...]))
+
+    @pl.when(pl.program_id(0) == 0)
+    def _():
+        sent_ref[...] = field
+
+    @pl.when(pl.program_id(0) == 1)
+    def _():
+        kept_ref[...] = field
+
+
+def add_cut(own, got, dp):
+    rows, columns = own.shape
+
+    def half(i, dp_ref):
+        return jnp.where(i == 0, 1 - dp_ref[0], dp_ref[0]), 0
+
+    block_of = pl.BlockSpec((rows // 2, columns), half)
+    whole = pl.BlockSpec((rows // 2, columns), lambda i, dp_ref: (0, 0))
+    sent, kept = pl.pallas_call(
+        add_cut_kernel,
+        grid_spec=pltpu.PrefetchScalarGridSpec(
+            num_scalar_prefetch=1, grid=(2,), in_specs=[block_of] * 2, out_specs=[whole] * 2
+        ),
+        out_shape=[jax.ShapeDtypeStruct((rows // 2, columns), jnp.bfloat16)] * 2,
+        compiler_params=pltpu.CompilerParams(vmem_limit_bytes=24 * 2**20),
+        cost_estimate=SHORT,
+    )(dp[None].astype(jnp.int32), own, got)
+    return kept, sent
+
+
 def from_pieces(put, place_ref, pieces):
     step = pl.program_id(0)
     for half in range(2):
@@ -1244,7 +1276,7 @@
         return field[:half_rows], field[half_rows:]
 
     def to_dealt(halves):
-        return in_order(dp == 0, halves[0], other_dp(halves[1]))
+        return halves[0], other_dp(halves[1])
 
     ct_0 = dealt_unit(cotangent, deal_order)
     order = ct_0[count_of_rows:]
@@ -1333,30 +1365,61 @@
 
     back_2 = ring_z(low(sum_blocks(back_2[0], back_2_other, back_1)))
     back_3_other, back_0_other = other_core(back_3[1]), other_core(back_0[1])
-    sums_1_other = other_core(sums_1[1])
+    sums_1_other, sums_0_other = other_core(sums_1[1]), other_core(sums_0[1])
     all_hidden, all_grad_out, all_grad_up, all_rows = kept
     half_width = model_width // 2
     up_first = low(matmul(all_rows.T, all_grad_up[:, :half_width]))
     up_second = low(matmul(all_rows.T, all_grad_up[:, half_width:]))
-    back_2, back_3_other, back_0_other, sums_1_other, up_first, up_second, all_grad_out = part(
-        back_2, back_3_other, back_0_other, sums_1_other, up_first, up_second, all_grad_out
+    (
+        back_2,
+        back_3_other,
+        back_0_other,
+        sums_1_other,
+        sums_0_other,
+        up_first,
+        up_second,
+        all_grad_out,
+    ) = part(
+        back_2,
+        back_3_other,
+        back_0_other,
+        sums_1_other,
+        sums_0_other,
+        up_first,
+        up_second,
+        all_grad_out,
     )
 
     back_3 = ring_z(low(sum_blocks(back_3[0], back_3_other, back_2)))
     down_first = low(matmul(all_hidden.T, all_grad_out[:, :half_width]))
     down_second = low(matmul(all_hidden.T, all_grad_out[:, half_width:]))
     sums_1 = low(sum_blocks(sums_1[0], sums_1_other))
-    sums_2_other = other_core(sums_2[1])
+    sums_2_other, sums_3_other = other_core(sums_2[1]), other_core(sums_3[1])
     up_second = block(up_second, dp, 2), block(up_second, 1 - dp, 2)
     down_second = block(down_second, dp, 2), block(down_second, 1 - dp, 2)
-    back_3, up_first, up_second, down_first, down_second, sums_1, sums_2_other = part(
-        back_3, up_first, up_second, down_first, down_second, sums_1, sums_2_other
+    (
+        back_3,
+        up_first,
+        up_second,
+        down_first,
+        down_second,
+        sums_1,
+        sums_2_other,
+        sums_3_other,
+    ) = part(
+        back_3,
+        up_first,
+        up_second,
+        down_first,
+        down_second,
+        sums_1,
+        sums_2_other,
+        sums_3_other,
     )
 
     sums_1 = ring_z(sums_1)
     up_first = up_first, to_owner(up_first)
     up_second = up_second[0], other_dp(up_second[1])
-    sums_0_other, sums_3_other = other_core(sums_0[1]), other_core(sums_3[1])
     grad_middle, grad_unit, grad_mix = middle_back(
         (back_0[0], back_0_other, back_3),
         gates,
@@ -1368,33 +1431,14 @@
         full_out,
     )
     grad_projected = attend_back(query, key, value, grad_mix, cosine, sine, segment)
-    (
-        sums_0_other,
-        sums_1,
-        sums_3_other,
-        grad_projected,
-        grad_unit,
-        up_first,
-        up_second,
-        down_first,
-        down_second,
-    ) = part(
-        sums_0_other,
-        sums_1,
-        sums_3_other,
-        grad_projected,
-        grad_unit,
-        up_first,
-        up_second,
-        down_first,
-        down_second,
+    sums_1, grad_projected, grad_unit, up_first, up_second, down_first, down_second = part(
+        sums_1, grad_projected, grad_unit, up_first, up_second, down_first, down_second
     )
 
     grads_projected, grad_units = swapped(grad_projected), swapped(grad_unit)
     down_first = down_first, to_owner(down_first)
     down_second = down_second[0], other_dp(down_second[1])
-    up_first, up_second = low(sum_blocks(*up_first)), low(sum_blocks(*up_second))
-    up_first = block(up_first, dp, 2), block(up_first, 1 - dp, 2)
+    up_first, up_second = add_cut(*up_first, dp), low(sum_blocks(*up_second))
     sums_2 = low(sum_blocks(sums_2[0], sums_2_other, sums_1))
     qkv = qkv_grads(normeds, grads_projected, place)
     sums_2, grad_units, qkv, down_first, down_second, up_first, up_second, grad_projected = part(
@@ -1453,10 +1497,13 @@
     qkv_grad, gain_first_grad = finish(
         finish_qkv_kernel, qkv, place, [qkv_weight, gain], [qkv_weight.shape[1], 1]
     )
-    out, qkv_grad, gain_first_grad, up_grad, down_grad = part(
-        out, qkv_grad, gain_first_grad, up_grad, down_grad
-    )
-
+    out, qkv_grad, gain_first_grad, up_grad, down_grad, layer_out, input_gradient = part(
+        out, qkv_grad, gain_first_grad, up_grad, down_grad, layer_out, input_gradient
+    )
+
+    layer_out, input_gradient = (
+        in_order(dp == 0, *field) for field in (layer_out, input_gradient)
+    )
     out_grad, small_grad = finish_out(out, place, True, [])
     (_, first), (_, second) = slab_spread_on(out)
     out_grad, small_grad = finish_out([first, second], place, False, [out_grad, small_grad])

time: 523 us -> 520 us (level)
  local copies, waits for them, and re-layouts: 40.5 us -> 34.4 us
    unnamed x205 -> x219, local copies, waits for them, and re-layouts: 21.9 us -> 16.4 us
    ppermute x17, waiting for transfers between devices: 41.9 us -> 36.6 us  [other_dp(): return lax.ppermute(field, 'dp', [(0, 1), (1, 0)])]
    convert_element_type x17 -> x16, other arithmetic: 23.7 us -> 22.8 us  [low(): return field.astype(jnp.bfloat16)]
  transfers between devices with their start and end apart: 82 -> 82, of which waited for: 33 -> 33; matrix products, arithmetic and copies ran while one was open for 23% -> 22% of each run, Pallas kernels for 26% -> 27%
where the time goes in v6:
time: 520 us; the launch traced here: 511 us
  waiting for transfers between devices  152 us (29%)
  Pallas kernels  140 us (27%)
  starting transfers between devices  81.8 us (16%)
  other arithmetic  56.9 us (11%)
  matrix products  43 us (8%)
  local copies, waits for them, and re-layouts  34.4 us (7%)
    pallas_call x4, Pallas kernels, expert_step(): pl.pallas_call(functools.partial(expert_kernel, columns=256), grid=(2,),...  82.2 us
    ppermute x12, waiting for transfers between devices, ring_z(): return lax.ppermute(field, 'expert', pairs)  56.5 us
    dot_general x11, matrix products, matmul(): lax.dot_general(left, right, dims, preferred_element_type=jnp.float32)  43 us
    ppermute x17, waiting for transfers between devices, other_dp(): return lax.ppermute(field, 'dp', [(0, 1), (1, 0)])  36.6 us
    ppermute x12, waiting for transfers between devices, across_z(): lax.ppermute(field, 'expert', [(i, i ^ 2 * distance) for i in range(8)])  31.5 us
    convert_element_type x16, other arithmetic, low(): return field.astype(jnp.bfloat16)  22.8 us
    ppermute x12, starting transfers between devices, across_z(): lax.ppermute(field, 'expert', [(i, i ^ 2 * distance) for i in range(8)])  18 us
    unnamed x219, local copies, waits for them, and re-layouts  16.4 us
  transfers between devices with their start and end apart: 82, of which 33 were waited for; matrix products, arithmetic and copies ran while one was open for 22% of the time, Pallas kernels for 27%

profile of v6, /device:TPU:0, one launch (start us, length us, event | category | flops | bytes accessed | tf_op | source)
XLA Modules:
  0.0 511.2 jit_solution(7096979689792472643)
XLA Ops:
  4.4 2.6 collective-permute-start.2
  8.7 5.5 %collective-permute-start.7 = (bf16[1536,1536]{1,0:T(8,128)(2,1)}, bf16[1536,1536]{1,0:T(8,128)(2,1)}, u32[]{:S(2)}, u32[]{:S(2)}) collective-permute-start(bf16[1536,1536]{1,0:T(8,128)(2,1)} %bitcast.61), channel_id=1, source_target_pairs={{0,2},{3,1},{4,6},{7,5},{8,10},{11,9},{12,14},{15,13},{16,18},{19,... | collective-permute-start | bytes 14155784 | tf_op jit(solution)/shard_map/ppermute | solution.py:398
  18.4 8.1 %maximum_select_fusion.weight_ref = bf16[1536,2048]{1,0:T(8,128)(2,1)} fusion(bf16[768,2048]{1,0:T(8,128)(2,1)} %collective-permute-done.1, bf16[768,2048]{1,0:T(8,128)(2,1)} %refs_4_.1, pred[]{:T(512)S(6)} %eq.180), kind=kLoop, calls=%fused_computation | loop fusion | flops 28311552 | bytes 12582913 | tf_op jit(solution)/shard_map/jit(_where)/select_n | solution.py:402
  29.4 2.6 fusion.77.query_in.key_in.value_in
  32.0 5.3 %collective-permute-done = bf16[400,1536]{1,0:T(8,128)(2,1)} collective-permute-done((bf16[400,1536]{1,0:T(8,128)(2,1)}, bf16[400,1536]{1,0:T(8,128)(2,1)}, u32[]{:S(2)}, u32[]{:S(2)}) %collective-permute-start) | collective-permute-done | bytes 1228832 | tf_op jit(solution)/shard_map/ppermute | solution.py:388
  40.7 3.5 collective-permute-start.12
  44.3 7.4 %shard_map.188 = (bf16[384,1536]{1,0:T(8,128)(2,1)S(1)}, bf16[384,256]{1,0:T(8,128)(2,1)S(1)}, bf16[384,256]{1,0:T(8,128)(2,1)S(1)}, bf16[384,1536]{1,0:T(8,128)(2,1)S(1)}) custom-call(f32[384,2048]{1,0:T(8,128)S(1)} %fusion.77.query_in.key_in.value_in, f32[384,2048]{1,0:T(8,128)S(1)} %fusion.77.query_in.key_in.value_in, ...), custom_call_target="tpu_custom_call" | custom-call | flops 1000 | bytes 1000 | tf_op jit(solution)/shard_map/pallas_call | solution.py:1133
  51.8 4.8 maximum_select_fusion.1.weight_ref
  56.6 2.7 shard_map.189
  61.5 5.3 %collective-permute-done.5 = bf16[400,1536]{1,0:T(8,128)(2,1)} collective-permute-done((bf16[400,1536]{1,0:T(8,128)(2,1)}, bf16[400,1536]{1,0:T(8,128)(2,1)}, u32[]{:S(2)}, u32[]{:S(2)}) %collective-permute-start.5) | collective-permute-done | bytes 1228832 | tf_op jit(solution)/shard_map/ppermute | solution.py:388
  71.7 14.3 %collective-permute-done.11 = bf16[192,1536]{1,0:T(8,128)(2,1)S(1)} collective-permute-done((bf16[192,1536]{1,0:T(8,128)(2,1)S(1)}, bf16[192,1536]{1,0:T(8,128)(2,1)S(1)}, u32[]{:S(2)}, u32[]{:S(2)}) %collective-permute-start.11) | collective-permute-done | bytes 589856 | tf_op jit(solution)/shard_map/ppermute | solution.py:363
  86.0 3.3 collective-permute-done.12.down_other
  89.4 5.8 %collective-permute-done.8.own_rows = bf16[400,1536]{1,0:T(8,128)(2,1)} collective-permute-done((bf16[400,1536]{1,0:T(8,128)(2,1)S(1)}, bf16[400,1536]{1,0:T(8,128)(2,1)}, u32[]{:S(2)}, u32[]{:S(2)}) %collective-permute-start.8) | collective-permute-done | bytes 1228832 | tf_op jit(solution)/shard_map/ppermute | solution.py:388
  98.7 2.3 constant_dynamic-slice_fusion.16
  101.7 20.5 %shard_map.190 = (bf16[384,1536]{1,0:T(8,128)(2,1)S(1)}, bf16[384,1536]{1,0:T(8,128)(2,1)S(1)}, bf16[400,1536]{1,0:T(8,128)(2,1)}, bf16[400,1536]{1,0:T(8,128)(2...) custom-call(s32[2]{0:T(128)S(1)} %pad_add_fusion.choice, ...), custom_call_target="tpu_custom_call" | custom-call | flops 1000 | bytes 1000 | tf_op jit(solution)/shard_map/pallas_call | solution.py:623
  123.6 3.6 collective-permute-start.17
  132.1 20.8 %shard_map.191 = (bf16[384,1536]{1,0:T(8,128)(2,1)S(1)}, bf16[384,1536]{1,0:T(8,128)(2,1)S(1)}, bf16[400,1536]{1,0:T(8,128)(2,1)}, bf16[400,1536]{1,0:T(8,128)(2...) custom-call(s32[2]{0:T(128)S(1)} %pad_add_fusion.choice, ...), custom_call_target="tpu_custom_call", output_to_operand_aliasing={{4}: (9, {}), {5}: (10, {}), {6}: (11, {}), {7}: (12, {})} | custom-call | flops 1000 | bytes 1000 | tf_op jit(solution)/shard_map/pallas_call | solution.py:623
  159.9 20.4 %shard_map.192 = (bf16[384,1536]{1,0:T(8,128)(2,1)S(1)}, bf16[384,1536]{1,0:T(8,128)(2,1)S(1)}, bf16[400,1536]{1,0:T(8,128)(2,1)}, bf16[400,1536]{1,0:T(8,128)(2...) custom-call(s32[2]{0:T(128)S(1)} %pad_add_fusion.choice, ...), custom_call_target="tpu_custom_call", output_to_operand_aliasing={{4}: (9, {}), {5}: (10, {}), {6}: (11, {}), {7}: (12, {})} | custom-call | flops 1000 | bytes 1000 | tf_op jit(solution)/shard_map/pallas_call | solution.py:623
  180.3 3.5 add_convert_fusion.2
  183.8 3.2 collective-permute-done.22.own_rows
  188.3 2.0 collective-permute-done.26.other_rows
  190.4 20.5 %shard_map.193 = (bf16[384,1536]{1,0:T(8,128)(2,1)S(1)}, bf16[384,1536]{1,0:T(8,128)(2,1)S(1)}, bf16[400,1536]{1,0:T(8,128)(2,1)}, bf16[400,1536]{1,0:T(8,128)(2...) custom-call(s32[2]{0:T(128)S(1)} %pad_add_fusion.choice, ...), custom_call_target="tpu_custom_call", output_to_operand_aliasing={{4}: (9, {}), {5}: (10, {}), {6}: (11, {}), {7}: (12, {})} | custom-call | flops 1000 | bytes 1000 | tf_op jit(solution)/shard_map/pallas_call | solution.py:623
  210.9 6.9 %collective-permute-done.27 = bf16[400,1536]{1,0:T(8,128)(2,1)} collective-permute-done((bf16[400,1536]{1,0:T(8,128)(2,1)}, bf16[400,1536]{1,0:T(8,128)(2,1)}, u32[]{:S(2)}, u32[]{:S(2)}) %collective-permute-start.27) | collective-permute-done | bytes 1228832 | tf_op jit(solution)/shard_map/ppermute | solution.py:388
  217.8 2.1 add_convert_fusion.1
  220.3 11.7 %fusion.11 = bf16[1536,768]{1,0:T(8,128)(2,1)S(1)} fusion(bf16[3072,1536]{1,0:T(8,128)(2,1)} %get-tuple-element.386, bf16[3072,1536]{1,0:T(8,128)(2,1)} %get-tuple-element.387), kind=kOutput, calls=%fused_computation.11 | convolution fusion | flops 7248936960 | bytes 16515072 | tf_op jit(solution)/shard_map/dot_general | solution.py:477
  232.1 12.7 %fusion.8.own_ref = bf16[1536,768]{1,0:T(8,128)(2,1)} fusion(bf16[3072,1536]{1,0:T(8,128)(2,1)} %get-tuple-element.386, bf16[3072,1536]{1,0:T(8,128)(2,1)} %get-tuple-element.387), kind=kOutput, calls=%fused_computation.10 | convolution fusion | flops 7248936960 | bytes 16515072 | tf_op jit(solution)/shard_map/dot_general | solution.py:477
  245.5 4.3 collective-permute-done.29
  250.7 2.6 add_convert_fusion.9
  253.3 3.9 fusion.20
  259.9 5.0 fusion.17
  264.9 14.5 %collective-permute-done.34.back_ring.extra_ring = bf16[400,1536]{1,0:T(8,128)(2,1)S(1)} collective-permute-done((bf16[400,1536]{1,0:T(8,128)(2,1)S(1)}, bf16[400,1536]{1,0:T(8,128)(2,1)S(1)}, u32[]{:S(2)}, u32[]{:S(2)}) %collective-permute-start.34) | collective-permute-done | bytes 1228832 | tf_op jit(solution)/shard_map/ppermute | solution.py:388
  281.3 9.8 %shard_map.194 = (f32[384,1536]{1,0:T(8,128)}, bf16[400,1536]{1,0:T(8,128)(2,1)}, bf16[384,1536]{1,0:T(8,128)(2,1)}) custom-call(bf16[400,1536]{1,0:T(8,128)(2,1)} %get-tuple-element.406.back_own.extra_own, bf16[400,1536]{1,0:T(8,128)(2,1)} %copy-done.65, bf16[400,1536]{1,0:T(8,128)(2,1)} %copy-done.66, ...), custom_call_target="tpu_custom_call" | custom-call | flops 1000 | bytes 1000 | tf_op jit(solution)/shard_map/pallas_call | solution.py:734
  293.7 8.8 %shard_map.195.right_own.grad_ref = bf16[384,2048]{1,0:T(8,128)(2,1)S(1)} custom-call(bf16[384,1536]{1,0:T(8,128)(2,1)S(1)} %copy-done.36, bf16[384,256]{1,0:T(8,128)(2,1)S(1)} %copy-done.49, bf16[384,256]{1,0:T(8,128)(2,1)S(1)} %copy-done.51, bf16[384,1536]{1,0:T(8,128)(2,1)S(1)} %copy-done.43, f32[384,128]{1,0:T(8,128)S(1)} %get-tuple-element.295.cos_ref, ...), custom_call_target="tpu_custom_call" | custom-call | flops 1000 | bytes 1000 | tf_op jit(solution)/shard_map/pallas_call | solution.py:1213
  302.6 8.0 %collective-permute-done.37 = bf16[384,1536]{1,0:T(8,128)(2,1)} collective-permute-done((bf16[384,1536]{1,0:T(8,128)(2,1)}, bf16[384,1536]{1,0:T(8,128)(2,1)}, u32[]{:S(2)}, u32[]{:S(2)}) %collective-permute-start.37) | collective-permute-done | bytes 1179680 | tf_op jit(solution)/shard_map/ppermute | solution.py:388
  313.4 3.1 shard_map.197
  316.6 2.8 add_convert_fusion.7
  319.4 2.9 add_convert_fusion.8
  322.3 7.2 %shard_map.196 = (bf16[192,2048]{1,0:T(8,128)(2,1)S(1)}, bf16[192,2048]{1,0:T(8,128)(2,1)S(1)}, bf16[192,2048]{1,0:T(8,128)(2,1)S(1)}, bf16[192,2048]{1,0:T(8,128)(2,1)}) custom-call(s32[3]{0:T(128)S(1)} %pad_add_fusion.1.place_ref, bf16[384,1536]{1,0:T(8,128)(2,1)S(1)} %copy-done.20, bf16[384,1536]{1,0:T(8,128)(2,1)S(1)} %copy-done.38, ...), custom_call_target="tpu_custom_call" | custom-call | flops 1000 | bytes 1000 | tf_op jit(solution)/shard_map/pallas_call | solution.py:887
  331.1 3.7 collective-permute-start.45
  335.5 3.4 collective-permute-start.47
  340.3 3.3 shard_map.199
  343.6 5.6 %shard_map.198 = (bf16[192,1664]{1,0:T(8,128)(2,1)S(1)}, bf16[192,1664]{1,0:T(8,128)(2,1)S(1)}, bf16[192,1664]{1,0:T(8,128)(2,1)S(1)}, bf16[192,1664]{1,0:T(8,128)(2,1)S(1)}) custom-call(s32[3]{0:T(128)S(1)} %pad_add_fusion.1.place_ref, bf16[384,1536]{1,0:T(8,128)(2,1)S(1)} %copy-done.17, bf16[400,1536]{1,0:T(8,128)(2,1)S(1)} %copy-done.12, ...), custom_call_target="tpu_custom_call" | custom-call | flops 1000 | bytes 1000 | tf_op jit(solution)/shard_map/pallas_call | solution.py:887
  357.4 3.3 collective-permute-done.44
  366.1 2.7 collective-permute-start.51
  377.1 8.0 %collective-permute-done.51 = bf16[384,768]{1,0:T(8,128)(2,1)S(1)} collective-permute-done((bf16[384,768]{1,0:T(8,128)(2,1)S(1)}, bf16[384,768]{1,0:T(8,128)(2,1)S(1)}, u32[]{:S(2)}, u32[]{:S(2)}) %collective-permute-start.51) | collective-permute-done | bytes 589856 | tf_op jit(solution)/shard_map/ppermute | solution.py:370
  385.0 8.6 %collective-permute-done.54 = bf16[192,1536]{1,0:T(8,128)(2,1)S(1)} collective-permute-done((bf16[192,1536]{1,0:T(8,128)(2,1)S(1)}, bf16[192,1536]{1,0:T(8,128)(2,1)S(1)}, u32[]{:S(2)}, u32[]{:S(2)}) %collective-permute-start.54) | collective-permute-done | bytes 589856 | tf_op jit(solution)/shard_map/ppermute | solution.py:363
  395.8 2.3 collective-permute-start.59
  403.5 5.6 %collective-permute-done.58 = bf16[48,2048]{1,0:T(8,128)(2,1)S(1)} collective-permute-done((bf16[48,2048]{1,0:T(8,128)(2,1)S(1)}, bf16[48,2048]{1,0:T(8,128)(2,1)S(1)}, u32[]{:S(2)}, u32[]{:S(2)}) %collective-permute-start.58) | collective-permute-done | bytes 196640 | tf_op jit(solution)/shard_map/ppermute | solution.py:383
  415.5 2.1 collective-permute-start.64
  417.6 2.9 collective-permute-start.61
  422.5 8.1 %collective-permute-done.63 = bf16[48,2048]{1,0:T(8,128)(2,1)S(1)} collective-permute-done((bf16[48,2048]{1,0:T(8,128)(2,1)S(1)}, bf16[48,2048]{1,0:T(8,128)(2,1)S(1)}, u32[]{:S(2)}, u32[]{:S(2)}) %collective-permute-start.63) | collective-permute-done | bytes 196640 | tf_op jit(solution)/shard_map/ppermute | solution.py:383
  433.1 7.3 %collective-permute-done.65 = bf16[192,1536]{1,0:T(8,128)(2,1)S(1)} collective-permute-done((bf16[192,1536]{1,0:T(8,128)(2,1)S(1)}, bf16[192,1536]{1,0:T(8,128)(2,1)S(1)}, u32[]{:S(2)}, u32[]{:S(2)}) %collective-permute-start.65) | collective-permute-done | bytes 589856 | tf_op jit(solution)/shard_map/ppermute | solution.py:363
  441.8 2.4 collective-permute-start.67
  446.6 2.7 collective-permute-done.66
  449.3 4.9 collective-permute-done.67
  455.8 2.4 collective-permute-start.71
  462.7 8.7 %collective-permute-done.72 = bf16[48,1664]{1,0:T(8,128)(2,1)S(1)} collective-permute-done((bf16[48,1664]{1,0:T(8,128)(2,1)S(1)}, bf16[48,1664]{1,0:T(8,128)(2,1)S(1)}, u32[]{:S(2)}, u32[]{:S(2)}) %collective-permute-start.72) | collective-permute-done | bytes 159776 | tf_op jit(solution)/shard_map/ppermute | solution.py:383
  471.7 6.6 %collective-permute-done.74.refs_1_ = bf16[192,2048]{1,0:T(8,128)(2,1)S(1)} collective-permute-done((bf16[192,2048]{1,0:T(8,128)(2,1)S(1)}, bf16[192,2048]{1,0:T(8,128)(2,1)S(1)}, u32[]{:S(2)}, u32[]{:S(2)}) %collective-permute-start.74) | collective-permute-done | bytes 786464 | tf_op jit(solution)/shard_map/ppermute | solution.py:374
  481.1 4.0 shard_map.201
  485.4 4.5 collective-permute-done.76
  496.5 2.1 shard_map.202
  499.3 3.0 bitcast_convert_fusion
  502.3 4.6 collective-permute-done.80.first
  507.2 2.1 shard_map.203
  (448 shorter events, 119.7 us)
Async XLA Ops:
  3.9 14.5 %collective-permute-start.1 = (bf16[768,2048]{1,0:T(8,128)(2,1)}, bf16[768,2048]{1,0:T(8,128)(2,1)}, u32[]{:S(2)}, u32[]{:S(2)}) collective-permute-start(bf16[768,2048]{1,0:T(8,128)(2,1)} %refs_4_.1), channel_id=1, source_target_pairs={{0,1},{1,0},{2,3},{3,2},{4,5},{5,4},{6,7},{7,6},{8,9},{9,8},{10,11... | collective-permute-start | bytes 9437192 | tf_op jit(solution)/shard_map/ppermute | solution.py:359
  4.4 22.1 %collective-permute-start.2 = (bf16[192,1536]{1,0:T(8,128)(2,1)S(1)}, bf16[192,1536]{1,0:T(8,128)(2,1)S(1)}, u32[]{:S(2)}, u32[]{:S(2)}) collective-permute-start(bf16[192,1536]{1,0:T(8,128)(2,1)S(1)} %constant_dynamic-slice_fusion.22), channel_id=1, source_target_pairs={{0,16},{16,0},{1,17},{17,1},{2,18},{18,2},{3,19},{19,3},{4,20},{20... | collective-permute-start | bytes 1769480 | tf_op jit(solution)/shard_map/ppermute | solution.py:363
  7.0 30.3 %collective-permute-start = (bf16[400,1536]{1,0:T(8,128)(2,1)}, bf16[400,1536]{1,0:T(8,128)(2,1)}, u32[]{:S(2)}, u32[]{:S(2)}) collective-permute-start(bf16[400,1536]{1,0:T(8,128)(2,1)} %shard_map.187), channel_id=1, source_target_pairs={{0,4},{2,6},{4,12},{6,14},{8,0},{10,2},{12,8},{14,10},{1,5},{3,7},... | collective-permute-start | bytes 3686408 | tf_op jit(solution)/shard_map/ppermute | solution.py:388
  8.7 58.1 %collective-permute-start.7 = (bf16[1536,1536]{1,0:T(8,128)(2,1)}, bf16[1536,1536]{1,0:T(8,128)(2,1)}, u32[]{:S(2)}, u32[]{:S(2)}) collective-permute-start(bf16[1536,1536]{1,0:T(8,128)(2,1)} %bitcast.61), channel_id=1, source_target_pairs={{0,2},{3,1},{4,6},{7,5},{8,10},{11,9},{12,14},{15,13},{16,18},{19,... | collective-permute-start | bytes 14155784 | tf_op jit(solution)/shard_map/ppermute | solution.py:398
  17.6 19.7 %collective-permute-start.4 = (bf16[768,1536]{1,0:T(8,128)(2,1)}, bf16[768,1536]{1,0:T(8,128)(2,1)}, u32[]{:S(2)}, u32[]{:S(2)}) collective-permute-start(bf16[768,1536]{1,0:T(8,128)(2,1)} %param.20), channel_id=1, source_target_pairs={{0,1},{1,0},{2,3},{3,2},{4,5},{5,4},{6,7},{7,6},{8,9},{9,8},{10,11... | collective-permute-start | bytes 7077896 | tf_op jit(solution)/shard_map/ppermute | solution.py:359
  37.3 29.5 %collective-permute-start.5 = (bf16[400,1536]{1,0:T(8,128)(2,1)}, bf16[400,1536]{1,0:T(8,128)(2,1)}, u32[]{:S(2)}, u32[]{:S(2)}) collective-permute-start(bf16[400,1536]{1,0:T(8,128)(2,1)} %collective-permute-done), channel_id=1, source_target_pairs={{0,4},{2,6},{4,12},{6,14},{8,0},{10,2},{12,8},{14,10},{1,5},{3,7},... | collective-permute-start | bytes 3686408 | tf_op jit(solution)/shard_map/ppermute | solution.py:388
  40.1 21.4 %collective-permute-start.6 = (bf16[192,1536]{1,0:T(8,128)(2,1)S(1)}, bf16[192,1536]{1,0:T(8,128)(2,1)S(1)}, u32[]{:S(2)}, u32[]{:S(2)}) collective-permute-start(bf16[192,1536]{1,0:T(8,128)(2,1)S(1)} %get-tuple-element.604), channel_id=1, source_target_pairs={{0,16},{16,0},{1,17},{17,1},{2,18},{18,2},{3,19},{19,3},{4,20},{20... | collective-permute-start | bytes 1769480 | tf_op jit(solution)/shard_map/ppermute | solution.py:363
  40.7 48.6 %collective-permute-start.12 = (bf16[768,1536]{1,0:T(8,128)(2,1)}, bf16[768,1536]{1,0:T(8,128)(2,1)S(1)}, u32[]{:S(2)}, u32[]{:S(2)}) collective-permute-start(bf16[768,1536]{1,0:T(8,128)(2,1)} %bitcast.68), channel_id=1, source_target_pairs={{0,2},{3,1},{4,6},{7,5},{8,10},{11,9},{12,14},{15,13},{16,18},{19,... | collective-permute-start | bytes 7077896 | tf_op jit(solution)/shard_map/ppermute | solution.py:398
  66.8 28.3 %collective-permute-start.8 = (bf16[400,1536]{1,0:T(8,128)(2,1)S(1)}, bf16[400,1536]{1,0:T(8,128)(2,1)}, u32[]{:S(2)}, u32[]{:S(2)}) collective-permute-start(bf16[400,1536]{1,0:T(8,128)(2,1)S(1)} %get-tuple-element.316.own_rows.refs_1_), channel_id=1, source_target_pairs={{0,4},{2,6},{4,12},{6,14},{8,0},{10,2},{12,8},{14,10},{1,5},{3,7},... | collective-permute-start | bytes 3686408 | tf_op jit(solution)/shard_map/ppermute | solution.py:388
  67.6 27.6 %collective-permute-start.9 = (bf16[400,1536]{1,0:T(8,128)(2,1)S(1)}, bf16[400,1536]{1,0:T(8,128)(2,1)S(1)}, u32[]{:S(2)}, u32[]{:S(2)}) collective-permute-start(bf16[400,1536]{1,0:T(8,128)(2,1)S(1)} %get-tuple-element.316.own_rows.refs_1_), channel_id=1, source_target_pairs={{0,1},{1,0},{2,3},{3,2},{4,5},{5,4},{6,7},{7,6},{8,9},{9,8},{10,11... | collective-permute-start | bytes 3686408 | tf_op jit(solution)/shard_map/ppermute | solution.py:359
  68.5 20.9 %collective-permute-start.10 = (bf16[384,1536]{1,0:T(8,128)(2,1)S(1)}, bf16[384,1536]{1,0:T(8,128)(2,1)S(1)}, u32[]{:S(2)}, u32[]{:S(2)}) collective-permute-start(bf16[384,1536]{1,0:T(8,128)(2,1)S(1)} %convolution_convert_fusion.4.own_ct.ct_ref), channel_id=1, source_target_pairs={{0,1},{1,0},{2,3},{3,2},{4,5},{5,4},{6,7},{7,6},{8,9},{9,8},{10,11... | collective-permute-start | bytes 3538952 | tf_op jit(solution)/shard_map/ppermute | solution.py:359
  70.3 15.7 %collective-permute-start.11 = (bf16[192,1536]{1,0:T(8,128)(2,1)S(1)}, bf16[192,1536]{1,0:T(8,128)(2,1)S(1)}, u32[]{:S(2)}, u32[]{:S(2)}) collective-permute-start(bf16[192,1536]{1,0:T(8,128)(2,1)S(1)} %get-tuple-element.602), channel_id=1, source_target_pairs={{0,16},{16,0},{1,17},{17,1},{2,18},{18,2},{3,19},{19,3},{4,20},{20... | collective-permute-start | bytes 1769480 | tf_op jit(solution)/shard_map/ppermute | solution.py:363
  95.2 28.4 %collective-permute-start.13 = (bf16[400,1536]{1,0:T(8,128)(2,1)}, bf16[400,1536]{1,0:T(8,128)(2,1)}, u32[]{:S(2)}, u32[]{:S(2)}) collective-permute-start(bf16[400,1536]{1,0:T(8,128)(2,1)} %collective-permute-done.5), channel_id=1, source_target_pairs={{0,4},{2,6},{4,12},{6,14},{8,0},{10,2},{12,8},{14,10},{1,5},{3,7},... | collective-permute-start | bytes 3686408 | tf_op jit(solution)/shard_map/ppermute | solution.py:388
  96.3 27.3 %collective-permute-start.15 = (bf16[400,1536]{1,0:T(8,128)(2,1)}, bf16[400,1536]{1,0:T(8,128)(2,1)}, u32[]{:S(2)}, u32[]{:S(2)}) collective-permute-start(bf16[400,1536]{1,0:T(8,128)(2,1)} %collective-permute-done.8.own_rows), channel_id=1, source_target_pairs={{0,1},{1,0},{2,3},{3,2},{4,5},{5,4},{6,7},{7,6},{8,9},{9,8},{10,11... | collective-permute-start | bytes 3686408 | tf_op jit(solution)/shard_map/ppermute | solution.py:359
  98.2 25.4 %collective-permute-start.14 = (bf16[384,1536]{1,0:T(8,128)(2,1)}, bf16[384,1536]{1,0:T(8,128)(2,1)}, u32[]{:S(2)}, u32[]{:S(2)}) collective-permute-start(bf16[384,1536]{1,0:T(8,128)(2,1)} %convolution_convert_fusion.3.own_ct), channel_id=1, source_target_pairs={{0,1},{1,0},{2,3},{3,2},{4,5},{5,4},{6,7},{7,6},{8,9},{9,8},{10,11... | collective-permute-start | bytes 3538952 | tf_op jit(solution)/shard_map/ppermute | solution.py:359
  101.0 22.1 %collective-permute-start.16 = (bf16[192,1536]{1,0:T(8,128)(2,1)}, bf16[192,1536]{1,0:T(8,128)(2,1)}, u32[]{:S(2)}, u32[]{:S(2)}) collective-permute-start(bf16[192,1536]{1,0:T(8,128)(2,1)} %get-tuple-element.600), channel_id=1, source_target_pairs={{0,16},{16,0},{1,17},{17,1},{2,18},{18,2},{3,19},{19,3},{4,20},{20... | collective-permute-start | bytes 1769480 | tf_op jit(solution)/shard_map/ppermute | solution.py:363
  101.6 52.2 %collective-permute-start.20 = (bf16[384,1536]{1,0:T(8,128)(2,1)S(1)}, bf16[384,1536]{1,0:T(8,128)(2,1)S(1)}, u32[]{:S(2)}, u32[]{:S(2)}) collective-permute-start(bf16[384,1536]{1,0:T(8,128)(2,1)S(1)} %copy-done.16), channel_id=1, source_target_pairs={{0,1},{1,0},{2,3},{3,2},{4,5},{5,4},{6,7},{7,6},{8,9},{9,8},{10,11... | collective-permute-start | bytes 3538952 | tf_op jit(solution)/shard_map/ppermute | solution.py:359
  123.1 30.7 %collective-permute-start.21 = (bf16[384,1536]{1,0:T(8,128)(2,1)S(1)}, bf16[384,1536]{1,0:T(8,128)(2,1)S(1)}, u32[]{:S(2)}, u32[]{:S(2)}) collective-permute-start(bf16[384,1536]{1,0:T(8,128)(2,1)S(1)} %copy-done.19), channel_id=1, source_target_pairs={{0,1},{1,0},{2,3},{3,2},{4,5},{5,4},{6,7},{7,6},{8,9},{9,8},{10,11... | collective-permute-start | bytes 3538952 | tf_op jit(solution)/shard_map/ppermute | solution.py:359
  123.6 31.3 %collective-permute-start.17 = (bf16[400,1536]{1,0:T(8,128)(2,1)}, bf16[400,1536]{1,0:T(8,128)(2,1)S(1)}, u32[]{:S(2)}, u32[]{:S(2)}) collective-permute-start(bf16[400,1536]{1,0:T(8,128)(2,1)} %collective-permute-done.8.own_rows), channel_id=1, source_target_pairs={{0,4},{2,6},{4,12},{6,14},{8,0},{10,2},{12,8},{14,10},{1,5},{3,7},... | collective-permute-start | bytes 3686408 | tf_op jit(solution)/shard_map/ppermute | solution.py:388
  129.1 25.8 %collective-permute-start.19 = (bf16[384,1536]{1,0:T(8,128)(2,1)S(1)}, bf16[384,1536]{1,0:T(8,128)(2,1)S(1)}, u32[]{:S(2)}, u32[]{:S(2)}) collective-permute-start(bf16[384,1536]{1,0:T(8,128)(2,1)S(1)} %convolution_convert_fusion.2.own_ct), channel_id=1, source_target_pairs={{0,1},{1,0},{2,3},{3,2},{4,5},{5,4},{6,7},{7,6},{8,9},{9,8},{10,11... | collective-permute-start | bytes 3538952 | tf_op jit(solution)/shard_map/ppermute | solution.py:359
  130.5 24.4 %collective-permute-start.18 = (bf16[192,1536]{1,0:T(8,128)(2,1)S(1)}, bf16[192,1536]{1,0:T(8,128)(2,1)S(1)}, u32[]{:S(2)}, u32[]{:S(2)}) collective-permute-start(bf16[192,1536]{1,0:T(8,128)(2,1)S(1)} %get-tuple-element.598), channel_id=1, source_target_pairs={{0,16},{16,0},{1,17},{17,1},{2,18},{18,2},{3,19},{19,3},{4,20},{20... | collective-permute-start | bytes 1769480 | tf_op jit(solution)/shard_map/ppermute | solution.py:363
  156.1 24.2 %collective-permute-start.23 = (bf16[400,1536]{1,0:T(8,128)(2,1)}, bf16[400,1536]{1,0:T(8,128)(2,1)}, u32[]{:S(2)}, u32[]{:S(2)}) collective-permute-start(bf16[400,1536]{1,0:T(8,128)(2,1)} %get-tuple-element.346), channel_id=1, source_target_pairs={{0,1},{1,0},{2,3},{3,2},{4,5},{5,4},{6,7},{7,6},{8,9},{9,8},{10,11... | collective-permute-start | bytes 3686408 | tf_op jit(solution)/shard_map/ppermute | solution.py:359
  156.4 30.6 %collective-permute-start.22 = (bf16[400,1536]{1,0:T(8,128)(2,1)S(1)}, bf16[400,1536]{1,0:T(8,128)(2,1)}, u32[]{:S(2)}, u32[]{:S(2)}) collective-permute-start(bf16[400,1536]{1,0:T(8,128)(2,1)S(1)} %collective-permute-done.17.own_rows), channel_id=1, source_target_pairs={{0,4},{2,6},{4,12},{6,14},{8,0},{10,2},{12,8},{14,10},{1,5},{3,7},... | collective-permute-start | bytes 3686408 | tf_op jit(solution)/shard_map/ppermute | solution.py:388
  158.3 25.6 %collective-permute-start.24 = (bf16[384,1536]{1,0:T(8,128)(2,1)S(1)}, bf16[384,1536]{1,0:T(8,128)(2,1)S(1)}, u32[]{:S(2)}, u32[]{:S(2)}) collective-permute-start(bf16[384,1536]{1,0:T(8,128)(2,1)S(1)} %convolution_convert_fusion.1.own_ct), channel_id=1, source_target_pairs={{0,1},{1,0},{2,3},{3,2},{4,5},{5,4},{6,7},{7,6},{8,9},{9,8},{10,11... | collective-permute-start | bytes 3538952 | tf_op jit(solution)/shard_map/ppermute | solution.py:359
  187.0 30.8 %collective-permute-start.27 = (bf16[400,1536]{1,0:T(8,128)(2,1)}, bf16[400,1536]{1,0:T(8,128)(2,1)}, u32[]{:S(2)}, u32[]{:S(2)}) collective-permute-start(bf16[400,1536]{1,0:T(8,128)(2,1)} %add_convert_fusion.2), channel_id=1, source_target_pairs={{0,4},{2,6},{4,12},{6,14},{8,0},{10,2},{12,8},{14,10},{1,5},{3,7},... | collective-permute-start | bytes 3686408 | tf_op jit(solution)/shard_map/ppermute | solution.py:388
  187.2 30.6 %collective-permute-start.28 = (bf16[400,1536]{1,0:T(8,128)(2,1)}, bf16[400,1536]{1,0:T(8,128)(2,1)}, u32[]{:S(2)}, u32[]{:S(2)}) collective-permute-start(bf16[400,1536]{1,0:T(8,128)(2,1)} %get-tuple-element.371), channel_id=1, source_target_pairs={{0,1},{1,0},{2,3},{3,2},{4,5},{5,4},{6,7},{7,6},{8,9},{9,8},{10,11... | collective-permute-start | bytes 3686408 | tf_op jit(solution)/shard_map/ppermute | solution.py:359
  187.8 57.6 %collective-permute-start.31 = (bf16[400,1536]{1,0:T(8,128)(2,1)}, bf16[400,1536]{1,0:T(8,128)(2,1)S(1)}, u32[]{:S(2)}, u32[]{:S(2)}) collective-permute-start(bf16[400,1536]{1,0:T(8,128)(2,1)} %get-tuple-element.383), channel_id=1, source_target_pairs={{0,1},{1,0},{2,3},{3,2},{4,5},{5,4},{6,7},{7,6},{8,9},{9,8},{10,11... | collective-permute-start | bytes 3686408 | tf_op jit(solution)/shard_map/ppermute | solution.py:359
  187.8 57.0 %collective-permute-start.33 = (bf16[384,1536]{1,0:T(8,128)(2,1)S(1)}, bf16[384,1536]{1,0:T(8,128)(2,1)S(1)}, u32[]{:S(2)}, u32[]{:S(2)}) collective-permute-start(bf16[384,1536]{1,0:T(8,128)(2,1)S(1)} %copy-done.60), channel_id=1, source_target_pairs={{0,1},{1,0},{2,3},{3,2},{4,5},{5,4},{6,7},{7,6},{8,9},{9,8},{10,11... | collective-permute-start | bytes 3538952 | tf_op jit(solution)/shard_map/ppermute | solution.py:359
  190.3 55.2 %collective-permute-start.32 = (bf16[384,1536]{1,0:T(8,128)(2,1)}, bf16[384,1536]{1,0:T(8,128)(2,1)}, u32[]{:S(2)}, u32[]{:S(2)}) collective-permute-start(bf16[384,1536]{1,0:T(8,128)(2,1)} %copy-done.61), channel_id=1, source_target_pairs={{0,1},{1,0},{2,3},{3,2},{4,5},{5,4},{6,7},{7,6},{8,9},{9,8},{10,11... | collective-permute-start | bytes 3538952 | tf_op jit(solution)/shard_map/ppermute | solution.py:359
  219.9 29.8 %collective-permute-start.29 = (bf16[400,1536]{1,0:T(8,128)(2,1)S(1)}, bf16[400,1536]{1,0:T(8,128)(2,1)S(1)}, u32[]{:S(2)}, u32[]{:S(2)}) collective-permute-start(bf16[400,1536]{1,0:T(8,128)(2,1)S(1)} %add_convert_fusion.1), channel_id=1, source_target_pairs={{0,4},{2,6},{4,12},{6,14},{8,0},{10,2},{12,8},{14,10},{1,5},{3,7},... | collective-permute-start | bytes 3686408 | tf_op jit(solution)/shard_map/ppermute | solution.py:388
  220.2 29.5 %collective-permute-start.30 = (bf16[400,1536]{1,0:T(8,128)(2,1)}, bf16[400,1536]{1,0:T(8,128)(2,1)S(1)}, u32[]{:S(2)}, u32[]{:S(2)}) collective-permute-start(bf16[400,1536]{1,0:T(8,128)(2,1)} %get-tuple-element.382), channel_id=1, source_target_pairs={{0,1},{1,0},{2,3},{3,2},{4,5},{5,4},{6,7},{7,6},{8,9},{9,8},{10,11... | collective-permute-start | bytes 3686408 | tf_op jit(solution)/shard_map/ppermute | solution.py:359
  244.9 20.0 %collective-permute-start.35 = (bf16[384,1536]{1,0:T(8,128)(2,1)S(1)}, bf16[384,1536]{1,0:T(8,128)(2,1)S(1)}, u32[]{:S(2)}, u32[]{:S(2)}) collective-permute-start(bf16[384,1536]{1,0:T(8,128)(2,1)S(1)} %copy-done.63), channel_id=1, source_target_pairs={{0,1},{1,0},{2,3},{3,2},{4,5},{5,4},{6,7},{7,6},{8,9},{9,8},{10,11... | collective-permute-start | bytes 3538952 | tf_op jit(solution)/shard_map/ppermute | solution.py:359
  245.4 19.5 %collective-permute-start.36 = (bf16[384,1536]{1,0:T(8,128)(2,1)S(1)}, bf16[384,1536]{1,0:T(8,128)(2,1)S(1)}, u32[]{:S(2)}, u32[]{:S(2)}) collective-permute-start(bf16[384,1536]{1,0:T(8,128)(2,1)S(1)} %get-tuple-element.398), channel_id=1, source_target_pairs={{0,1},{1,0},{2,3},{3,2},{4,5},{5,4},{6,7},{7,6},{8,9},{9,8},{10,11... | collective-permute-start | bytes 3538952 | tf_op jit(solution)/shard_map/ppermute | solution.py:359
  250.2 29.1 %collective-permute-start.34 = (bf16[400,1536]{1,0:T(8,128)(2,1)S(1)}, bf16[400,1536]{1,0:T(8,128)(2,1)S(1)}, u32[]{:S(2)}, u32[]{:S(2)}) collective-permute-start(bf16[400,1536]{1,0:T(8,128)(2,1)S(1)} %add_convert_fusion), channel_id=1, source_target_pairs={{0,4},{2,6},{4,12},{6,14},{8,0},{10,2},{12,8},{14,10},{1,5},{3,7},... | collective-permute-start | bytes 3686408 | tf_op jit(solution)/shard_map/ppermute | solution.py:388
  279.4 31.2 %collective-permute-start.38 = (bf16[1536,768]{1,0:T(8,128)(2,1)}, bf16[1536,768]{1,0:T(8,128)(2,1)}, u32[]{:S(2)}, u32[]{:S(2)}) collective-permute-start(bf16[1536,768]{1,0:T(8,128)(2,1)} %fusion.8.own_ref), channel_id=1, source_target_pairs={{1,3},{2,0},{5,7},{6,4},{9,11},{10,8},{13,15},{14,12},{17,19},{18,... | collective-permute-start | bytes 7077896 | tf_op jit(solution)/shard_map/ppermute | solution.py:393
  280.7 29.9 %collective-permute-start.37 = (bf16[384,1536]{1,0:T(8,128)(2,1)}, bf16[384,1536]{1,0:T(8,128)(2,1)}, u32[]{:S(2)}, u32[]{:S(2)}) collective-permute-start(bf16[384,1536]{1,0:T(8,128)(2,1)} %add_convert_fusion.9), channel_id=1, source_target_pairs={{0,4},{2,6},{4,12},{6,14},{8,0},{10,2},{12,8},{14,10},{1,5},{3,7},... | collective-permute-start | bytes 3538952 | tf_op jit(solution)/shard_map/ppermute | solution.py:388
  280.7 29.9 %collective-permute-start.39 = (bf16[768,768]{1,0:T(8,128)(2,1)}, bf16[768,768]{1,0:T(8,128)(2,1)}, u32[]{:S(2)}, u32[]{:S(2)}) collective-permute-start(bf16[768,768]{1,0:T(8,128)(2,1)} %get-tuple-element.416), channel_id=1, source_target_pairs={{0,16},{16,0},{1,17},{17,1},{2,18},{18,2},{3,19},{19,3},{4,20},{20... | collective-permute-start | bytes 3538952 | tf_op jit(solution)/shard_map/ppermute | solution.py:363
  310.7 18.8 %collective-permute-start.40 = (bf16[400,1536]{1,0:T(8,128)(2,1)S(1)}, bf16[400,1536]{1,0:T(8,128)(2,1)}, u32[]{:S(2)}, u32[]{:S(2)}) collective-permute-start(bf16[400,1536]{1,0:T(8,128)(2,1)S(1)} %copy-done.5), channel_id=1, source_target_pairs={{0,1},{1,0},{2,3},{3,2},{4,5},{5,4},{6,7},{7,6},{8,9},{9,8},{10,11... | collective-permute-start | bytes 3686408 | tf_op jit(solution)/shard_map/ppermute | solution.py:359
  311.1 18.4 %collective-permute-start.42 = (bf16[768,768]{1,0:T(8,128)(2,1)}, bf16[768,768]{1,0:T(8,128)(2,1)}, u32[]{:S(2)}, u32[]{:S(2)}) collective-permute-start(bf16[768,768]{1,0:T(8,128)(2,1)} %fusion.17), channel_id=1, source_target_pairs={{1,3},{2,0},{5,7},{6,4},{9,11},{10,8},{13,15},{14,12},{17,19},{18,... | collective-permute-start | bytes 3538952 | tf_op jit(solution)/shard_map/ppermute | solution.py:393
  312.8 16.7 %collective-permute-start.43 = (bf16[384,768]{1,0:T(8,128)(2,1)}, bf16[384,768]{1,0:T(8,128)(2,1)S(1)}, u32[]{:S(2)}, u32[]{:S(2)}) collective-permute-start(bf16[384,768]{1,0:T(8,128)(2,1)} %get-tuple-element.431), channel_id=1, source_target_pairs={{0,16},{16,0},{1,17},{17,1},{2,18},{18,2},{3,19},{19,3},{4,20},{20... | collective-permute-start | bytes 1769480 | tf_op jit(solution)/shard_map/ppermute | solution.py:363
  329.5 21.3 %collective-permute-start.46 = (bf16[192,2048]{1,0:T(8,128)(2,1)}, bf16[192,2048]{1,0:T(8,128)(2,1)}, u32[]{:S(2)}, u32[]{:S(2)}) collective-permute-start(bf16[192,2048]{1,0:T(8,128)(2,1)} %get-tuple-element.454), channel_id=1, source_target_pairs={{0,16},{16,0},{1,17},{17,1},{2,18},{18,2},{3,19},{19,3},{4,20},{20... | collective-permute-start | bytes 2359304 | tf_op jit(solution)/shard_map/ppermute | solution.py:363
  331.1 21.7 %collective-permute-start.45 = (bf16[192,2048]{1,0:T(8,128)(2,1)S(1)}, bf16[192,2048]{1,0:T(8,128)(2,1)}, u32[]{:S(2)}, u32[]{:S(2)}) collective-permute-start(bf16[192,2048]{1,0:T(8,128)(2,1)S(1)} %get-tuple-element.452), channel_id=1, source_target_pairs={{0,2},{2,0},{4,6},{6,4},{8,10},{10,8},{12,14},{14,12},{1,3},{3,1},... | collective-permute-start | bytes 2359304 | tf_op jit(solution)/shard_map/ppermute | solution.py:374
  334.7 26.0 %collective-permute-start.44 = (bf16[384,1536]{1,0:T(8,128)(2,1)}, bf16[384,1536]{1,0:T(8,128)(2,1)}, u32[]{:S(2)}, u32[]{:S(2)}) collective-permute-start(bf16[384,1536]{1,0:T(8,128)(2,1)} %add_convert_fusion.8), channel_id=1, source_target_pairs={{0,4},{2,6},{4,12},{6,14},{8,0},{10,2},{12,8},{14,10},{1,5},{3,7},... | collective-permute-start | bytes 3538952 | tf_op jit(solution)/shard_map/ppermute | solution.py:388
  335.5 27.4 %collective-permute-start.47 = (bf16[768,768]{1,0:T(8,128)(2,1)S(1)}, bf16[768,768]{1,0:T(8,128)(2,1)}, u32[]{:S(2)}, u32[]{:S(2)}) collective-permute-start(bf16[768,768]{1,0:T(8,128)(2,1)S(1)} %get-tuple-element.460), channel_id=1, source_target_pairs={{0,16},{3,19},{4,20},{7,23},{8,24},{11,27},{12,28},{15,31},{16,0},... | collective-permute-start | bytes 3538952 | tf_op jit(solution)/shard_map/ppermute | solution.py:370
  338.9 25.0 %collective-permute-start.48 = (bf16[768,768]{1,0:T(8,128)(2,1)}, bf16[768,768]{1,0:T(8,128)(2,1)}, u32[]{:S(2)}, u32[]{:S(2)}) collective-permute-start(bf16[768,768]{1,0:T(8,128)(2,1)} %add_convert_fusion.7), channel_id=1, source_target_pairs={{1,3},{2,0},{5,7},{6,4},{9,11},{10,8},{13,15},{14,12},{17,19},{18,... | collective-permute-start | bytes 3538952 | tf_op jit(solution)/shard_map/ppermute | solution.py:393
  364.8 28.9 %collective-permute-start.53 = (bf16[384,1536]{1,0:T(8,128)(2,1)S(1)}, bf16[384,1536]{1,0:T(8,128)(2,1)S(1)}, u32[]{:S(2)}, u32[]{:S(2)}) collective-permute-start(bf16[384,1536]{1,0:T(8,128)(2,1)S(1)} %add_convert_fusion.6), channel_id=1, source_target_pairs={{0,4},{2,6},{4,12},{6,14},{8,0},{10,2},{12,8},{14,10},{1,5},{3,7},... | collective-permute-start | bytes 3538952 | tf_op jit(solution)/shard_map/ppermute | solution.py:388
  366.1 19.0 %collective-permute-start.51 = (bf16[384,768]{1,0:T(8,128)(2,1)S(1)}, bf16[384,768]{1,0:T(8,128)(2,1)S(1)}, u32[]{:S(2)}, u32[]{:S(2)}) collective-permute-start(bf16[384,768]{1,0:T(8,128)(2,1)S(1)} %get-tuple-element.481), channel_id=1, source_target_pairs={{0,16},{3,19},{4,20},{7,23},{8,24},{11,27},{12,28},{15,31},{16,0},... | collective-permute-start | bytes 1769480 | tf_op jit(solution)/shard_map/ppermute | solution.py:370
  368.8 16.3 %collective-permute-start.52 = (bf16[384,768]{1,0:T(8,128)(2,1)S(1)}, bf16[384,768]{1,0:T(8,128)(2,1)S(1)}, u32[]{:S(2)}, u32[]{:S(2)}) collective-permute-start(bf16[384,768]{1,0:T(8,128)(2,1)S(1)} %add_convert_fusion.16), channel_id=1, source_target_pairs={{1,3},{2,0},{5,7},{6,4},{9,11},{10,8},{13,15},{14,12},{17,19},{18,... | collective-permute-start | bytes 1769480 | tf_op jit(solution)/shard_map/ppermute | solution.py:393
  375.0 18.6 %collective-permute-start.54 = (bf16[192,1536]{1,0:T(8,128)(2,1)S(1)}, bf16[192,1536]{1,0:T(8,128)(2,1)S(1)}, u32[]{:S(2)}, u32[]{:S(2)}) collective-permute-start(bf16[192,1536]{1,0:T(8,128)(2,1)S(1)} %get-tuple-element.485), channel_id=1, source_target_pairs={{0,16},{16,0},{1,17},{17,1},{2,18},{18,2},{3,19},{19,3},{4,20},{20... | collective-permute-start | bytes 1769480 | tf_op jit(solution)/shard_map/ppermute | solution.py:363
  394.3 14.8 %collective-permute-start.58 = (bf16[48,2048]{1,0:T(8,128)(2,1)S(1)}, bf16[48,2048]{1,0:T(8,128)(2,1)S(1)}, u32[]{:S(2)}, u32[]{:S(2)}) collective-permute-start(bf16[48,2048]{1,0:T(8,128)(2,1)S(1)} %get-tuple-element.492), channel_id=1, source_target_pairs={{0,8},{2,10},{4,12},{6,14},{8,0},{10,2},{12,4},{14,6},{1,9},{3,11}... | collective-permute-start | bytes 589832 | tf_op jit(solution)/shard_map/ppermute | solution.py:383
  395.8 13.3 %collective-permute-start.59 = (bf16[48,2048]{1,0:T(8,128)(2,1)S(1)}, bf16[48,2048]{1,0:T(8,128)(2,1)S(1)}, u32[]{:S(2)}, u32[]{:S(2)}) collective-permute-start(bf16[48,2048]{1,0:T(8,128)(2,1)S(1)} %get-tuple-element.493), channel_id=1, source_target_pairs={{0,12},{2,14},{4,8},{6,10},{8,4},{10,6},{12,0},{14,2},{1,13},{3,15... | collective-permute-start | bytes 589832 | tf_op jit(solution)/shard_map/ppermute | solution.py:383
  398.1 12.6 %collective-permute-start.56 = (bf16[192,1664]{1,0:T(8,128)(2,1)S(1)}, bf16[192,1664]{1,0:T(8,128)(2,1)S(1)}, u32[]{:S(2)}, u32[]{:S(2)}) collective-permute-start(bf16[192,1664]{1,0:T(8,128)(2,1)S(1)} %get-tuple-element.489), channel_id=1, source_target_pairs={{0,16},{16,0},{1,17},{17,1},{2,18},{18,2},{3,19},{19,3},{4,20},{20... | collective-permute-start | bytes 1916936 | tf_op jit(solution)/shard_map/ppermute | solution.py:363
  398.6 13.6 %collective-permute-start.55 = (bf16[192,1664]{1,0:T(8,128)(2,1)S(1)}, bf16[192,1664]{1,0:T(8,128)(2,1)S(1)}, u32[]{:S(2)}, u32[]{:S(2)}) collective-permute-start(bf16[192,1664]{1,0:T(8,128)(2,1)S(1)} %get-tuple-element.487), channel_id=1, source_target_pairs={{0,2},{2,0},{4,6},{6,4},{8,10},{10,8},{12,14},{14,12},{1,3},{3,1},... | collective-permute-start | bytes 1916936 | tf_op jit(solution)/shard_map/ppermute | solution.py:374
  415.1 15.5 %collective-permute-start.63 = (bf16[48,2048]{1,0:T(8,128)(2,1)S(1)}, bf16[48,2048]{1,0:T(8,128)(2,1)S(1)}, u32[]{:S(2)}, u32[]{:S(2)}) collective-permute-start(bf16[48,2048]{1,0:T(8,128)(2,1)S(1)} %add_convert_fusion.21), channel_id=1, source_target_pairs={{0,8},{2,10},{4,12},{6,14},{8,0},{10,2},{12,4},{14,6},{1,9},{3,11}... | collective-permute-start | bytes 589832 | tf_op jit(solution)/shard_map/ppermute | solution.py:383
  415.5 15.1 %collective-permute-start.64 = (bf16[48,2048]{1,0:T(8,128)(2,1)S(1)}, bf16[48,2048]{1,0:T(8,128)(2,1)S(1)}, u32[]{:S(2)}, u32[]{:S(2)}) collective-permute-start(bf16[48,2048]{1,0:T(8,128)(2,1)S(1)} %add_convert_fusion.21), channel_id=1, source_target_pairs={{0,12},{2,14},{4,8},{6,10},{8,4},{10,6},{12,0},{14,2},{1,13},{3,15... | collective-permute-start | bytes 589832 | tf_op jit(solution)/shard_map/ppermute | solution.py:383
  417.6 13.2 %collective-permute-start.61 = (bf16[96,1664]{1,0:T(8,128)(2,1)}, bf16[96,1664]{1,0:T(8,128)(2,1)S(1)}, u32[]{:S(2)}, u32[]{:S(2)}) collective-permute-start(bf16[96,1664]{1,0:T(8,128)(2,1)} %get-tuple-element.508), channel_id=1, source_target_pairs={{0,2},{2,0},{4,6},{6,4},{8,10},{10,8},{12,14},{14,12},{1,3},{3,1},... | collective-permute-start | bytes 958472 | tf_op jit(solution)/shard_map/ppermute | solution.py:374
  421.2 19.2 %collective-permute-start.65 = (bf16[192,1536]{1,0:T(8,128)(2,1)S(1)}, bf16[192,1536]{1,0:T(8,128)(2,1)S(1)}, u32[]{:S(2)}, u32[]{:S(2)}) collective-permute-start(bf16[192,1536]{1,0:T(8,128)(2,1)S(1)} %get-tuple-element.511), channel_id=1, source_target_pairs={{0,16},{16,0},{1,17},{17,1},{2,18},{18,2},{3,19},{19,3},{4,20},{20... | collective-permute-start | bytes 1769480 | tf_op jit(solution)/shard_map/ppermute | solution.py:363
  441.8 12.4 %collective-permute-start.67 = (bf16[48,1664]{1,0:T(8,128)(2,1)}, bf16[48,1664]{1,0:T(8,128)(2,1)}, u32[]{:S(2)}, u32[]{:S(2)}) collective-permute-start(bf16[48,1664]{1,0:T(8,128)(2,1)} %get-tuple-element.518), channel_id=1, source_target_pairs={{0,8},{2,10},{4,12},{6,14},{8,0},{10,2},{12,4},{14,6},{1,9},{3,11}... | collective-permute-start | bytes 479240 | tf_op jit(solution)/shard_map/ppermute | solution.py:383
  458.1 13.3 %collective-permute-start.72 = (bf16[48,1664]{1,0:T(8,128)(2,1)S(1)}, bf16[48,1664]{1,0:T(8,128)(2,1)S(1)}, u32[]{:S(2)}, u32[]{:S(2)}) collective-permute-start(bf16[48,1664]{1,0:T(8,128)(2,1)S(1)} %add_convert_fusion.22), channel_id=1, source_target_pairs={{0,8},{2,10},{4,12},{6,14},{8,0},{10,2},{12,4},{14,6},{1,9},{3,11}... | collective-permute-start | bytes 479240 | tf_op jit(solution)/shard_map/ppermute | solution.py:383
  459.1 12.3 %collective-permute-start.73 = (bf16[48,1664]{1,0:T(8,128)(2,1)S(1)}, bf16[48,1664]{1,0:T(8,128)(2,1)S(1)}, u32[]{:S(2)}, u32[]{:S(2)}) collective-permute-start(bf16[48,1664]{1,0:T(8,128)(2,1)S(1)} %add_convert_fusion.22), channel_id=1, source_target_pairs={{0,12},{2,14},{4,8},{6,10},{8,4},{10,6},{12,0},{14,2},{1,13},{3,15... | collective-permute-start | bytes 479240 | tf_op jit(solution)/shard_map/ppermute | solution.py:383
  460.6 17.7 %collective-permute-start.74 = (bf16[192,2048]{1,0:T(8,128)(2,1)S(1)}, bf16[192,2048]{1,0:T(8,128)(2,1)S(1)}, u32[]{:S(2)}, u32[]{:S(2)}) collective-permute-start(bf16[192,2048]{1,0:T(8,128)(2,1)S(1)} %maximum_select_fusion.4.refs_0_), channel_id=1, source_target_pairs={{0,2},{2,0},{4,6},{6,4},{8,10},{10,8},{12,14},{14,12},{1,3},{3,1},... | collective-permute-start | bytes 2359304 | tf_op jit(solution)/shard_map/ppermute | solution.py:374
  461.1 17.2 %collective-permute-start.75 = (bf16[192,2048]{1,0:T(8,128)(2,1)S(1)}, bf16[192,2048]{1,0:T(8,128)(2,1)S(1)}, u32[]{:S(2)}, u32[]{:S(2)}) collective-permute-start(bf16[192,2048]{1,0:T(8,128)(2,1)S(1)} %maximum_select_fusion.5.refs_2_), channel_id=1, source_target_pairs={{0,16},{16,0},{1,17},{17,1},{2,18},{18,2},{3,19},{19,3},{4,20},{20... | collective-permute-start | bytes 2359304 | tf_op jit(solution)/shard_map/ppermute | solution.py:363
  491.3 15.5 %collective-permute-start.80 = (bf16[192,1664]{1,0:T(8,128)(2,1)S(1)}, bf16[192,1664]{1,0:T(8,128)(2,1)S(1)}, u32[]{:S(2)}, u32[]{:S(2)}) collective-permute-start(bf16[192,1664]{1,0:T(8,128)(2,1)S(1)} %maximum_select_fusion.6.first), channel_id=1, source_target_pairs={{0,2},{2,0},{4,6},{6,4},{8,10},{10,8},{12,14},{14,12},{1,3},{3,1},... | collective-permute-start | bytes 1916936 | tf_op jit(solution)/shard_map/ppermute | solution.py:374
  492.0 15.2 %collective-permute-start.81 = (bf16[192,1664]{1,0:T(8,128)(2,1)S(1)}, bf16[192,1664]{1,0:T(8,128)(2,1)S(1)}, u32[]{:S(2)}, u32[]{:S(2)}) collective-permute-start(bf16[192,1664]{1,0:T(8,128)(2,1)S(1)} %maximum_select_fusion.7.second), channel_id=1, source_target_pairs={{0,16},{16,0},{1,17},{17,1},{2,18},{18,2},{3,19},{19,3},{4,20},{20... | collective-permute-start | bytes 1916936 | tf_op jit(solution)/shard_map/ppermute | solution.py:363
  (127 other events, 1112.5 us)

commit v7 on v6

--- a/solution.py
+++ b/solution.py
@@ -1368,35 +1368,39 @@
     sums_1_other, sums_0_other = other_core(sums_1[1]), other_core(sums_0[1])
     all_hidden, all_grad_out, all_grad_up, all_rows = kept
     half_width = model_width // 2
-    up_first = low(matmul(all_rows.T, all_grad_up[:, :half_width]))
-    up_second = low(matmul(all_rows.T, all_grad_up[:, half_width:]))
+    down_first = low(matmul(all_hidden.T, all_grad_out[:, :half_width]))
+    down_second = low(matmul(all_hidden.T, all_grad_out[:, half_width:]))
+    down_second = block(down_second, dp, 2), block(down_second, 1 - dp, 2)
     (
         back_2,
         back_3_other,
         back_0_other,
         sums_1_other,
         sums_0_other,
-        up_first,
-        up_second,
-        all_grad_out,
+        down_first,
+        down_second,
+        all_grad_up,
+        all_rows,
     ) = part(
         back_2,
         back_3_other,
         back_0_other,
         sums_1_other,
         sums_0_other,
-        up_first,
-        up_second,
-        all_grad_out,
+        down_first,
+        down_second,
+        all_grad_up,
+        all_rows,
     )
 
     back_3 = ring_z(low(sum_blocks(back_3[0], back_3_other, back_2)))
-    down_first = low(matmul(all_hidden.T, all_grad_out[:, :half_width]))
-    down_second = low(matmul(all_hidden.T, all_grad_out[:, half_width:]))
+    down_first = down_first, to_owner(down_first)
+    down_second = down_second[0], other_dp(down_second[1])
+    up_second = low(matmul(all_rows.T, all_grad_up[:, half_width:]))
+    up_first = low(matmul(all_rows.T, all_grad_up[:, :half_width]))
     sums_1 = low(sum_blocks(sums_1[0], sums_1_other))
     sums_2_other, sums_3_other = other_core(sums_2[1]), other_core(sums_3[1])
     up_second = block(up_second, dp, 2), block(up_second, 1 - dp, 2)
-    down_second = block(down_second, dp, 2), block(down_second, 1 - dp, 2)
     (
         back_3,
         up_first,
@@ -1436,8 +1440,6 @@
     )
 
     grads_projected, grad_units = swapped(grad_projected), swapped(grad_unit)
-    down_first = down_first, to_owner(down_first)
-    down_second = down_second[0], other_dp(down_second[1])
     up_first, up_second = add_cut(*up_first, dp), low(sum_blocks(*up_second))
     sums_2 = low(sum_blocks(sums_2[0], sums_2_other, sums_1))
     qkv = qkv_grads(normeds, grads_projected, place)

time: 520 us -> 527 us (1.013)
  waiting for transfers between devices: 152 us -> 160 us
    ppermute x17, waiting for transfers between devices: 36.6 us -> 51.9 us  [other_dp(): return lax.ppermute(field, 'dp', [(0, 1), (1, 0)])]
    ppermute x12, waiting for transfers between devices: 56.5 us -> 50.9 us  [ring_z(): return lax.ppermute(field, 'expert', pairs)]
    unnamed x219 -> x243, local copies, waits for them, and re-layouts: 16.4 us -> 18.1 us
  transfers between devices with their start and end apart: 82 -> 82, of which waited for: 33 -> 33; matrix products, arithmetic and copies ran while one was open for 22% -> 22% of each run, Pallas kernels for 27% -> 26%
where the time goes in v7:
time: 527 us; the launch traced here: 518 us
  waiting for transfers between devices  160 us (30%)
  Pallas kernels  140 us (27%)
  starting transfers between devices  81 us (15%)
  other arithmetic  55.5 us (11%)
  matrix products  42.5 us (8%)
  local copies, waits for them, and re-layouts  36.1 us (7%)
    pallas_call x4, Pallas kernels, expert_step(): pl.pallas_call(functools.partial(expert_kernel, columns=256), grid=(2,),...  82.2 us
    ppermute x17, waiting for transfers between devices, other_dp(): return lax.ppermute(field, 'dp', [(0, 1), (1, 0)])  51.9 us
    ppermute x12, waiting for transfers between devices, ring_z(): return lax.ppermute(field, 'expert', pairs)  50.9 us
    dot_general x11, matrix products, matmul(): lax.dot_general(left, right, dims, preferred_element_type=jnp.float32)  42.5 us
    ppermute x12, waiting for transfers between devices, across_z(): lax.ppermute(field, 'expert', [(i, i ^ 2 * distance) for i in range(8)])  29.7 us
    convert_element_type x16, other arithmetic, low(): return field.astype(jnp.bfloat16)  21.3 us
    ppermute x17, starting transfers between devices, other_dp(): return lax.ppermute(field, 'dp', [(0, 1), (1, 0)])  18.7 us
    ppermute x12, starting transfers between devices, across_z(): lax.ppermute(field, 'expert', [(i, i ^ 2 * distance) for i in range(8)])  18.1 us
  transfers between devices with their start and end apart: 82, of which 33 were waited for; matrix products, arithmetic and copies ran while one was open for 22% of the time, Pallas kernels for 26%

profile of v7, /device:TPU:0, one launch (start us, length us, event | category | flops | bytes accessed | tf_op | source)
XLA Modules:
  0.0 517.8 jit_solution(9839269394968715867)
XLA Ops:
  4.4 2.6 collective-permute-start.2
  8.7 5.5 %collective-permute-start.7 = (bf16[1536,1536]{1,0:T(8,128)(2,1)}, bf16[1536,1536]{1,0:T(8,128)(2,1)}, u32[]{:S(2)}, u32[]{:S(2)}) collective-permute-start(bf16[1536,1536]{1,0:T(8,128)(2,1)} %bitcast.65), channel_id=1, source_target_pairs={{0,2},{3,1},{4,6},{7,5},{8,10},{11,9},{12,14},{15,13},{16,18},{19,... | collective-permute-start | bytes 14155784 | tf_op jit(solution)/shard_map/ppermute | solution.py:398
  18.4 8.1 %maximum_select_fusion.weight_ref = bf16[1536,2048]{1,0:T(8,128)(2,1)} fusion(bf16[768,2048]{1,0:T(8,128)(2,1)} %collective-permute-done.1, bf16[768,2048]{1,0:T(8,128)(2,1)} %refs_4_.1, pred[]{:T(512)S(6)} %eq.180), kind=kLoop, calls=%fused_computation | loop fusion | flops 28311552 | bytes 12582913 | tf_op jit(solution)/shard_map/jit(_where)/select_n | solution.py:402
  29.4 2.6 fusion.77.query_in.key_in.value_in
  32.0 5.3 %collective-permute-done = bf16[400,1536]{1,0:T(8,128)(2,1)} collective-permute-done((bf16[400,1536]{1,0:T(8,128)(2,1)}, bf16[400,1536]{1,0:T(8,128)(2,1)}, u32[]{:S(2)}, u32[]{:S(2)}) %collective-permute-start) | collective-permute-done | bytes 1228832 | tf_op jit(solution)/shard_map/ppermute | solution.py:388
  40.7 3.5 collective-permute-start.12
  44.3 7.4 %shard_map.188 = (bf16[384,1536]{1,0:T(8,128)(2,1)S(1)}, bf16[384,256]{1,0:T(8,128)(2,1)S(1)}, bf16[384,256]{1,0:T(8,128)(2,1)S(1)}, bf16[384,1536]{1,0:T(8,128)(2,1)S(1)}) custom-call(f32[384,2048]{1,0:T(8,128)S(1)} %fusion.77.query_in.key_in.value_in, f32[384,2048]{1,0:T(8,128)S(1)} %fusion.77.query_in.key_in.value_in, ...), custom_call_target="tpu_custom_call" | custom-call | flops 1000 | bytes 1000 | tf_op jit(solution)/shard_map/pallas_call | solution.py:1133
  51.8 4.7 maximum_select_fusion.1.weight_ref
  56.6 2.7 shard_map.189
  61.5 5.3 %collective-permute-done.5 = bf16[400,1536]{1,0:T(8,128)(2,1)} collective-permute-done((bf16[400,1536]{1,0:T(8,128)(2,1)}, bf16[400,1536]{1,0:T(8,128)(2,1)}, u32[]{:S(2)}, u32[]{:S(2)}) %collective-permute-start.5) | collective-permute-done | bytes 1228832 | tf_op jit(solution)/shard_map/ppermute | solution.py:388
  71.7 14.3 %collective-permute-done.11 = bf16[192,1536]{1,0:T(8,128)(2,1)S(1)} collective-permute-done((bf16[192,1536]{1,0:T(8,128)(2,1)S(1)}, bf16[192,1536]{1,0:T(8,128)(2,1)S(1)}, u32[]{:S(2)}, u32[]{:S(2)}) %collective-permute-start.11) | collective-permute-done | bytes 589856 | tf_op jit(solution)/shard_map/ppermute | solution.py:363
  86.0 3.3 collective-permute-done.12.down_other
  89.4 5.8 %collective-permute-done.8.own_rows = bf16[400,1536]{1,0:T(8,128)(2,1)} collective-permute-done((bf16[400,1536]{1,0:T(8,128)(2,1)S(1)}, bf16[400,1536]{1,0:T(8,128)(2,1)}, u32[]{:S(2)}, u32[]{:S(2)}) %collective-permute-start.8) | collective-permute-done | bytes 1228832 | tf_op jit(solution)/shard_map/ppermute | solution.py:388
  98.8 2.3 constant_dynamic-slice_fusion.16
  101.7 20.5 %shard_map.190 = (bf16[384,1536]{1,0:T(8,128)(2,1)S(1)}, bf16[384,1536]{1,0:T(8,128)(2,1)S(1)}, bf16[400,1536]{1,0:T(8,128)(2,1)}, bf16[400,1536]{1,0:T(8,128)(2...) custom-call(s32[2]{0:T(128)S(1)} %pad_add_fusion.choice, ...), custom_call_target="tpu_custom_call" | custom-call | flops 1000 | bytes 1000 | tf_op jit(solution)/shard_map/pallas_call | solution.py:623
  123.6 3.6 collective-permute-start.17
  132.1 20.8 %shard_map.191 = (bf16[384,1536]{1,0:T(8,128)(2,1)S(1)}, bf16[384,1536]{1,0:T(8,128)(2,1)S(1)}, bf16[400,1536]{1,0:T(8,128)(2,1)}, bf16[400,1536]{1,0:T(8,128)(2...) custom-call(s32[2]{0:T(128)S(1)} %pad_add_fusion.choice, ...), custom_call_target="tpu_custom_call", output_to_operand_aliasing={{4}: (9, {}), {5}: (10, {}), {6}: (11, {}), {7}: (12, {})} | custom-call | flops 1000 | bytes 1000 | tf_op jit(solution)/shard_map/pallas_call | solution.py:623
  159.7 20.4 %shard_map.192 = (bf16[384,1536]{1,0:T(8,128)(2,1)S(1)}, bf16[384,1536]{1,0:T(8,128)(2,1)S(1)}, bf16[400,1536]{1,0:T(8,128)(2,1)}, bf16[400,1536]{1,0:T(8,128)(2...) custom-call(s32[2]{0:T(128)S(1)} %pad_add_fusion.choice, ...), custom_call_target="tpu_custom_call", output_to_operand_aliasing={{4}: (9, {}), {5}: (10, {}), {6}: (11, {}), {7}: (12, {})} | custom-call | flops 1000 | bytes 1000 | tf_op jit(solution)/shard_map/pallas_call | solution.py:623
  180.2 3.5 add_convert_fusion.2
  183.8 3.1 collective-permute-done.22.own_rows
  188.2 2.0 collective-permute-done.26.other_rows
  190.3 20.5 %shard_map.193 = (bf16[384,1536]{1,0:T(8,128)(2,1)S(1)}, bf16[384,1536]{1,0:T(8,128)(2,1)S(1)}, bf16[400,1536]{1,0:T(8,128)(2,1)}, bf16[400,1536]{1,0:T(8,128)(2...) custom-call(s32[2]{0:T(128)S(1)} %pad_add_fusion.choice, ...), custom_call_target="tpu_custom_call", output_to_operand_aliasing={{4}: (9, {}), {5}: (10, {}), {6}: (11, {}), {7}: (12, {})} | custom-call | flops 1000 | bytes 1000 | tf_op jit(solution)/shard_map/pallas_call | solution.py:623
  210.8 6.9 %collective-permute-done.27 = bf16[400,1536]{1,0:T(8,128)(2,1)} collective-permute-done((bf16[400,1536]{1,0:T(8,128)(2,1)}, bf16[400,1536]{1,0:T(8,128)(2,1)}, u32[]{:S(2)}, u32[]{:S(2)}) %collective-permute-start.27) | collective-permute-done | bytes 1228832 | tf_op jit(solution)/shard_map/ppermute | solution.py:388
  217.7 2.3 add_convert_fusion.1
  220.4 8.4 %fusion.20 = bf16[768,768]{1,0:T(8,128)(2,1)S(1)} fusion(bf16[3072,768]{1,0:T(8,128)(2,1)} %get-tuple-element.390, bf16[3072,1536]{1,0:T(8,128)(2,1)} %get-tuple-element.391), kind=kOutput, calls=%fused_computation.40 | convolution fusion | flops 3624468480 | bytes 10616832 | tf_op jit(solution)/shard_map/dot_general | solution.py:477
  230.0 5.0 fusion.17
  235.7 14.2 %collective-permute-done.29 = bf16[400,1536]{1,0:T(8,128)(2,1)S(1)} collective-permute-done((bf16[400,1536]{1,0:T(8,128)(2,1)S(1)}, bf16[400,1536]{1,0:T(8,128)(2,1)S(1)}, u32[]{:S(2)}, u32[]{:S(2)}) %collective-permute-start.29) | collective-permute-done | bytes 1228832 | tf_op jit(solution)/shard_map/ppermute | solution.py:388
  252.3 10.5 %fusion.11 = bf16[1536,768]{1,0:T(8,128)(2,1)S(1)} fusion(bf16[3072,1536]{1,0:T(8,128)(2,1)} %get-tuple-element.396, bf16[3072,1536]{1,0:T(8,128)(2,1)S(1)} %bitcast.62), kind=kOutput, calls=%fused_computation.11 | convolution fusion | flops 7248936960 | bytes 16515072 | tf_op jit(solution)/shard_map/dot_general | solution.py:477
  262.8 9.0 %fusion.8.own_ref = bf16[1536,768]{1,0:T(8,128)(2,1)} fusion(bf16[3072,1536]{1,0:T(8,128)(2,1)S(1)} %bitcast.64, bf16[3072,1536]{1,0:T(8,128)(2,1)S(1)} %bitcast.62), kind=kOutput, calls=%fused_computation.10 | convolution fusion | flops 7248936960 | bytes 16515072 | tf_op jit(solution)/shard_map/dot_general | solution.py:477
  273.9 2.6 add_convert_fusion.9
  276.6 10.9 %collective-permute-done.36 = bf16[384,768]{1,0:T(8,128)(2,1)S(1)} collective-permute-done((bf16[384,768]{1,0:T(8,128)(2,1)S(1)}, bf16[384,768]{1,0:T(8,128)(2,1)S(1)}, u32[]{:S(2)}, u32[]{:S(2)}) %collective-permute-start.36) | collective-permute-done | bytes 589856 | tf_op jit(solution)/shard_map/ppermute | solution.py:363
  292.0 9.7 %shard_map.194 = (f32[384,1536]{1,0:T(8,128)}, bf16[400,1536]{1,0:T(8,128)(2,1)}, bf16[384,1536]{1,0:T(8,128)(2,1)}) custom-call(bf16[400,1536]{1,0:T(8,128)(2,1)} %get-tuple-element.412.back_own.extra_own, bf16[400,1536]{1,0:T(8,128)(2,1)} %copy-done.65, bf16[400,1536]{1,0:T(8,128)(2,1)} %copy-done.66, ...), custom_call_target="tpu_custom_call" | custom-call | flops 1000 | bytes 1000 | tf_op jit(solution)/shard_map/pallas_call | solution.py:734
  304.3 8.8 %shard_map.195.right_own.grad_ref = bf16[384,2048]{1,0:T(8,128)(2,1)S(1)} custom-call(bf16[384,1536]{1,0:T(8,128)(2,1)S(1)} %copy-done.36, bf16[384,256]{1,0:T(8,128)(2,1)S(1)} %copy-done.49, bf16[384,256]{1,0:T(8,128)(2,1)S(1)} %copy-done.51, bf16[384,1536]{1,0:T(8,128)(2,1)S(1)} %copy-done.43, f32[384,128]{1,0:T(8,128)S(1)} %get-tuple-element.299.cos_ref, ...), custom_call_target="tpu_custom_call" | custom-call | flops 1000 | bytes 1000 | tf_op jit(solution)/shard_map/pallas_call | solution.py:1213
  313.1 6.2 %collective-permute-done.39 = bf16[384,1536]{1,0:T(8,128)(2,1)} collective-permute-done((bf16[384,1536]{1,0:T(8,128)(2,1)}, bf16[384,1536]{1,0:T(8,128)(2,1)}, u32[]{:S(2)}, u32[]{:S(2)}) %collective-permute-start.39) | collective-permute-done | bytes 1179680 | tf_op jit(solution)/shard_map/ppermute | solution.py:388
  320.4 4.1 shard_map.197
  324.5 2.7 add_convert_fusion.7
  327.2 2.9 add_convert_fusion.8
  330.1 7.5 %shard_map.196 = (bf16[192,2048]{1,0:T(8,128)(2,1)S(1)}, bf16[192,2048]{1,0:T(8,128)(2,1)}, bf16[192,2048]{1,0:T(8,128)(2,1)S(1)}, bf16[192,2048]{1,0:T(8,128)(2,1)}) custom-call(s32[3]{0:T(128)S(1)} %pad_add_fusion.1.place_ref, bf16[384,1536]{1,0:T(8,128)(2,1)S(1)} %copy-done.20, bf16[384,1536]{1,0:T(8,128)(2,1)S(1)} %copy-done.38, ...), custom_call_target="tpu_custom_call" | custom-call | flops 1000 | bytes 1000 | tf_op jit(solution)/shard_map/pallas_call | solution.py:887
  339.4 2.5 collective-permute-start.47
  343.5 3.3 shard_map.199
  346.8 4.4 shard_map.198
  352.9 4.5 collective-permute-done.46
  363.7 4.1 collective-permute-done.44
  372.2 3.3 collective-permute-start.51
  383.3 9.1 %collective-permute-done.51 = bf16[384,768]{1,0:T(8,128)(2,1)S(1)} collective-permute-done((bf16[384,768]{1,0:T(8,128)(2,1)S(1)}, bf16[384,768]{1,0:T(8,128)(2,1)S(1)}, u32[]{:S(2)}, u32[]{:S(2)}) %collective-permute-start.51) | collective-permute-done | bytes 589856 | tf_op jit(solution)/shard_map/ppermute | solution.py:370
  392.4 8.5 %collective-permute-done.54 = bf16[192,1536]{1,0:T(8,128)(2,1)S(1)} collective-permute-done((bf16[192,1536]{1,0:T(8,128)(2,1)S(1)}, bf16[192,1536]{1,0:T(8,128)(2,1)S(1)}, u32[]{:S(2)}, u32[]{:S(2)}) %collective-permute-start.54) | collective-permute-done | bytes 589856 | tf_op jit(solution)/shard_map/ppermute | solution.py:363
  403.2 2.1 collective-permute-start.59
  410.2 6.7 %collective-permute-done.58 = bf16[48,2048]{1,0:T(8,128)(2,1)S(1)} collective-permute-done((bf16[48,2048]{1,0:T(8,128)(2,1)S(1)}, bf16[48,2048]{1,0:T(8,128)(2,1)S(1)}, u32[]{:S(2)}, u32[]{:S(2)}) %collective-permute-start.58) | collective-permute-done | bytes 196640 | tf_op jit(solution)/shard_map/ppermute | solution.py:383
  425.1 2.3 collective-permute-start.61
  428.2 2.8 collective-permute-start.65
  431.1 6.4 %collective-permute-done.63 = bf16[48,2048]{1,0:T(8,128)(2,1)S(1)} collective-permute-done((bf16[48,2048]{1,0:T(8,128)(2,1)S(1)}, bf16[48,2048]{1,0:T(8,128)(2,1)S(1)}, u32[]{:S(2)}, u32[]{:S(2)}) %collective-permute-start.63) | collective-permute-done | bytes 196640 | tf_op jit(solution)/shard_map/ppermute | solution.py:383
  440.0 7.0 %collective-permute-done.65 = bf16[192,1536]{1,0:T(8,128)(2,1)S(1)} collective-permute-done((bf16[192,1536]{1,0:T(8,128)(2,1)S(1)}, bf16[192,1536]{1,0:T(8,128)(2,1)S(1)}, u32[]{:S(2)}, u32[]{:S(2)}) %collective-permute-start.65) | collective-permute-done | bytes 589856 | tf_op jit(solution)/shard_map/ppermute | solution.py:363
  448.3 2.0 collective-permute-start.67
  453.2 2.5 collective-permute-done.66
  455.7 4.5 collective-permute-done.67
  461.8 2.3 collective-permute-start.71
  469.0 9.0 %collective-permute-done.72 = bf16[48,1664]{1,0:T(8,128)(2,1)S(1)} collective-permute-done((bf16[48,1664]{1,0:T(8,128)(2,1)S(1)}, bf16[48,1664]{1,0:T(8,128)(2,1)S(1)}, u32[]{:S(2)}, u32[]{:S(2)}) %collective-permute-start.72) | collective-permute-done | bytes 159776 | tf_op jit(solution)/shard_map/ppermute | solution.py:383
  478.3 6.3 %collective-permute-done.74.refs_1_ = bf16[192,2048]{1,0:T(8,128)(2,1)S(1)} collective-permute-done((bf16[192,2048]{1,0:T(8,128)(2,1)S(1)}, bf16[192,2048]{1,0:T(8,128)(2,1)S(1)}, u32[]{:S(2)}, u32[]{:S(2)}) %collective-permute-start.74) | collective-permute-done | bytes 786464 | tf_op jit(solution)/shard_map/ppermute | solution.py:374
  488.2 4.0 shard_map.201
  492.3 4.3 collective-permute-done.76
  503.5 2.1 shard_map.202
  506.4 3.0 bitcast_convert_fusion
  509.3 4.2 collective-permute-done.80.first
  513.9 2.1 shard_map.203
  (474 shorter events, 122.0 us)
Async XLA Ops:
  3.9 14.5 %collective-permute-start.1 = (bf16[768,2048]{1,0:T(8,128)(2,1)}, bf16[768,2048]{1,0:T(8,128)(2,1)}, u32[]{:S(2)}, u32[]{:S(2)}) collective-permute-start(bf16[768,2048]{1,0:T(8,128)(2,1)} %refs_4_.1), channel_id=1, source_target_pairs={{0,1},{1,0},{2,3},{3,2},{4,5},{5,4},{6,7},{7,6},{8,9},{9,8},{10,11... | collective-permute-start | bytes 9437192 | tf_op jit(solution)/shard_map/ppermute | solution.py:359
  4.4 22.1 %collective-permute-start.2 = (bf16[192,1536]{1,0:T(8,128)(2,1)S(1)}, bf16[192,1536]{1,0:T(8,128)(2,1)S(1)}, u32[]{:S(2)}, u32[]{:S(2)}) collective-permute-start(bf16[192,1536]{1,0:T(8,128)(2,1)S(1)} %constant_dynamic-slice_fusion.22), channel_id=1, source_target_pairs={{0,16},{16,0},{1,17},{17,1},{2,18},{18,2},{3,19},{19,3},{4,20},{20... | collective-permute-start | bytes 1769480 | tf_op jit(solution)/shard_map/ppermute | solution.py:363
  7.0 30.3 %collective-permute-start = (bf16[400,1536]{1,0:T(8,128)(2,1)}, bf16[400,1536]{1,0:T(8,128)(2,1)}, u32[]{:S(2)}, u32[]{:S(2)}) collective-permute-start(bf16[400,1536]{1,0:T(8,128)(2,1)} %shard_map.187), channel_id=1, source_target_pairs={{0,4},{2,6},{4,12},{6,14},{8,0},{10,2},{12,8},{14,10},{1,5},{3,7},... | collective-permute-start | bytes 3686408 | tf_op jit(solution)/shard_map/ppermute | solution.py:388
  8.7 58.1 %collective-permute-start.7 = (bf16[1536,1536]{1,0:T(8,128)(2,1)}, bf16[1536,1536]{1,0:T(8,128)(2,1)}, u32[]{:S(2)}, u32[]{:S(2)}) collective-permute-start(bf16[1536,1536]{1,0:T(8,128)(2,1)} %bitcast.65), channel_id=1, source_target_pairs={{0,2},{3,1},{4,6},{7,5},{8,10},{11,9},{12,14},{15,13},{16,18},{19,... | collective-permute-start | bytes 14155784 | tf_op jit(solution)/shard_map/ppermute | solution.py:398
  17.6 19.7 %collective-permute-start.4 = (bf16[768,1536]{1,0:T(8,128)(2,1)}, bf16[768,1536]{1,0:T(8,128)(2,1)}, u32[]{:S(2)}, u32[]{:S(2)}) collective-permute-start(bf16[768,1536]{1,0:T(8,128)(2,1)} %param.20), channel_id=1, source_target_pairs={{0,1},{1,0},{2,3},{3,2},{4,5},{5,4},{6,7},{7,6},{8,9},{9,8},{10,11... | collective-permute-start | bytes 7077896 | tf_op jit(solution)/shard_map/ppermute | solution.py:359
  37.3 29.5 %collective-permute-start.5 = (bf16[400,1536]{1,0:T(8,128)(2,1)}, bf16[400,1536]{1,0:T(8,128)(2,1)}, u32[]{:S(2)}, u32[]{:S(2)}) collective-permute-start(bf16[400,1536]{1,0:T(8,128)(2,1)} %collective-permute-done), channel_id=1, source_target_pairs={{0,4},{2,6},{4,12},{6,14},{8,0},{10,2},{12,8},{14,10},{1,5},{3,7},... | collective-permute-start | bytes 3686408 | tf_op jit(solution)/shard_map/ppermute | solution.py:388
  40.1 21.3 %collective-permute-start.6 = (bf16[192,1536]{1,0:T(8,128)(2,1)S(1)}, bf16[192,1536]{1,0:T(8,128)(2,1)S(1)}, u32[]{:S(2)}, u32[]{:S(2)}) collective-permute-start(bf16[192,1536]{1,0:T(8,128)(2,1)S(1)} %get-tuple-element.612), channel_id=1, source_target_pairs={{0,16},{16,0},{1,17},{17,1},{2,18},{18,2},{3,19},{19,3},{4,20},{20... | collective-permute-start | bytes 1769480 | tf_op jit(solution)/shard_map/ppermute | solution.py:363
  40.7 48.6 %collective-permute-start.12 = (bf16[768,1536]{1,0:T(8,128)(2,1)}, bf16[768,1536]{1,0:T(8,128)(2,1)S(1)}, u32[]{:S(2)}, u32[]{:S(2)}) collective-permute-start(bf16[768,1536]{1,0:T(8,128)(2,1)} %bitcast.72), channel_id=1, source_target_pairs={{0,2},{3,1},{4,6},{7,5},{8,10},{11,9},{12,14},{15,13},{16,18},{19,... | collective-permute-start | bytes 7077896 | tf_op jit(solution)/shard_map/ppermute | solution.py:398
  66.8 28.3 %collective-permute-start.8 = (bf16[400,1536]{1,0:T(8,128)(2,1)S(1)}, bf16[400,1536]{1,0:T(8,128)(2,1)}, u32[]{:S(2)}, u32[]{:S(2)}) collective-permute-start(bf16[400,1536]{1,0:T(8,128)(2,1)S(1)} %get-tuple-element.320.own_rows.refs_1_), channel_id=1, source_target_pairs={{0,4},{2,6},{4,12},{6,14},{8,0},{10,2},{12,8},{14,10},{1,5},{3,7},... | collective-permute-start | bytes 3686408 | tf_op jit(solution)/shard_map/ppermute | solution.py:388
  67.6 27.6 %collective-permute-start.9 = (bf16[400,1536]{1,0:T(8,128)(2,1)S(1)}, bf16[400,1536]{1,0:T(8,128)(2,1)S(1)}, u32[]{:S(2)}, u32[]{:S(2)}) collective-permute-start(bf16[400,1536]{1,0:T(8,128)(2,1)S(1)} %get-tuple-element.320.own_rows.refs_1_), channel_id=1, source_target_pairs={{0,1},{1,0},{2,3},{3,2},{4,5},{5,4},{6,7},{7,6},{8,9},{9,8},{10,11... | collective-permute-start | bytes 3686408 | tf_op jit(solution)/shard_map/ppermute | solution.py:359
  68.5 20.9 %collective-permute-start.10 = (bf16[384,1536]{1,0:T(8,128)(2,1)S(1)}, bf16[384,1536]{1,0:T(8,128)(2,1)S(1)}, u32[]{:S(2)}, u32[]{:S(2)}) collective-permute-start(bf16[384,1536]{1,0:T(8,128)(2,1)S(1)} %convolution_convert_fusion.4.own_ct.ct_ref), channel_id=1, source_target_pairs={{0,1},{1,0},{2,3},{3,2},{4,5},{5,4},{6,7},{7,6},{8,9},{9,8},{10,11... | collective-permute-start | bytes 3538952 | tf_op jit(solution)/shard_map/ppermute | solution.py:359
  70.3 15.7 %collective-permute-start.11 = (bf16[192,1536]{1,0:T(8,128)(2,1)S(1)}, bf16[192,1536]{1,0:T(8,128)(2,1)S(1)}, u32[]{:S(2)}, u32[]{:S(2)}) collective-permute-start(bf16[192,1536]{1,0:T(8,128)(2,1)S(1)} %get-tuple-element.610), channel_id=1, source_target_pairs={{0,16},{16,0},{1,17},{17,1},{2,18},{18,2},{3,19},{19,3},{4,20},{20... | collective-permute-start | bytes 1769480 | tf_op jit(solution)/shard_map/ppermute | solution.py:363
  95.2 28.4 %collective-permute-start.13 = (bf16[400,1536]{1,0:T(8,128)(2,1)}, bf16[400,1536]{1,0:T(8,128)(2,1)}, u32[]{:S(2)}, u32[]{:S(2)}) collective-permute-start(bf16[400,1536]{1,0:T(8,128)(2,1)} %collective-permute-done.5), channel_id=1, source_target_pairs={{0,4},{2,6},{4,12},{6,14},{8,0},{10,2},{12,8},{14,10},{1,5},{3,7},... | collective-permute-start | bytes 3686408 | tf_op jit(solution)/shard_map/ppermute | solution.py:388
  96.3 27.3 %collective-permute-start.15 = (bf16[400,1536]{1,0:T(8,128)(2,1)}, bf16[400,1536]{1,0:T(8,128)(2,1)}, u32[]{:S(2)}, u32[]{:S(2)}) collective-permute-start(bf16[400,1536]{1,0:T(8,128)(2,1)} %collective-permute-done.8.own_rows), channel_id=1, source_target_pairs={{0,1},{1,0},{2,3},{3,2},{4,5},{5,4},{6,7},{7,6},{8,9},{9,8},{10,11... | collective-permute-start | bytes 3686408 | tf_op jit(solution)/shard_map/ppermute | solution.py:359
  98.2 25.4 %collective-permute-start.14 = (bf16[384,1536]{1,0:T(8,128)(2,1)}, bf16[384,1536]{1,0:T(8,128)(2,1)}, u32[]{:S(2)}, u32[]{:S(2)}) collective-permute-start(bf16[384,1536]{1,0:T(8,128)(2,1)} %convolution_convert_fusion.3.own_ct), channel_id=1, source_target_pairs={{0,1},{1,0},{2,3},{3,2},{4,5},{5,4},{6,7},{7,6},{8,9},{9,8},{10,11... | collective-permute-start | bytes 3538952 | tf_op jit(solution)/shard_map/ppermute | solution.py:359
  101.1 22.0 %collective-permute-start.16 = (bf16[192,1536]{1,0:T(8,128)(2,1)}, bf16[192,1536]{1,0:T(8,128)(2,1)}, u32[]{:S(2)}, u32[]{:S(2)}) collective-permute-start(bf16[192,1536]{1,0:T(8,128)(2,1)} %get-tuple-element.608), channel_id=1, source_target_pairs={{0,16},{16,0},{1,17},{17,1},{2,18},{18,2},{3,19},{19,3},{4,20},{20... | collective-permute-start | bytes 1769480 | tf_op jit(solution)/shard_map/ppermute | solution.py:363
  101.6 52.1 %collective-permute-start.20 = (bf16[384,1536]{1,0:T(8,128)(2,1)S(1)}, bf16[384,1536]{1,0:T(8,128)(2,1)S(1)}, u32[]{:S(2)}, u32[]{:S(2)}) collective-permute-start(bf16[384,1536]{1,0:T(8,128)(2,1)S(1)} %copy-done.16), channel_id=1, source_target_pairs={{0,1},{1,0},{2,3},{3,2},{4,5},{5,4},{6,7},{7,6},{8,9},{9,8},{10,11... | collective-permute-start | bytes 3538952 | tf_op jit(solution)/shard_map/ppermute | solution.py:359
  123.1 30.6 %collective-permute-start.21 = (bf16[384,1536]{1,0:T(8,128)(2,1)S(1)}, bf16[384,1536]{1,0:T(8,128)(2,1)S(1)}, u32[]{:S(2)}, u32[]{:S(2)}) collective-permute-start(bf16[384,1536]{1,0:T(8,128)(2,1)S(1)} %copy-done.19), channel_id=1, source_target_pairs={{0,1},{1,0},{2,3},{3,2},{4,5},{5,4},{6,7},{7,6},{8,9},{9,8},{10,11... | collective-permute-start | bytes 3538952 | tf_op jit(solution)/shard_map/ppermute | solution.py:359
  123.6 31.2 %collective-permute-start.17 = (bf16[400,1536]{1,0:T(8,128)(2,1)}, bf16[400,1536]{1,0:T(8,128)(2,1)S(1)}, u32[]{:S(2)}, u32[]{:S(2)}) collective-permute-start(bf16[400,1536]{1,0:T(8,128)(2,1)} %collective-permute-done.8.own_rows), channel_id=1, source_target_pairs={{0,4},{2,6},{4,12},{6,14},{8,0},{10,2},{12,8},{14,10},{1,5},{3,7},... | collective-permute-start | bytes 3686408 | tf_op jit(solution)/shard_map/ppermute | solution.py:388
  129.1 25.7 %collective-permute-start.19 = (bf16[384,1536]{1,0:T(8,128)(2,1)S(1)}, bf16[384,1536]{1,0:T(8,128)(2,1)S(1)}, u32[]{:S(2)}, u32[]{:S(2)}) collective-permute-start(bf16[384,1536]{1,0:T(8,128)(2,1)S(1)} %convolution_convert_fusion.2.own_ct), channel_id=1, source_target_pairs={{0,1},{1,0},{2,3},{3,2},{4,5},{5,4},{6,7},{7,6},{8,9},{9,8},{10,11... | collective-permute-start | bytes 3538952 | tf_op jit(solution)/shard_map/ppermute | solution.py:359
  130.5 24.3 %collective-permute-start.18 = (bf16[192,1536]{1,0:T(8,128)(2,1)S(1)}, bf16[192,1536]{1,0:T(8,128)(2,1)S(1)}, u32[]{:S(2)}, u32[]{:S(2)}) collective-permute-start(bf16[192,1536]{1,0:T(8,128)(2,1)S(1)} %get-tuple-element.606), channel_id=1, source_target_pairs={{0,16},{16,0},{1,17},{17,1},{2,18},{18,2},{3,19},{19,3},{4,20},{20... | collective-permute-start | bytes 1769480 | tf_op jit(solution)/shard_map/ppermute | solution.py:363
  156.0 24.2 %collective-permute-start.23 = (bf16[400,1536]{1,0:T(8,128)(2,1)}, bf16[400,1536]{1,0:T(8,128)(2,1)}, u32[]{:S(2)}, u32[]{:S(2)}) collective-permute-start(bf16[400,1536]{1,0:T(8,128)(2,1)} %get-tuple-element.350), channel_id=1, source_target_pairs={{0,1},{1,0},{2,3},{3,2},{4,5},{5,4},{6,7},{7,6},{8,9},{9,8},{10,11... | collective-permute-start | bytes 3686408 | tf_op jit(solution)/shard_map/ppermute | solution.py:359
  156.3 30.6 %collective-permute-start.22 = (bf16[400,1536]{1,0:T(8,128)(2,1)S(1)}, bf16[400,1536]{1,0:T(8,128)(2,1)}, u32[]{:S(2)}, u32[]{:S(2)}) collective-permute-start(bf16[400,1536]{1,0:T(8,128)(2,1)S(1)} %collective-permute-done.17.own_rows), channel_id=1, source_target_pairs={{0,4},{2,6},{4,12},{6,14},{8,0},{10,2},{12,8},{14,10},{1,5},{3,7},... | collective-permute-start | bytes 3686408 | tf_op jit(solution)/shard_map/ppermute | solution.py:388
  158.3 25.5 %collective-permute-start.24 = (bf16[384,1536]{1,0:T(8,128)(2,1)S(1)}, bf16[384,1536]{1,0:T(8,128)(2,1)S(1)}, u32[]{:S(2)}, u32[]{:S(2)}) collective-permute-start(bf16[384,1536]{1,0:T(8,128)(2,1)S(1)} %convolution_convert_fusion.1.own_ct), channel_id=1, source_target_pairs={{0,1},{1,0},{2,3},{3,2},{4,5},{5,4},{6,7},{7,6},{8,9},{9,8},{10,11... | collective-permute-start | bytes 3538952 | tf_op jit(solution)/shard_map/ppermute | solution.py:359
  186.9 30.8 %collective-permute-start.27 = (bf16[400,1536]{1,0:T(8,128)(2,1)}, bf16[400,1536]{1,0:T(8,128)(2,1)}, u32[]{:S(2)}, u32[]{:S(2)}) collective-permute-start(bf16[400,1536]{1,0:T(8,128)(2,1)} %add_convert_fusion.2), channel_id=1, source_target_pairs={{0,4},{2,6},{4,12},{6,14},{8,0},{10,2},{12,8},{14,10},{1,5},{3,7},... | collective-permute-start | bytes 3686408 | tf_op jit(solution)/shard_map/ppermute | solution.py:388
  187.1 30.6 %collective-permute-start.28 = (bf16[400,1536]{1,0:T(8,128)(2,1)}, bf16[400,1536]{1,0:T(8,128)(2,1)}, u32[]{:S(2)}, u32[]{:S(2)}) collective-permute-start(bf16[400,1536]{1,0:T(8,128)(2,1)} %get-tuple-element.375), channel_id=1, source_target_pairs={{0,1},{1,0},{2,3},{3,2},{4,5},{5,4},{6,7},{7,6},{8,9},{9,8},{10,11... | collective-permute-start | bytes 3686408 | tf_op jit(solution)/shard_map/ppermute | solution.py:359
  187.6 47.9 %collective-permute-start.31 = (bf16[400,1536]{1,0:T(8,128)(2,1)}, bf16[400,1536]{1,0:T(8,128)(2,1)S(1)}, u32[]{:S(2)}, u32[]{:S(2)}) collective-permute-start(bf16[400,1536]{1,0:T(8,128)(2,1)} %get-tuple-element.387), channel_id=1, source_target_pairs={{0,1},{1,0},{2,3},{3,2},{4,5},{5,4},{6,7},{7,6},{8,9},{9,8},{10,11... | collective-permute-start | bytes 3686408 | tf_op jit(solution)/shard_map/ppermute | solution.py:359
  187.7 47.3 %collective-permute-start.33 = (bf16[384,1536]{1,0:T(8,128)(2,1)S(1)}, bf16[384,1536]{1,0:T(8,128)(2,1)S(1)}, u32[]{:S(2)}, u32[]{:S(2)}) collective-permute-start(bf16[384,1536]{1,0:T(8,128)(2,1)S(1)} %copy-done.60), channel_id=1, source_target_pairs={{0,1},{1,0},{2,3},{3,2},{4,5},{5,4},{6,7},{7,6},{8,9},{9,8},{10,11... | collective-permute-start | bytes 3538952 | tf_op jit(solution)/shard_map/ppermute | solution.py:359
  190.2 45.5 %collective-permute-start.32 = (bf16[384,1536]{1,0:T(8,128)(2,1)}, bf16[384,1536]{1,0:T(8,128)(2,1)}, u32[]{:S(2)}, u32[]{:S(2)}) collective-permute-start(bf16[384,1536]{1,0:T(8,128)(2,1)} %copy-done.61), channel_id=1, source_target_pairs={{0,1},{1,0},{2,3},{3,2},{4,5},{5,4},{6,7},{7,6},{8,9},{9,8},{10,11... | collective-permute-start | bytes 3538952 | tf_op jit(solution)/shard_map/ppermute | solution.py:359
  220.0 29.8 %collective-permute-start.29 = (bf16[400,1536]{1,0:T(8,128)(2,1)S(1)}, bf16[400,1536]{1,0:T(8,128)(2,1)S(1)}, u32[]{:S(2)}, u32[]{:S(2)}) collective-permute-start(bf16[400,1536]{1,0:T(8,128)(2,1)S(1)} %add_convert_fusion.1), channel_id=1, source_target_pairs={{0,4},{2,6},{4,12},{6,14},{8,0},{10,2},{12,8},{14,10},{1,5},{3,7},... | collective-permute-start | bytes 3686408 | tf_op jit(solution)/shard_map/ppermute | solution.py:388
  220.3 29.5 %collective-permute-start.30 = (bf16[400,1536]{1,0:T(8,128)(2,1)}, bf16[400,1536]{1,0:T(8,128)(2,1)S(1)}, u32[]{:S(2)}, u32[]{:S(2)}) collective-permute-start(bf16[400,1536]{1,0:T(8,128)(2,1)} %get-tuple-element.386), channel_id=1, source_target_pairs={{0,1},{1,0},{2,3},{3,2},{4,5},{5,4},{6,7},{7,6},{8,9},{9,8},{10,11... | collective-permute-start | bytes 3686408 | tf_op jit(solution)/shard_map/ppermute | solution.py:359
  235.0 41.5 %collective-permute-start.37 = (bf16[384,1536]{1,0:T(8,128)(2,1)S(1)}, bf16[384,1536]{1,0:T(8,128)(2,1)S(1)}, u32[]{:S(2)}, u32[]{:S(2)}) collective-permute-start(bf16[384,1536]{1,0:T(8,128)(2,1)S(1)} %copy-done.63), channel_id=1, source_target_pairs={{0,1},{1,0},{2,3},{3,2},{4,5},{5,4},{6,7},{7,6},{8,9},{9,8},{10,11... | collective-permute-start | bytes 3538952 | tf_op jit(solution)/shard_map/ppermute | solution.py:359
  235.6 41.0 %collective-permute-start.38 = (bf16[384,1536]{1,0:T(8,128)(2,1)S(1)}, bf16[384,1536]{1,0:T(8,128)(2,1)S(1)}, u32[]{:S(2)}, u32[]{:S(2)}) collective-permute-start(bf16[384,1536]{1,0:T(8,128)(2,1)S(1)} %get-tuple-element.404), channel_id=1, source_target_pairs={{0,1},{1,0},{2,3},{3,2},{4,5},{5,4},{6,7},{7,6},{8,9},{9,8},{10,11... | collective-permute-start | bytes 3538952 | tf_op jit(solution)/shard_map/ppermute | solution.py:359
  250.4 37.1 %collective-permute-start.34 = (bf16[400,1536]{1,0:T(8,128)(2,1)S(1)}, bf16[400,1536]{1,0:T(8,128)(2,1)S(1)}, u32[]{:S(2)}, u32[]{:S(2)}) collective-permute-start(bf16[400,1536]{1,0:T(8,128)(2,1)S(1)} %add_convert_fusion), channel_id=1, source_target_pairs={{0,4},{2,6},{4,12},{6,14},{8,0},{10,2},{12,8},{14,10},{1,5},{3,7},... | collective-permute-start | bytes 3686408 | tf_op jit(solution)/shard_map/ppermute | solution.py:388
  250.4 37.0 %collective-permute-start.35 = (bf16[768,768]{1,0:T(8,128)(2,1)}, bf16[768,768]{1,0:T(8,128)(2,1)S(1)}, u32[]{:S(2)}, u32[]{:S(2)}) collective-permute-start(bf16[768,768]{1,0:T(8,128)(2,1)} %fusion.17), channel_id=1, source_target_pairs={{1,3},{2,0},{5,7},{6,4},{9,11},{10,8},{13,15},{14,12},{17,19},{18,... | collective-permute-start | bytes 3538952 | tf_op jit(solution)/shard_map/ppermute | solution.py:393
  271.8 15.7 %collective-permute-start.36 = (bf16[384,768]{1,0:T(8,128)(2,1)S(1)}, bf16[384,768]{1,0:T(8,128)(2,1)S(1)}, u32[]{:S(2)}, u32[]{:S(2)}) collective-permute-start(bf16[384,768]{1,0:T(8,128)(2,1)S(1)} %copy-done.97), channel_id=1, source_target_pairs={{0,16},{16,0},{1,17},{17,1},{2,18},{18,2},{3,19},{19,3},{4,20},{20... | collective-permute-start | bytes 1769480 | tf_op jit(solution)/shard_map/ppermute | solution.py:363
  287.5 32.1 %collective-permute-start.40 = (bf16[1536,768]{1,0:T(8,128)(2,1)}, bf16[1536,768]{1,0:T(8,128)(2,1)}, u32[]{:S(2)}, u32[]{:S(2)}) collective-permute-start(bf16[1536,768]{1,0:T(8,128)(2,1)} %fusion.8.own_ref), channel_id=1, source_target_pairs={{1,3},{2,0},{5,7},{6,4},{9,11},{10,8},{13,15},{14,12},{17,19},{18,... | collective-permute-start | bytes 7077896 | tf_op jit(solution)/shard_map/ppermute | solution.py:393
  288.8 30.6 %collective-permute-start.39 = (bf16[384,1536]{1,0:T(8,128)(2,1)}, bf16[384,1536]{1,0:T(8,128)(2,1)}, u32[]{:S(2)}, u32[]{:S(2)}) collective-permute-start(bf16[384,1536]{1,0:T(8,128)(2,1)} %add_convert_fusion.9), channel_id=1, source_target_pairs={{0,4},{2,6},{4,12},{6,14},{8,0},{10,2},{12,8},{14,10},{1,5},{3,7},... | collective-permute-start | bytes 3538952 | tf_op jit(solution)/shard_map/ppermute | solution.py:388
  290.5 29.1 %collective-permute-start.41 = (bf16[768,768]{1,0:T(8,128)(2,1)}, bf16[768,768]{1,0:T(8,128)(2,1)}, u32[]{:S(2)}, u32[]{:S(2)}) collective-permute-start(bf16[768,768]{1,0:T(8,128)(2,1)} %get-tuple-element.422), channel_id=1, source_target_pairs={{0,16},{16,0},{1,17},{17,1},{2,18},{18,2},{3,19},{19,3},{4,20},{20... | collective-permute-start | bytes 3538952 | tf_op jit(solution)/shard_map/ppermute | solution.py:363
  319.6 18.1 %collective-permute-start.42 = (bf16[400,1536]{1,0:T(8,128)(2,1)S(1)}, bf16[400,1536]{1,0:T(8,128)(2,1)S(1)}, u32[]{:S(2)}, u32[]{:S(2)}) collective-permute-start(bf16[400,1536]{1,0:T(8,128)(2,1)S(1)} %copy-done.5), channel_id=1, source_target_pairs={{0,1},{1,0},{2,3},{3,2},{4,5},{5,4},{6,7},{7,6},{8,9},{9,8},{10,11... | collective-permute-start | bytes 3686408 | tf_op jit(solution)/shard_map/ppermute | solution.py:359
  337.6 19.8 %collective-permute-start.46 = (bf16[192,2048]{1,0:T(8,128)(2,1)}, bf16[192,2048]{1,0:T(8,128)(2,1)}, u32[]{:S(2)}, u32[]{:S(2)}) collective-permute-start(bf16[192,2048]{1,0:T(8,128)(2,1)} %get-tuple-element.462), channel_id=1, source_target_pairs={{0,16},{16,0},{1,17},{17,1},{2,18},{18,2},{3,19},{19,3},{4,20},{20... | collective-permute-start | bytes 2359304 | tf_op jit(solution)/shard_map/ppermute | solution.py:363
  338.9 20.0 %collective-permute-start.45 = (bf16[192,2048]{1,0:T(8,128)(2,1)}, bf16[192,2048]{1,0:T(8,128)(2,1)}, u32[]{:S(2)}, u32[]{:S(2)}) collective-permute-start(bf16[192,2048]{1,0:T(8,128)(2,1)} %get-tuple-element.460), channel_id=1, source_target_pairs={{0,2},{2,0},{4,6},{6,4},{8,10},{10,8},{12,14},{14,12},{1,3},{3,1},... | collective-permute-start | bytes 2359304 | tf_op jit(solution)/shard_map/ppermute | solution.py:374
  338.9 28.9 %collective-permute-start.44 = (bf16[384,1536]{1,0:T(8,128)(2,1)}, bf16[384,1536]{1,0:T(8,128)(2,1)}, u32[]{:S(2)}, u32[]{:S(2)}) collective-permute-start(bf16[384,1536]{1,0:T(8,128)(2,1)} %add_convert_fusion.8), channel_id=1, source_target_pairs={{0,4},{2,6},{4,12},{6,14},{8,0},{10,2},{12,8},{14,10},{1,5},{3,7},... | collective-permute-start | bytes 3538952 | tf_op jit(solution)/shard_map/ppermute | solution.py:388
  339.4 30.7 %collective-permute-start.47 = (bf16[768,768]{1,0:T(8,128)(2,1)}, bf16[768,768]{1,0:T(8,128)(2,1)}, u32[]{:S(2)}, u32[]{:S(2)}) collective-permute-start(bf16[768,768]{1,0:T(8,128)(2,1)} %get-tuple-element.468), channel_id=1, source_target_pairs={{0,16},{3,19},{4,20},{7,23},{8,24},{11,27},{12,28},{15,31},{16,0},... | collective-permute-start | bytes 3538952 | tf_op jit(solution)/shard_map/ppermute | solution.py:370
  341.9 29.2 %collective-permute-start.48 = (bf16[768,768]{1,0:T(8,128)(2,1)}, bf16[768,768]{1,0:T(8,128)(2,1)}, u32[]{:S(2)}, u32[]{:S(2)}) collective-permute-start(bf16[768,768]{1,0:T(8,128)(2,1)} %add_convert_fusion.7), channel_id=1, source_target_pairs={{1,3},{2,0},{5,7},{6,4},{9,11},{10,8},{13,15},{14,12},{17,19},{18,... | collective-permute-start | bytes 3538952 | tf_op jit(solution)/shard_map/ppermute | solution.py:393
  372.1 28.8 %collective-permute-start.53 = (bf16[384,1536]{1,0:T(8,128)(2,1)S(1)}, bf16[384,1536]{1,0:T(8,128)(2,1)S(1)}, u32[]{:S(2)}, u32[]{:S(2)}) collective-permute-start(bf16[384,1536]{1,0:T(8,128)(2,1)S(1)} %add_convert_fusion.6), channel_id=1, source_target_pairs={{0,4},{2,6},{4,12},{6,14},{8,0},{10,2},{12,8},{14,10},{1,5},{3,7},... | collective-permute-start | bytes 3538952 | tf_op jit(solution)/shard_map/ppermute | solution.py:388
  372.2 20.2 %collective-permute-start.51 = (bf16[384,768]{1,0:T(8,128)(2,1)S(1)}, bf16[384,768]{1,0:T(8,128)(2,1)S(1)}, u32[]{:S(2)}, u32[]{:S(2)}) collective-permute-start(bf16[384,768]{1,0:T(8,128)(2,1)S(1)} %get-tuple-element.489), channel_id=1, source_target_pairs={{0,16},{3,19},{4,20},{7,23},{8,24},{11,27},{12,28},{15,31},{16,0},... | collective-permute-start | bytes 1769480 | tf_op jit(solution)/shard_map/ppermute | solution.py:370
  375.6 16.8 %collective-permute-start.52 = (bf16[384,768]{1,0:T(8,128)(2,1)S(1)}, bf16[384,768]{1,0:T(8,128)(2,1)S(1)}, u32[]{:S(2)}, u32[]{:S(2)}) collective-permute-start(bf16[384,768]{1,0:T(8,128)(2,1)S(1)} %add_convert_fusion.16), channel_id=1, source_target_pairs={{1,3},{2,0},{5,7},{6,4},{9,11},{10,8},{13,15},{14,12},{17,19},{18,... | collective-permute-start | bytes 1769480 | tf_op jit(solution)/shard_map/ppermute | solution.py:393
  381.8 19.1 %collective-permute-start.54 = (bf16[192,1536]{1,0:T(8,128)(2,1)S(1)}, bf16[192,1536]{1,0:T(8,128)(2,1)S(1)}, u32[]{:S(2)}, u32[]{:S(2)}) collective-permute-start(bf16[192,1536]{1,0:T(8,128)(2,1)S(1)} %get-tuple-element.493), channel_id=1, source_target_pairs={{0,16},{16,0},{1,17},{17,1},{2,18},{18,2},{3,19},{19,3},{4,20},{20... | collective-permute-start | bytes 1769480 | tf_op jit(solution)/shard_map/ppermute | solution.py:363
  401.4 15.5 %collective-permute-start.58 = (bf16[48,2048]{1,0:T(8,128)(2,1)S(1)}, bf16[48,2048]{1,0:T(8,128)(2,1)S(1)}, u32[]{:S(2)}, u32[]{:S(2)}) collective-permute-start(bf16[48,2048]{1,0:T(8,128)(2,1)S(1)} %get-tuple-element.500), channel_id=1, source_target_pairs={{0,8},{2,10},{4,12},{6,14},{8,0},{10,2},{12,4},{14,6},{1,9},{3,11}... | collective-permute-start | bytes 589832 | tf_op jit(solution)/shard_map/ppermute | solution.py:383
  403.2 13.8 %collective-permute-start.59 = (bf16[48,2048]{1,0:T(8,128)(2,1)S(1)}, bf16[48,2048]{1,0:T(8,128)(2,1)S(1)}, u32[]{:S(2)}, u32[]{:S(2)}) collective-permute-start(bf16[48,2048]{1,0:T(8,128)(2,1)S(1)} %get-tuple-element.501), channel_id=1, source_target_pairs={{0,12},{2,14},{4,8},{6,10},{8,4},{10,6},{12,0},{14,2},{1,13},{3,15... | collective-permute-start | bytes 589832 | tf_op jit(solution)/shard_map/ppermute | solution.py:383
  405.3 13.1 %collective-permute-start.56 = (bf16[192,1664]{1,0:T(8,128)(2,1)S(1)}, bf16[192,1664]{1,0:T(8,128)(2,1)S(1)}, u32[]{:S(2)}, u32[]{:S(2)}) collective-permute-start(bf16[192,1664]{1,0:T(8,128)(2,1)S(1)} %get-tuple-element.497), channel_id=1, source_target_pairs={{0,16},{16,0},{1,17},{17,1},{2,18},{18,2},{3,19},{19,3},{4,20},{20... | collective-permute-start | bytes 1916936 | tf_op jit(solution)/shard_map/ppermute | solution.py:363
  406.1 13.6 %collective-permute-start.55 = (bf16[192,1664]{1,0:T(8,128)(2,1)S(1)}, bf16[192,1664]{1,0:T(8,128)(2,1)S(1)}, u32[]{:S(2)}, u32[]{:S(2)}) collective-permute-start(bf16[192,1664]{1,0:T(8,128)(2,1)S(1)} %get-tuple-element.495), channel_id=1, source_target_pairs={{0,2},{2,0},{4,6},{6,4},{8,10},{10,8},{12,14},{14,12},{1,3},{3,1},... | collective-permute-start | bytes 1916936 | tf_op jit(solution)/shard_map/ppermute | solution.py:374
  421.9 15.6 %collective-permute-start.63 = (bf16[48,2048]{1,0:T(8,128)(2,1)S(1)}, bf16[48,2048]{1,0:T(8,128)(2,1)S(1)}, u32[]{:S(2)}, u32[]{:S(2)}) collective-permute-start(bf16[48,2048]{1,0:T(8,128)(2,1)S(1)} %add_convert_fusion.21), channel_id=1, source_target_pairs={{0,8},{2,10},{4,12},{6,14},{8,0},{10,2},{12,4},{14,6},{1,9},{3,11}... | collective-permute-start | bytes 589832 | tf_op jit(solution)/shard_map/ppermute | solution.py:383
  423.7 13.9 %collective-permute-start.64 = (bf16[48,2048]{1,0:T(8,128)(2,1)S(1)}, bf16[48,2048]{1,0:T(8,128)(2,1)S(1)}, u32[]{:S(2)}, u32[]{:S(2)}) collective-permute-start(bf16[48,2048]{1,0:T(8,128)(2,1)S(1)} %add_convert_fusion.21), channel_id=1, source_target_pairs={{0,12},{2,14},{4,8},{6,10},{8,4},{10,6},{12,0},{14,2},{1,13},{3,15... | collective-permute-start | bytes 589832 | tf_op jit(solution)/shard_map/ppermute | solution.py:383
  425.1 12.7 %collective-permute-start.61 = (bf16[96,1664]{1,0:T(8,128)(2,1)}, bf16[96,1664]{1,0:T(8,128)(2,1)S(1)}, u32[]{:S(2)}, u32[]{:S(2)}) collective-permute-start(bf16[96,1664]{1,0:T(8,128)(2,1)} %get-tuple-element.516), channel_id=1, source_target_pairs={{0,2},{2,0},{4,6},{6,4},{8,10},{10,8},{12,14},{14,12},{1,3},{3,1},... | collective-permute-start | bytes 958472 | tf_op jit(solution)/shard_map/ppermute | solution.py:374
  428.2 18.8 %collective-permute-start.65 = (bf16[192,1536]{1,0:T(8,128)(2,1)S(1)}, bf16[192,1536]{1,0:T(8,128)(2,1)S(1)}, u32[]{:S(2)}, u32[]{:S(2)}) collective-permute-start(bf16[192,1536]{1,0:T(8,128)(2,1)S(1)} %get-tuple-element.519), channel_id=1, source_target_pairs={{0,16},{16,0},{1,17},{17,1},{2,18},{18,2},{3,19},{19,3},{4,20},{20... | collective-permute-start | bytes 1769480 | tf_op jit(solution)/shard_map/ppermute | solution.py:363
  448.3 12.0 %collective-permute-start.67 = (bf16[48,1664]{1,0:T(8,128)(2,1)}, bf16[48,1664]{1,0:T(8,128)(2,1)}, u32[]{:S(2)}, u32[]{:S(2)}) collective-permute-start(bf16[48,1664]{1,0:T(8,128)(2,1)} %get-tuple-element.526), channel_id=1, source_target_pairs={{0,8},{2,10},{4,12},{6,14},{8,0},{10,2},{12,4},{14,6},{1,9},{3,11}... | collective-permute-start | bytes 479240 | tf_op jit(solution)/shard_map/ppermute | solution.py:383
  464.1 13.9 %collective-permute-start.72 = (bf16[48,1664]{1,0:T(8,128)(2,1)S(1)}, bf16[48,1664]{1,0:T(8,128)(2,1)S(1)}, u32[]{:S(2)}, u32[]{:S(2)}) collective-permute-start(bf16[48,1664]{1,0:T(8,128)(2,1)S(1)} %add_convert_fusion.22), channel_id=1, source_target_pairs={{0,8},{2,10},{4,12},{6,14},{8,0},{10,2},{12,4},{14,6},{1,9},{3,11}... | collective-permute-start | bytes 479240 | tf_op jit(solution)/shard_map/ppermute | solution.py:383
  465.3 12.7 %collective-permute-start.73 = (bf16[48,1664]{1,0:T(8,128)(2,1)S(1)}, bf16[48,1664]{1,0:T(8,128)(2,1)S(1)}, u32[]{:S(2)}, u32[]{:S(2)}) collective-permute-start(bf16[48,1664]{1,0:T(8,128)(2,1)S(1)} %add_convert_fusion.22), channel_id=1, source_target_pairs={{0,12},{2,14},{4,8},{6,10},{8,4},{10,6},{12,0},{14,2},{1,13},{3,15... | collective-permute-start | bytes 479240 | tf_op jit(solution)/shard_map/ppermute | solution.py:383
  466.7 17.9 %collective-permute-start.74 = (bf16[192,2048]{1,0:T(8,128)(2,1)S(1)}, bf16[192,2048]{1,0:T(8,128)(2,1)S(1)}, u32[]{:S(2)}, u32[]{:S(2)}) collective-permute-start(bf16[192,2048]{1,0:T(8,128)(2,1)S(1)} %maximum_select_fusion.4.refs_0_), channel_id=1, source_target_pairs={{0,2},{2,0},{4,6},{6,4},{8,10},{10,8},{12,14},{14,12},{1,3},{3,1},... | collective-permute-start | bytes 2359304 | tf_op jit(solution)/shard_map/ppermute | solution.py:374
  467.3 17.7 %collective-permute-start.75 = (bf16[192,2048]{1,0:T(8,128)(2,1)S(1)}, bf16[192,2048]{1,0:T(8,128)(2,1)S(1)}, u32[]{:S(2)}, u32[]{:S(2)}) collective-permute-start(bf16[192,2048]{1,0:T(8,128)(2,1)S(1)} %maximum_select_fusion.5.refs_2_), channel_id=1, source_target_pairs={{0,16},{16,0},{1,17},{17,1},{2,18},{18,2},{3,19},{19,3},{4,20},{20... | collective-permute-start | bytes 2359304 | tf_op jit(solution)/shard_map/ppermute | solution.py:363
  498.0 15.5 %collective-permute-start.80 = (bf16[192,1664]{1,0:T(8,128)(2,1)S(1)}, bf16[192,1664]{1,0:T(8,128)(2,1)S(1)}, u32[]{:S(2)}, u32[]{:S(2)}) collective-permute-start(bf16[192,1664]{1,0:T(8,128)(2,1)S(1)} %maximum_select_fusion.6.first), channel_id=1, source_target_pairs={{0,2},{2,0},{4,6},{6,4},{8,10},{10,8},{12,14},{14,12},{1,3},{3,1},... | collective-permute-start | bytes 1916936 | tf_op jit(solution)/shard_map/ppermute | solution.py:374
  498.6 15.2 %collective-permute-start.81 = (bf16[192,1664]{1,0:T(8,128)(2,1)S(1)}, bf16[192,1664]{1,0:T(8,128)(2,1)S(1)}, u32[]{:S(2)}, u32[]{:S(2)}) collective-permute-start(bf16[192,1664]{1,0:T(8,128)(2,1)S(1)} %maximum_select_fusion.7.second), channel_id=1, source_target_pairs={{0,16},{16,0},{1,17},{17,1},{2,18},{18,2},{3,19},{19,3},{4,20},{20... | collective-permute-start | bytes 1916936 | tf_op jit(solution)/shard_map/ppermute | solution.py:363
  (139 other events, 1130.0 us)
